TPU v7x, 32 devices: a whole 2x2x4 slice. The times are simulated.
32 devices in a mesh: grp: 2 (over y), row: 4 (over x, core), col: 4 (over z).
Axes of the slice: x: 2, y: 2, z: 4, core: 2. Of those that a mesh axis runs over, the one named last changes fastest.
Arguments:
- homolog_tensor: bfloat16 [16, 160, 256], P(('grp', 'row')), parts along dimension 0, may hold values from -6 to 6
- couple_tensor: bfloat16 [320, 160, 128], P(('grp', 'row'), 'col'), parts along dimension 0, may hold values from -6 to 6
- polymer_identity: int32 [320], P('grp'), parts along dimension 0, may hold values from 0 to 3, never falling along the last dimension, each value on 1 to 80 neighbouring positions
- couple_validity: int32 [320, 160], P(('grp', 'row'), 'col'), parts along dimension 0, may hold values 0 or 1
- intra_inter_bias: float32 [2, 128], replicated, may hold values from -6 to 6
- homolog_factor_kernels: bfloat16 [256, 64], replicated, may hold values from -0.375 to 0.375
- tensor_average_kernel: bfloat16 [1024, 128], replicated, may hold values from -1 to 1
- trilateral_input_kernels: bfloat16 [128, 512], replicated, may hold values from -0.5 to 0.5
- sigmoid_filter_kernel: bfloat16 [128, 128], replicated, may hold values from -0.5 to 0.5
- trilateral_final_kernel: bfloat16 [128, 128], replicated, may hold values from -0.5 to 0.5
Outputs:
- updated_pair: bfloat16 [320, 160, 128], P(('grp', 'row'), 'col'), parts along dimension 0
There are 2 independent parts, one for each index of `grp`. A program takes and returns all parts, laid end to end along the dimension named above; an argument that names none is the same for every part. Nothing has to cross between parts.
Inputs may be any that keep to these rules, and one draw needn't show every extreme that they name: `polymer_identity`: chain ids never fall along the residues; every chain holds 1 to 80 residues, one exactly that many.
All inputs are finite; a program needn't handle non-finite values. No bound on the sum of `couple_validity` on one device may be relied on, other than what follows from the above.
Results may differ from a plain program's by a relative error of at most 0.0075.
Values may be sent and summed in bfloat16 or wider, within the bound.
No kernel may reach another device: no remote copies, remote signals or barrier semaphores. Data moves between devices by JAX's collectives and lax.ppermute only.
A program may use at most 128 MiB of HBM per device.

v0:
```python
import math

import jax
import jax.numpy as jnp
from jax import lax
from jax.sharding import PartitionSpec as P

eps = 1e-05


def standardize_activations(values, mesh_axis):
    centre = values - jnp.mean(values, axis=mesh_axis, keepdims=True)
    spread = jnp.mean(centre * centre, axis=mesh_axis, keepdims=True)
    return centre * lax.rsqrt(spread + eps)


def project_alignment(residue_block, weight_matrix):
    normed = standardize_activations(residue_block.astype(jnp.float32), -1).astype(jnp.bfloat16)
    return jnp.einsum(
        "sic,cp->sip", normed, weight_matrix, preferred_element_type=jnp.float32
    ).astype(jnp.bfloat16)


def shards(
    homolog_tensor,
    couple_tensor,
    polymer_identity,
    couple_validity,
    intra_inter_bias,
    homolog_factor_kernels,
    tensor_average_kernel,
    trilateral_input_kernels,
    sigmoid_filter_kernel,
    trilateral_final_kernel,
):
    source_extent = couple_tensor.shape[0]
    target_extent = couple_tensor.shape[1]
    source_start_index = lax.axis_index("row") * source_extent
    target_start_index = lax.axis_index("col") * target_extent
    ids_rows = lax.dynamic_slice_in_dim(polymer_identity, source_start_index, source_extent, 0)
    ids_cols = lax.dynamic_slice_in_dim(polymer_identity, target_start_index, target_extent, 0)
    same_chain = (ids_rows[:, None] == ids_cols[None, :])[:, :, None]
    base = couple_tensor.astype(jnp.float32) + jnp.where(
        same_chain, intra_inter_bias[0], intra_inter_bias[1]
    )
    feature_width = homolog_factor_kernels.shape[1] // 2
    homolog_positions = lax.dynamic_slice_in_dim(
        homolog_tensor, target_start_index, target_extent, 1
    )
    complete_rows = lax.all_to_all(homolog_tensor, "row", split_axis=1, concat_axis=0, tiled=True)
    complete_columns = lax.all_gather(homolog_positions, "row", axis=0, tiled=True)
    alignment_left = project_alignment(complete_rows, homolog_factor_kernels[:, :feature_width])
    alignment_right = project_alignment(complete_columns, homolog_factor_kernels[:, feature_width:])
    sequence_total = alignment_left.shape[0]
    residue_block = math.gcd(source_extent, 8)
    left_block_list = jnp.transpose(
        alignment_left.reshape(
            sequence_total, source_extent // residue_block, residue_block, feature_width
        ),
        (1, 0, 2, 3),
    )

    def outer_rows(residue_slice):
        outer = (
            jnp.einsum(
                "ogy,owe->gwye", residue_slice, alignment_right, preferred_element_type=jnp.float32
            )
            / sequence_total
        )
        outer = outer.astype(jnp.bfloat16).reshape(
            residue_block, target_extent, feature_width * feature_width
        )
        return jnp.einsum(
            "ijf,fz->ijz", outer, tensor_average_kernel, preferred_element_type=jnp.float32
        )

    opm = lax.map(outer_rows, left_block_list).reshape(
        source_extent, target_extent, tensor_average_kernel.shape[1]
    )
    pair_sum = (base + opm).astype(jnp.bfloat16)
    pair_norm = standardize_activations(pair_sum.astype(jnp.float32), -1).astype(jnp.bfloat16)
    gate = jax.nn.sigmoid(
        jnp.einsum(
            "ijc,cd->ijd", pair_norm, sigmoid_filter_kernel, preferred_element_type=jnp.float32
        )
    )
    mask_wide = couple_validity.astype(jnp.float32)
    tri_width = trilateral_final_kernel.shape[0]
    projected = jnp.einsum(
        "ijc,cd->ijd", pair_norm, trilateral_input_kernels, preferred_element_type=jnp.float32
    )
    left = (
        mask_wide[:, :, None]
        * jax.nn.sigmoid(projected[:, :, :tri_width])
        * projected[:, :, tri_width : 2 * tri_width]
    ).astype(jnp.bfloat16)
    right = (
        mask_wide[:, :, None]
        * jax.nn.sigmoid(projected[:, :, 2 * tri_width : 3 * tri_width])
        * projected[:, :, 3 * tri_width :]
    ).astype(jnp.bfloat16)
    right_all = lax.all_gather(right, "row", axis=0, tiled=True)
    residue_slice = right_all
    summed = lax.psum_scatter(
        jnp.einsum("ikc,jkc->jic", left, residue_slice, preferred_element_type=jnp.float32).astype(
            jnp.bfloat16
        ),
        "col",
        scatter_dimension=0,
        tiled=True,
    ).astype(jnp.float32)
    mixed_norm = standardize_activations(jnp.swapaxes(summed, 0, 1), -1).astype(jnp.bfloat16)
    update = jnp.einsum(
        "ijc,cz->ijz", mixed_norm, trilateral_final_kernel, preferred_element_type=jnp.float32
    )
    result = pair_sum.astype(jnp.float32) + gate * update
    return result.astype(jnp.bfloat16)


def solution(mesh):
    placed = (
        P(("grp", "row"), None, None),
        P(("grp", "row"), "col", None),
        P("grp"),
        P(("grp", "row"), "col"),
        P(),
        P(),
        P(),
        P(),
        P(),
        P(),
    )
    return jax.shard_map(
        shards,
        mesh=mesh,
        in_specs=placed,
        out_specs=P(("grp", "row"), "col", None),
        check_vma=False,
    )
```

profile of v0, /device:TPU:0, one launch (start us, length us, event | category | flops | bytes accessed | tf_op | source)
XLA Modules:
  0.0 184.0 jit_solution(6844861872541203601)
XLA Ops:
  6.5 1.8 copy.144
  8.3 4.2 %all-to-all-start = ((bf16[2,160,256]{2,0,1:T(2,128)(2,1)}), bf16[2,160,256]{2,0,1:T(2,128)(2,1)S(1)}, u32[]{:S(2)}, u32[]{:S(2)}) async-start(bf16[2,160,256]{2,0,1:T(2,128)(2,1)} %copy.144), calls=%async_computation | async-start | bytes 327680 | tf_op jit(solution)/shard_map/all_to_all | solution.py:50
  12.5 0.0 all-gather.2.cloned.1.call-start
  12.5 0.8 constant_dynamic-slice_fusion
  13.3 5.9 %all_gather.6 = bf16[8,40,256]{2,1,0:T(8,128)(2,1)S(1)} all-gather(bf16[2,40,256]{2,1,0:T(8,128)(2,1)S(1)} %constant_dynamic-slice_fusion), channel_id=1, replica_groups=mesh['grp'=2,'row'=4,'col'=4] {'row'}, dimensions={0}, use_global_device_ids=true | all-gather | bytes 204800 | tf_op jit(solution)/shard_map/all_gather | solution.py:51
  19.2 0.1 convert_reduce_fusion.1
  19.4 0.2 fusion.33
  19.6 1.0 convolution_convert_fusion
  20.6 1.3 convert_element_type.88
  22.0 0.8 fusion.51
  22.8 0.7 broadcast_compare_fusion
  23.5 1.3 slice_bitcast_fusion.1
  24.8 0.0 all-to-all-done
  24.8 0.1 fusion.40
  24.9 0.2 multiply_reduce_fusion
  25.2 0.2 fusion.36
  25.4 0.2 convolution_convert_fusion.1
  25.6 0.2 copy.165
  25.7 63.8 %while.10 = (s32[]{:T(128)}, f32[5,8,40,128]{3,2,1,0:T(8,128)}, bf16[5,8,8,32]{3,1,2,0:T(8,128)(2,1)S(1)}, bf16[8,40,32]{1,0,2:T(8,128)(2,1)S(1)}, bf16[1024,128]{1,0:T(8,128)(2,1)}, /*index=5*/s32[]{:T(128)}) while((s32[]{:T(128)}, f32[5,8,40,128]{3,2,1,0:T(8,128)}, bf16[5,8,8,32]{3,1,2,0:T(8,128)(2,1)S(1)}, ...), condition=%wide.region_5.6_spmd, body=%wide.region_4.5_spmd.sunk | while | flops 89784320 | bytes 4440649 | solution.py:77
  25.8 2.1 %fusion.66 = bf16[8,40,32,32]{1,2,3,0:T(8,128)(2,1)} fusion(bf16[8,40,32]{1,0,2:T(8,128)(2,1)S(1)} %get-tuple-element.145, bf16[5,8,8,32]{3,1,2,0:T(8,128)(2,1)S(1)} %get-tuple-element.144, s32[]{:T(128)} %get-tuple-element.136), kind=kOutput, calls=%fused_computation.1.clone.1 | convolution fusion | flops 5898240 | bytes 737284 | tf_op jit(solution)/shard_map/while/body/eval_jaxpr/ogy,owe->gwye/dot_general | solution.py:65
  27.9 5.9 %copy.171 = bf16[8,40,32,32]{3,2,1,0:T(8,128)(2,1)S(1)} copy(bf16[8,40,32,32]{1,2,3,0:T(8,128)(2,1)} %fusion.66) | data formatting | bytes 1310720 | tf_op jit(solution)/shard_map/while/body/eval_jaxpr/convert_element_type | solution.py:70
  33.8 2.7 %reshape.122 = bf16[8,40,1024]{2,1,0:T(8,128)(2,1)S(1)} reshape(bf16[8,40,32,32]{3,2,1,0:T(8,128)(2,1)S(1)} %copy.171) | data formatting | bytes 1310720 | tf_op jit(solution)/shard_map/while/body/eval_jaxpr/reshape | solution.py:70
  36.5 2.0 %fusion.67 = f32[5,8,40,128]{3,2,1,0:T(8,128)} fusion(f32[5,8,40,128]{3,2,1,0:T(8,128)} %get-tuple-element.137, s32[]{:T(128)} %get-tuple-element.136, bf16[8,40,1024]{2,1,0:T(8,128)(2,1)S(1)} %reshape.122, bf16[1024,128]{1,0:T(8,128)(2,1)} %get-tuple-element.146), kind=kOutput, calls=%fused_computation.3.clone.1 | convolution fusion | flops 83886080 | bytes 1081856 | tf_op jit(solution)/shard_map/while/body/eval_jaxpr/ijf,fz->ijz/dot_general | solution.py:73
  38.5 2.1 %fusion.66 = bf16[8,40,32,32]{1,2,3,0:T(8,128)(2,1)} fusion(bf16[8,40,32]{1,0,2:T(8,128)(2,1)S(1)} %get-tuple-element.145, bf16[5,8,8,32]{3,1,2,0:T(8,128)(2,1)S(1)} %get-tuple-element.144, s32[]{:T(128)} %get-tuple-element.136), kind=kOutput, calls=%fused_computation.1.clone.1 | convolution fusion | flops 5898240 | bytes 737284 | tf_op jit(solution)/shard_map/while/body/eval_jaxpr/ogy,owe->gwye/dot_general | solution.py:65
  40.6 5.9 %copy.171 = bf16[8,40,32,32]{3,2,1,0:T(8,128)(2,1)S(1)} copy(bf16[8,40,32,32]{1,2,3,0:T(8,128)(2,1)} %fusion.66) | data formatting | bytes 1310720 | tf_op jit(solution)/shard_map/while/body/eval_jaxpr/convert_element_type | solution.py:70
  46.6 2.7 %reshape.122 = bf16[8,40,1024]{2,1,0:T(8,128)(2,1)S(1)} reshape(bf16[8,40,32,32]{3,2,1,0:T(8,128)(2,1)S(1)} %copy.171) | data formatting | bytes 1310720 | tf_op jit(solution)/shard_map/while/body/eval_jaxpr/reshape | solution.py:70
  49.3 2.0 %fusion.67 = f32[5,8,40,128]{3,2,1,0:T(8,128)} fusion(f32[5,8,40,128]{3,2,1,0:T(8,128)} %get-tuple-element.137, s32[]{:T(128)} %get-tuple-element.136, bf16[8,40,1024]{2,1,0:T(8,128)(2,1)S(1)} %reshape.122, bf16[1024,128]{1,0:T(8,128)(2,1)} %get-tuple-element.146), kind=kOutput, calls=%fused_computation.3.clone.1 | convolution fusion | flops 83886080 | bytes 1081856 | tf_op jit(solution)/shard_map/while/body/eval_jaxpr/ijf,fz->ijz/dot_general | solution.py:73
  51.3 2.1 %fusion.66 = bf16[8,40,32,32]{1,2,3,0:T(8,128)(2,1)} fusion(bf16[8,40,32]{1,0,2:T(8,128)(2,1)S(1)} %get-tuple-element.145, bf16[5,8,8,32]{3,1,2,0:T(8,128)(2,1)S(1)} %get-tuple-element.144, s32[]{:T(128)} %get-tuple-element.136), kind=kOutput, calls=%fused_computation.1.clone.1 | convolution fusion | flops 5898240 | bytes 737284 | tf_op jit(solution)/shard_map/while/body/eval_jaxpr/ogy,owe->gwye/dot_general | solution.py:65
  53.4 5.9 %copy.171 = bf16[8,40,32,32]{3,2,1,0:T(8,128)(2,1)S(1)} copy(bf16[8,40,32,32]{1,2,3,0:T(8,128)(2,1)} %fusion.66) | data formatting | bytes 1310720 | tf_op jit(solution)/shard_map/while/body/eval_jaxpr/convert_element_type | solution.py:70
  59.3 2.7 %reshape.122 = bf16[8,40,1024]{2,1,0:T(8,128)(2,1)S(1)} reshape(bf16[8,40,32,32]{3,2,1,0:T(8,128)(2,1)S(1)} %copy.171) | data formatting | bytes 1310720 | tf_op jit(solution)/shard_map/while/body/eval_jaxpr/reshape | solution.py:70
  62.1 2.0 %fusion.67 = f32[5,8,40,128]{3,2,1,0:T(8,128)} fusion(f32[5,8,40,128]{3,2,1,0:T(8,128)} %get-tuple-element.137, s32[]{:T(128)} %get-tuple-element.136, bf16[8,40,1024]{2,1,0:T(8,128)(2,1)S(1)} %reshape.122, bf16[1024,128]{1,0:T(8,128)(2,1)} %get-tuple-element.146), kind=kOutput, calls=%fused_computation.3.clone.1 | convolution fusion | flops 83886080 | bytes 1081856 | tf_op jit(solution)/shard_map/while/body/eval_jaxpr/ijf,fz->ijz/dot_general | solution.py:73
  64.0 2.1 %fusion.66 = bf16[8,40,32,32]{1,2,3,0:T(8,128)(2,1)} fusion(bf16[8,40,32]{1,0,2:T(8,128)(2,1)S(1)} %get-tuple-element.145, bf16[5,8,8,32]{3,1,2,0:T(8,128)(2,1)S(1)} %get-tuple-element.144, s32[]{:T(128)} %get-tuple-element.136), kind=kOutput, calls=%fused_computation.1.clone.1 | convolution fusion | flops 5898240 | bytes 737284 | tf_op jit(solution)/shard_map/while/body/eval_jaxpr/ogy,owe->gwye/dot_general | solution.py:65
  66.1 5.9 %copy.171 = bf16[8,40,32,32]{3,2,1,0:T(8,128)(2,1)S(1)} copy(bf16[8,40,32,32]{1,2,3,0:T(8,128)(2,1)} %fusion.66) | data formatting | bytes 1310720 | tf_op jit(solution)/shard_map/while/body/eval_jaxpr/convert_element_type | solution.py:70
  72.1 2.7 %reshape.122 = bf16[8,40,1024]{2,1,0:T(8,128)(2,1)S(1)} reshape(bf16[8,40,32,32]{3,2,1,0:T(8,128)(2,1)S(1)} %copy.171) | data formatting | bytes 1310720 | tf_op jit(solution)/shard_map/while/body/eval_jaxpr/reshape | solution.py:70
  74.8 2.0 %fusion.67 = f32[5,8,40,128]{3,2,1,0:T(8,128)} fusion(f32[5,8,40,128]{3,2,1,0:T(8,128)} %get-tuple-element.137, s32[]{:T(128)} %get-tuple-element.136, bf16[8,40,1024]{2,1,0:T(8,128)(2,1)S(1)} %reshape.122, bf16[1024,128]{1,0:T(8,128)(2,1)} %get-tuple-element.146), kind=kOutput, calls=%fused_computation.3.clone.1 | convolution fusion | flops 83886080 | bytes 1081856 | tf_op jit(solution)/shard_map/while/body/eval_jaxpr/ijf,fz->ijz/dot_general | solution.py:73
  76.8 2.1 %fusion.66 = bf16[8,40,32,32]{1,2,3,0:T(8,128)(2,1)} fusion(bf16[8,40,32]{1,0,2:T(8,128)(2,1)S(1)} %get-tuple-element.145, bf16[5,8,8,32]{3,1,2,0:T(8,128)(2,1)S(1)} %get-tuple-element.144, s32[]{:T(128)} %get-tuple-element.136), kind=kOutput, calls=%fused_computation.1.clone.1 | convolution fusion | flops 5898240 | bytes 737284 | tf_op jit(solution)/shard_map/while/body/eval_jaxpr/ogy,owe->gwye/dot_general | solution.py:65
  78.9 5.9 %copy.171 = bf16[8,40,32,32]{3,2,1,0:T(8,128)(2,1)S(1)} copy(bf16[8,40,32,32]{1,2,3,0:T(8,128)(2,1)} %fusion.66) | data formatting | bytes 1310720 | tf_op jit(solution)/shard_map/while/body/eval_jaxpr/convert_element_type | solution.py:70
  84.8 2.7 %reshape.122 = bf16[8,40,1024]{2,1,0:T(8,128)(2,1)S(1)} reshape(bf16[8,40,32,32]{3,2,1,0:T(8,128)(2,1)S(1)} %copy.171) | data formatting | bytes 1310720 | tf_op jit(solution)/shard_map/while/body/eval_jaxpr/reshape | solution.py:70
  87.6 2.0 %fusion.67 = f32[5,8,40,128]{3,2,1,0:T(8,128)} fusion(f32[5,8,40,128]{3,2,1,0:T(8,128)} %get-tuple-element.137, s32[]{:T(128)} %get-tuple-element.136, bf16[8,40,1024]{2,1,0:T(8,128)(2,1)S(1)} %reshape.122, bf16[1024,128]{1,0:T(8,128)(2,1)} %get-tuple-element.146), kind=kOutput, calls=%fused_computation.3.clone.1 | convolution fusion | flops 83886080 | bytes 1081856 | tf_op jit(solution)/shard_map/while/body/eval_jaxpr/ijf,fz->ijz/dot_general | solution.py:73
  89.5 1.6 bitcast_add_fusion
  91.1 0.3 convert_reduce_fusion
  91.4 0.5 fusion.14
  92.0 0.7 fusion.37
  92.7 1.2 fusion.16
  93.9 0.0 all-gather.2.cloned.1.call-update
  93.9 0.2 reduce-scatter.2.cloned.1.call-start
  94.2 2.0 %copy.157 = bf16[40,40,128]{1,0,2:T(8,128)(2,1)} copy(bf16[40,40,128]{2,1,0:T(8,128)(2,1)S(1)} %get-tuple-element.93) | data formatting | bytes 819200 | tf_op jit(solution)/shard_map/convert_element_type | solution.py:96
  96.2 19.9 %all-gather.2.cloned.1.call-done = bf16[160,40,128]{2,1,0:T(8,128)(2,1)} async-done(((bf16[40,40,128]{2,1,0:T(8,128)(2,1)}), bf16[160,40,128]{2,1,0:T(8,128)(2,1)}) %all-gather.2.cloned.1.call-update) | async-done | bytes 1638416 | tf_op jit(solution)/shard_map/all_gather | solution.py:102
  116.1 8.7 %copy.156 = bf16[160,40,128]{1,0,2:T(8,128)(2,1)} copy(bf16[160,40,128]{2,1,0:T(8,128)(2,1)} %all-gather.2.cloned.1.call-done) | data formatting | bytes 3276800 | tf_op jit(solution)/shard_map/all_gather | solution.py:102
  124.7 6.3 %convert_bitcast_fusion = bf16[160,40,128]{0,1,2:T(8,128)(2,1)S(1)} fusion(bf16[160,40,128]{1,0,2:T(8,128)(2,1)} %copy.156, bf16[40,40,128]{1,0,2:T(8,128)(2,1)} %copy.157), kind=kOutput, calls=%fused_computation.9 | convolution fusion | flops 66355200 | bytes 3686400 | tf_op jit(solution)/shard_map/ikc,jkc->jic/dot_general | solution.py:105
  131.1 0.0 copy-start.4
  131.1 3.8 %copy.158 = bf16[160,40,128]{2,1,0:T(8,128)(2,1)} copy(bf16[160,40,128]{0,1,2:T(8,128)(2,1)S(1)} %convert_bitcast_fusion) | data formatting | bytes 3276800 | tf_op jit(solution)/shard_map/convert_element_type | solution.py:105
  134.9 0.0 reduce-scatter.2.cloned.1.call-update
  134.9 0.0 copy-start.2
  134.9 0.9 fusion.10
  135.8 35.5 %reduce-scatter.2.cloned.1.call-done = bf16[40,40,128]{2,1,0:T(8,128)(2,1)} async-done(((bf16[160,40,128]{2,1,0:T(8,128)(2,1)}), bf16[40,40,128]{2,1,0:T(8,128)(2,1)}) %reduce-scatter.2.cloned.1.call-update) | async-done | bytes 409616 | tf_op jit(solution)/shard_map/reduce_scatter | solution.py:104
  171.3 1.3 bitcast_reduce_fusion
  172.6 0.1 copy.159
  172.7 0.1 copy.160
  172.8 1.5 fusion.28
  174.3 0.1 copy.161
  174.4 0.1 copy.162
  174.5 1.5 fusion.29
  176.0 1.1 fusion.11
  (23 shorter events, 0.2 us)
Async XLA Ops:
  6.5 85.4 %copy-start = (bf16[128,512]{1,0:T(8,128)(2,1)S(1)}, bf16[128,512]{1,0:T(8,128)(2,1)}, u32[]{:S(2)}) copy-start(bf16[128,512]{1,0:T(8,128)(2,1)} %param.19) | copy-start | bytes 393220
  6.5 18.9 %copy-start.3 = (bf16[256,64]{0,1:T(8,128)(2,1)S(1)}, bf16[256,64]{0,1:T(8,128)(2,1)}, u32[]{:S(2)}) copy-start(bf16[256,64]{0,1:T(8,128)(2,1)} %param.17) | copy-start | bytes 98308
  8.3 16.4 %all-to-all-start = ((bf16[2,160,256]{2,0,1:T(2,128)(2,1)}), bf16[2,160,256]{2,0,1:T(2,128)(2,1)S(1)}, u32[]{:S(2)}, u32[]{:S(2)}) async-start(bf16[2,160,256]{2,0,1:T(2,128)(2,1)} %copy.144), calls=%async_computation | async-start | bytes 327680 | tf_op jit(solution)/shard_map/all_to_all | solution.py:50
  12.5 103.5 %all-gather.2.cloned.1.call-start = ((), (), s32[]{:S(2)}) async-start(), calls=%async_computation.2 | async-start | bytes 2048000 | tf_op jit(solution)/shard_map/all_gather | solution.py:102
  89.5 3.1 %copy-start.1 = (f32[40,40]{1,0:T(8,128)S(1)}, f32[40,40]{1,0:T(8,128)}, u32[]{:S(2)}) copy-start(f32[40,40]{1,0:T(8,128)} %convert_element_type.88) | copy-start | bytes 19204
  93.9 77.4 %reduce-scatter.2.cloned.1.call-start = ((), (), s32[]{:S(2)}) async-start(), calls=%async_computation.3 | async-start | bytes 2048000 | tf_op jit(solution)/shard_map/reduce_scatter | solution.py:104
  131.1 3.8 %copy-start.4 = (bf16[128,128]{1,0:T(8,128)(2,1)S(1)}, bf16[128,128]{1,0:T(8,128)(2,1)}, u32[]{:S(2)}) copy-start(bf16[128,128]{1,0:T(8,128)(2,1)} %param.20) | copy-start | bytes 98308
  134.9 41.1 %copy-start.2 = (bf16[128,128]{1,0:T(8,128)(2,1)S(1)}, bf16[128,128]{1,0:T(8,128)(2,1)}, u32[]{:S(2)}) copy-start(bf16[128,128]{1,0:T(8,128)(2,1)} %param.21) | copy-start | bytes 98308
Sparse Core Ops, SparseCore 0:
  94.1 21.9 all-gather.1
  135.0 36.2 reduce-scatter.1
where the time goes:
time: 185 us; the launch traced here: 184 us
  local copies, waits for them, and re-layouts  63.1 us (34%)
  waiting for transfers between devices  55.4 us (30%)
  matrix products  30.6 us (17%)
  between operations  13.7 us (7%)
  other arithmetic  10.8 us (6%)
  blocking collectives  5.91 us (3%)
  starting transfers between devices  4.43 us (2%)
    reduce_scatter x1, waiting for transfers between devices, shards(): lax.psum_scatter(jnp.einsum('ikc,jkc->jic', left, residue_slice, preferre...  35.5 us
    convert_element_type x5, local copies, waits for them, and re-layouts, outer_rows(): outer.astype(jnp.bfloat16)  29.7 us
    all_gather x1, waiting for transfers between devices, shards(): right_all = lax.all_gather(right, 'row', axis=0, tiled=True)  19.9 us
    reshape x5, local copies, waits for them, and re-layouts, outer_rows(): outer.astype(jnp.bfloat16)  13.6 us
    dot_general x5, matrix products, outer_rows(): jnp.einsum('ogy,owe->gwye', residue_slice, alignment_right, preferred_ele...  10.5 us
    dot_general x5, matrix products, outer_rows(): jnp.einsum('ijf,fz->ijz', outer, tensor_average_kernel, preferred_element...  9.88 us
    all_gather x1, local copies, waits for them, and re-layouts, shards(): right_all = lax.all_gather(right, 'row', axis=0, tiled=True)  8.66 us
    dot_general x1, matrix products, shards(): jnp.einsum('ikc,jkc->jic', left, residue_slice, preferred_element_type=jn...  6.32 us
  transfers between devices with their start and end apart: 3, of which 2 were waited for; matrix products, arithmetic and copies ran while one was open for 5% of the time, Pallas kernels for 0%

commit v1 on v0

v1 whole, which is shorter than its diff:
```python
import functools

import jax
import jax.numpy as jnp
from jax import lax
from jax.experimental import pallas as pl
from jax.experimental.pallas import tpu as pltpu
from jax.sharding import PartitionSpec as P

eps = 1e-05
f32 = jnp.float32
bf16 = jnp.bfloat16
VMEM = pl.BlockSpec(memory_space=pltpu.VMEM)
SMEM = pl.BlockSpec(memory_space=pltpu.SMEM)
PARAMS = pltpu.CompilerParams(vmem_limit_bytes=56 * 1024 * 1024)


def round_up(n, m):
    return (n + m - 1) // m * m


def standardize(values):
    centre = values - jnp.mean(values, axis=-1, keepdims=True)
    spread = jnp.mean(centre * centre, axis=-1, keepdims=True)
    return centre * lax.rsqrt(spread + eps)


def sigmoid(v):
    return 0.5 * jnp.tanh(0.5 * v) + 0.5


def align_body(own_i, own_j, x_ref, w_ref, out_ref, y_ref):
    seqs, residues, depth = x_ref.shape
    width = w_ref.shape[1] // 2
    blocks, _, lanes = out_ref.shape
    at = round_up(own_i, 16)
    z = lax.axis_index("col")
    x = x_ref[...].astype(f32).reshape(seqs * residues, depth)
    normed = standardize(x).astype(bf16)
    y_ref[...] = jnp.dot(normed, w_ref[...], preferred_element_type=f32)
    start = pl.multiple_of(z * own_j, 8)
    right = [y_ref[pl.ds(s * residues + start, own_j), width:] for s in range(seqs)]
    pad = [jnp.zeros((own_j, lanes - seqs * width), f32)] if lanes > seqs * width else []
    right = jnp.concatenate(right + pad, axis=1).astype(bf16)
    for r in range(blocks):
        left = [y_ref[pl.ds(s * residues + r * own_i, own_i), :width] for s in range(seqs)]
        pad = [jnp.zeros((own_i, lanes - seqs * width), f32)] if lanes > seqs * width else []
        out_ref[r, pl.ds(0, own_i), :] = jnp.concatenate(left + pad, axis=1).astype(bf16)
        out_ref[r, pl.ds(at, own_j), :] = right


def pair_body(
    seqs,
    width,
    msg_ref,
    couple_ref,
    ids_ref,
    valid_ref,
    bias_ref,
    avg_ref,
    win_ref,
    wgate_ref,
    left_ref,
    right_ref,
    psum_ref,
    gate_ref,
    xl_ref,
    t_ref,
    wf_ref,
    idc_ref,
):
    own_i, own_j, chans = couple_ref.shape
    blocks, _, lanes = msg_ref.shape
    total = seqs * blocks
    at = round_up(own_i, 16)
    x0 = lax.axis_index("row") * own_i
    z0 = lax.axis_index("col") * own_j
    tri = win_ref.shape[1] // 4

    for r in range(blocks):
        m = msg_ref[r, pl.ds(0, own_i), :].astype(f32)
        for s in range(seqs):
            turned = m if s == 0 else pltpu.roll(m, lanes - s * width, 1)
            xl_ref[pl.ds(r * seqs + s, own_i, stride=total), :] = turned[:, :128]
    lhs = xl_ref[:, :width].astype(bf16)

    row = lax.broadcasted_iota(jnp.int32, (lanes, width * total), 0)
    col = lax.broadcasted_iota(jnp.int32, (lanes, width * total), 1)
    place = (row % width) * total + row // width
    rmat = jnp.zeros((own_j, width * total), f32)
    for r in range(blocks):
        pick = (col == place + r * seqs) & (row < seqs * width)
        pick = jnp.where(pick, 1.0, 0.0).astype(bf16)
        rmat += jnp.dot(msg_ref[r, pl.ds(at, own_j), :], pick, preferred_element_type=f32)
    rmat = rmat.astype(bf16)

    wf_ref[...] = avg_ref[...].astype(f32)

    def expand(h, carry):
        q = h * 2
        both = [wf_ref[pl.ds(q + d, width, stride=width), :] for d in range(2)]
        rhs = jnp.concatenate(both, axis=1).astype(bf16)
        out = jnp.dot(lhs, rhs, preferred_element_type=f32)
        parts = [out[:, d * chans : (d + 1) * chans].reshape(own_i, total, chans) for d in range(2)]
        block = jnp.concatenate(parts, axis=1).astype(bf16)
        t_ref[:, pl.ds(pl.multiple_of(q * total, 16), 2 * total), :] = block
        return carry

    lax.fori_loop(0, width // 2, expand, 0)

    for j in range(own_j):
        idc_ref[pl.ds(j, 1), :] = jnp.full((1, chans), ids_ref[z0 + j], jnp.int32)
    idc = idc_ref[...]
    valid_t = valid_ref[...].astype(f32).T
    lane = lax.broadcasted_iota(jnp.int32, valid_t.shape, 1)
    same_bias = bias_ref[0:1, :]
    cross_bias = bias_ref[1:2, :]
    group = 8 if own_i % 8 == 0 else 1

    def rows(b, carry):
        i0 = b * group
        normed = []
        masks = []
        for g in range(group):
            i = i0 + g
            opm = jnp.dot(rmat, t_ref[i], preferred_element_type=f32) * (1.0 / total)
            base = couple_ref[i].astype(f32) + jnp.where(idc == ids_ref[x0 + i], same_bias, cross_bias)
            psum = (base + opm).astype(bf16)
            psum_ref[i] = psum
            normed.append(standardize(psum.astype(f32)))
            masks.append(jnp.sum(jnp.where(lane == i, valid_t, 0.0), axis=1, keepdims=True))
        flat = jnp.concatenate(normed, axis=0).astype(bf16)
        mask = jnp.concatenate(masks, axis=0)
        proj = jnp.dot(flat, win_ref[...], preferred_element_type=f32)
        left = mask * sigmoid(proj[:, :tri]) * proj[:, tri : 2 * tri]
        right = mask * sigmoid(proj[:, 2 * tri : 3 * tri]) * proj[:, 3 * tri :]
        gate = sigmoid(jnp.dot(flat, wgate_ref[...], preferred_element_type=f32))
        left_ref[pl.ds(i0, group)] = left.reshape(group, own_j, tri).astype(bf16)
        right_ref[pl.ds(i0, group)] = right.reshape(group, own_j, tri).astype(bf16)
        gate_ref[pl.ds(i0, group)] = gate.reshape(group, own_j, chans)
        return carry

    lax.fori_loop(0, own_i // group, rows, 0)


def contract(lf_ref, rk_ref, i0, group, depth, init):
    step = 8

    def add(kb, acc):
        k0 = pl.multiple_of(kb * step, step)
        lefts = [lf_ref[i0 + t, pl.ds(k0, step), :] for t in range(group)]
        acc = list(acc)
        for d in range(step):
            right = rk_ref[k0 + d]
            for t in range(group):
                acc[t] = acc[t] + lefts[t][d : d + 1, :] * right
        return tuple(acc)

    return lax.fori_loop(0, depth // step, add, tuple(init))


def spread_right(r_ref, flat_ref, rk_ref):
    extent, depth, _ = r_ref.shape

    def widen(j, carry):
        flat_ref[pl.ds(pl.multiple_of(j * depth, 8), depth), :] = r_ref[j].astype(f32)
        return carry

    lax.fori_loop(0, extent, widen, 0, unroll=4)

    def turn(k, carry):
        rk_ref[k] = flat_ref[pl.ds(k, extent, stride=depth), :]
        return carry

    lax.fori_loop(0, depth, turn, 0, unroll=4)


def triangle_body(l_ref, r_ref, o_ref, lf_ref, flat_ref, rk_ref):
    own_i, depth, chans = l_ref.shape
    extent = r_ref.shape[0]
    group = 8 if own_i % 8 == 0 else 1

    @pl.when(pl.program_id(0) == 0)
    def _():
        lf_ref[...] = l_ref[...].astype(f32)

    spread_right(r_ref, flat_ref, rk_ref)

    def rows(b, carry):
        i0 = b * group
        zero = [jnp.zeros((extent, chans), f32) for _ in range(group)]
        acc = contract(lf_ref, rk_ref, i0, group, depth, zero)
        for t in range(group):
            o_ref[0, i0 + t] = acc[t].astype(bf16)
        return carry

    lax.fori_loop(0, own_i // group, rows, 0)


def finish_body(sum_ref, psum_ref, gate_ref, w_ref, out_ref):
    parts, own_i, extent, chans = sum_ref.shape
    group = 8 if own_i % 8 == 0 else 1

    def rows(b, carry):
        i0 = b * group
        for part in range(parts):
            cut = pl.ds(part * extent, extent)
            mixed = sum_ref[part, pl.ds(i0, group)].astype(f32)
            normed = standardize(mixed).reshape(group * extent, chans).astype(bf16)
            update = jnp.dot(normed, w_ref[...], preferred_element_type=f32).reshape(group, extent, -1)
            base = psum_ref[pl.ds(i0, group), cut, :].astype(f32)
            gate = gate_ref[pl.ds(i0, group), cut, :]
            out_ref[pl.ds(i0, group), cut, :] = (base + gate * update).astype(bf16)
        return carry

    lax.fori_loop(0, own_i // group, rows, 0)


def shards(homolog, couple, ids, valid, bias, factors, average, w_in, w_gate, w_final):
    rows, cols = lax.axis_size("row"), lax.axis_size("col")
    own_seqs, residues, depth = homolog.shape
    own_i, own_j, chans = couple.shape
    width = factors.shape[1] // 2
    tri = w_final.shape[0]
    total = own_seqs * rows
    lanes = round_up(own_seqs * width, 128)
    height = round_up(own_i, 16) + round_up(own_j, 16)

    msg = pl.pallas_call(
        functools.partial(align_body, own_i, own_j),
        out_shape=jax.ShapeDtypeStruct((rows, height, lanes), bf16),
        in_specs=[VMEM] * 2,
        out_specs=VMEM,
        scratch_shapes=[pltpu.VMEM((own_seqs * residues, 2 * width), f32)],
        compiler_params=PARAMS,
        name="align",
    )(homolog, factors)
    msg = lax.all_to_all(msg, "row", split_axis=0, concat_axis=0, tiled=True)

    block = jax.ShapeDtypeStruct((own_i, own_j, tri), bf16)
    left, right, psum, gate = pl.pallas_call(
        functools.partial(pair_body, own_seqs, width),
        out_shape=[block, block, jax.ShapeDtypeStruct((own_i, own_j, chans), bf16),
                   jax.ShapeDtypeStruct((own_i, own_j, chans), f32)],
        in_specs=[VMEM, VMEM, SMEM, VMEM, VMEM, VMEM, VMEM, VMEM],
        out_specs=[VMEM] * 4,
        scratch_shapes=[
            pltpu.VMEM((own_i * total, 128), f32),
            pltpu.VMEM((own_i, width * total, chans), bf16),
            pltpu.VMEM((width * width, chans), f32),
            pltpu.VMEM((own_j, chans), jnp.int32),
        ],
        compiler_params=PARAMS,
        name="pair",
    )(msg, couple, ids, valid, bias, average, w_in, w_gate)

    right_all = lax.all_gather(right, "row", axis=0, tiled=True)
    partial = pl.pallas_call(
        triangle_body,
        grid=(rows,),
        out_shape=jax.ShapeDtypeStruct((rows, own_i, own_i, tri), bf16),
        in_specs=[
            pl.BlockSpec((own_i, own_j, tri), lambda r: (0, 0, 0)),
            pl.BlockSpec((own_i, own_j, tri), lambda r: (r, 0, 0)),
        ],
        out_specs=pl.BlockSpec((1, own_i, own_i, tri), lambda r: (r, 0, 0, 0)),
        scratch_shapes=[
            pltpu.VMEM((own_i, own_j, tri), f32),
            pltpu.VMEM((own_i * own_j, tri), f32),
            pltpu.VMEM((own_j, own_i, tri), f32),
        ],
        compiler_params=PARAMS,
        name="triangle",
    )(left, right_all)
    summed = lax.psum_scatter(partial, "col", scatter_dimension=0, tiled=True)
    return pl.pallas_call(
        finish_body,
        out_shape=jax.ShapeDtypeStruct((own_i, own_j, chans), bf16),
        in_specs=[VMEM] * 4,
        out_specs=VMEM,
        compiler_params=PARAMS,
        name="finish",
    )(summed, psum, gate, w_final)


def solution(mesh):
    placed = (
        P(("grp", "row"), None, None),
        P(("grp", "row"), "col", None),
        P("grp"),
        P(("grp", "row"), "col"),
        P(),
        P(),
        P(),
        P(),
        P(),
        P(),
    )
    return jax.shard_map(
        shards,
        mesh=mesh,
        in_specs=placed,
        out_specs=P(("grp", "row"), "col", None),
        check_vma=False,
    )
```

time: 185 us -> 110 us (0.59)
  local copies, waits for them, and re-layouts: 63.1 us -> 1.48 us
  matrix products: 30.6 us -> 0 us
  Pallas kernels: 0 us -> 28.1 us
  other arithmetic: 10.8 us -> 0 us
  starting transfers between devices: 4.43 us -> 0.04 us
  blocking collectives: 5.91 us -> 9.22 us
  waiting for transfers between devices: 55.4 us -> 57.4 us
    convert_element_type x8 -> x0, local copies, waits for them, and re-layouts: 35.5 us -> none  [the longest x5 29.7 us: outer_rows(): outer.astype(jnp.bfloat16)]
    dot_general x16 -> x0, matrix products: 30.6 us -> none  [the longest x5 10.5 us: outer_rows(): jnp.einsum('ogy,owe->gwye', residue_slice, alignment_right, preferred_ele...]
    pallas_call x0 -> x4, Pallas kernels: none -> 28.1 us  [the longest x1 13.2 us: shards(): pl.pallas_call(triangle_body, grid=(rows,), out_shape=jax.ShapeDtypeStruc...]
    reshape x5 -> x0, local copies, waits for them, and re-layouts: 13.6 us -> none  [outer_rows(): outer.astype(jnp.bfloat16)]
    all_to_all x0 -> x1, blocking collectives: none -> 9.22 us  [shards(): msg = lax.all_to_all(msg, 'row', split_axis=0, concat_axis=0, tiled=True)]
    all_gather x1 -> x0, local copies, waits for them, and re-layouts: 8.66 us -> none  [shards(): right_all = lax.all_gather(right, 'row', axis=0, tiled=True)]
    all_gather x1 -> x0, blocking collectives: 5.91 us -> none  [shards(): lax.all_gather(homolog_positions, 'row', axis=0, tiled=True)]
    convert_element_type x5 -> x0, other arithmetic: 4.24 us -> none  [the longest x1 1.5 us: shards(): standardize_activations(jnp.swapaxes(summed, 0, 1), -1).astype(jnp.bfloat16)]
  transfers between devices with their start and end apart: 3 -> 2, of which waited for: 2 -> 2; matrix products, arithmetic and copies ran while one was open for 5% -> 0% of each run, Pallas kernels for 0% -> 0%
where the time goes in v1:
time: 110 us
  waiting for transfers between devices  57.4 us (52%)
  Pallas kernels  28.1 us (26%)
  between operations  13.4 us (12%)
  blocking collectives  9.22 us (8%)
  local copies, waits for them, and re-layouts  1.48 us (1%)
    reduce_scatter x1, waiting for transfers between devices, shards(): summed = lax.psum_scatter(partial, 'col', scatter_dimension=0, tiled=True)  36.5 us
    all_gather x1, waiting for transfers between devices, shards(): right_all = lax.all_gather(right, 'row', axis=0, tiled=True)  20.9 us
    pallas_call x1, Pallas kernels, shards(): pl.pallas_call(triangle_body, grid=(rows,), out_shape=jax.ShapeDtypeStruc...  13.2 us
    all_to_all x1, blocking collectives, shards(): msg = lax.all_to_all(msg, 'row', split_axis=0, concat_axis=0, tiled=True)  9.22 us
    pallas_call x1, Pallas kernels, shards(): pl.pallas_call(functools.partial(pair_body, own_seqs, width), out_shape=[...  9.13 us
    pallas_call x1, Pallas kernels, shards(): pl.pallas_call(finish_body, out_shape=jax.ShapeDtypeStruct((own_i, own_j,...  3.81 us
  transfers between devices with their start and end apart: 2, of which 2 were waited for; matrix products, arithmetic and copies ran while one was open for 0% of the time, Pallas kernels for 0%

profile of v1, /device:TPU:0, one launch (start us, length us, event | category | flops | bytes accessed | tf_op | source)
XLA Modules:
  0.0 109.7 jit_solution(7875845827816766668)
XLA Ops:
  6.5 0.0 all-gather.2.cloned.1.call-start
  6.5 1.5 %copy.12.w_ref = bf16[256,64]{1,0:T(8,128)(2,1)} copy(bf16[256,64]{0,1:T(8,128)(2,1)} %param.15) | data formatting | bytes 65536 | tf_op args[5]
  8.0 2.0 %align.1 = bf16[4,96,128]{2,1,0:T(8,128)(2,1)} custom-call(bf16[2,160,256]{2,1,0:T(8,128)(2,1)} %x_ref.1, bf16[256,64]{1,0:T(8,128)(2,1)} %copy.12.w_ref), custom_call_target="tpu_custom_call" | custom-call | tf_op jit(solution)/shard_map/align/pallas_call | solution.py:229
  10.0 9.2 %all_to_all.5.msg_ref = bf16[4,96,128]{2,1,0:T(8,128)(2,1)} all-to-all(bf16[4,96,128]{2,1,0:T(8,128)(2,1)} %align.1), channel_id=1, replica_groups=mesh['grp'=2,'row'=4,'col'=4] {'row'}, dimensions={0} | all-to-all | bytes 196608 | tf_op jit(solution)/shard_map/all_to_all | solution.py:238
  19.2 9.1 %pair.1 = (bf16[40,40,128]{2,1,0:T(8,128)(2,1)}, bf16[40,40,128]{2,1,0:T(8,128)(2,1)}, bf16[40,40,128]{2,1,0:T(8,128)(2,1)}, f32[40,40,128]{2,1,0:T(8,128)}) custom-call(bf16[4,96,128]{2,1,0:T(8,128)(2,1)} %all_to_all.5.msg_ref, bf16[40,40,128]{2,1,0:T(8,128)(2,1)} %couple_ref.1, s32[160]{0:T(256)} %ids_ref.1, s32[40,40]{1,0:T(8,128)} %valid_ref.1, ...), custom_call_target="tpu_custom_call" | custom-call | tf_op jit(solution)/shard_map/pair/pallas_call | solution.py:241
  28.4 0.0 all-gather.2.cloned.1.call-update
  28.4 0.0 reduce-scatter.2.cloned.1.call-start
  28.4 20.9 %all-gather.2.cloned.1.call-done.r_ref = bf16[160,40,128]{2,1,0:T(8,128)(2,1)} async-done(((bf16[40,40,128]{2,1,0:T(8,128)(2,1)}), bf16[160,40,128]{2,1,0:T(8,128)(2,1)}) %all-gather.2.cloned.1.call-update) | async-done | bytes 1638416 | tf_op jit(solution)/shard_map/all_gather | solution.py:257
  49.4 13.2 %triangle.1 = bf16[4,40,40,128]{3,2,1,0:T(8,128)(2,1)} custom-call(bf16[40,40,128]{2,1,0:T(8,128)(2,1)} %get-tuple-element.9.l_ref, bf16[160,40,128]{2,1,0:T(8,128)(2,1)} %all-gather.2.cloned.1.call-done.r_ref), custom_call_target="tpu_custom_call" | custom-call | tf_op jit(solution)/shard_map/triangle/pallas_call | solution.py:258
  62.5 0.0 reduce-scatter.2.cloned.1.call-update
  62.5 36.5 %reduce-scatter.2.cloned.1.call-done.sum_ref = bf16[1,40,40,128]{3,2,1,0:T(8,128)(2,1)} async-done(((bf16[4,40,40,128]{3,2,1,0:T(8,128)(2,1)}), bf16[1,40,40,128]{3,2,1,0:T(8,128)(2,1)}) %reduce-scatter.2.cloned.1.call-update) | async-done | bytes 409616 | tf_op jit(solution)/shard_map/reduce_scatter | solution.py:275
  99.0 3.8 %finish.1 = bf16[40,40,128]{2,1,0:T(8,128)(2,1)} custom-call(bf16[1,40,40,128]{3,2,1,0:T(8,128)(2,1)} %reduce-scatter.2.cloned.1.call-done.sum_ref, bf16[40,40,128]{2,1,0:T(8,128)(2,1)} %get-tuple-element.11.psum_ref, f32[40,40,128]{2,1,0:T(8,128)} %get-tuple-element.12.gate_ref, bf16[128,128]{1,0:T(8,128)(2,1)} %w_ref.2), custom_call_target="tpu_custom_call" | custom-call | tf_op jit(solution)/shard_map/finish/pallas_call | solution.py:276
Async XLA Ops:
  6.5 42.8 %all-gather.2.cloned.1.call-start = ((), (), s32[]{:S(2)}) async-start(), calls=%async_computation.2 | async-start | bytes 2048000 | tf_op jit(solution)/shard_map/all_gather | solution.py:257
  28.4 70.6 %reduce-scatter.2.cloned.1.call-start = ((), (), s32[]{:S(2)}) async-start(), calls=%async_computation.3 | async-start | bytes 2048000 | tf_op jit(solution)/shard_map/reduce_scatter | solution.py:275
Sparse Core Ops, SparseCore 0:
  28.5 20.8 all-gather.1
  62.7 36.2 reduce-scatter.1

commit v2 on v1

v2 whole, which is shorter than its diff:
```python
import functools

import jax
import jax.numpy as jnp
from jax import lax
from jax.experimental import pallas as pl
from jax.experimental.pallas import tpu as pltpu
from jax.sharding import PartitionSpec as P

eps = 1e-05
f32 = jnp.float32
bf16 = jnp.bfloat16
VMEM = pl.BlockSpec(memory_space=pltpu.VMEM)
SMEM = pl.BlockSpec(memory_space=pltpu.SMEM)
ANY = pl.BlockSpec(memory_space=pl.ANY)


def limit(mib, scale=1):
    return pltpu.CompilerParams(vmem_limit_bytes=min(56, mib * scale) * 1024 * 1024)


def round_up(n, m):
    return (n + m - 1) // m * m


def standardize(values):
    centre = values - jnp.mean(values, axis=-1, keepdims=True)
    spread = jnp.mean(centre * centre, axis=-1, keepdims=True)
    return centre * lax.rsqrt(spread + eps)


def sigmoid(v):
    return 0.5 * jnp.tanh(0.5 * v) + 0.5


def align_body(own_i, own_j, x_ref, w_ref, *refs):
    outs, y_ref = refs[:-1], refs[-1]
    seqs, residues, depth = x_ref.shape
    width = w_ref.shape[0] // 2
    height, lanes = outs[0].shape
    me = lax.axis_index("row")
    z = lax.axis_index("col")
    x = x_ref[...].astype(f32).reshape(seqs * residues, depth)
    normed = standardize(x).astype(bf16)
    y_ref[...] = lax.dot_general(
        normed, w_ref[...], (((1,), (1,)), ((), ())), preferred_element_type=f32
    )
    start = pl.multiple_of(z * own_j, 8)
    extent = max(own_i, own_j)

    def tall(v):
        gap = extent - v.shape[0]
        return jnp.concatenate([v, jnp.zeros((gap, v.shape[1]), f32)], axis=0) if gap else v

    right = [tall(y_ref[pl.ds(s * residues + start, own_j), width:]) for s in range(seqs)]
    gap = lanes - 2 * seqs * width
    right += [jnp.zeros((extent, gap), f32)] if gap else []
    for d, out in enumerate(outs):
        first = pl.multiple_of((me ^ d) * own_i, 8)
        left = [tall(y_ref[pl.ds(s * residues + first, own_i), :width]) for s in range(seqs)]
        out[pl.ds(0, extent), :] = jnp.concatenate(left + right, axis=1).astype(bf16)


def prepare_body(couple_ref, ids_ref, valid_ref, bias_ref, avg_ref, base_ref, mask_ref, wq_ref, wf_ref, idc_ref):
    own_i, own_j, chans = couple_ref.shape
    pairs, width, _ = wq_ref.shape
    x0 = lax.axis_index("row") * own_i
    z0 = lax.axis_index("col") * own_j
    wf_ref[...] = avg_ref[...].astype(f32)
    for h in range(pairs):
        both = [wf_ref[pl.ds(2 * h + d, width, stride=width), :] for d in range(2)]
        wq_ref[h] = jnp.concatenate(both, axis=1).astype(bf16)
    for j in range(own_j):
        idc_ref[pl.ds(j, 1), :] = jnp.full((1, chans), ids_ref[z0 + j], jnp.int32)
    idc = idc_ref[...]
    valid_t = valid_ref[...].astype(f32).T
    lane = lax.broadcasted_iota(jnp.int32, valid_t.shape, 1)
    same_bias = bias_ref[0:1, :]
    cross_bias = bias_ref[1:2, :]

    def row(i, carry):
        bias = jnp.where(idc == ids_ref[x0 + i], same_bias, cross_bias)
        base_ref[i] = couple_ref[i].astype(f32) + bias
        column = jnp.sum(jnp.where(lane == i, valid_t, 0.0), axis=1, keepdims=True)
        mask_ref[i] = jnp.broadcast_to(column, (own_j, mask_ref.shape[2])).astype(bf16)
        return carry

    lax.fori_loop(0, own_i, row, 0, unroll=4)


def pair_body(seqs, width, turned, *refs):
    blocks = len(refs) - 10
    msgs = refs[:blocks]
    base_ref, mask_ref, wq_ref, win_ref = refs[blocks : blocks + 4]
    psum_ref, norm_ref, right_ref = refs[blocks + 4 : blocks + 7]
    xl_ref, t_ref, flat_ref = refs[blocks + 7 :]
    own_i, own_j, chans = base_ref.shape
    height, lanes = msgs[0].shape
    total = seqs * blocks
    tri = win_ref.shape[1] // 4

    for r in range(blocks):
        m = msgs[r][pl.ds(0, own_i), :].astype(f32)
        for s in range(seqs):
            moved = m if s == 0 else pltpu.roll(m, lanes - s * width, 1)
            xl_ref[pl.ds(r * seqs + s, own_i, stride=total), :] = moved[:, :128]
    lhs = xl_ref[:, :width].astype(bf16)

    row = lax.broadcasted_iota(jnp.int32, (lanes, width * total), 0)
    col = lax.broadcasted_iota(jnp.int32, (lanes, width * total), 1)
    unit = row - seqs * width
    place = (unit % width) * total + unit // width
    inside = (unit >= 0) & (unit < seqs * width)
    rmat = jnp.zeros((own_j, width * total), f32)
    for r in range(blocks):
        pick = jnp.where((col == place + r * seqs) & inside, 1.0, 0.0).astype(bf16)
        rmat += jnp.dot(msgs[r][pl.ds(0, own_j), :], pick, preferred_element_type=f32)
    rmat = rmat.astype(bf16)

    def expand(h, carry):
        out = jnp.dot(lhs, wq_ref[h], preferred_element_type=f32)
        parts = [out[:, d * chans : (d + 1) * chans].reshape(own_i, total, chans) for d in range(2)]
        block = jnp.concatenate(parts, axis=1).astype(bf16)
        t_ref[:, pl.ds(pl.multiple_of(h * 2 * total, 16), 2 * total), :] = block
        return carry

    lax.fori_loop(0, width // 2, expand, 0, unroll=2)

    group = 8 if own_i % 8 == 0 else 1

    def rows(b, carry):
        i0 = b * group
        normed = []
        for g in range(group):
            i = i0 + g
            opm = jnp.dot(rmat, t_ref[i], preferred_element_type=f32) * (1.0 / total)
            psum = (base_ref[i] + opm).astype(bf16)
            psum_ref[i] = psum
            normed.append(standardize(psum.astype(f32)))
        flat = jnp.concatenate(normed, axis=0).astype(bf16)
        norm_ref[pl.ds(pl.multiple_of(i0 * own_j, 16), group * own_j), :] = flat
        mask = mask_ref[pl.ds(i0, group)].astype(f32).reshape(group * own_j, tri)
        proj = jnp.dot(flat, win_ref[:, 2 * tri :], preferred_element_type=f32)
        right = mask * sigmoid(proj[:, :tri]) * proj[:, tri:]
        if turned:
            flat_ref[pl.ds(pl.multiple_of(i0 * own_j, 8), group * own_j), :] = right
        else:
            right_ref[pl.ds(i0, group)] = right.reshape(group, own_j, tri).astype(bf16)
        return carry

    lax.fori_loop(0, own_i // group, rows, 0)

    def turn(k, carry):
        right_ref[k] = flat_ref[pl.ds(k, own_i, stride=own_j), :].astype(bf16)
        return carry

    if turned:
        lax.fori_loop(0, own_j, turn, 0, unroll=8)


def left_body(norm_ref, mask_ref, win_ref, *outs):
    own_i, own_j, tri = mask_ref.shape
    group = 8 if own_i % 8 == 0 else 1
    at = 0
    for out in outs:
        first = at

        def rows(b, carry):
            i0 = first + b * group
            flat = norm_ref[pl.ds(pl.multiple_of(i0 * own_j, 16), group * own_j), :]
            mask = mask_ref[pl.ds(i0, group)].astype(f32).reshape(group * own_j, tri)
            proj = jnp.dot(flat, win_ref[:, : 2 * tri], preferred_element_type=f32)
            left = mask * sigmoid(proj[:, :tri]) * proj[:, tri:]
            out[pl.ds(b * group, group)] = left.reshape(group, own_j, tri).astype(bf16)
            return carry

        lax.fori_loop(0, out.shape[0] // group, rows, 0)
        at += out.shape[0]


def contract(lf_ref, rk_ref, i0, group, depth):
    step = 8

    def add(kb, acc):
        k0 = pl.multiple_of(kb * step, step)
        acc = list(acc)
        for d in range(step):
            right = rk_ref[k0 + d].astype(f32)
            for t in range(group):
                acc[t] = acc[t] + lf_ref[i0 + t, pl.ds(k0 + d, 1), :] * right
        return tuple(acc)

    zero = jnp.zeros(rk_ref.shape[1:], f32)
    return lax.fori_loop(0, depth // step, add, (zero,) * group)


def pick_right(own_pair, refs, rk_ref, sem):
    own, p_own, got, p_got, late, p_late = refs
    r, z = lax.axis_index("row"), lax.axis_index("col")
    keeper = (r % 2) == (z % 2)
    near = ((r // 2) == (z // 2)) == own_pair
    depth = own.shape[0]
    table = [
        (near & keeper, own, p_got),
        (near & ~keeper, p_own, got),
        (~near & keeper, got, p_late),
        (~near & ~keeper, p_got, late),
    ]
    for cond, a, b in table:

        @pl.when(cond)
        def _():
            for h, src in enumerate((a, b)):
                pltpu.make_async_copy(src, rk_ref.at[pl.ds(h * depth, depth)], sem.at[h]).start()

    def wait():
        for h in range(2):
            pltpu.make_async_copy(own, rk_ref.at[pl.ds(h * depth, depth)], sem.at[h]).wait()

    return wait


def send_body(*refs):
    rights, (l_ref, m_ref, o_ref, lf_ref, rk_ref, sem) = refs[:6], refs[6:]
    own_i, depth, chans = l_ref.shape
    wait = pick_right(False, rights, rk_ref, sem)
    lf_ref[:, pl.ds(0, depth), :] = l_ref[...].astype(f32)
    lf_ref[:, pl.ds(depth, depth), :] = m_ref[...].astype(f32)
    wait()
    group = 8

    def rows(b, carry):
        acc = contract(lf_ref, rk_ref, b * group, group, 2 * depth)
        for t in range(group):
            o_ref[b * group + t] = acc[t].astype(bf16)
        return carry

    lax.fori_loop(0, own_i // group, rows, 0)


def keep_body(cuts, *refs):
    rights, refs = refs[:6], refs[6:]
    lefts, mets = refs[:cuts], refs[cuts : 2 * cuts]
    norm_ref, wgate_ref, o_ref, gate_ref, lf_ref, rk_ref, sem = refs[2 * cuts :]
    own_i, depth, chans = o_ref.shape
    wait = pick_right(True, rights, rk_ref, sem)
    at = 0
    for l_ref, m_ref in zip(lefts, mets):
        n = l_ref.shape[0]
        lf_ref[pl.ds(at, n), pl.ds(0, depth), :] = l_ref[...].astype(f32)
        lf_ref[pl.ds(at, n), pl.ds(depth, depth), :] = m_ref[...].astype(f32)
        at += n
    group = 8

    def gates(b, carry):
        flat = norm_ref[pl.ds(pl.multiple_of(b * group * depth, 16), group * depth), :]
        gate = sigmoid(jnp.dot(flat, wgate_ref[...], preferred_element_type=f32))
        gate_ref[pl.ds(b * group, group)] = gate.reshape(group, depth, -1)
        return carry

    lax.fori_loop(0, own_i // group, gates, 0)
    wait()

    def rows(b, carry):
        acc = contract(lf_ref, rk_ref, b * group, group, 2 * depth)
        for t in range(group):
            o_ref[b * group + t] = acc[t]
        return carry

    lax.fori_loop(0, own_i // group, rows, 0)


def join_body(cuts, *refs):
    sums, (own_ref, psum_ref, gate_ref, w_ref, out_ref) = refs[:cuts], refs[cuts:]
    own_i, extent, chans = out_ref.shape
    group = 8
    at = 0
    for part in sums:
        first = at

        def rows(b, carry):
            rows_ = pl.ds(first + b * group, group)
            mixed = own_ref[rows_] + part[pl.ds(b * group, group)].astype(f32)
            normed = standardize(mixed).reshape(group * extent, -1).astype(bf16)
            update = jnp.dot(normed, w_ref[...], preferred_element_type=f32).reshape(group, extent, -1)
            out_ref[rows_] = (psum_ref[rows_].astype(f32) + gate_ref[rows_] * update).astype(bf16)
            return carry

        lax.fori_loop(0, part.shape[0] // group, rows, 0)
        at += part.shape[0]


def triangle_body(l_ref, r_ref, o_ref, lf_ref, flat_ref, rk_ref):
    own_i, depth, chans = l_ref.shape
    extent = r_ref.shape[0]
    group = 8 if own_i % 8 == 0 else 1

    @pl.when(pl.program_id(0) == 0)
    def _():
        lf_ref[...] = l_ref[...].astype(f32)

    def widen(j, carry):
        flat_ref[pl.ds(pl.multiple_of(j * depth, 8), depth), :] = r_ref[j].astype(f32)
        return carry

    lax.fori_loop(0, extent, widen, 0)

    def turn(k, carry):
        rk_ref[k] = flat_ref[pl.ds(k, extent, stride=depth), :]
        return carry

    lax.fori_loop(0, depth, turn, 0)

    def rows(b, carry):
        i0 = b * group
        acc = contract(lf_ref, rk_ref, i0, group, depth)
        for t in range(group):
            o_ref[0, i0 + t] = acc[t].astype(bf16)
        return carry

    lax.fori_loop(0, own_i // group, rows, 0)


def finish_body(sum_ref, psum_ref, norm_ref, wgate_ref, w_ref, out_ref):
    parts, own_i, extent, chans = sum_ref.shape
    own_j = psum_ref.shape[1]

    def row(i, carry):
        flat = norm_ref[pl.ds(pl.multiple_of(i * own_j, 16), own_j), :]
        gate = sigmoid(jnp.dot(flat, wgate_ref[...], preferred_element_type=f32))
        normed = [standardize(sum_ref[part, i].astype(f32)) for part in range(parts)]
        normed = jnp.concatenate(normed, axis=0).astype(bf16)
        update = jnp.dot(normed, w_ref[...], preferred_element_type=f32)
        out_ref[i] = (psum_ref[i].astype(f32) + gate * update).astype(bf16)
        return carry

    lax.fori_loop(0, own_i, row, 0)


def gathered_plan(left, right, psum, norm, w_gate, w_final):
    own_i, own_j, chans = psum.shape
    rows = lax.axis_size("row")
    tri = w_final.shape[0]
    right_all = lax.all_gather(right, "row", axis=0, tiled=True)
    partial = pl.pallas_call(
        triangle_body,
        grid=(rows,),
        out_shape=jax.ShapeDtypeStruct((rows, own_i, own_i, tri), bf16),
        in_specs=[
            pl.BlockSpec((own_i, own_j, tri), lambda r: (0, 0, 0)),
            pl.BlockSpec((own_i, own_j, tri), lambda r: (r, 0, 0)),
        ],
        out_specs=pl.BlockSpec((1, own_i, own_i, tri), lambda r: (r, 0, 0, 0)),
        scratch_shapes=[
            pltpu.VMEM((own_i, own_j, tri), f32),
            pltpu.VMEM((own_i * own_j, tri), f32),
            pltpu.VMEM((own_j, own_i, tri), f32),
        ],
        compiler_params=limit(56),
        name="triangle",
    )(left, right_all)
    summed = lax.psum_scatter(partial, "col", scatter_dimension=0, tiled=True)
    return pl.pallas_call(
        finish_body,
        out_shape=jax.ShapeDtypeStruct((own_i, own_j, chans), bf16),
        in_specs=[VMEM] * 5,
        out_specs=VMEM,
        compiler_params=limit(56),
        name="finish",
    )(summed, psum, norm, w_gate, w_final)


def paired_plan(lefts, right, psum, norm, w_gate, w_final):
    own_i, own_j, chans = psum.shape
    tri = w_final.shape[0]
    cuts = len(lefts)
    cells = [(r, z) for r in range(4) for z in range(4)]

    def move(value, where, step):
        pairs = [(r * 4 + z, step(r, z)) for r, z in cells if where(r, z)]
        pairs = [(src, r * 4 + z) for src, (r, z) in pairs]
        return lax.ppermute(value, ("row", "col"), pairs)

    every = lambda r, z: True
    keeper = lambda r, z: r % 2 == z % 2
    other = lambda r, z: r % 2 != z % 2
    got = move(right, every, lambda r, z: (r ^ 2, z) if r % 2 == z % 2 else (r ^ 1, z ^ 1))
    mets = [move(left, every, lambda r, z: (r, z ^ 1)) for left in lefts]
    late = move(got, other, lambda r, z: (r ^ 2, z))
    p_own = move(right, keeper, lambda r, z: (r ^ 1, z))
    p_got = move(got, every, lambda r, z: (r ^ 1, z))
    p_late = move(late, other, lambda r, z: (r ^ 1, z))
    rights = (right, p_own, got, p_got, late, p_late)

    sums = []
    for left, met in zip(lefts, mets):
        n = left.shape[0]
        part = pl.pallas_call(
            send_body,
            out_shape=jax.ShapeDtypeStruct((n, own_j, tri), bf16),
            in_specs=[ANY] * 6 + [VMEM] * 2,
            out_specs=VMEM,
            scratch_shapes=[
                pltpu.VMEM((n, 2 * own_j, tri), f32),
                pltpu.VMEM((2 * own_j, own_i, tri), bf16),
                pltpu.SemaphoreType.DMA((2,)),
            ],
            compiler_params=limit(12),
            name="send_sums",
        )(*rights, left, met)
        sums.append(move(part, every, lambda r, z: (r, z ^ 2)))

    own, gate = pl.pallas_call(
        functools.partial(keep_body, cuts),
        out_shape=[jax.ShapeDtypeStruct((own_i, own_j, tri), f32),
                   jax.ShapeDtypeStruct((own_i, own_j, chans), f32)],
        in_specs=[ANY] * 6 + [VMEM] * (2 * cuts + 2),
        out_specs=[VMEM] * 2,
        scratch_shapes=[
            pltpu.VMEM((own_i, 2 * own_j, tri), f32),
            pltpu.VMEM((2 * own_j, own_i, tri), bf16),
            pltpu.SemaphoreType.DMA((2,)),
        ],
        compiler_params=limit(16),
        name="keep_sums",
    )(*rights, *lefts, *mets, norm, w_gate)
    return pl.pallas_call(
        functools.partial(join_body, cuts),
        out_shape=jax.ShapeDtypeStruct((own_i, own_j, chans), bf16),
        in_specs=[VMEM] * (cuts + 4),
        out_specs=VMEM,
        compiler_params=limit(12),
        name="join",
    )(*sums, own, psum, gate, w_final)


def shards(homolog, couple, ids, valid, bias, factors, average, w_in, w_gate, w_final):
    rows, cols = lax.axis_size("row"), lax.axis_size("col")
    own_seqs, residues, depth = homolog.shape
    own_i, own_j, chans = couple.shape
    width = factors.shape[1] // 2
    tri = w_final.shape[0]
    total = own_seqs * rows
    lanes = round_up(2 * own_seqs * width, 128)
    height = round_up(max(own_i, own_j), 16)
    paired = rows == 4 and cols == 4 and own_i == own_j and own_i % 8 == 0
    scale = 1 if paired else 8

    msgs = pl.pallas_call(
        functools.partial(align_body, own_i, own_j),
        out_shape=[jax.ShapeDtypeStruct((height, lanes), bf16)] * rows,
        in_specs=[VMEM] * 2,
        out_specs=[VMEM] * rows,
        scratch_shapes=[pltpu.VMEM((own_seqs * residues, 2 * width), f32)],
        compiler_params=limit(8, scale),
        name="align",
    )(homolog, factors.T)
    msgs = [msgs[0]] + [
        lax.ppermute(msg, "row", [(r, r ^ d) for r in range(rows)])
        for d, msg in enumerate(msgs) if d
    ]

    base, mask, wq = pl.pallas_call(
        prepare_body,
        out_shape=[jax.ShapeDtypeStruct((own_i, own_j, chans), f32),
                   jax.ShapeDtypeStruct((own_i, own_j, tri), bf16),
                   jax.ShapeDtypeStruct((width // 2, width, 2 * chans), bf16)],
        in_specs=[VMEM, SMEM, VMEM, VMEM, VMEM],
        out_specs=[VMEM] * 3,
        scratch_shapes=[
            pltpu.VMEM((width * width, chans), f32),
            pltpu.VMEM((own_j, chans), jnp.int32),
        ],
        compiler_params=limit(8, scale),
        name="prepare",
    )(couple, ids, valid, bias, average)

    extents = (own_j, own_i) if paired else (own_i, own_j)
    psum, norm, right = pl.pallas_call(
        functools.partial(pair_body, own_seqs, width, paired),
        out_shape=[jax.ShapeDtypeStruct((own_i, own_j, chans), bf16),
                   jax.ShapeDtypeStruct((own_i * own_j, chans), bf16),
                   jax.ShapeDtypeStruct(extents + (tri,), bf16)],
        in_specs=[VMEM] * (rows + 4),
        out_specs=[VMEM] * 3,
        scratch_shapes=[
            pltpu.VMEM((own_i * total, 128), f32),
            pltpu.VMEM((own_i, width * total, chans), bf16),
            pltpu.VMEM((own_i * own_j, tri), f32),
        ],
        compiler_params=limit(16, scale),
        name="pair",
    )(*msgs, base, mask, wq, w_in)

    cuts = [16, own_i - 16] if paired else [own_i]
    lefts = pl.pallas_call(
        left_body,
        out_shape=[jax.ShapeDtypeStruct((n, own_j, tri), bf16) for n in cuts],
        in_specs=[VMEM] * 3,
        out_specs=[VMEM] * len(cuts),
        compiler_params=limit(8, scale),
        name="left",
    )(norm, mask, w_in)
    if paired:
        return paired_plan(lefts, right, psum, norm, w_gate, w_final)
    return gathered_plan(lefts[0], right, psum, norm, w_gate, w_final)


def solution(mesh):
    placed = (
        P(("grp", "row"), None, None),
        P(("grp", "row"), "col", None),
        P("grp"),
        P(("grp", "row"), "col"),
        P(),
        P(),
        P(),
        P(),
        P(),
        P(),
    )
    return jax.shard_map(
        shards,
        mesh=mesh,
        in_specs=placed,
        out_specs=P(("grp", "row"), "col", None),
        check_vma=False,
    )
```

time: 110 us -> 67.2 us (0.61)
  waiting for transfers between devices: 57.4 us -> 19.3 us
  starting transfers between devices: 0.04 us -> 20.4 us
  between operations: 13.4 us -> 0.17 us
  blocking collectives: 9.22 us -> 0 us
  Pallas kernels: 28.1 us -> 23.3 us
  local copies, waits for them, and re-layouts: 1.48 us -> 3.65 us
    reduce_scatter x1 -> x0, waiting for transfers between devices: 36.5 us -> none  [shards(): summed = lax.psum_scatter(partial, 'col', scatter_dimension=0, tiled=True)]
    all_gather x1 -> x0, waiting for transfers between devices: 20.9 us -> none  [shards(): right_all = lax.all_gather(right, 'row', axis=0, tiled=True)]
    ppermute x0 -> x12, starting transfers between devices: none -> 20.4 us  [the longest x9 17.2 us: move(): return lax.ppermute(value, ('row', 'col'), pairs)]
    ppermute x0 -> x12, waiting for transfers between devices: none -> 19.3 us  [the longest x9 19.3 us: move(): return lax.ppermute(value, ('row', 'col'), pairs)]
    all_to_all x1 -> x0, blocking collectives: 9.22 us -> none  [shards(): msg = lax.all_to_all(msg, 'row', split_axis=0, concat_axis=0, tiled=True)]
    pallas_call x4 -> x8, Pallas kernels: 28.1 us -> 23.3 us  [the longest x1 6.51 us: paired_plan(): pl.pallas_call(functools.partial(keep_body, cuts), out_shape=[jax.ShapeDt...]
    unnamed x1 -> x20, local copies, waits for them, and re-layouts: 1.48 us -> 3.65 us
  transfers between devices with their start and end apart: 2 -> 12, of which waited for: 2 -> 3; matrix products, arithmetic and copies ran while one was open for 0% -> 0% of each run, Pallas kernels for 0% -> 23%
where the time goes in v2:
time: 67.2 us; the launch traced here: 66.9 us
  Pallas kernels  23.3 us (35%)
  starting transfers between devices  20.4 us (30%)
  waiting for transfers between devices  19.3 us (29%)
  local copies, waits for them, and re-layouts  3.65 us (5%)
    ppermute x9, waiting for transfers between devices, move(): return lax.ppermute(value, ('row', 'col'), pairs)  19.3 us
    ppermute x9, starting transfers between devices, move(): return lax.ppermute(value, ('row', 'col'), pairs)  17.2 us
    pallas_call x1, Pallas kernels, paired_plan(): pl.pallas_call(functools.partial(keep_body, cuts), out_shape=[jax.ShapeDt...  6.51 us
    pallas_call x2, Pallas kernels, paired_plan(): pl.pallas_call(send_body, out_shape=jax.ShapeDtypeStruct((n, own_j, tri),...  6.17 us
    pallas_call x1, Pallas kernels, shards(): pl.pallas_call(functools.partial(pair_body, own_seqs, width, paired), out...  4.92 us
    unnamed x20, local copies, waits for them, and re-layouts  3.65 us
    ppermute x3, starting transfers between devices, shards(): lax.ppermute(msg, 'row', [(r, r ^ d) for r in range(rows)])  3.23 us
    pallas_call x1, Pallas kernels, paired_plan(): pl.pallas_call(functools.partial(join_body, cuts), out_shape=jax.ShapeDty...  2.42 us
  transfers between devices with their start and end apart: 12, of which 3 were waited for; matrix products, arithmetic and copies ran while one was open for 0% of the time, Pallas kernels for 23%

profile of v2, /device:TPU:0, one launch (start us, length us, event | category | flops | bytes accessed | tf_op | source)
XLA Modules:
  0.0 66.9 jit_solution(5300807797078382728)
XLA Ops:
  0.0 0.0 copy-start.3
  0.0 0.9 %copy-done.3 = bf16[2,160,256]{2,1,0:T(8,128)(2,1)S(1)} copy-done((bf16[2,160,256]{2,1,0:T(8,128)(2,1)S(1)}, bf16[2,160,256]{2,1,0:T(8,128)(2,1)}, u32[]{:S(2)}) %copy-start.3) | copy-done | bytes 163864
  0.9 0.0 copy-start.6
  0.9 0.8 %copy-done.6 = bf16[256,64]{0,1:T(8,128)(2,1)S(1)} copy-done((bf16[256,64]{0,1:T(8,128)(2,1)S(1)}, bf16[256,64]{0,1:T(8,128)(2,1)}, u32[]{:S(2)}) %copy-start.6) | copy-done | bytes 32792
  1.7 0.0 copy-start.7
  1.7 0.4 align.1
  2.1 0.5 collective-permute-start
  2.6 0.0 copy-start.9
  2.6 0.0 copy-start.8
  2.6 2.6 %collective-permute-start.1 = (bf16[48,128]{1,0:T(8,128)(2,1)S(1)}, bf16[48,128]{1,0:T(8,128)(2,1)S(1)}, u32[]{:S(2)}, u32[]{:S(2)}) collective-permute-start(bf16[48,128]{1,0:T(8,128)(2,1)S(1)} %get-tuple-element.21), channel_id=1, source_target_pairs={{0,8},{4,12},{8,0},{12,4},{1,9},{5,13},{9,1},{13,5},{2,10},{6,14},... | collective-permute-start | bytes 36872 | tf_op jit(solution)/shard_map/ppermute | solution.py:459
  5.2 0.0 copy-start
  5.2 0.1 collective-permute-start.2
  5.4 0.0 copy-done.7
  5.4 0.0 copy-done.9
  5.4 0.0 copy-done.8
  5.4 0.0 copy-start.1
  5.4 1.0 %copy-done.1 = bf16[40,40,128]{2,1,0:T(8,128)(2,1)S(1)} copy-done((bf16[40,40,128]{2,1,0:T(8,128)(2,1)S(1)}, bf16[40,40,128]{2,1,0:T(8,128)(2,1)}, u32[]{:S(2)}) %copy-start.1) | copy-done | bytes 409624
  6.4 0.0 copy-start.2
  6.4 0.9 %copy-done.2 = bf16[1024,128]{1,0:T(8,128)(2,1)S(1)} copy-done((bf16[1024,128]{1,0:T(8,128)(2,1)S(1)}, bf16[1024,128]{1,0:T(8,128)(2,1)}, u32[]{:S(2)}) %copy-start.2) | copy-done | bytes 262168
  7.3 1.9 %prepare.1 = (f32[40,40,128]{2,1,0:T(8,128)S(1)}, bf16[40,40,128]{2,1,0:T(8,128)(2,1)S(1)}, bf16[16,32,256]{2,1,0:T(8,128)(2,1)S(1)}) custom-call(bf16[40,40,128]{2,1,0:T(8,128)(2,1)S(1)} %copy-done.1, s32[160]{0:T(256)S(1)} %copy-done.8, s32[40,40]{1,0:T(8,128)S(1)} %copy-done.7, f32[2,128]{1,0:T(2,128)S(1)} %copy-done.9, bf16[1024,128]{1,0:T(8,128)(2,1)S(1)} %copy-done.2), custom_call_target="tpu_custom_call" | custom-call | tf_op jit(solution)/shard_map/prepare/pallas_call | solution.py:463
  9.2 0.0 collective-permute-done.refs_1_
  9.2 0.0 collective-permute-done.1.refs_2_
  9.2 0.0 collective-permute-done.2.refs_3_
  9.2 0.0 copy-done
  9.3 4.9 %pair.1 = (bf16[40,40,128]{2,1,0:T(8,128)(2,1)S(1)}, bf16[1600,128]{1,0:T(8,128)(2,1)S(1)}, bf16[40,40,128]{2,1,0:T(8,128)(2,1)S(1)}) custom-call(bf16[48,128]{1,0:T(8,128)(2,1)S(1)} %get-tuple-element.19.refs_0_, bf16[48,128]{1,0:T(8,128)(2,1)S(1)} %collective-permute-done.refs_1_, bf16[48,128]{1,0:T(8,128)(2,1)S(1)} %collective-permute-done.1.refs_2_, ...), custom_call_target="tpu_custom_call" | custom-call | tf_op jit(solution)/shard_map/pair/pallas_call | solution.py:479
  14.2 1.7 %collective-permute-start.4 = (bf16[40,40,128]{2,1,0:T(8,128)(2,1)S(1)}, bf16[40,40,128]{2,1,0:T(8,128)(2,1)S(1)}, u32[]{:S(2)}, u32[]{:S(2)}) collective-permute-start(bf16[40,40,128]{2,1,0:T(8,128)(2,1)S(1)} %get-tuple-element.26.refs_0_), channel_id=1, source_target_pairs={{0,8},{1,4},{2,10},{3,6},{4,1},{5,13},{6,3},{7,15},{8,0},{9,12},{1... | collective-permute-start | bytes 1228808 | tf_op jit(solution)/shard_map/ppermute | solution.py:382
  15.9 6.3 %collective-permute-done.4.refs_2_ = bf16[40,40,128]{2,1,0:T(8,128)(2,1)S(1)} collective-permute-done((bf16[40,40,128]{2,1,0:T(8,128)(2,1)S(1)}, bf16[40,40,128]{2,1,0:T(8,128)(2,1)S(1)}, u32[]{:S(2)}, u32[]{:S(2)}) %collective-permute-start.4) | collective-permute-done | bytes 409632 | tf_op jit(solution)/shard_map/ppermute | solution.py:382
  22.2 0.7 %collective-permute-start.6 = (bf16[40,40,128]{2,1,0:T(8,128)(2,1)S(1)}, bf16[40,40,128]{2,1,0:T(8,128)(2,1)S(1)}, u32[]{:S(2)}, u32[]{:S(2)}) collective-permute-start(bf16[40,40,128]{2,1,0:T(8,128)(2,1)S(1)} %collective-permute-done.4.refs_2_), channel_id=1, source_target_pairs={{1,9},{3,11},{4,12},{6,14},{9,1},{11,3},{12,4},{14,6},{17,25},{19,... | collective-permute-start | bytes 1228808 | tf_op jit(solution)/shard_map/ppermute | solution.py:382
  22.9 4.6 %collective-permute-start.3 = (bf16[40,40,128]{2,1,0:T(8,128)(2,1)S(1)}, bf16[40,40,128]{2,1,0:T(8,128)(2,1)S(1)}, u32[]{:S(2)}, u32[]{:S(2)}) collective-permute-start(bf16[40,40,128]{2,1,0:T(8,128)(2,1)S(1)} %get-tuple-element.26.refs_0_), channel_id=1, source_target_pairs={{0,4},{2,6},{5,1},{7,3},{8,12},{10,14},{13,9},{15,11},{16,20},{18,... | collective-permute-start | bytes 1228808 | tf_op jit(solution)/shard_map/ppermute | solution.py:382
  27.5 0.1 collective-permute-start.5
  27.6 0.0 collective-permute-done.6.refs_4_
  27.6 1.3 %collective-permute-start.7 = (bf16[40,40,128]{2,1,0:T(8,128)(2,1)S(1)}, bf16[40,40,128]{2,1,0:T(8,128)(2,1)S(1)}, u32[]{:S(2)}, u32[]{:S(2)}) collective-permute-start(bf16[40,40,128]{2,1,0:T(8,128)(2,1)S(1)} %collective-permute-done.6.refs_4_), channel_id=1, source_target_pairs={{1,5},{3,7},{4,0},{6,2},{9,13},{11,15},{12,8},{14,10},{17,21},{19,... | collective-permute-start | bytes 1228808 | tf_op jit(solution)/shard_map/ppermute | solution.py:382
  28.9 1.0 %left.1 = (bf16[16,40,128]{2,1,0:T(8,128)(2,1)S(1)}, bf16[24,40,128]{2,1,0:T(8,128)(2,1)S(1)}) custom-call(bf16[1600,128]{1,0:T(8,128)(2,1)S(1)} %get-tuple-element.27.norm_ref.refs_10_, bf16[40,40,128]{2,1,0:T(8,128)(2,1)S(1)} %get-tuple-element.24.refs_5_.mask_ref, bf16[128,512]{1,0:T(8,128)(2,1)S(1)} %copy-done), custom_call_target="tpu_custom_call" | custom-call | tf_op jit(solution)/shard_map/left/pallas_call | solution.py:496
  29.9 5.7 %collective-permute-start.10 = (bf16[24,40,128]{2,1,0:T(8,128)(2,1)S(1)}, bf16[24,40,128]{2,1,0:T(8,128)(2,1)S(1)}, u32[]{:S(2)}, u32[]{:S(2)}) collective-permute-start(bf16[24,40,128]{2,1,0:T(8,128)(2,1)S(1)} %get-tuple-element.29.refs_6_.refs_7_), channel_id=1, source_target_pairs={{0,1},{1,0},{2,3},{3,2},{4,5},{5,4},{6,7},{7,6},{8,9},{9,8},{10,11... | collective-permute-start | bytes 737288 | tf_op jit(solution)/shard_map/ppermute | solution.py:382
  35.5 0.1 collective-permute-start.8
  35.6 6.8 %collective-permute-done.10.refs_7_.refs_9_ = bf16[24,40,128]{2,1,0:T(8,128)(2,1)S(1)} collective-permute-done((bf16[24,40,128]{2,1,0:T(8,128)(2,1)S(1)}, bf16[24,40,128]{2,1,0:T(8,128)(2,1)S(1)}, u32[]{:S(2)}, u32[]{:S(2)}) %collective-permute-start.10) | collective-permute-done | bytes 245792 | tf_op jit(solution)/shard_map/ppermute | solution.py:382
  42.4 0.0 collective-permute-done.3.refs_1_
  42.4 0.0 collective-permute-done.5.refs_3_
  42.4 0.0 collective-permute-done.7.refs_5_
  42.4 3.6 %send_sums.3 = bf16[24,40,128]{2,1,0:T(8,128)(2,1)S(1)} custom-call(bf16[40,40,128]{2,1,0:T(8,128)(2,1)S(1)} %get-tuple-element.26.refs_0_, bf16[40,40,128]{2,1,0:T(8,128)(2,1)S(1)} %collective-permute-done.3.refs_1_, bf16[40,40,128]{2,1,0:T(8,128)(2,1)S(1)} %collective-permute-done.4.refs_2_, bf16[40,40,128]{2,1,0:T(8,128)(2,1)S(1)} %collective-permute-done.5.refs_3_, ...), custom_call_target="tpu_custom_call" | custom-call | tf_op jit(solution)/shard_map/send_sums/pallas_call | solution.py:398
  46.0 0.0 copy-start.4
  46.0 2.6 %collective-permute-start.11 = (bf16[24,40,128]{2,1,0:T(8,128)(2,1)S(1)}, bf16[24,40,128]{2,1,0:T(8,128)(2,1)S(1)}, u32[]{:S(2)}, u32[]{:S(2)}) collective-permute-start(bf16[24,40,128]{2,1,0:T(8,128)(2,1)S(1)} %send_sums.3), channel_id=1, source_target_pairs={{0,2},{1,3},{2,0},{3,1},{4,6},{5,7},{6,4},{7,5},{8,10},{9,11},{10,... | collective-permute-start | bytes 737288 | tf_op jit(solution)/shard_map/ppermute | solution.py:382
  48.7 0.0 collective-permute-done.8.refs_7_.refs_8_
  48.7 2.5 %send_sums.2 = bf16[16,40,128]{2,1,0:T(8,128)(2,1)S(1)} custom-call(bf16[40,40,128]{2,1,0:T(8,128)(2,1)S(1)} %get-tuple-element.26.refs_0_, bf16[40,40,128]{2,1,0:T(8,128)(2,1)S(1)} %collective-permute-done.3.refs_1_, bf16[40,40,128]{2,1,0:T(8,128)(2,1)S(1)} %collective-permute-done.4.refs_2_, bf16[40,40,128]{2,1,0:T(8,128)(2,1)S(1)} %collective-permute-done.5.refs_3_, ...), custom_call_target="tpu_custom_call" | custom-call | tf_op jit(solution)/shard_map/send_sums/pallas_call | solution.py:398
  51.2 0.0 copy-start.5
  51.2 0.4 collective-permute-start.9
  51.7 0.0 copy-done.4
  51.7 6.5 %keep_sums.1 = (f32[40,40,128]{2,1,0:T(8,128)S(1)}, f32[40,40,128]{2,1,0:T(8,128)S(1)}) custom-call(bf16[40,40,128]{2,1,0:T(8,128)(2,1)S(1)} %get-tuple-element.26.refs_0_, bf16[40,40,128]{2,1,0:T(8,128)(2,1)S(1)} %collective-permute-done.3.refs_1_, bf16[40,40,128]{2,1,0:T(8,128)(2,1)S(1)} %collective-permute-done.4.refs_2_, ...), custom_call_target="tpu_custom_call" | custom-call | tf_op jit(solution)/shard_map/keep_sums/pallas_call | solution.py:413
  58.2 6.3 %collective-permute-done.9.refs_0_ = bf16[16,40,128]{2,1,0:T(8,128)(2,1)S(1)} collective-permute-done((bf16[16,40,128]{2,1,0:T(8,128)(2,1)S(1)}, bf16[16,40,128]{2,1,0:T(8,128)(2,1)S(1)}, u32[]{:S(2)}, u32[]{:S(2)}) %collective-permute-start.9) | collective-permute-done | bytes 163872 | tf_op jit(solution)/shard_map/ppermute | solution.py:382
  64.5 0.0 collective-permute-done.11.refs_1_
  64.5 0.0 copy-done.5
  64.5 2.4 %join.1 = bf16[40,40,128]{2,1,0:T(8,128)(2,1)} custom-call(bf16[16,40,128]{2,1,0:T(8,128)(2,1)S(1)} %collective-permute-done.9.refs_0_, bf16[24,40,128]{2,1,0:T(8,128)(2,1)S(1)} %collective-permute-done.11.refs_1_, f32[40,40,128]{2,1,0:T(8,128)S(1)} %get-tuple-element.30.refs_2_, bf16[40,40,128]{2,1,0:T(8,128)(2,1)S(1)} %get-tuple-element.31.refs_3_, ...), custom_call_target="tpu_custom_call" | custom-call | tf_op jit(solution)/shard_map/join/pallas_call | solution.py:427
Async XLA Ops:
  0.0 0.9 %copy-start.3 = (bf16[2,160,256]{2,1,0:T(8,128)(2,1)S(1)}, bf16[2,160,256]{2,1,0:T(8,128)(2,1)}, u32[]{:S(2)}) copy-start(bf16[2,160,256]{2,1,0:T(8,128)(2,1)} %x_ref.1) | copy-start | bytes 491524
  0.9 0.8 %copy-start.6 = (bf16[256,64]{0,1:T(8,128)(2,1)S(1)}, bf16[256,64]{0,1:T(8,128)(2,1)}, u32[]{:S(2)}) copy-start(bf16[256,64]{0,1:T(8,128)(2,1)} %param.15) | copy-start | bytes 98308
  1.7 3.7 %copy-start.7 = (s32[40,40]{1,0:T(8,128)S(1)}, s32[40,40]{1,0:T(8,128)}, u32[]{:S(2)}) copy-start(s32[40,40]{1,0:T(8,128)} %valid_ref.1) | copy-start | bytes 19204
  2.1 7.1 %collective-permute-start = (bf16[48,128]{1,0:T(8,128)(2,1)S(1)}, bf16[48,128]{1,0:T(8,128)(2,1)S(1)}, u32[]{:S(2)}, u32[]{:S(2)}) collective-permute-start(bf16[48,128]{1,0:T(8,128)(2,1)S(1)} %get-tuple-element.20), channel_id=1, source_target_pairs={{0,4},{4,0},{8,12},{12,8},{1,5},{5,1},{9,13},{13,9},{2,6},{6,2},{1... | collective-permute-start | bytes 36872 | tf_op jit(solution)/shard_map/ppermute | solution.py:459
  2.6 2.7 %copy-start.9 = (f32[2,128]{1,0:T(2,128)S(1)}, f32[2,128]{1,0:T(2,128)}, u32[]{:S(2)}) copy-start(f32[2,128]{1,0:T(2,128)} %bias_ref.1) | copy-start | bytes 3076
  2.6 2.7 %copy-start.8 = (s32[160]{0:T(256)S(1)}, s32[160]{0:T(256)}, u32[]{:S(2)}) copy-start(s32[160]{0:T(256)} %ids_ref.1) | copy-start | bytes 1924
  2.6 6.6 %collective-permute-start.1 = (bf16[48,128]{1,0:T(8,128)(2,1)S(1)}, bf16[48,128]{1,0:T(8,128)(2,1)S(1)}, u32[]{:S(2)}, u32[]{:S(2)}) collective-permute-start(bf16[48,128]{1,0:T(8,128)(2,1)S(1)} %get-tuple-element.21), channel_id=1, source_target_pairs={{0,8},{4,12},{8,0},{12,4},{1,9},{5,13},{9,1},{13,5},{2,10},{6,14},... | collective-permute-start | bytes 36872 | tf_op jit(solution)/shard_map/ppermute | solution.py:459
  5.2 4.0 %copy-start = (bf16[128,512]{1,0:T(8,128)(2,1)S(1)}, bf16[128,512]{1,0:T(8,128)(2,1)}, u32[]{:S(2)}) copy-start(bf16[128,512]{1,0:T(8,128)(2,1)} %win_ref.1) | copy-start | bytes 393220
  5.2 4.0 %collective-permute-start.2 = (bf16[48,128]{1,0:T(8,128)(2,1)S(1)}, bf16[48,128]{1,0:T(8,128)(2,1)S(1)}, u32[]{:S(2)}, u32[]{:S(2)}) collective-permute-start(bf16[48,128]{1,0:T(8,128)(2,1)S(1)} %get-tuple-element.22), channel_id=1, source_target_pairs={{0,12},{4,8},{8,4},{12,0},{1,13},{5,9},{9,5},{13,1},{2,14},{6,10},... | collective-permute-start | bytes 36872 | tf_op jit(solution)/shard_map/ppermute | solution.py:459
  5.4 1.0 %copy-start.1 = (bf16[40,40,128]{2,1,0:T(8,128)(2,1)S(1)}, bf16[40,40,128]{2,1,0:T(8,128)(2,1)}, u32[]{:S(2)}) copy-start(bf16[40,40,128]{2,1,0:T(8,128)(2,1)} %couple_ref.1) | copy-start | bytes 1228804
  6.4 0.9 %copy-start.2 = (bf16[1024,128]{1,0:T(8,128)(2,1)S(1)}, bf16[1024,128]{1,0:T(8,128)(2,1)}, u32[]{:S(2)}) copy-start(bf16[1024,128]{1,0:T(8,128)(2,1)} %avg_ref.1) | copy-start | bytes 786436
  14.2 8.0 %collective-permute-start.4 = (bf16[40,40,128]{2,1,0:T(8,128)(2,1)S(1)}, bf16[40,40,128]{2,1,0:T(8,128)(2,1)S(1)}, u32[]{:S(2)}, u32[]{:S(2)}) collective-permute-start(bf16[40,40,128]{2,1,0:T(8,128)(2,1)S(1)} %get-tuple-element.26.refs_0_), channel_id=1, source_target_pairs={{0,8},{1,4},{2,10},{3,6},{4,1},{5,13},{6,3},{7,15},{8,0},{9,12},{1... | collective-permute-start | bytes 1228808 | tf_op jit(solution)/shard_map/ppermute | solution.py:382
  22.2 5.4 %collective-permute-start.6 = (bf16[40,40,128]{2,1,0:T(8,128)(2,1)S(1)}, bf16[40,40,128]{2,1,0:T(8,128)(2,1)S(1)}, u32[]{:S(2)}, u32[]{:S(2)}) collective-permute-start(bf16[40,40,128]{2,1,0:T(8,128)(2,1)S(1)} %collective-permute-done.4.refs_2_), channel_id=1, source_target_pairs={{1,9},{3,11},{4,12},{6,14},{9,1},{11,3},{12,4},{14,6},{17,25},{19,... | collective-permute-start | bytes 1228808 | tf_op jit(solution)/shard_map/ppermute | solution.py:382
  22.9 19.5 %collective-permute-start.3 = (bf16[40,40,128]{2,1,0:T(8,128)(2,1)S(1)}, bf16[40,40,128]{2,1,0:T(8,128)(2,1)S(1)}, u32[]{:S(2)}, u32[]{:S(2)}) collective-permute-start(bf16[40,40,128]{2,1,0:T(8,128)(2,1)S(1)} %get-tuple-element.26.refs_0_), channel_id=1, source_target_pairs={{0,4},{2,6},{5,1},{7,3},{8,12},{10,14},{13,9},{15,11},{16,20},{18,... | collective-permute-start | bytes 1228808 | tf_op jit(solution)/shard_map/ppermute | solution.py:382
  27.5 14.9 %collective-permute-start.5 = (bf16[40,40,128]{2,1,0:T(8,128)(2,1)S(1)}, bf16[40,40,128]{2,1,0:T(8,128)(2,1)S(1)}, u32[]{:S(2)}, u32[]{:S(2)}) collective-permute-start(bf16[40,40,128]{2,1,0:T(8,128)(2,1)S(1)} %collective-permute-done.4.refs_2_), channel_id=1, source_target_pairs={{0,4},{1,5},{2,6},{3,7},{4,0},{5,1},{6,2},{7,3},{8,12},{9,13},{10,... | collective-permute-start | bytes 1228808 | tf_op jit(solution)/shard_map/ppermute | solution.py:382
  27.6 14.8 %collective-permute-start.7 = (bf16[40,40,128]{2,1,0:T(8,128)(2,1)S(1)}, bf16[40,40,128]{2,1,0:T(8,128)(2,1)S(1)}, u32[]{:S(2)}, u32[]{:S(2)}) collective-permute-start(bf16[40,40,128]{2,1,0:T(8,128)(2,1)S(1)} %collective-permute-done.6.refs_4_), channel_id=1, source_target_pairs={{1,5},{3,7},{4,0},{6,2},{9,13},{11,15},{12,8},{14,10},{17,21},{19,... | collective-permute-start | bytes 1228808 | tf_op jit(solution)/shard_map/ppermute | solution.py:382
  29.9 12.5 %collective-permute-start.10 = (bf16[24,40,128]{2,1,0:T(8,128)(2,1)S(1)}, bf16[24,40,128]{2,1,0:T(8,128)(2,1)S(1)}, u32[]{:S(2)}, u32[]{:S(2)}) collective-permute-start(bf16[24,40,128]{2,1,0:T(8,128)(2,1)S(1)} %get-tuple-element.29.refs_6_.refs_7_), channel_id=1, source_target_pairs={{0,1},{1,0},{2,3},{3,2},{4,5},{5,4},{6,7},{7,6},{8,9},{9,8},{10,11... | collective-permute-start | bytes 737288 | tf_op jit(solution)/shard_map/ppermute | solution.py:382
  35.5 13.1 %collective-permute-start.8 = (bf16[16,40,128]{2,1,0:T(8,128)(2,1)S(1)}, bf16[16,40,128]{2,1,0:T(8,128)(2,1)S(1)}, u32[]{:S(2)}, u32[]{:S(2)}) collective-permute-start(bf16[16,40,128]{2,1,0:T(8,128)(2,1)S(1)} %get-tuple-element.28.refs_6_), channel_id=1, source_target_pairs={{0,1},{1,0},{2,3},{3,2},{4,5},{5,4},{6,7},{7,6},{8,9},{9,8},{10,11... | collective-permute-start | bytes 491528 | tf_op jit(solution)/shard_map/ppermute | solution.py:382
  46.0 5.6 %copy-start.4 = (bf16[128,128]{1,0:T(8,128)(2,1)S(1)}, bf16[128,128]{1,0:T(8,128)(2,1)}, u32[]{:S(2)}) copy-start(bf16[128,128]{1,0:T(8,128)(2,1)} %refs_11_.1) | copy-start | bytes 98308
  46.0 18.4 %collective-permute-start.11 = (bf16[24,40,128]{2,1,0:T(8,128)(2,1)S(1)}, bf16[24,40,128]{2,1,0:T(8,128)(2,1)S(1)}, u32[]{:S(2)}, u32[]{:S(2)}) collective-permute-start(bf16[24,40,128]{2,1,0:T(8,128)(2,1)S(1)} %send_sums.3), channel_id=1, source_target_pairs={{0,2},{1,3},{2,0},{3,1},{4,6},{5,7},{6,4},{7,5},{8,10},{9,11},{10,... | collective-permute-start | bytes 737288 | tf_op jit(solution)/shard_map/ppermute | solution.py:382
  51.2 13.2 %copy-start.5 = (bf16[128,128]{1,0:T(8,128)(2,1)S(1)}, bf16[128,128]{1,0:T(8,128)(2,1)}, u32[]{:S(2)}) copy-start(bf16[128,128]{1,0:T(8,128)(2,1)} %refs_5_.1) | copy-start | bytes 98308
  51.2 13.2 %collective-permute-start.9 = (bf16[16,40,128]{2,1,0:T(8,128)(2,1)S(1)}, bf16[16,40,128]{2,1,0:T(8,128)(2,1)S(1)}, u32[]{:S(2)}, u32[]{:S(2)}) collective-permute-start(bf16[16,40,128]{2,1,0:T(8,128)(2,1)S(1)} %send_sums.2), channel_id=1, source_target_pairs={{0,2},{1,3},{2,0},{3,1},{4,6},{5,7},{6,4},{7,5},{8,10},{9,11},{10,... | collective-permute-start | bytes 491528 | tf_op jit(solution)/shard_map/ppermute | solution.py:382

commit v3 on v2

--- a/solution.py
+++ b/solution.py
@@ -12,7 +12,7 @@
 bf16 = jnp.bfloat16
 VMEM = pl.BlockSpec(memory_space=pltpu.VMEM)
 SMEM = pl.BlockSpec(memory_space=pltpu.SMEM)
-ANY = pl.BlockSpec(memory_space=pl.ANY)
+HBM = pl.BlockSpec(memory_space=pltpu.HBM)
 
 
 def limit(mib, scale=1):
@@ -21,6 +21,21 @@
 
 def round_up(n, m):
     return (n + m - 1) // m * m
+
+
+def cost(us):
+    return pl.CostEstimate(flops=0, bytes_accessed=int(us * 3.69e6), transcendentals=0)
+
+
+def hold(x):
+    return pltpu.with_memory_space_constraint(x, pltpu.HBM)
+
+
+def fetch(pairs, sem):
+    copies = [pltpu.make_async_copy(src, dst, sem.at[n]) for n, (src, dst) in enumerate(pairs)]
+    for copy in copies:
+        copy.start()
+    return copies
 
 
 def standardize(values):
@@ -33,15 +48,18 @@
     return 0.5 * jnp.tanh(0.5 * v) + 0.5
 
 
-def align_body(own_i, own_j, x_ref, w_ref, *refs):
-    outs, y_ref = refs[:-1], refs[-1]
+def align_body(own_i, own_j, count, x_hbm, w_hbm, *refs):
+    outs, (x_ref, w_ref, y_ref, sem) = refs[:count], refs[count:]
+    copies = fetch([(x_hbm, x_ref), (w_hbm, w_ref)], sem)
     seqs, residues, depth = x_ref.shape
     width = w_ref.shape[0] // 2
     height, lanes = outs[0].shape
     me = lax.axis_index("row")
     z = lax.axis_index("col")
+    copies[0].wait()
     x = x_ref[...].astype(f32).reshape(seqs * residues, depth)
     normed = standardize(x).astype(bf16)
+    copies[1].wait()
     y_ref[...] = lax.dot_general(
         normed, w_ref[...], (((1,), (1,)), ((), ())), preferred_element_type=f32
     )
@@ -61,43 +79,63 @@
         out[pl.ds(0, extent), :] = jnp.concatenate(left + right, axis=1).astype(bf16)
 
 
-def prepare_body(couple_ref, ids_ref, valid_ref, bias_ref, avg_ref, base_ref, mask_ref, wq_ref, wf_ref, idc_ref):
+def prepare_body(seqs, couple_hbm, ids_ref, valid_hbm, bias_hbm, avg_hbm, base_ref, mask_ref, wq_ref, pick_ref,
+                 couple_ref, valid_ref, bias_ref, avg_ref, wf_ref, idc_ref, sem):
+    sources = (avg_hbm, valid_hbm, bias_hbm, couple_hbm)
+    copies = fetch(list(zip(sources, (avg_ref, valid_ref, bias_ref, couple_ref))), sem)
     own_i, own_j, chans = couple_ref.shape
     pairs, width, _ = wq_ref.shape
+    blocks, lanes, _ = pick_ref.shape
+    total = blocks * seqs
     x0 = lax.axis_index("row") * own_i
     z0 = lax.axis_index("col") * own_j
+
+    row = lax.broadcasted_iota(jnp.int32, pick_ref.shape[1:], 0)
+    col = lax.broadcasted_iota(jnp.int32, pick_ref.shape[1:], 1)
+    unit = row - seqs * width
+    place = lax.rem(unit, width) * total + lax.div(unit, width)
+    place = jnp.where((unit >= 0) & (unit < seqs * width), col - place, -1)
+
+    def pick(r, carry):
+        pick_ref[r] = jnp.where(place == r * seqs, 1.0, 0.0).astype(bf16)
+        return carry
+
+    lax.fori_loop(0, blocks, pick, 0)
+    for j in range(own_j):
+        idc_ref[pl.ds(j, 1), :] = jnp.full((1, chans), ids_ref[z0 + j], jnp.int32)
+    copies[0].wait()
     wf_ref[...] = avg_ref[...].astype(f32)
     for h in range(pairs):
         both = [wf_ref[pl.ds(2 * h + d, width, stride=width), :] for d in range(2)]
         wq_ref[h] = jnp.concatenate(both, axis=1).astype(bf16)
-    for j in range(own_j):
-        idc_ref[pl.ds(j, 1), :] = jnp.full((1, chans), ids_ref[z0 + j], jnp.int32)
+    for copy in copies[1:]:
+        copy.wait()
     idc = idc_ref[...]
     valid_t = valid_ref[...].astype(f32).T
     lane = lax.broadcasted_iota(jnp.int32, valid_t.shape, 1)
     same_bias = bias_ref[0:1, :]
     cross_bias = bias_ref[1:2, :]
 
-    def row(i, carry):
+    def rows(i, carry):
         bias = jnp.where(idc == ids_ref[x0 + i], same_bias, cross_bias)
         base_ref[i] = couple_ref[i].astype(f32) + bias
         column = jnp.sum(jnp.where(lane == i, valid_t, 0.0), axis=1, keepdims=True)
         mask_ref[i] = jnp.broadcast_to(column, (own_j, mask_ref.shape[2])).astype(bf16)
         return carry
 
-    lax.fori_loop(0, own_i, row, 0, unroll=4)
-
-
-def pair_body(seqs, width, turned, *refs):
-    blocks = len(refs) - 10
+    lax.fori_loop(0, own_i, rows, 0, unroll=8)
+
+
+def pair_body(seqs, width, blocks, turned, *refs):
     msgs = refs[:blocks]
-    base_ref, mask_ref, wq_ref, win_ref = refs[blocks : blocks + 4]
-    psum_ref, norm_ref, right_ref = refs[blocks + 4 : blocks + 7]
-    xl_ref, t_ref, flat_ref = refs[blocks + 7 :]
+    base_ref, mask_ref, wq_ref, pick_ref, win_ref = refs[blocks : blocks + 5]
+    psum_ref, norm_ref, right_ref = refs[blocks + 5 : blocks + 8]
+    xl_ref, t_ref, flat_ref = refs[blocks + 8 :]
     own_i, own_j, chans = base_ref.shape
     height, lanes = msgs[0].shape
     total = seqs * blocks
     tri = win_ref.shape[1] // 4
+    half = own_i // 2
 
     for r in range(blocks):
         m = msgs[r][pl.ds(0, own_i), :].astype(f32)
@@ -106,49 +144,50 @@
             xl_ref[pl.ds(r * seqs + s, own_i, stride=total), :] = moved[:, :128]
     lhs = xl_ref[:, :width].astype(bf16)
 
-    row = lax.broadcasted_iota(jnp.int32, (lanes, width * total), 0)
-    col = lax.broadcasted_iota(jnp.int32, (lanes, width * total), 1)
-    unit = row - seqs * width
-    place = (unit % width) * total + unit // width
-    inside = (unit >= 0) & (unit < seqs * width)
     rmat = jnp.zeros((own_j, width * total), f32)
     for r in range(blocks):
-        pick = jnp.where((col == place + r * seqs) & inside, 1.0, 0.0).astype(bf16)
-        rmat += jnp.dot(msgs[r][pl.ds(0, own_j), :], pick, preferred_element_type=f32)
+        rmat += jnp.dot(msgs[r][pl.ds(0, own_j), :], pick_ref[r], preferred_element_type=f32)
     rmat = rmat.astype(bf16)
 
     def expand(h, carry):
         out = jnp.dot(lhs, wq_ref[h], preferred_element_type=f32)
         parts = [out[:, d * chans : (d + 1) * chans].reshape(own_i, total, chans) for d in range(2)]
         block = jnp.concatenate(parts, axis=1).astype(bf16)
-        t_ref[:, pl.ds(pl.multiple_of(h * 2 * total, 16), 2 * total), :] = block
-        return carry
-
-    lax.fori_loop(0, width // 2, expand, 0, unroll=2)
-
-    group = 8 if own_i % 8 == 0 else 1
+        where = pl.ds(pl.multiple_of(h * 2 * total, 16), 2 * total)
+        t_ref[:, where, :chans] = block[:half]
+        t_ref[:, where, chans:] = block[half:]
+        return carry
+
+    lax.fori_loop(0, width // 2, expand, 0, unroll=4)
+
+    step = 4 if half % 4 == 0 else 1
 
     def rows(b, carry):
-        i0 = b * group
-        normed = []
-        for g in range(group):
-            i = i0 + g
-            opm = jnp.dot(rmat, t_ref[i], preferred_element_type=f32) * (1.0 / total)
-            psum = (base_ref[i] + opm).astype(bf16)
-            psum_ref[i] = psum
-            normed.append(standardize(psum.astype(f32)))
-        flat = jnp.concatenate(normed, axis=0).astype(bf16)
-        norm_ref[pl.ds(pl.multiple_of(i0 * own_j, 16), group * own_j), :] = flat
-        mask = mask_ref[pl.ds(i0, group)].astype(f32).reshape(group * own_j, tri)
+        normed = [[], []]
+        for g in range(step):
+            i = b * step + g
+            both = jnp.dot(rmat, t_ref[i], preferred_element_type=f32) * (1.0 / total)
+            for side in range(2):
+                at = i + side * half
+                psum = (base_ref[at] + both[:, side * chans : (side + 1) * chans]).astype(bf16)
+                psum_ref[at] = psum
+                normed[side].append(standardize(psum.astype(f32)))
+        flat = jnp.concatenate(normed[0] + normed[1], axis=0).astype(bf16)
         proj = jnp.dot(flat, win_ref[:, 2 * tri :], preferred_element_type=f32)
-        right = mask * sigmoid(proj[:, :tri]) * proj[:, tri:]
-        if turned:
-            flat_ref[pl.ds(pl.multiple_of(i0 * own_j, 8), group * own_j), :] = right
-        else:
-            right_ref[pl.ds(i0, group)] = right.reshape(group, own_j, tri).astype(bf16)
-        return carry
-
-    lax.fori_loop(0, own_i // group, rows, 0)
+        count = step * own_j
+        for side in range(2):
+            cut = slice(side * count, (side + 1) * count)
+            i0 = b * step + side * half
+            norm_ref[pl.ds(pl.multiple_of(i0 * own_j, 16), count), :] = flat[cut]
+            mask = mask_ref[pl.ds(i0, step)].astype(f32).reshape(count, tri)
+            right = mask * sigmoid(proj[cut, :tri]) * proj[cut, tri:]
+            if turned:
+                flat_ref[pl.ds(pl.multiple_of(i0 * own_j, 8), count), :] = right
+            else:
+                right_ref[pl.ds(i0, step)] = right.reshape(step, own_j, tri).astype(bf16)
+        return carry
+
+    lax.fori_loop(0, half // step, rows, 0, unroll=True)
 
     def turn(k, carry):
         right_ref[k] = flat_ref[pl.ds(k, own_i, stride=own_j), :].astype(bf16)
@@ -174,32 +213,34 @@
             out[pl.ds(b * group, group)] = left.reshape(group, own_j, tri).astype(bf16)
             return carry
 
-        lax.fori_loop(0, out.shape[0] // group, rows, 0)
+        lax.fori_loop(0, out.shape[0] // group, rows, 0, unroll=True)
         at += out.shape[0]
 
 
-def contract(lf_ref, rk_ref, i0, group, depth):
+def contract(lf_ref, halves, i0, group):
     step = 8
-
-    def add(kb, acc):
-        k0 = pl.multiple_of(kb * step, step)
-        acc = list(acc)
-        for d in range(step):
-            right = rk_ref[k0 + d].astype(f32)
-            for t in range(group):
-                acc[t] = acc[t] + lf_ref[i0 + t, pl.ds(k0 + d, 1), :] * right
-        return tuple(acc)
-
-    zero = jnp.zeros(rk_ref.shape[1:], f32)
-    return lax.fori_loop(0, depth // step, add, (zero,) * group)
-
-
-def pick_right(own_pair, refs, rk_ref, sem):
+    acc = (jnp.zeros(halves[0].shape[1:], f32),) * group
+    for h, r_ref in enumerate(halves):
+        depth = r_ref.shape[0]
+
+        def add(kb, acc):
+            k0 = kb * step
+            acc = list(acc)
+            for d in range(step):
+                right = r_ref[k0 + d].astype(f32)
+                for t in range(group):
+                    acc[t] = acc[t] + lf_ref[i0 + t, pl.ds(h * depth + k0 + d, 1), :] * right
+            return tuple(acc)
+
+        acc = lax.fori_loop(0, depth // step, add, acc)
+    return acc
+
+
+def with_right(own_pair, refs, use):
     own, p_own, got, p_got, late, p_late = refs
     r, z = lax.axis_index("row"), lax.axis_index("col")
     keeper = (r % 2) == (z % 2)
     near = ((r // 2) == (z // 2)) == own_pair
-    depth = own.shape[0]
     table = [
         (near & keeper, own, p_got),
         (near & ~keeper, p_own, got),
@@ -207,43 +248,33 @@
         (~near & ~keeper, p_got, late),
     ]
     for cond, a, b in table:
-
-        @pl.when(cond)
-        def _():
-            for h, src in enumerate((a, b)):
-                pltpu.make_async_copy(src, rk_ref.at[pl.ds(h * depth, depth)], sem.at[h]).start()
-
-    def wait():
-        for h in range(2):
-            pltpu.make_async_copy(own, rk_ref.at[pl.ds(h * depth, depth)], sem.at[h]).wait()
-
-    return wait
-
-
-def send_body(*refs):
-    rights, (l_ref, m_ref, o_ref, lf_ref, rk_ref, sem) = refs[:6], refs[6:]
-    own_i, depth, chans = l_ref.shape
-    wait = pick_right(False, rights, rk_ref, sem)
-    lf_ref[:, pl.ds(0, depth), :] = l_ref[...].astype(f32)
-    lf_ref[:, pl.ds(depth, depth), :] = m_ref[...].astype(f32)
-    wait()
+        pl.when(cond)(functools.partial(use, (a, b)))
+
+
+def send_body(first, *refs):
+    rights, (l_ref, m_ref, o_ref, lf_ref) = refs[:6], refs[6:]
+    count, depth = o_ref.shape[0], l_ref.shape[1]
     group = 8
-
-    def rows(b, carry):
-        acc = contract(lf_ref, rk_ref, b * group, group, 2 * depth)
-        for t in range(group):
-            o_ref[b * group + t] = acc[t].astype(bf16)
-        return carry
-
-    lax.fori_loop(0, own_i // group, rows, 0)
+    lf_ref[:, pl.ds(0, depth), :] = l_ref[pl.ds(first, count)].astype(f32)
+    lf_ref[:, pl.ds(depth, depth), :] = m_ref[pl.ds(first, count)].astype(f32)
+
+    def use(halves):
+        def rows(b, carry):
+            acc = contract(lf_ref, halves, b * group, group)
+            for t in range(group):
+                o_ref[b * group + t] = acc[t].astype(bf16)
+            return carry
+
+        lax.fori_loop(0, count // group, rows, 0)
+
+    with_right(False, rights, use)
 
 
 def keep_body(cuts, *refs):
     rights, refs = refs[:6], refs[6:]
     lefts, mets = refs[:cuts], refs[cuts : 2 * cuts]
-    norm_ref, wgate_ref, o_ref, gate_ref, lf_ref, rk_ref, sem = refs[2 * cuts :]
+    norm_ref, wgate_ref, o_ref, gate_ref, lf_ref = refs[2 * cuts :]
     own_i, depth, chans = o_ref.shape
-    wait = pick_right(True, rights, rk_ref, sem)
     at = 0
     for l_ref, m_ref in zip(lefts, mets):
         n = l_ref.shape[0]
@@ -258,16 +289,18 @@
         gate_ref[pl.ds(b * group, group)] = gate.reshape(group, depth, -1)
         return carry
 
-    lax.fori_loop(0, own_i // group, gates, 0)
-    wait()
-
-    def rows(b, carry):
-        acc = contract(lf_ref, rk_ref, b * group, group, 2 * depth)
-        for t in range(group):
-            o_ref[b * group + t] = acc[t]
-        return carry
-
-    lax.fori_loop(0, own_i // group, rows, 0)
+    lax.fori_loop(0, own_i // group, gates, 0, unroll=True)
+
+    def use(halves):
+        def rows(b, carry):
+            acc = contract(lf_ref, halves, b * group, group)
+            for t in range(group):
+                o_ref[b * group + t] = acc[t]
+            return carry
+
+        lax.fori_loop(0, own_i // group, rows, 0)
+
+    with_right(True, rights, use)
 
 
 def join_body(cuts, *refs):
@@ -313,7 +346,7 @@
 
     def rows(b, carry):
         i0 = b * group
-        acc = contract(lf_ref, rk_ref, i0, group, depth)
+        acc = contract(lf_ref, [rk_ref], i0, group)
         for t in range(group):
             o_ref[0, i0 + t] = acc[t].astype(bf16)
         return carry
@@ -385,51 +418,47 @@
     keeper = lambda r, z: r % 2 == z % 2
     other = lambda r, z: r % 2 != z % 2
     got = move(right, every, lambda r, z: (r ^ 2, z) if r % 2 == z % 2 else (r ^ 1, z ^ 1))
+    p_own = move(right, keeper, lambda r, z: (r ^ 1, z))
     mets = [move(left, every, lambda r, z: (r, z ^ 1)) for left in lefts]
+    got, *_ = lax.optimization_barrier((got, *lefts))
     late = move(got, other, lambda r, z: (r ^ 2, z))
-    p_own = move(right, keeper, lambda r, z: (r ^ 1, z))
     p_got = move(got, every, lambda r, z: (r ^ 1, z))
+    late, *mets = lax.optimization_barrier((late, *mets))
     p_late = move(late, other, lambda r, z: (r ^ 1, z))
     rights = (right, p_own, got, p_got, late, p_late)
 
     sums = []
-    for left, met in zip(lefts, mets):
-        n = left.shape[0]
+    for at, first, n in ((0, 0, 8), (0, 8, 16), (0, 24, own_i - 24)):
         part = pl.pallas_call(
-            send_body,
+            functools.partial(send_body, first),
             out_shape=jax.ShapeDtypeStruct((n, own_j, tri), bf16),
-            in_specs=[ANY] * 6 + [VMEM] * 2,
+            in_specs=[VMEM] * 8,
             out_specs=VMEM,
-            scratch_shapes=[
-                pltpu.VMEM((n, 2 * own_j, tri), f32),
-                pltpu.VMEM((2 * own_j, own_i, tri), bf16),
-                pltpu.SemaphoreType.DMA((2,)),
-            ],
-            compiler_params=limit(12),
+            scratch_shapes=[pltpu.VMEM((n, 2 * own_j, tri), f32)],
+            compiler_params=limit(8),
+            cost_estimate=cost(0.12 * n + 0.4),
             name="send_sums",
-        )(*rights, left, met)
+        )(*rights, lefts[at], mets[at])
         sums.append(move(part, every, lambda r, z: (r, z ^ 2)))
 
     own, gate = pl.pallas_call(
         functools.partial(keep_body, cuts),
         out_shape=[jax.ShapeDtypeStruct((own_i, own_j, tri), f32),
                    jax.ShapeDtypeStruct((own_i, own_j, chans), f32)],
-        in_specs=[ANY] * 6 + [VMEM] * (2 * cuts + 2),
+        in_specs=[VMEM] * (6 + 2 * cuts + 2),
         out_specs=[VMEM] * 2,
-        scratch_shapes=[
-            pltpu.VMEM((own_i, 2 * own_j, tri), f32),
-            pltpu.VMEM((2 * own_j, own_i, tri), bf16),
-            pltpu.SemaphoreType.DMA((2,)),
-        ],
-        compiler_params=limit(16),
+        scratch_shapes=[pltpu.VMEM((own_i, 2 * own_j, tri), f32)],
+        compiler_params=limit(12),
+        cost_estimate=cost(6),
         name="keep_sums",
     )(*rights, *lefts, *mets, norm, w_gate)
     return pl.pallas_call(
-        functools.partial(join_body, cuts),
+        functools.partial(join_body, len(sums)),
         out_shape=jax.ShapeDtypeStruct((own_i, own_j, chans), bf16),
-        in_specs=[VMEM] * (cuts + 4),
+        in_specs=[VMEM] * (len(sums) + 4),
         out_specs=VMEM,
         compiler_params=limit(12),
+        cost_estimate=cost(2.4),
         name="join",
     )(*sums, own, psum, gate, w_final)
 
@@ -443,62 +472,77 @@
     total = own_seqs * rows
     lanes = round_up(2 * own_seqs * width, 128)
     height = round_up(max(own_i, own_j), 16)
-    paired = rows == 4 and cols == 4 and own_i == own_j and own_i % 8 == 0
+    paired = rows == 4 and cols == 4 and own_i == own_j and own_i % 8 == 0 and own_i > 24
     scale = 1 if paired else 8
 
     msgs = pl.pallas_call(
-        functools.partial(align_body, own_i, own_j),
+        functools.partial(align_body, own_i, own_j, rows),
         out_shape=[jax.ShapeDtypeStruct((height, lanes), bf16)] * rows,
-        in_specs=[VMEM] * 2,
+        in_specs=[HBM] * 2,
         out_specs=[VMEM] * rows,
-        scratch_shapes=[pltpu.VMEM((own_seqs * residues, 2 * width), f32)],
+        scratch_shapes=[
+            pltpu.VMEM(homolog.shape, bf16),
+            pltpu.VMEM((2 * width, depth), bf16),
+            pltpu.VMEM((own_seqs * residues, 2 * width), f32),
+            pltpu.SemaphoreType.DMA((2,)),
+        ],
         compiler_params=limit(8, scale),
+        cost_estimate=cost(1.5),
         name="align",
-    )(homolog, factors.T)
+    )(hold(homolog), hold(factors.T))
     msgs = [msgs[0]] + [
         lax.ppermute(msg, "row", [(r, r ^ d) for r in range(rows)])
         for d, msg in enumerate(msgs) if d
     ]
 
-    base, mask, wq = pl.pallas_call(
-        prepare_body,
+    base, mask, wq, pick = pl.pallas_call(
+        functools.partial(prepare_body, own_seqs),
         out_shape=[jax.ShapeDtypeStruct((own_i, own_j, chans), f32),
                    jax.ShapeDtypeStruct((own_i, own_j, tri), bf16),
-                   jax.ShapeDtypeStruct((width // 2, width, 2 * chans), bf16)],
-        in_specs=[VMEM, SMEM, VMEM, VMEM, VMEM],
-        out_specs=[VMEM] * 3,
+                   jax.ShapeDtypeStruct((width // 2, width, 2 * chans), bf16),
+                   jax.ShapeDtypeStruct((rows, lanes, width * total), bf16)],
+        in_specs=[HBM, SMEM, HBM, HBM, HBM],
+        out_specs=[VMEM] * 4,
         scratch_shapes=[
-            pltpu.VMEM((width * width, chans), f32),
+            pltpu.VMEM(couple.shape, bf16),
+            pltpu.VMEM(valid.shape, jnp.int32),
+            pltpu.VMEM(bias.shape, f32),
+            pltpu.VMEM(average.shape, bf16),
+            pltpu.VMEM(average.shape, f32),
             pltpu.VMEM((own_j, chans), jnp.int32),
+            pltpu.SemaphoreType.DMA((4,)),
         ],
         compiler_params=limit(8, scale),
+        cost_estimate=cost(2.5),
         name="prepare",
-    )(couple, ids, valid, bias, average)
+    )(hold(couple), ids, hold(valid), hold(bias), hold(average))
 
     extents = (own_j, own_i) if paired else (own_i, own_j)
     psum, norm, right = pl.pallas_call(
-        functools.partial(pair_body, own_seqs, width, paired),
+        functools.partial(pair_body, own_seqs, width, rows, paired),
         out_shape=[jax.ShapeDtypeStruct((own_i, own_j, chans), bf16),
                    jax.ShapeDtypeStruct((own_i * own_j, chans), bf16),
                    jax.ShapeDtypeStruct(extents + (tri,), bf16)],
-        in_specs=[VMEM] * (rows + 4),
+        in_specs=[VMEM] * (rows + 5),
         out_specs=[VMEM] * 3,
         scratch_shapes=[
             pltpu.VMEM((own_i * total, 128), f32),
-            pltpu.VMEM((own_i, width * total, chans), bf16),
+            pltpu.VMEM((own_i // 2, width * total, 2 * chans), bf16),
             pltpu.VMEM((own_i * own_j, tri), f32),
         ],
         compiler_params=limit(16, scale),
+        cost_estimate=cost(4.5),
         name="pair",
-    )(*msgs, base, mask, wq, w_in)
-
-    cuts = [16, own_i - 16] if paired else [own_i]
+    )(*msgs, base, mask, wq, pick, w_in)
+
+    cuts = [own_i]
     lefts = pl.pallas_call(
         left_body,
         out_shape=[jax.ShapeDtypeStruct((n, own_j, tri), bf16) for n in cuts],
         in_specs=[VMEM] * 3,
         out_specs=[VMEM] * len(cuts),
         compiler_params=limit(8, scale),
+        cost_estimate=cost(1),
         name="left",
     )(norm, mask, w_in)
     if paired:

time: 67.2 us -> 59.2 us (0.88)
  local copies, waits for them, and re-layouts: 3.65 us -> 0.02 us
  Pallas kernels: 23.3 us -> 21.2 us
  waiting for transfers between devices: 19.3 us -> 17.8 us
    unnamed x20 -> x8, local copies, waits for them, and re-layouts: 3.65 us -> 0.02 us
    ppermute x9, waiting for transfers between devices: 19.3 us -> 17.3 us  [move(): return lax.ppermute(value, ('row', 'col'), pairs)]
    pallas_call x1, Pallas kernels: 6.51 us -> 5.36 us  [paired_plan(): pl.pallas_call(functools.partial(keep_body, cuts), out_shape=[jax.ShapeDt...]
    pallas_call x6 -> x7, Pallas kernels: 15.8 us -> 15.5 us  [the longest x3 5.16 us: paired_plan(): pl.pallas_call(functools.partial(send_body, first), out_shape=jax.ShapeDt...]
  transfers between devices with their start and end apart: 12 -> 12, of which waited for: 3 -> 5; matrix products, arithmetic and copies ran while one was open for 0% -> 0% of each run, Pallas kernels for 23% -> 19%
where the time goes in v3:
time: 59.2 us; the launch traced here: 59 us
  Pallas kernels  21.2 us (36%)
  starting transfers between devices  19.9 us (34%)
  waiting for transfers between devices  17.8 us (30%)
    ppermute x9, waiting for transfers between devices, move(): return lax.ppermute(value, ('row', 'col'), pairs)  17.3 us
    ppermute x9, starting transfers between devices, move(): return lax.ppermute(value, ('row', 'col'), pairs)  16.7 us
    pallas_call x1, Pallas kernels, paired_plan(): pl.pallas_call(functools.partial(keep_body, cuts), out_shape=[jax.ShapeDt...  5.36 us
    pallas_call x3, Pallas kernels, paired_plan(): pl.pallas_call(functools.partial(send_body, first), out_shape=jax.ShapeDt...  5.16 us
    pallas_call x1, Pallas kernels, shards(): pl.pallas_call(functools.partial(pair_body, own_seqs, width, rows, paired...  3.92 us
    ppermute x3, starting transfers between devices, shards(): lax.ppermute(msg, 'row', [(r, r ^ d) for r in range(rows)])  3.15 us
    pallas_call x1, Pallas kernels, shards(): pl.pallas_call(functools.partial(prepare_body, own_seqs), out_shape=[jax....  2.54 us
    pallas_call x1, Pallas kernels, paired_plan(): pl.pallas_call(functools.partial(join_body, len(sums)), out_shape=jax.Sha...  2.41 us
  transfers between devices with their start and end apart: 12, of which 5 were waited for; matrix products, arithmetic and copies ran while one was open for 0% of the time, Pallas kernels for 19%

profile of v3, /device:TPU:0, one launch (start us, length us, event | category | flops | bytes accessed | tf_op | source)
XLA Modules:
  0.0 59.0 jit_solution(7072051763021913144)
XLA Ops:
  0.0 1.4 %align.1 = (bf16[48,128]{1,0:T(8,128)(2,1)S(1)}, bf16[48,128]{1,0:T(8,128)(2,1)S(1)}, bf16[48,128]{1,0:T(8,128)(2,1)S(1)}, bf16[48,128]{1,0:T(8,128)(2,1)S(1)}) custom-call(bf16[2,160,256]{2,1,0:T(8,128)(2,1)} %x_hbm.1, bf16[64,256]{1,0:T(8,128)(2,1)} %bitcast.1), custom_call_target="tpu_custom_call" | custom-call | bytes 5535000 | tf_op jit(solution)/shard_map/align/pallas_call | solution.py:478
  1.4 0.5 collective-permute-start
  1.9 0.0 copy-start.3
  2.0 2.6 %collective-permute-start.1 = (bf16[48,128]{1,0:T(8,128)(2,1)S(1)}, bf16[48,128]{1,0:T(8,128)(2,1)S(1)}, u32[]{:S(2)}, u32[]{:S(2)}) collective-permute-start(bf16[48,128]{1,0:T(8,128)(2,1)S(1)} %get-tuple-element.23), channel_id=1, source_target_pairs={{0,8},{4,12},{8,0},{12,4},{1,9},{5,13},{9,1},{13,5},{2,10},{6,14},... | collective-permute-start | bytes 36872 | tf_op jit(solution)/shard_map/ppermute | solution.py:494
  4.5 0.0 copy-start
  4.5 0.1 collective-permute-start.2
  4.6 0.0 copy-done.3
  4.6 2.5 %prepare.1 = (f32[40,40,128]{2,1,0:T(8,128)S(1)}, bf16[40,40,128]{2,1,0:T(8,128)(2,1)S(1)}, bf16[16,32,256]{2,1,0:T(8,128)(2,1)S(1)}, bf16[4,128,256]{2,1,0:T(8,128)(2,1)S(1)}) custom-call(bf16[40,40,128]{2,1,0:T(8,128)(2,1)} %couple_hbm.1, s32[160]{0:T(256)S(1)} %copy-done.3, s32[40,40]{1,0:T(8,128)} %valid_hbm.1, f32[2,128]{1,0:T(2,128)} %bias_hbm.1, ...), custom_call_target="tpu_custom_call" | custom-call | bytes 9225000 | tf_op jit(solution)/shard_map/prepare/pallas_call | solution.py:498
  7.1 0.0 collective-permute-done.refs_1_
  7.2 0.0 collective-permute-done.1.refs_2_
  7.2 0.5 collective-permute-done.2.refs_3_
  7.7 0.0 copy-done
  7.7 3.9 %pair.1 = (bf16[40,40,128]{2,1,0:T(8,128)(2,1)S(1)}, bf16[1600,128]{1,0:T(8,128)(2,1)S(1)}, bf16[40,40,128]{2,1,0:T(8,128)(2,1)S(1)}) custom-call(bf16[48,128]{1,0:T(8,128)(2,1)S(1)} %get-tuple-element.21.refs_0_, bf16[48,128]{1,0:T(8,128)(2,1)S(1)} %collective-permute-done.refs_1_, bf16[48,128]{1,0:T(8,128)(2,1)S(1)} %collective-permute-done.1.refs_2_, ...), custom_call_target="tpu_custom_call" | custom-call | bytes 16605000 | tf_op jit(solution)/shard_map/pair/pallas_call | solution.py:521
  11.6 1.3 %collective-permute-start.4 = (bf16[40,40,128]{2,1,0:T(8,128)(2,1)S(1)}, bf16[40,40,128]{2,1,0:T(8,128)(2,1)S(1)}, u32[]{:S(2)}, u32[]{:S(2)}) collective-permute-start(bf16[40,40,128]{2,1,0:T(8,128)(2,1)S(1)} %get-tuple-element.29.refs_0_), channel_id=1, source_target_pairs={{0,8},{1,4},{2,10},{3,6},{4,1},{5,13},{6,3},{7,15},{8,0},{9,12},{1... | collective-permute-start | bytes 1228808 | tf_op jit(solution)/shard_map/ppermute | solution.py:415
  12.9 0.4 left.1.refs_6_
  13.3 0.6 %collective-permute-start.7 = (bf16[40,40,128]{2,1,0:T(8,128)(2,1)S(1)}, bf16[40,40,128]{2,1,0:T(8,128)(2,1)S(1)}, u32[]{:S(2)}, u32[]{:S(2)}) collective-permute-start(bf16[40,40,128]{2,1,0:T(8,128)(2,1)S(1)} %left.1.refs_6_), channel_id=1, source_target_pairs={{0,1},{1,0},{2,3},{3,2},{4,5},{5,4},{6,7},{7,6},{8,9},{9,8},{10,11... | collective-permute-start | bytes 1228808 | tf_op jit(solution)/shard_map/ppermute | solution.py:415
  13.9 5.7 %collective-permute-done.4.refs_2_ = bf16[40,40,128]{2,1,0:T(8,128)(2,1)S(1)} collective-permute-done((bf16[40,40,128]{2,1,0:T(8,128)(2,1)S(1)}, bf16[40,40,128]{2,1,0:T(8,128)(2,1)S(1)}, u32[]{:S(2)}, u32[]{:S(2)}) %collective-permute-start.4) | collective-permute-done | bytes 409632 | tf_op jit(solution)/shard_map/ppermute | solution.py:415
  19.6 0.7 %collective-permute-start.6 = (bf16[40,40,128]{2,1,0:T(8,128)(2,1)S(1)}, bf16[40,40,128]{2,1,0:T(8,128)(2,1)S(1)}, u32[]{:S(2)}, u32[]{:S(2)}) collective-permute-start(bf16[40,40,128]{2,1,0:T(8,128)(2,1)S(1)} %collective-permute-done.4.refs_2_), channel_id=1, source_target_pairs={{1,9},{3,11},{4,12},{6,14},{9,1},{11,3},{12,4},{14,6},{17,25},{19,... | collective-permute-start | bytes 1228808 | tf_op jit(solution)/shard_map/ppermute | solution.py:415
  20.3 7.1 %collective-permute-start.3 = (bf16[40,40,128]{2,1,0:T(8,128)(2,1)S(1)}, bf16[40,40,128]{2,1,0:T(8,128)(2,1)S(1)}, u32[]{:S(2)}, u32[]{:S(2)}) collective-permute-start(bf16[40,40,128]{2,1,0:T(8,128)(2,1)S(1)} %get-tuple-element.29.refs_0_), channel_id=1, source_target_pairs={{0,4},{2,6},{5,1},{7,3},{8,12},{10,14},{13,9},{15,11},{16,20},{18,... | collective-permute-start | bytes 1228808 | tf_op jit(solution)/shard_map/ppermute | solution.py:415
  27.4 0.1 collective-permute-start.5
  27.4 0.7 %collective-permute-done.7.refs_7_ = bf16[40,40,128]{2,1,0:T(8,128)(2,1)S(1)} collective-permute-done((bf16[40,40,128]{2,1,0:T(8,128)(2,1)S(1)}, bf16[40,40,128]{2,1,0:T(8,128)(2,1)S(1)}, u32[]{:S(2)}, u32[]{:S(2)}) %collective-permute-start.7) | collective-permute-done | bytes 409632 | tf_op jit(solution)/shard_map/ppermute | solution.py:415
  28.1 0.0 collective-permute-done.6.refs_4_
  28.1 1.3 %collective-permute-start.8 = (bf16[40,40,128]{2,1,0:T(8,128)(2,1)S(1)}, bf16[40,40,128]{2,1,0:T(8,128)(2,1)S(1)}, u32[]{:S(2)}, u32[]{:S(2)}) collective-permute-start(bf16[40,40,128]{2,1,0:T(8,128)(2,1)S(1)} %collective-permute-done.6.refs_4_), channel_id=1, source_target_pairs={{1,5},{3,7},{4,0},{6,2},{9,13},{11,15},{12,8},{14,10},{17,21},{19,... | collective-permute-start | bytes 1228808 | tf_op jit(solution)/shard_map/ppermute | solution.py:415
  29.4 0.0 collective-permute-done.3.refs_1_
  29.4 0.0 collective-permute-done.5.refs_3_
  29.4 3.8 %collective-permute-done.8.refs_5_ = bf16[40,40,128]{2,1,0:T(8,128)(2,1)S(1)} collective-permute-done((bf16[40,40,128]{2,1,0:T(8,128)(2,1)S(1)}, bf16[40,40,128]{2,1,0:T(8,128)(2,1)S(1)}, u32[]{:S(2)}, u32[]{:S(2)}) %collective-permute-start.8) | collective-permute-done | bytes 409632 | tf_op jit(solution)/shard_map/ppermute | solution.py:415
  33.3 2.1 %send_sums.5 = bf16[16,40,128]{2,1,0:T(8,128)(2,1)S(1)} custom-call(bf16[40,40,128]{2,1,0:T(8,128)(2,1)S(1)} %get-tuple-element.29.refs_0_, bf16[40,40,128]{2,1,0:T(8,128)(2,1)S(1)} %collective-permute-done.3.refs_1_, bf16[40,40,128]{2,1,0:T(8,128)(2,1)S(1)} %collective-permute-done.4.refs_2_, bf16[40,40,128]{2,1,0:T(8,128)(2,1)S(1)} %collective-permute-done.5.refs_3_, ...), custom_call_target="tpu_custom_call" | custom-call | bytes 8560800 | tf_op jit(solution)/shard_map/send_sums/pallas_call | solution.py:432
  35.3 2.7 %collective-permute-start.11 = (bf16[16,40,128]{2,1,0:T(8,128)(2,1)S(1)}, bf16[16,40,128]{2,1,0:T(8,128)(2,1)S(1)}, u32[]{:S(2)}, u32[]{:S(2)}) collective-permute-start(bf16[16,40,128]{2,1,0:T(8,128)(2,1)S(1)} %send_sums.5), channel_id=1, source_target_pairs={{0,2},{1,3},{2,0},{3,1},{4,6},{5,7},{6,4},{7,5},{8,10},{9,11},{10,... | collective-permute-start | bytes 491528 | tf_op jit(solution)/shard_map/ppermute | solution.py:415
  38.0 2.1 %send_sums.4 = bf16[16,40,128]{2,1,0:T(8,128)(2,1)S(1)} custom-call(bf16[40,40,128]{2,1,0:T(8,128)(2,1)S(1)} %get-tuple-element.29.refs_0_, bf16[40,40,128]{2,1,0:T(8,128)(2,1)S(1)} %collective-permute-done.3.refs_1_, bf16[40,40,128]{2,1,0:T(8,128)(2,1)S(1)} %collective-permute-done.4.refs_2_, bf16[40,40,128]{2,1,0:T(8,128)(2,1)S(1)} %collective-permute-done.5.refs_3_, ...), custom_call_target="tpu_custom_call" | custom-call | bytes 8560800 | tf_op jit(solution)/shard_map/send_sums/pallas_call | solution.py:432
  40.1 0.0 copy-start.1
  40.1 0.4 collective-permute-start.10
  40.5 1.0 %send_sums.3 = bf16[8,40,128]{2,1,0:T(8,128)(2,1)S(1)} custom-call(bf16[40,40,128]{2,1,0:T(8,128)(2,1)S(1)} %get-tuple-element.29.refs_0_, bf16[40,40,128]{2,1,0:T(8,128)(2,1)S(1)} %collective-permute-done.3.refs_1_, bf16[40,40,128]{2,1,0:T(8,128)(2,1)S(1)} %collective-permute-done.4.refs_2_, bf16[40,40,128]{2,1,0:T(8,128)(2,1)S(1)} %collective-permute-done.5.refs_3_, ...), custom_call_target="tpu_custom_call" | custom-call | bytes 5018400 | tf_op jit(solution)/shard_map/send_sums/pallas_call | solution.py:432
  41.5 0.0 copy-start.2
  41.5 2.7 %collective-permute-start.9 = (bf16[8,40,128]{2,1,0:T(8,128)(2,1)S(1)}, bf16[8,40,128]{2,1,0:T(8,128)(2,1)S(1)}, u32[]{:S(2)}, u32[]{:S(2)}) collective-permute-start(bf16[8,40,128]{2,1,0:T(8,128)(2,1)S(1)} %send_sums.3), channel_id=1, source_target_pairs={{0,2},{1,3},{2,0},{3,1},{4,6},{5,7},{6,4},{7,5},{8,10},{9,11},{10,... | collective-permute-start | bytes 245768 | tf_op jit(solution)/shard_map/ppermute | solution.py:415
  44.2 0.0 copy-done.1
  44.2 5.4 %keep_sums.1 = (f32[40,40,128]{2,1,0:T(8,128)S(1)}, f32[40,40,128]{2,1,0:T(8,128)S(1)}) custom-call(bf16[40,40,128]{2,1,0:T(8,128)(2,1)S(1)} %get-tuple-element.29.refs_0_, bf16[40,40,128]{2,1,0:T(8,128)(2,1)S(1)} %collective-permute-done.3.refs_1_, bf16[40,40,128]{2,1,0:T(8,128)(2,1)S(1)} %collective-permute-done.4.refs_2_, ...), custom_call_target="tpu_custom_call" | custom-call | bytes 22140000 | tf_op jit(solution)/shard_map/keep_sums/pallas_call | solution.py:444
  49.6 7.0 %collective-permute-done.9.refs_0_ = bf16[8,40,128]{2,1,0:T(8,128)(2,1)S(1)} collective-permute-done((bf16[8,40,128]{2,1,0:T(8,128)(2,1)S(1)}, bf16[8,40,128]{2,1,0:T(8,128)(2,1)S(1)}, u32[]{:S(2)}, u32[]{:S(2)}) %collective-permute-start.9) | collective-permute-done | bytes 81952 | tf_op jit(solution)/shard_map/ppermute | solution.py:415
  56.6 0.0 collective-permute-done.11.refs_2_
  56.6 0.0 collective-permute-done.10.refs_1_
  56.6 0.0 copy-done.2
  56.6 2.4 %join.1 = bf16[40,40,128]{2,1,0:T(8,128)(2,1)} custom-call(bf16[8,40,128]{2,1,0:T(8,128)(2,1)S(1)} %collective-permute-done.9.refs_0_, bf16[16,40,128]{2,1,0:T(8,128)(2,1)S(1)} %collective-permute-done.10.refs_1_, bf16[16,40,128]{2,1,0:T(8,128)(2,1)S(1)} %collective-permute-done.11.refs_2_, f32[40,40,128]{2,1,0:T(8,128)S(1)} %get-tuple-element.34.refs_3_, ...), custom_call_target="tpu_custom_call" | custom-call | bytes 8856000 | tf_op jit(solution)/shard_map/join/pallas_call | solution.py:455
Async XLA Ops:
  1.4 5.7 %collective-permute-start = (bf16[48,128]{1,0:T(8,128)(2,1)S(1)}, bf16[48,128]{1,0:T(8,128)(2,1)S(1)}, u32[]{:S(2)}, u32[]{:S(2)}) collective-permute-start(bf16[48,128]{1,0:T(8,128)(2,1)S(1)} %get-tuple-element.22), channel_id=1, source_target_pairs={{0,4},{4,0},{8,12},{12,8},{1,5},{5,1},{9,13},{13,9},{2,6},{6,2},{1... | collective-permute-start | bytes 36872 | tf_op jit(solution)/shard_map/ppermute | solution.py:494
  1.9 2.6 %copy-start.3 = (s32[160]{0:T(256)S(1)}, s32[160]{0:T(256)}, u32[]{:S(2)}) copy-start(s32[160]{0:T(256)} %ids_ref.1) | copy-start | bytes 1924
  2.0 5.2 %collective-permute-start.1 = (bf16[48,128]{1,0:T(8,128)(2,1)S(1)}, bf16[48,128]{1,0:T(8,128)(2,1)S(1)}, u32[]{:S(2)}, u32[]{:S(2)}) collective-permute-start(bf16[48,128]{1,0:T(8,128)(2,1)S(1)} %get-tuple-element.23), channel_id=1, source_target_pairs={{0,8},{4,12},{8,0},{12,4},{1,9},{5,13},{9,1},{13,5},{2,10},{6,14},... | collective-permute-start | bytes 36872 | tf_op jit(solution)/shard_map/ppermute | solution.py:494
  4.5 3.1 %copy-start = (bf16[128,512]{1,0:T(8,128)(2,1)S(1)}, bf16[128,512]{1,0:T(8,128)(2,1)}, u32[]{:S(2)}) copy-start(bf16[128,512]{1,0:T(8,128)(2,1)} %win_ref.1) | copy-start | bytes 393220
  4.5 3.1 %collective-permute-start.2 = (bf16[48,128]{1,0:T(8,128)(2,1)S(1)}, bf16[48,128]{1,0:T(8,128)(2,1)S(1)}, u32[]{:S(2)}, u32[]{:S(2)}) collective-permute-start(bf16[48,128]{1,0:T(8,128)(2,1)S(1)} %get-tuple-element.24), channel_id=1, source_target_pairs={{0,12},{4,8},{8,4},{12,0},{1,13},{5,9},{9,5},{13,1},{2,14},{6,10},... | collective-permute-start | bytes 36872 | tf_op jit(solution)/shard_map/ppermute | solution.py:494
  11.6 8.0 %collective-permute-start.4 = (bf16[40,40,128]{2,1,0:T(8,128)(2,1)S(1)}, bf16[40,40,128]{2,1,0:T(8,128)(2,1)S(1)}, u32[]{:S(2)}, u32[]{:S(2)}) collective-permute-start(bf16[40,40,128]{2,1,0:T(8,128)(2,1)S(1)} %get-tuple-element.29.refs_0_), channel_id=1, source_target_pairs={{0,8},{1,4},{2,10},{3,6},{4,1},{5,13},{6,3},{7,15},{8,0},{9,12},{1... | collective-permute-start | bytes 1228808 | tf_op jit(solution)/shard_map/ppermute | solution.py:415
  13.3 14.9 %collective-permute-start.7 = (bf16[40,40,128]{2,1,0:T(8,128)(2,1)S(1)}, bf16[40,40,128]{2,1,0:T(8,128)(2,1)S(1)}, u32[]{:S(2)}, u32[]{:S(2)}) collective-permute-start(bf16[40,40,128]{2,1,0:T(8,128)(2,1)S(1)} %left.1.refs_6_), channel_id=1, source_target_pairs={{0,1},{1,0},{2,3},{3,2},{4,5},{5,4},{6,7},{7,6},{8,9},{9,8},{10,11... | collective-permute-start | bytes 1228808 | tf_op jit(solution)/shard_map/ppermute | solution.py:415
  19.6 8.5 %collective-permute-start.6 = (bf16[40,40,128]{2,1,0:T(8,128)(2,1)S(1)}, bf16[40,40,128]{2,1,0:T(8,128)(2,1)S(1)}, u32[]{:S(2)}, u32[]{:S(2)}) collective-permute-start(bf16[40,40,128]{2,1,0:T(8,128)(2,1)S(1)} %collective-permute-done.4.refs_2_), channel_id=1, source_target_pairs={{1,9},{3,11},{4,12},{6,14},{9,1},{11,3},{12,4},{14,6},{17,25},{19,... | collective-permute-start | bytes 1228808 | tf_op jit(solution)/shard_map/ppermute | solution.py:415
  20.3 9.1 %collective-permute-start.3 = (bf16[40,40,128]{2,1,0:T(8,128)(2,1)S(1)}, bf16[40,40,128]{2,1,0:T(8,128)(2,1)S(1)}, u32[]{:S(2)}, u32[]{:S(2)}) collective-permute-start(bf16[40,40,128]{2,1,0:T(8,128)(2,1)S(1)} %get-tuple-element.29.refs_0_), channel_id=1, source_target_pairs={{0,4},{2,6},{5,1},{7,3},{8,12},{10,14},{13,9},{15,11},{16,20},{18,... | collective-permute-start | bytes 1228808 | tf_op jit(solution)/shard_map/ppermute | solution.py:415
  27.4 2.1 %collective-permute-start.5 = (bf16[40,40,128]{2,1,0:T(8,128)(2,1)S(1)}, bf16[40,40,128]{2,1,0:T(8,128)(2,1)S(1)}, u32[]{:S(2)}, u32[]{:S(2)}) collective-permute-start(bf16[40,40,128]{2,1,0:T(8,128)(2,1)S(1)} %collective-permute-done.4.refs_2_), channel_id=1, source_target_pairs={{0,4},{1,5},{2,6},{3,7},{4,0},{5,1},{6,2},{7,3},{8,12},{9,13},{10,... | collective-permute-start | bytes 1228808 | tf_op jit(solution)/shard_map/ppermute | solution.py:415
  28.1 5.1 %collective-permute-start.8 = (bf16[40,40,128]{2,1,0:T(8,128)(2,1)S(1)}, bf16[40,40,128]{2,1,0:T(8,128)(2,1)S(1)}, u32[]{:S(2)}, u32[]{:S(2)}) collective-permute-start(bf16[40,40,128]{2,1,0:T(8,128)(2,1)S(1)} %collective-permute-done.6.refs_4_), channel_id=1, source_target_pairs={{1,5},{3,7},{4,0},{6,2},{9,13},{11,15},{12,8},{14,10},{17,21},{19,... | collective-permute-start | bytes 1228808 | tf_op jit(solution)/shard_map/ppermute | solution.py:415
  35.3 21.3 %collective-permute-start.11 = (bf16[16,40,128]{2,1,0:T(8,128)(2,1)S(1)}, bf16[16,40,128]{2,1,0:T(8,128)(2,1)S(1)}, u32[]{:S(2)}, u32[]{:S(2)}) collective-permute-start(bf16[16,40,128]{2,1,0:T(8,128)(2,1)S(1)} %send_sums.5), channel_id=1, source_target_pairs={{0,2},{1,3},{2,0},{3,1},{4,6},{5,7},{6,4},{7,5},{8,10},{9,11},{10,... | collective-permute-start | bytes 491528 | tf_op jit(solution)/shard_map/ppermute | solution.py:415
  40.1 4.1 %copy-start.1 = (bf16[128,128]{1,0:T(8,128)(2,1)S(1)}, bf16[128,128]{1,0:T(8,128)(2,1)}, u32[]{:S(2)}) copy-start(bf16[128,128]{1,0:T(8,128)(2,1)} %refs_9_.1) | copy-start | bytes 98308
  40.1 16.5 %collective-permute-start.10 = (bf16[16,40,128]{2,1,0:T(8,128)(2,1)S(1)}, bf16[16,40,128]{2,1,0:T(8,128)(2,1)S(1)}, u32[]{:S(2)}, u32[]{:S(2)}) collective-permute-start(bf16[16,40,128]{2,1,0:T(8,128)(2,1)S(1)} %send_sums.4), channel_id=1, source_target_pairs={{0,2},{1,3},{2,0},{3,1},{4,6},{5,7},{6,4},{7,5},{8,10},{9,11},{10,... | collective-permute-start | bytes 491528 | tf_op jit(solution)/shard_map/ppermute | solution.py:415
  41.5 15.1 %copy-start.2 = (bf16[128,128]{1,0:T(8,128)(2,1)S(1)}, bf16[128,128]{1,0:T(8,128)(2,1)}, u32[]{:S(2)}) copy-start(bf16[128,128]{1,0:T(8,128)(2,1)} %refs_6_.1) | copy-start | bytes 98308
  41.5 15.1 %collective-permute-start.9 = (bf16[8,40,128]{2,1,0:T(8,128)(2,1)S(1)}, bf16[8,40,128]{2,1,0:T(8,128)(2,1)S(1)}, u32[]{:S(2)}, u32[]{:S(2)}) collective-permute-start(bf16[8,40,128]{2,1,0:T(8,128)(2,1)S(1)} %send_sums.3), channel_id=1, source_target_pairs={{0,2},{1,3},{2,0},{3,1},{4,6},{5,7},{6,4},{7,5},{8,10},{9,11},{10,... | collective-permute-start | bytes 245768 | tf_op jit(solution)/shard_map/ppermute | solution.py:415

commit v4 on v3

--- a/solution.py
+++ b/solution.py
@@ -303,24 +303,24 @@
     with_right(True, rights, use)
 
 
-def join_body(cuts, *refs):
-    sums, (own_ref, psum_ref, gate_ref, w_ref, out_ref) = refs[:cuts], refs[cuts:]
-    own_i, extent, chans = out_ref.shape
+def join_body(first, sum_ref, own_ref, psum_ref, gate_ref, w_ref, *refs):
+    out_hbm, done_ref, sem = refs[-3:]
+    count, extent, chans = done_ref.shape
     group = 8
-    at = 0
-    for part in sums:
-        first = at
-
-        def rows(b, carry):
-            rows_ = pl.ds(first + b * group, group)
-            mixed = own_ref[rows_] + part[pl.ds(b * group, group)].astype(f32)
-            normed = standardize(mixed).reshape(group * extent, -1).astype(bf16)
-            update = jnp.dot(normed, w_ref[...], preferred_element_type=f32).reshape(group, extent, -1)
-            out_ref[rows_] = (psum_ref[rows_].astype(f32) + gate_ref[rows_] * update).astype(bf16)
-            return carry
-
-        lax.fori_loop(0, part.shape[0] // group, rows, 0)
-        at += part.shape[0]
+
+    def rows(b, carry):
+        some = pl.ds(b * group, group)
+        all_ = pl.ds(first + b * group, group)
+        mixed = own_ref[all_] + sum_ref[some].astype(f32)
+        normed = standardize(mixed).reshape(group * extent, -1).astype(bf16)
+        update = jnp.dot(normed, w_ref[...], preferred_element_type=f32).reshape(group, extent, -1)
+        done_ref[some] = (psum_ref[all_].astype(f32) + gate_ref[all_] * update).astype(bf16)
+        return carry
+
+    lax.fori_loop(0, count // group, rows, 0, unroll=True)
+    copy = pltpu.make_async_copy(done_ref, out_hbm.at[pl.ds(first, count)], sem)
+    copy.start()
+    copy.wait()
 
 
 def triangle_body(l_ref, r_ref, o_ref, lf_ref, flat_ref, rk_ref):
@@ -416,19 +416,19 @@
 
     every = lambda r, z: True
     keeper = lambda r, z: r % 2 == z % 2
-    other = lambda r, z: r % 2 != z % 2
-    got = move(right, every, lambda r, z: (r ^ 2, z) if r % 2 == z % 2 else (r ^ 1, z ^ 1))
-    p_own = move(right, keeper, lambda r, z: (r ^ 1, z))
+    got = move(right, every, lambda r, z: (r ^ 2, z) if keeper(r, z) else (r ^ 1, z ^ 1))
+    p_own = move(right, every, lambda r, z: (r ^ 1, z))
+    got, p_own, *lefts = lax.optimization_barrier((got, p_own, *lefts))
+    late = move(got, every, lambda r, z: (r, z) if keeper(r, z) else (r ^ 2, z))
+    p_got = move(got, every, lambda r, z: (r ^ 1, z))
     mets = [move(left, every, lambda r, z: (r, z ^ 1)) for left in lefts]
-    got, *_ = lax.optimization_barrier((got, *lefts))
-    late = move(got, other, lambda r, z: (r ^ 2, z))
-    p_got = move(got, every, lambda r, z: (r ^ 1, z))
-    late, *mets = lax.optimization_barrier((late, *mets))
-    p_late = move(late, other, lambda r, z: (r ^ 1, z))
+    late, mets[0] = lax.optimization_barrier((late, mets[0]))
+    p_late = move(late, every, lambda r, z: (r ^ 1, z))
     rights = (right, p_own, got, p_got, late, p_late)
 
     sums = []
-    for at, first, n in ((0, 0, 8), (0, 8, 16), (0, 24, own_i - 24)):
+    chunks = ((0, 0, 0, 16), (1, 0, 24, own_i - 24), (0, 16, 16, 8))
+    for at, first, _, n in chunks:
         part = pl.pallas_call(
             functools.partial(send_body, first),
             out_shape=jax.ShapeDtypeStruct((n, own_j, tri), bf16),
@@ -452,15 +452,20 @@
         cost_estimate=cost(6),
         name="keep_sums",
     )(*rights, *lefts, *mets, norm, w_gate)
-    return pl.pallas_call(
-        functools.partial(join_body, len(sums)),
-        out_shape=jax.ShapeDtypeStruct((own_i, own_j, chans), bf16),
-        in_specs=[VMEM] * (len(sums) + 4),
-        out_specs=VMEM,
-        compiler_params=limit(12),
-        cost_estimate=cost(2.4),
-        name="join",
-    )(*sums, own, psum, gate, w_final)
+    out = []
+    for part, (_, _, first, n) in zip(sums, chunks):
+        out = [pl.pallas_call(
+            functools.partial(join_body, first),
+            out_shape=jax.ShapeDtypeStruct((own_i, own_j, chans), bf16),
+            in_specs=[VMEM] * 5 + [HBM] * len(out),
+            out_specs=HBM,
+            scratch_shapes=[pltpu.VMEM((n, own_j, chans), bf16), pltpu.SemaphoreType.DMA],
+            input_output_aliases={5: 0} if out else {},
+            compiler_params=limit(8),
+            cost_estimate=cost(0.06 * n),
+            name="join",
+        )(part, own, psum, gate, w_final, *out)]
+    return out[0]
 
 
 def shards(homolog, couple, ids, valid, bias, factors, average, w_in, w_gate, w_final):
@@ -535,7 +540,7 @@
         name="pair",
     )(*msgs, base, mask, wq, pick, w_in)
 
-    cuts = [own_i]
+    cuts = [24, own_i - 24] if paired else [own_i]
     lefts = pl.pallas_call(
         left_body,
         out_shape=[jax.ShapeDtypeStruct((n, own_j, tri), bf16) for n in cuts],

time: 59.2 us -> 56.8 us (0.959)
  starting transfers between devices: 19.9 us -> 15.2 us
  waiting for transfers between devices: 17.8 us -> 19.4 us
  Pallas kernels: 21.2 us -> 21.8 us
    ppermute x9 -> x10, starting transfers between devices: 16.7 us -> 12.1 us  [move(): return lax.ppermute(value, ('row', 'col'), pairs)]
    ppermute x9 -> x10, waiting for transfers between devices: 17.3 us -> 18.9 us  [move(): return lax.ppermute(value, ('row', 'col'), pairs)]
    pallas_call x1 -> x3, Pallas kernels: 2.41 us -> 3.09 us  [paired_plan(): pl.pallas_call(functools.partial(join_body, first), out_shape=jax.ShapeDt...]
  transfers between devices with their start and end apart: 12 -> 13, of which waited for: 5 -> 7; matrix products, arithmetic and copies ran while one was open for 0% -> 0% of each run, Pallas kernels for 19% -> 27%
where the time goes in v4:
time: 56.8 us; the launch traced here: 56.6 us
  Pallas kernels  21.8 us (38%)
  waiting for transfers between devices  19.4 us (34%)
  starting transfers between devices  15.2 us (27%)
    ppermute x10, waiting for transfers between devices, move(): return lax.ppermute(value, ('row', 'col'), pairs)  18.9 us
    ppermute x10, starting transfers between devices, move(): return lax.ppermute(value, ('row', 'col'), pairs)  12.1 us
    pallas_call x1, Pallas kernels, paired_plan(): pl.pallas_call(functools.partial(keep_body, cuts), out_shape=[jax.ShapeDt...  5.37 us
    pallas_call x3, Pallas kernels, paired_plan(): pl.pallas_call(functools.partial(send_body, first), out_shape=jax.ShapeDt...  5.16 us
    pallas_call x1, Pallas kernels, shards(): pl.pallas_call(functools.partial(pair_body, own_seqs, width, rows, paired...  3.9 us
    ppermute x3, starting transfers between devices, shards(): lax.ppermute(msg, 'row', [(r, r ^ d) for r in range(rows)])  3.15 us
    pallas_call x3, Pallas kernels, paired_plan(): pl.pallas_call(functools.partial(join_body, first), out_shape=jax.ShapeDt...  3.09 us
    pallas_call x1, Pallas kernels, shards(): pl.pallas_call(functools.partial(prepare_body, own_seqs), out_shape=[jax....  2.54 us
  transfers between devices with their start and end apart: 13, of which 7 were waited for; matrix products, arithmetic and copies ran while one was open for 0% of the time, Pallas kernels for 27%

profile of v4, /device:TPU:0, one launch (start us, length us, event | category | flops | bytes accessed | tf_op | source)
XLA Modules:
  0.0 56.6 jit_solution(7199830771749999019)
XLA Ops:
  0.0 1.4 %align.1 = (bf16[48,128]{1,0:T(8,128)(2,1)S(1)}, bf16[48,128]{1,0:T(8,128)(2,1)S(1)}, bf16[48,128]{1,0:T(8,128)(2,1)S(1)}, bf16[48,128]{1,0:T(8,128)(2,1)S(1)}) custom-call(bf16[2,160,256]{2,1,0:T(8,128)(2,1)} %x_hbm.1, bf16[64,256]{1,0:T(8,128)(2,1)} %bitcast.1), custom_call_target="tpu_custom_call" | custom-call | bytes 5535000 | tf_op jit(solution)/shard_map/align/pallas_call | solution.py:483
  1.4 0.5 collective-permute-start
  1.9 0.0 copy-start.3
  2.0 2.6 %collective-permute-start.1 = (bf16[48,128]{1,0:T(8,128)(2,1)S(1)}, bf16[48,128]{1,0:T(8,128)(2,1)S(1)}, u32[]{:S(2)}, u32[]{:S(2)}) collective-permute-start(bf16[48,128]{1,0:T(8,128)(2,1)S(1)} %get-tuple-element.28), channel_id=1, source_target_pairs={{0,8},{4,12},{8,0},{12,4},{1,9},{5,13},{9,1},{13,5},{2,10},{6,14},... | collective-permute-start | bytes 36872 | tf_op jit(solution)/shard_map/ppermute | solution.py:499
  4.5 0.0 copy-start
  4.5 0.1 collective-permute-start.2
  4.6 0.0 copy-done.3
  4.6 2.5 %prepare.1 = (f32[40,40,128]{2,1,0:T(8,128)S(1)}, bf16[40,40,128]{2,1,0:T(8,128)(2,1)S(1)}, bf16[16,32,256]{2,1,0:T(8,128)(2,1)S(1)}, bf16[4,128,256]{2,1,0:T(8,128)(2,1)S(1)}) custom-call(bf16[40,40,128]{2,1,0:T(8,128)(2,1)} %couple_hbm.1, s32[160]{0:T(256)S(1)} %copy-done.3, s32[40,40]{1,0:T(8,128)} %valid_hbm.1, f32[2,128]{1,0:T(2,128)} %bias_hbm.1, ...), custom_call_target="tpu_custom_call" | custom-call | bytes 9225000 | tf_op jit(solution)/shard_map/prepare/pallas_call | solution.py:503
  7.1 0.0 collective-permute-done.refs_1_
  7.2 0.0 collective-permute-done.1.refs_2_
  7.2 0.5 collective-permute-done.2.refs_3_
  7.7 0.0 copy-done
  7.7 3.9 %pair.1 = (bf16[40,40,128]{2,1,0:T(8,128)(2,1)S(1)}, bf16[1600,128]{1,0:T(8,128)(2,1)S(1)}, bf16[40,40,128]{2,1,0:T(8,128)(2,1)S(1)}) custom-call(bf16[48,128]{1,0:T(8,128)(2,1)S(1)} %get-tuple-element.26.refs_0_, bf16[48,128]{1,0:T(8,128)(2,1)S(1)} %collective-permute-done.refs_1_, bf16[48,128]{1,0:T(8,128)(2,1)S(1)} %collective-permute-done.1.refs_2_, ...), custom_call_target="tpu_custom_call" | custom-call | bytes 16605000 | tf_op jit(solution)/shard_map/pair/pallas_call | solution.py:526
  11.6 1.3 %collective-permute-start.3 = (bf16[40,40,128]{2,1,0:T(8,128)(2,1)S(1)}, bf16[40,40,128]{2,1,0:T(8,128)(2,1)S(1)}, u32[]{:S(2)}, u32[]{:S(2)}) collective-permute-start(bf16[40,40,128]{2,1,0:T(8,128)(2,1)S(1)} %get-tuple-element.34.refs_0_), channel_id=1, source_target_pairs={{0,8},{1,4},{2,10},{3,6},{4,1},{5,13},{6,3},{7,15},{8,0},{9,12},{1... | collective-permute-start | bytes 1228808 | tf_op jit(solution)/shard_map/ppermute | solution.py:415
  12.9 0.4 collective-permute-start.4
  13.3 0.4 left.1
  13.7 5.9 %collective-permute-done.3.refs_2_ = bf16[40,40,128]{2,1,0:T(8,128)(2,1)S(1)} collective-permute-done((bf16[40,40,128]{2,1,0:T(8,128)(2,1)S(1)}, bf16[40,40,128]{2,1,0:T(8,128)(2,1)S(1)}, u32[]{:S(2)}, u32[]{:S(2)}) %collective-permute-start.3) | collective-permute-done | bytes 409632 | tf_op jit(solution)/shard_map/ppermute | solution.py:415
  19.6 0.0 collective-permute-done.4.refs_1_
  19.6 0.7 %collective-permute-start.6 = (bf16[40,40,128]{2,1,0:T(8,128)(2,1)S(1)}, bf16[40,40,128]{2,1,0:T(8,128)(2,1)S(1)}, u32[]{:S(2)}, u32[]{:S(2)}) collective-permute-start(bf16[40,40,128]{2,1,0:T(8,128)(2,1)S(1)} %collective-permute-done.3.refs_2_), channel_id=1, source_target_pairs={{0,0},{1,9},{2,2},{3,11},{4,12},{5,5},{6,14},{7,7},{8,8},{9,1},{10... | collective-permute-start | bytes 1228808 | tf_op jit(solution)/shard_map/ppermute | solution.py:415
  20.3 3.6 %collective-permute-start.7 = (bf16[24,40,128]{2,1,0:T(8,128)(2,1)S(1)}, bf16[24,40,128]{2,1,0:T(8,128)(2,1)S(1)}, u32[]{:S(2)}, u32[]{:S(2)}) collective-permute-start(bf16[24,40,128]{2,1,0:T(8,128)(2,1)S(1)} %get-tuple-element.40.refs_6_), channel_id=1, source_target_pairs={{0,1},{1,0},{2,3},{3,2},{4,5},{5,4},{6,7},{7,6},{8,9},{9,8},{10,11... | collective-permute-start | bytes 737288 | tf_op jit(solution)/shard_map/ppermute | solution.py:415
  23.8 0.0 collective-permute-start.5
  23.8 6.7 %collective-permute-done.7.refs_7_.refs_8_ = bf16[24,40,128]{2,1,0:T(8,128)(2,1)S(1)} collective-permute-done((bf16[24,40,128]{2,1,0:T(8,128)(2,1)S(1)}, bf16[24,40,128]{2,1,0:T(8,128)(2,1)S(1)}, u32[]{:S(2)}, u32[]{:S(2)}) %collective-permute-start.7) | collective-permute-done | bytes 245792 | tf_op jit(solution)/shard_map/ppermute | solution.py:415
  30.5 0.0 collective-permute-done.6.refs_4_
  30.5 0.0 collective-permute-start.8
  30.5 0.3 collective-permute-start.10
  30.8 0.0 collective-permute-done.5.refs_3_
  30.8 1.5 %collective-permute-done.8.refs_5_ = bf16[40,40,128]{2,1,0:T(8,128)(2,1)S(1)} collective-permute-done((bf16[40,40,128]{2,1,0:T(8,128)(2,1)S(1)}, bf16[40,40,128]{2,1,0:T(8,128)(2,1)S(1)}, u32[]{:S(2)}, u32[]{:S(2)}) %collective-permute-start.8) | collective-permute-done | bytes 409632 | tf_op jit(solution)/shard_map/ppermute | solution.py:415
  32.2 2.1 %send_sums.5 = bf16[16,40,128]{2,1,0:T(8,128)(2,1)S(1)} custom-call(bf16[40,40,128]{2,1,0:T(8,128)(2,1)S(1)} %get-tuple-element.34.refs_0_, bf16[40,40,128]{2,1,0:T(8,128)(2,1)S(1)} %collective-permute-done.4.refs_1_, bf16[40,40,128]{2,1,0:T(8,128)(2,1)S(1)} %collective-permute-done.3.refs_2_, bf16[40,40,128]{2,1,0:T(8,128)(2,1)S(1)} %collective-permute-done.5.refs_3_, ...), custom_call_target="tpu_custom_call" | custom-call | bytes 8560800 | tf_op jit(solution)/shard_map/send_sums/pallas_call | solution.py:432
  34.3 2.7 %collective-permute-start.12 = (bf16[16,40,128]{2,1,0:T(8,128)(2,1)S(1)}, bf16[16,40,128]{2,1,0:T(8,128)(2,1)S(1)}, u32[]{:S(2)}, u32[]{:S(2)}) collective-permute-start(bf16[16,40,128]{2,1,0:T(8,128)(2,1)S(1)} %send_sums.5), channel_id=1, source_target_pairs={{0,2},{1,3},{2,0},{3,1},{4,6},{5,7},{6,4},{7,5},{8,10},{9,11},{10,... | collective-permute-start | bytes 491528 | tf_op jit(solution)/shard_map/ppermute | solution.py:415
  37.0 0.1 collective-permute-done.10.refs_9_.refs_7_
  37.1 2.1 %send_sums.4 = bf16[16,40,128]{2,1,0:T(8,128)(2,1)S(1)} custom-call(bf16[40,40,128]{2,1,0:T(8,128)(2,1)S(1)} %get-tuple-element.34.refs_0_, bf16[40,40,128]{2,1,0:T(8,128)(2,1)S(1)} %collective-permute-done.4.refs_1_, bf16[40,40,128]{2,1,0:T(8,128)(2,1)S(1)} %collective-permute-done.3.refs_2_, bf16[40,40,128]{2,1,0:T(8,128)(2,1)S(1)} %collective-permute-done.5.refs_3_, ...), custom_call_target="tpu_custom_call" | custom-call | bytes 8560800 | tf_op jit(solution)/shard_map/send_sums/pallas_call | solution.py:432
  39.2 0.0 copy-start.2
  39.2 3.0 %collective-permute-start.11 = (bf16[16,40,128]{2,1,0:T(8,128)(2,1)S(1)}, bf16[16,40,128]{2,1,0:T(8,128)(2,1)S(1)}, u32[]{:S(2)}, u32[]{:S(2)}) collective-permute-start(bf16[16,40,128]{2,1,0:T(8,128)(2,1)S(1)} %send_sums.4), channel_id=1, source_target_pairs={{0,2},{1,3},{2,0},{3,1},{4,6},{5,7},{6,4},{7,5},{8,10},{9,11},{10,... | collective-permute-start | bytes 491528 | tf_op jit(solution)/shard_map/ppermute | solution.py:415
  42.2 1.0 %send_sums.3 = bf16[8,40,128]{2,1,0:T(8,128)(2,1)S(1)} custom-call(bf16[40,40,128]{2,1,0:T(8,128)(2,1)S(1)} %get-tuple-element.34.refs_0_, bf16[40,40,128]{2,1,0:T(8,128)(2,1)S(1)} %collective-permute-done.4.refs_1_, bf16[40,40,128]{2,1,0:T(8,128)(2,1)S(1)} %collective-permute-done.3.refs_2_, bf16[40,40,128]{2,1,0:T(8,128)(2,1)S(1)} %collective-permute-done.5.refs_3_, ...), custom_call_target="tpu_custom_call" | custom-call | bytes 5018400 | tf_op jit(solution)/shard_map/send_sums/pallas_call | solution.py:432
  43.3 0.0 copy-start.1
  43.3 0.1 collective-permute-start.9
  43.4 0.0 copy-done.2
  43.4 5.4 %keep_sums.1 = (f32[40,40,128]{2,1,0:T(8,128)S(1)}, f32[40,40,128]{2,1,0:T(8,128)S(1)}) custom-call(bf16[40,40,128]{2,1,0:T(8,128)(2,1)S(1)} %get-tuple-element.34.refs_0_, bf16[40,40,128]{2,1,0:T(8,128)(2,1)S(1)} %collective-permute-done.4.refs_1_, bf16[40,40,128]{2,1,0:T(8,128)(2,1)S(1)} %collective-permute-done.3.refs_2_, ...), custom_call_target="tpu_custom_call" | custom-call | bytes 22140000 | tf_op jit(solution)/shard_map/keep_sums/pallas_call | solution.py:444
  48.7 2.3 %collective-permute-done.12.sum_ref = bf16[16,40,128]{2,1,0:T(8,128)(2,1)S(1)} collective-permute-done((bf16[16,40,128]{2,1,0:T(8,128)(2,1)S(1)}, bf16[16,40,128]{2,1,0:T(8,128)(2,1)S(1)}, u32[]{:S(2)}, u32[]{:S(2)}) %collective-permute-start.12) | collective-permute-done | bytes 163872 | tf_op jit(solution)/shard_map/ppermute | solution.py:415
  51.0 0.0 copy-done.1
  51.0 1.1 %join.3.refs_0_ = bf16[40,40,128]{2,1,0:T(8,128)(2,1)} custom-call(bf16[16,40,128]{2,1,0:T(8,128)(2,1)S(1)} %collective-permute-done.12.sum_ref, f32[40,40,128]{2,1,0:T(8,128)S(1)} %get-tuple-element.44.own_ref, bf16[40,40,128]{2,1,0:T(8,128)(2,1)S(1)} %get-tuple-element.45.psum_ref, f32[40,40,128]{2,1,0:T(8,128)S(1)} %get-tuple-element.46.gate_ref, ...), custom_call_target="tpu_custom_call" | custom-call | bytes 3542400 | tf_op jit(solution)/shard_map/join/pallas_call | solution.py:457
  52.1 2.4 %collective-permute-done.11.sum_ref = bf16[16,40,128]{2,1,0:T(8,128)(2,1)S(1)} collective-permute-done((bf16[16,40,128]{2,1,0:T(8,128)(2,1)S(1)}, bf16[16,40,128]{2,1,0:T(8,128)(2,1)S(1)}, u32[]{:S(2)}, u32[]{:S(2)}) %collective-permute-start.11) | collective-permute-done | bytes 163872 | tf_op jit(solution)/shard_map/ppermute | solution.py:415
  54.5 1.1 %join.4.refs_0_ = bf16[40,40,128]{2,1,0:T(8,128)(2,1)} custom-call(bf16[16,40,128]{2,1,0:T(8,128)(2,1)S(1)} %collective-permute-done.11.sum_ref, f32[40,40,128]{2,1,0:T(8,128)S(1)} %get-tuple-element.44.own_ref, bf16[40,40,128]{2,1,0:T(8,128)(2,1)S(1)} %get-tuple-element.45.psum_ref, ...), custom_call_target="tpu_custom_call", output_to_operand_aliasing={{}: (5, {})} | custom-call | bytes 3542400 | tf_op jit(solution)/shard_map/join/pallas_call | solution.py:457
  55.6 0.0 collective-permute-done.9.sum_ref
  55.6 1.0 %join.5 = bf16[40,40,128]{2,1,0:T(8,128)(2,1)} custom-call(bf16[8,40,128]{2,1,0:T(8,128)(2,1)S(1)} %collective-permute-done.9.sum_ref, f32[40,40,128]{2,1,0:T(8,128)S(1)} %get-tuple-element.44.own_ref, bf16[40,40,128]{2,1,0:T(8,128)(2,1)S(1)} %get-tuple-element.45.psum_ref, ...), custom_call_target="tpu_custom_call", output_to_operand_aliasing={{}: (5, {})} | custom-call | bytes 1771200 | tf_op jit(solution)/shard_map/join/pallas_call | solution.py:457
Async XLA Ops:
  1.4 5.7 %collective-permute-start = (bf16[48,128]{1,0:T(8,128)(2,1)S(1)}, bf16[48,128]{1,0:T(8,128)(2,1)S(1)}, u32[]{:S(2)}, u32[]{:S(2)}) collective-permute-start(bf16[48,128]{1,0:T(8,128)(2,1)S(1)} %get-tuple-element.27), channel_id=1, source_target_pairs={{0,4},{4,0},{8,12},{12,8},{1,5},{5,1},{9,13},{13,9},{2,6},{6,2},{1... | collective-permute-start | bytes 36872 | tf_op jit(solution)/shard_map/ppermute | solution.py:499
  1.9 2.6 %copy-start.3 = (s32[160]{0:T(256)S(1)}, s32[160]{0:T(256)}, u32[]{:S(2)}) copy-start(s32[160]{0:T(256)} %ids_ref.1) | copy-start | bytes 1924
  2.0 5.2 %collective-permute-start.1 = (bf16[48,128]{1,0:T(8,128)(2,1)S(1)}, bf16[48,128]{1,0:T(8,128)(2,1)S(1)}, u32[]{:S(2)}, u32[]{:S(2)}) collective-permute-start(bf16[48,128]{1,0:T(8,128)(2,1)S(1)} %get-tuple-element.28), channel_id=1, source_target_pairs={{0,8},{4,12},{8,0},{12,4},{1,9},{5,13},{9,1},{13,5},{2,10},{6,14},... | collective-permute-start | bytes 36872 | tf_op jit(solution)/shard_map/ppermute | solution.py:499
  4.5 3.1 %copy-start = (bf16[128,512]{1,0:T(8,128)(2,1)S(1)}, bf16[128,512]{1,0:T(8,128)(2,1)}, u32[]{:S(2)}) copy-start(bf16[128,512]{1,0:T(8,128)(2,1)} %win_ref.1) | copy-start | bytes 393220
  4.5 3.1 %collective-permute-start.2 = (bf16[48,128]{1,0:T(8,128)(2,1)S(1)}, bf16[48,128]{1,0:T(8,128)(2,1)S(1)}, u32[]{:S(2)}, u32[]{:S(2)}) collective-permute-start(bf16[48,128]{1,0:T(8,128)(2,1)S(1)} %get-tuple-element.29), channel_id=1, source_target_pairs={{0,12},{4,8},{8,4},{12,0},{1,13},{5,9},{9,5},{13,1},{2,14},{6,10},... | collective-permute-start | bytes 36872 | tf_op jit(solution)/shard_map/ppermute | solution.py:499
  11.6 8.0 %collective-permute-start.3 = (bf16[40,40,128]{2,1,0:T(8,128)(2,1)S(1)}, bf16[40,40,128]{2,1,0:T(8,128)(2,1)S(1)}, u32[]{:S(2)}, u32[]{:S(2)}) collective-permute-start(bf16[40,40,128]{2,1,0:T(8,128)(2,1)S(1)} %get-tuple-element.34.refs_0_), channel_id=1, source_target_pairs={{0,8},{1,4},{2,10},{3,6},{4,1},{5,13},{6,3},{7,15},{8,0},{9,12},{1... | collective-permute-start | bytes 1228808 | tf_op jit(solution)/shard_map/ppermute | solution.py:415
  12.9 6.7 %collective-permute-start.4 = (bf16[40,40,128]{2,1,0:T(8,128)(2,1)S(1)}, bf16[40,40,128]{2,1,0:T(8,128)(2,1)S(1)}, u32[]{:S(2)}, u32[]{:S(2)}) collective-permute-start(bf16[40,40,128]{2,1,0:T(8,128)(2,1)S(1)} %get-tuple-element.34.refs_0_), channel_id=1, source_target_pairs={{0,4},{1,5},{2,6},{3,7},{4,0},{5,1},{6,2},{7,3},{8,12},{9,13},{10,... | collective-permute-start | bytes 1228808 | tf_op jit(solution)/shard_map/ppermute | solution.py:415
  19.6 10.9 %collective-permute-start.6 = (bf16[40,40,128]{2,1,0:T(8,128)(2,1)S(1)}, bf16[40,40,128]{2,1,0:T(8,128)(2,1)S(1)}, u32[]{:S(2)}, u32[]{:S(2)}) collective-permute-start(bf16[40,40,128]{2,1,0:T(8,128)(2,1)S(1)} %collective-permute-done.3.refs_2_), channel_id=1, source_target_pairs={{0,0},{1,9},{2,2},{3,11},{4,12},{5,5},{6,14},{7,7},{8,8},{9,1},{10... | collective-permute-start | bytes 1228808 | tf_op jit(solution)/shard_map/ppermute | solution.py:415
  20.3 10.2 %collective-permute-start.7 = (bf16[24,40,128]{2,1,0:T(8,128)(2,1)S(1)}, bf16[24,40,128]{2,1,0:T(8,128)(2,1)S(1)}, u32[]{:S(2)}, u32[]{:S(2)}) collective-permute-start(bf16[24,40,128]{2,1,0:T(8,128)(2,1)S(1)} %get-tuple-element.40.refs_6_), channel_id=1, source_target_pairs={{0,1},{1,0},{2,3},{3,2},{4,5},{5,4},{6,7},{7,6},{8,9},{9,8},{10,11... | collective-permute-start | bytes 737288 | tf_op jit(solution)/shard_map/ppermute | solution.py:415
  23.8 7.0 %collective-permute-start.5 = (bf16[40,40,128]{2,1,0:T(8,128)(2,1)S(1)}, bf16[40,40,128]{2,1,0:T(8,128)(2,1)S(1)}, u32[]{:S(2)}, u32[]{:S(2)}) collective-permute-start(bf16[40,40,128]{2,1,0:T(8,128)(2,1)S(1)} %collective-permute-done.3.refs_2_), channel_id=1, source_target_pairs={{0,4},{1,5},{2,6},{3,7},{4,0},{5,1},{6,2},{7,3},{8,12},{9,13},{10,... | collective-permute-start | bytes 1228808 | tf_op jit(solution)/shard_map/ppermute | solution.py:415
  30.5 1.7 %collective-permute-start.8 = (bf16[40,40,128]{2,1,0:T(8,128)(2,1)S(1)}, bf16[40,40,128]{2,1,0:T(8,128)(2,1)S(1)}, u32[]{:S(2)}, u32[]{:S(2)}) collective-permute-start(bf16[40,40,128]{2,1,0:T(8,128)(2,1)S(1)} %collective-permute-done.6.refs_4_), channel_id=1, source_target_pairs={{0,4},{1,5},{2,6},{3,7},{4,0},{5,1},{6,2},{7,3},{8,12},{9,13},{10,... | collective-permute-start | bytes 1228808 | tf_op jit(solution)/shard_map/ppermute | solution.py:415
  30.5 6.6 %collective-permute-start.10 = (bf16[16,40,128]{2,1,0:T(8,128)(2,1)S(1)}, bf16[16,40,128]{2,1,0:T(8,128)(2,1)S(1)}, u32[]{:S(2)}, u32[]{:S(2)}) collective-permute-start(bf16[16,40,128]{2,1,0:T(8,128)(2,1)S(1)} %get-tuple-element.43.refs_7_.refs_6_), channel_id=1, source_target_pairs={{0,1},{1,0},{2,3},{3,2},{4,5},{5,4},{6,7},{7,6},{8,9},{9,8},{10,11... | collective-permute-start | bytes 491528 | tf_op jit(solution)/shard_map/ppermute | solution.py:415
  34.3 16.7 %collective-permute-start.12 = (bf16[16,40,128]{2,1,0:T(8,128)(2,1)S(1)}, bf16[16,40,128]{2,1,0:T(8,128)(2,1)S(1)}, u32[]{:S(2)}, u32[]{:S(2)}) collective-permute-start(bf16[16,40,128]{2,1,0:T(8,128)(2,1)S(1)} %send_sums.5), channel_id=1, source_target_pairs={{0,2},{1,3},{2,0},{3,1},{4,6},{5,7},{6,4},{7,5},{8,10},{9,11},{10,... | collective-permute-start | bytes 491528 | tf_op jit(solution)/shard_map/ppermute | solution.py:415
  39.2 4.2 %copy-start.2 = (bf16[128,128]{1,0:T(8,128)(2,1)S(1)}, bf16[128,128]{1,0:T(8,128)(2,1)}, u32[]{:S(2)}) copy-start(bf16[128,128]{1,0:T(8,128)(2,1)} %refs_11_.1) | copy-start | bytes 98308
  39.2 15.4 %collective-permute-start.11 = (bf16[16,40,128]{2,1,0:T(8,128)(2,1)S(1)}, bf16[16,40,128]{2,1,0:T(8,128)(2,1)S(1)}, u32[]{:S(2)}, u32[]{:S(2)}) collective-permute-start(bf16[16,40,128]{2,1,0:T(8,128)(2,1)S(1)} %send_sums.4), channel_id=1, source_target_pairs={{0,2},{1,3},{2,0},{3,1},{4,6},{5,7},{6,4},{7,5},{8,10},{9,11},{10,... | collective-permute-start | bytes 491528 | tf_op jit(solution)/shard_map/ppermute | solution.py:415
  43.3 7.8 %copy-start.1 = (bf16[128,128]{1,0:T(8,128)(2,1)S(1)}, bf16[128,128]{1,0:T(8,128)(2,1)}, u32[]{:S(2)}) copy-start(bf16[128,128]{1,0:T(8,128)(2,1)} %w_ref.5) | copy-start | bytes 98308
  43.3 12.3 %collective-permute-start.9 = (bf16[8,40,128]{2,1,0:T(8,128)(2,1)S(1)}, bf16[8,40,128]{2,1,0:T(8,128)(2,1)S(1)}, u32[]{:S(2)}, u32[]{:S(2)}) collective-permute-start(bf16[8,40,128]{2,1,0:T(8,128)(2,1)S(1)} %send_sums.3), channel_id=1, source_target_pairs={{0,2},{1,3},{2,0},{3,1},{4,6},{5,7},{6,4},{7,5},{8,10},{9,11},{10,... | collective-permute-start | bytes 245768 | tf_op jit(solution)/shard_map/ppermute | solution.py:415

commit v5 on v4

--- a/solution.py
+++ b/solution.py
@@ -237,22 +237,22 @@
 
 
 def with_right(own_pair, refs, use):
-    own, p_own, got, p_got, late, p_late = refs
+    own, got, p_got, far, p_far = refs
     r, z = lax.axis_index("row"), lax.axis_index("col")
     keeper = (r % 2) == (z % 2)
     near = ((r // 2) == (z // 2)) == own_pair
     table = [
         (near & keeper, own, p_got),
-        (near & ~keeper, p_own, got),
-        (~near & keeper, got, p_late),
-        (~near & ~keeper, p_got, late),
+        (near & ~keeper, far, got),
+        (~near & keeper, got, far),
+        (~near & ~keeper, p_got, p_far),
     ]
     for cond, a, b in table:
         pl.when(cond)(functools.partial(use, (a, b)))
 
 
 def send_body(first, *refs):
-    rights, (l_ref, m_ref, o_ref, lf_ref) = refs[:6], refs[6:]
+    rights, (l_ref, m_ref, o_ref, lf_ref) = refs[:5], refs[5:]
     count, depth = o_ref.shape[0], l_ref.shape[1]
     group = 8
     lf_ref[:, pl.ds(0, depth), :] = l_ref[pl.ds(first, count)].astype(f32)
@@ -271,7 +271,7 @@
 
 
 def keep_body(cuts, *refs):
-    rights, refs = refs[:6], refs[6:]
+    rights, refs = refs[:5], refs[5:]
     lefts, mets = refs[:cuts], refs[cuts : 2 * cuts]
     norm_ref, wgate_ref, o_ref, gate_ref, lf_ref = refs[2 * cuts :]
     own_i, depth, chans = o_ref.shape
@@ -417,22 +417,20 @@
     every = lambda r, z: True
     keeper = lambda r, z: r % 2 == z % 2
     got = move(right, every, lambda r, z: (r ^ 2, z) if keeper(r, z) else (r ^ 1, z ^ 1))
-    p_own = move(right, every, lambda r, z: (r ^ 1, z))
-    got, p_own, *lefts = lax.optimization_barrier((got, p_own, *lefts))
-    late = move(got, every, lambda r, z: (r, z) if keeper(r, z) else (r ^ 2, z))
+    far = move(right, every, lambda r, z: (r ^ 1, z) if keeper(r, z) else (r ^ 2, z ^ 1))
+    mets = [move(left, every, lambda r, z: (r, z ^ 1)) for left in lefts]
+    got, far, mets[0] = lax.optimization_barrier((got, far, mets[0]))
     p_got = move(got, every, lambda r, z: (r ^ 1, z))
-    mets = [move(left, every, lambda r, z: (r, z ^ 1)) for left in lefts]
-    late, mets[0] = lax.optimization_barrier((late, mets[0]))
-    p_late = move(late, every, lambda r, z: (r ^ 1, z))
-    rights = (right, p_own, got, p_got, late, p_late)
+    p_far = move(far, every, lambda r, z: (r ^ 1, z))
+    rights = (right, got, p_got, far, p_far)
 
     sums = []
-    chunks = ((0, 0, 0, 16), (1, 0, 24, own_i - 24), (0, 16, 16, 8))
+    chunks = ((0, 0, 0, 16), (1, 0, 16, 16), (1, 16, 32, own_i - 32))
     for at, first, _, n in chunks:
         part = pl.pallas_call(
             functools.partial(send_body, first),
             out_shape=jax.ShapeDtypeStruct((n, own_j, tri), bf16),
-            in_specs=[VMEM] * 8,
+            in_specs=[VMEM] * 7,
             out_specs=VMEM,
             scratch_shapes=[pltpu.VMEM((n, 2 * own_j, tri), f32)],
             compiler_params=limit(8),
@@ -445,7 +443,7 @@
         functools.partial(keep_body, cuts),
         out_shape=[jax.ShapeDtypeStruct((own_i, own_j, tri), f32),
                    jax.ShapeDtypeStruct((own_i, own_j, chans), f32)],
-        in_specs=[VMEM] * (6 + 2 * cuts + 2),
+        in_specs=[VMEM] * (5 + 2 * cuts + 2),
         out_specs=[VMEM] * 2,
         scratch_shapes=[pltpu.VMEM((own_i, 2 * own_j, tri), f32)],
         compiler_params=limit(12),
@@ -477,7 +475,7 @@
     total = own_seqs * rows
     lanes = round_up(2 * own_seqs * width, 128)
     height = round_up(max(own_i, own_j), 16)
-    paired = rows == 4 and cols == 4 and own_i == own_j and own_i % 8 == 0 and own_i > 24
+    paired = rows == 4 and cols == 4 and own_i == own_j and own_i % 8 == 0 and own_i > 32
     scale = 1 if paired else 8
 
     msgs = pl.pallas_call(
@@ -540,7 +538,7 @@
         name="pair",
     )(*msgs, base, mask, wq, pick, w_in)
 
-    cuts = [24, own_i - 24] if paired else [own_i]
+    cuts = [16, own_i - 16] if paired else [own_i]
     lefts = pl.pallas_call(
         left_body,
         out_shape=[jax.ShapeDtypeStruct((n, own_j, tri), bf16) for n in cuts],

time: 56.8 us -> 54.2 us (0.954)
  starting transfers between devices: 15.2 us -> 13.6 us
  waiting for transfers between devices: 19.4 us -> 18.4 us
    ppermute x10 -> x9, starting transfers between devices: 12.1 us -> 10.5 us  [move(): return lax.ppermute(value, ('row', 'col'), pairs)]
    ppermute x10 -> x9, waiting for transfers between devices: 18.9 us -> 17.9 us  [move(): return lax.ppermute(value, ('row', 'col'), pairs)]
  transfers between devices with their start and end apart: 13 -> 12, of which waited for: 7 -> 6; matrix products, arithmetic and copies ran while one was open for 0% -> 0% of each run, Pallas kernels for 27% -> 29%
where the time goes in v5:
time: 54.2 us; the launch traced here: 54.1 us
  Pallas kernels  21.8 us (40%)
  waiting for transfers between devices  18.4 us (34%)
  starting transfers between devices  13.6 us (25%)
    ppermute x9, waiting for transfers between devices, move(): return lax.ppermute(value, ('row', 'col'), pairs)  17.9 us
    ppermute x9, starting transfers between devices, move(): return lax.ppermute(value, ('row', 'col'), pairs)  10.5 us
    pallas_call x1, Pallas kernels, paired_plan(): pl.pallas_call(functools.partial(keep_body, cuts), out_shape=[jax.ShapeDt...  5.36 us
    pallas_call x3, Pallas kernels, paired_plan(): pl.pallas_call(functools.partial(send_body, first), out_shape=jax.ShapeDt...  5.16 us
    pallas_call x1, Pallas kernels, shards(): pl.pallas_call(functools.partial(pair_body, own_seqs, width, rows, paired...  3.9 us
    ppermute x3, starting transfers between devices, shards(): lax.ppermute(msg, 'row', [(r, r ^ d) for r in range(rows)])  3.15 us
    pallas_call x3, Pallas kernels, paired_plan(): pl.pallas_call(functools.partial(join_body, first), out_shape=jax.ShapeDt...  3.09 us
    pallas_call x1, Pallas kernels, shards(): pl.pallas_call(functools.partial(prepare_body, own_seqs), out_shape=[jax....  2.54 us
  transfers between devices with their start and end apart: 12, of which 6 were waited for; matrix products, arithmetic and copies ran while one was open for 0% of the time, Pallas kernels for 29%

profile of v5, /device:TPU:0, one launch (start us, length us, event | category | flops | bytes accessed | tf_op | source)
XLA Modules:
  0.0 54.1 jit_solution(10111028035861896289)
XLA Ops:
  0.0 1.4 %align.1 = (bf16[48,128]{1,0:T(8,128)(2,1)S(1)}, bf16[48,128]{1,0:T(8,128)(2,1)S(1)}, bf16[48,128]{1,0:T(8,128)(2,1)S(1)}, bf16[48,128]{1,0:T(8,128)(2,1)S(1)}) custom-call(bf16[2,160,256]{2,1,0:T(8,128)(2,1)} %x_hbm.1, bf16[64,256]{1,0:T(8,128)(2,1)} %bitcast.1), custom_call_target="tpu_custom_call" | custom-call | bytes 5535000 | tf_op jit(solution)/shard_map/align/pallas_call | solution.py:481
  1.4 0.5 collective-permute-start
  1.9 0.0 copy-start.3
  2.0 2.6 %collective-permute-start.1 = (bf16[48,128]{1,0:T(8,128)(2,1)S(1)}, bf16[48,128]{1,0:T(8,128)(2,1)S(1)}, u32[]{:S(2)}, u32[]{:S(2)}) collective-permute-start(bf16[48,128]{1,0:T(8,128)(2,1)S(1)} %get-tuple-element.25), channel_id=1, source_target_pairs={{0,8},{4,12},{8,0},{12,4},{1,9},{5,13},{9,1},{13,5},{2,10},{6,14},... | collective-permute-start | bytes 36872 | tf_op jit(solution)/shard_map/ppermute | solution.py:497
  4.5 0.0 copy-start
  4.5 0.1 collective-permute-start.2
  4.6 0.0 copy-done.3
  4.6 2.5 %prepare.1 = (f32[40,40,128]{2,1,0:T(8,128)S(1)}, bf16[40,40,128]{2,1,0:T(8,128)(2,1)S(1)}, bf16[16,32,256]{2,1,0:T(8,128)(2,1)S(1)}, bf16[4,128,256]{2,1,0:T(8,128)(2,1)S(1)}) custom-call(bf16[40,40,128]{2,1,0:T(8,128)(2,1)} %couple_hbm.1, s32[160]{0:T(256)S(1)} %copy-done.3, s32[40,40]{1,0:T(8,128)} %valid_hbm.1, f32[2,128]{1,0:T(2,128)} %bias_hbm.1, ...), custom_call_target="tpu_custom_call" | custom-call | bytes 9225000 | tf_op jit(solution)/shard_map/prepare/pallas_call | solution.py:501
  7.1 0.0 collective-permute-done.refs_1_
  7.2 0.0 collective-permute-done.1.refs_2_
  7.2 0.5 collective-permute-done.2.refs_3_
  7.7 0.0 copy-done
  7.7 3.9 %pair.1 = (bf16[40,40,128]{2,1,0:T(8,128)(2,1)S(1)}, bf16[1600,128]{1,0:T(8,128)(2,1)S(1)}, bf16[40,40,128]{2,1,0:T(8,128)(2,1)S(1)}) custom-call(bf16[48,128]{1,0:T(8,128)(2,1)S(1)} %get-tuple-element.23.refs_0_, bf16[48,128]{1,0:T(8,128)(2,1)S(1)} %collective-permute-done.refs_1_, bf16[48,128]{1,0:T(8,128)(2,1)S(1)} %collective-permute-done.1.refs_2_, ...), custom_call_target="tpu_custom_call" | custom-call | bytes 16605000 | tf_op jit(solution)/shard_map/pair/pallas_call | solution.py:524
  11.6 1.3 %collective-permute-start.3 = (bf16[40,40,128]{2,1,0:T(8,128)(2,1)S(1)}, bf16[40,40,128]{2,1,0:T(8,128)(2,1)S(1)}, u32[]{:S(2)}, u32[]{:S(2)}) collective-permute-start(bf16[40,40,128]{2,1,0:T(8,128)(2,1)S(1)} %get-tuple-element.31.refs_0_), channel_id=1, source_target_pairs={{0,8},{1,4},{2,10},{3,6},{4,1},{5,13},{6,3},{7,15},{8,0},{9,12},{1... | collective-permute-start | bytes 1228808 | tf_op jit(solution)/shard_map/ppermute | solution.py:415
  12.9 0.4 collective-permute-start.4
  13.3 0.4 left.1
  13.7 1.9 %collective-permute-start.5 = (bf16[16,40,128]{2,1,0:T(8,128)(2,1)S(1)}, bf16[16,40,128]{2,1,0:T(8,128)(2,1)S(1)}, u32[]{:S(2)}, u32[]{:S(2)}) collective-permute-start(bf16[16,40,128]{2,1,0:T(8,128)(2,1)S(1)} %get-tuple-element.33.refs_5_), channel_id=1, source_target_pairs={{0,1},{1,0},{2,3},{3,2},{4,5},{5,4},{6,7},{7,6},{8,9},{9,8},{10,11... | collective-permute-start | bytes 491528 | tf_op jit(solution)/shard_map/ppermute | solution.py:415
  15.6 11.7 %collective-permute-done.5.refs_7_.refs_6_ = bf16[16,40,128]{2,1,0:T(8,128)(2,1)S(1)} collective-permute-done((bf16[16,40,128]{2,1,0:T(8,128)(2,1)S(1)}, bf16[16,40,128]{2,1,0:T(8,128)(2,1)S(1)}, u32[]{:S(2)}, u32[]{:S(2)}) %collective-permute-start.5) | collective-permute-done | bytes 163872 | tf_op jit(solution)/shard_map/ppermute | solution.py:415
  27.2 0.0 collective-permute-done.3.refs_1_
  27.2 0.0 collective-permute-done.4.refs_3_
  27.3 0.0 collective-permute-start.6
  27.3 0.5 collective-permute-start.7
  27.8 0.6 %collective-permute-start.8 = (bf16[24,40,128]{2,1,0:T(8,128)(2,1)S(1)}, bf16[24,40,128]{2,1,0:T(8,128)(2,1)S(1)}, u32[]{:S(2)}, u32[]{:S(2)}) collective-permute-start(bf16[24,40,128]{2,1,0:T(8,128)(2,1)S(1)} %get-tuple-element.36.refs_5_.refs_6_), channel_id=1, source_target_pairs={{0,1},{1,0},{2,3},{3,2},{4,5},{5,4},{6,7},{7,6},{8,9},{9,8},{10,11... | collective-permute-start | bytes 737288 | tf_op jit(solution)/shard_map/ppermute | solution.py:415
  28.4 0.6 %collective-permute-done.6.refs_2_ = bf16[40,40,128]{2,1,0:T(8,128)(2,1)S(1)} collective-permute-done((bf16[40,40,128]{2,1,0:T(8,128)(2,1)S(1)}, bf16[40,40,128]{2,1,0:T(8,128)(2,1)S(1)}, u32[]{:S(2)}, u32[]{:S(2)}) %collective-permute-start.6) | collective-permute-done | bytes 409632 | tf_op jit(solution)/shard_map/ppermute | solution.py:415
  29.0 0.6 %collective-permute-done.7.refs_4_ = bf16[40,40,128]{2,1,0:T(8,128)(2,1)S(1)} collective-permute-done((bf16[40,40,128]{2,1,0:T(8,128)(2,1)S(1)}, bf16[40,40,128]{2,1,0:T(8,128)(2,1)S(1)}, u32[]{:S(2)}, u32[]{:S(2)}) %collective-permute-start.7) | collective-permute-done | bytes 409632 | tf_op jit(solution)/shard_map/ppermute | solution.py:415
  29.6 2.1 %send_sums.5 = bf16[16,40,128]{2,1,0:T(8,128)(2,1)S(1)} custom-call(bf16[40,40,128]{2,1,0:T(8,128)(2,1)S(1)} %get-tuple-element.31.refs_0_, bf16[40,40,128]{2,1,0:T(8,128)(2,1)S(1)} %collective-permute-done.3.refs_1_, bf16[40,40,128]{2,1,0:T(8,128)(2,1)S(1)} %collective-permute-done.6.refs_2_, bf16[40,40,128]{2,1,0:T(8,128)(2,1)S(1)} %collective-permute-done.4.refs_3_, ...), custom_call_target="tpu_custom_call" | custom-call | bytes 8560800 | tf_op jit(solution)/shard_map/send_sums/pallas_call | solution.py:430
  31.7 2.7 %collective-permute-start.11 = (bf16[16,40,128]{2,1,0:T(8,128)(2,1)S(1)}, bf16[16,40,128]{2,1,0:T(8,128)(2,1)S(1)}, u32[]{:S(2)}, u32[]{:S(2)}) collective-permute-start(bf16[16,40,128]{2,1,0:T(8,128)(2,1)S(1)} %send_sums.5), channel_id=1, source_target_pairs={{0,2},{1,3},{2,0},{3,1},{4,6},{5,7},{6,4},{7,5},{8,10},{9,11},{10,... | collective-permute-start | bytes 491528 | tf_op jit(solution)/shard_map/ppermute | solution.py:415
  34.3 3.1 %collective-permute-done.8.refs_6_.refs_8_ = bf16[24,40,128]{2,1,0:T(8,128)(2,1)S(1)} collective-permute-done((bf16[24,40,128]{2,1,0:T(8,128)(2,1)S(1)}, bf16[24,40,128]{2,1,0:T(8,128)(2,1)S(1)}, u32[]{:S(2)}, u32[]{:S(2)}) %collective-permute-start.8) | collective-permute-done | bytes 245792 | tf_op jit(solution)/shard_map/ppermute | solution.py:415
  37.4 2.1 %send_sums.4 = bf16[16,40,128]{2,1,0:T(8,128)(2,1)S(1)} custom-call(bf16[40,40,128]{2,1,0:T(8,128)(2,1)S(1)} %get-tuple-element.31.refs_0_, bf16[40,40,128]{2,1,0:T(8,128)(2,1)S(1)} %collective-permute-done.3.refs_1_, bf16[40,40,128]{2,1,0:T(8,128)(2,1)S(1)} %collective-permute-done.6.refs_2_, bf16[40,40,128]{2,1,0:T(8,128)(2,1)S(1)} %collective-permute-done.4.refs_3_, ...), custom_call_target="tpu_custom_call" | custom-call | bytes 8560800 | tf_op jit(solution)/shard_map/send_sums/pallas_call | solution.py:430
  39.5 0.0 copy-start.2
  39.5 1.8 %collective-permute-start.10 = (bf16[16,40,128]{2,1,0:T(8,128)(2,1)S(1)}, bf16[16,40,128]{2,1,0:T(8,128)(2,1)S(1)}, u32[]{:S(2)}, u32[]{:S(2)}) collective-permute-start(bf16[16,40,128]{2,1,0:T(8,128)(2,1)S(1)} %send_sums.4), channel_id=1, source_target_pairs={{0,2},{1,3},{2,0},{3,1},{4,6},{5,7},{6,4},{7,5},{8,10},{9,11},{10,... | collective-permute-start | bytes 491528 | tf_op jit(solution)/shard_map/ppermute | solution.py:415
  41.3 1.0 %send_sums.3 = bf16[8,40,128]{2,1,0:T(8,128)(2,1)S(1)} custom-call(bf16[40,40,128]{2,1,0:T(8,128)(2,1)S(1)} %get-tuple-element.31.refs_0_, bf16[40,40,128]{2,1,0:T(8,128)(2,1)S(1)} %collective-permute-done.3.refs_1_, bf16[40,40,128]{2,1,0:T(8,128)(2,1)S(1)} %collective-permute-done.6.refs_2_, bf16[40,40,128]{2,1,0:T(8,128)(2,1)S(1)} %collective-permute-done.4.refs_3_, ...), custom_call_target="tpu_custom_call" | custom-call | bytes 5018400 | tf_op jit(solution)/shard_map/send_sums/pallas_call | solution.py:430
  42.4 0.0 copy-start.1
  42.4 1.3 %collective-permute-start.9 = (bf16[8,40,128]{2,1,0:T(8,128)(2,1)S(1)}, bf16[8,40,128]{2,1,0:T(8,128)(2,1)S(1)}, u32[]{:S(2)}, u32[]{:S(2)}) collective-permute-start(bf16[8,40,128]{2,1,0:T(8,128)(2,1)S(1)} %send_sums.3), channel_id=1, source_target_pairs={{0,2},{1,3},{2,0},{3,1},{4,6},{5,7},{6,4},{7,5},{8,10},{9,11},{10,... | collective-permute-start | bytes 245768 | tf_op jit(solution)/shard_map/ppermute | solution.py:415
  43.6 0.0 copy-done.2
  43.6 5.4 %keep_sums.1 = (f32[40,40,128]{2,1,0:T(8,128)S(1)}, f32[40,40,128]{2,1,0:T(8,128)S(1)}) custom-call(bf16[40,40,128]{2,1,0:T(8,128)(2,1)S(1)} %get-tuple-element.31.refs_0_, bf16[40,40,128]{2,1,0:T(8,128)(2,1)S(1)} %collective-permute-done.3.refs_1_, bf16[40,40,128]{2,1,0:T(8,128)(2,1)S(1)} %collective-permute-done.6.refs_2_, ...), custom_call_target="tpu_custom_call" | custom-call | bytes 22140000 | tf_op jit(solution)/shard_map/keep_sums/pallas_call | solution.py:442
  49.0 0.0 collective-permute-done.11.sum_ref
  49.0 0.0 copy-done.1
  49.0 1.1 %join.3.refs_0_ = bf16[40,40,128]{2,1,0:T(8,128)(2,1)} custom-call(bf16[16,40,128]{2,1,0:T(8,128)(2,1)S(1)} %collective-permute-done.11.sum_ref, f32[40,40,128]{2,1,0:T(8,128)S(1)} %get-tuple-element.38.own_ref, bf16[40,40,128]{2,1,0:T(8,128)(2,1)S(1)} %get-tuple-element.39.psum_ref, f32[40,40,128]{2,1,0:T(8,128)S(1)} %get-tuple-element.40.gate_ref, ...), custom_call_target="tpu_custom_call" | custom-call | bytes 3542400 | tf_op jit(solution)/shard_map/join/pallas_call | solution.py:455
  50.1 1.9 %collective-permute-done.10.sum_ref = bf16[16,40,128]{2,1,0:T(8,128)(2,1)S(1)} collective-permute-done((bf16[16,40,128]{2,1,0:T(8,128)(2,1)S(1)}, bf16[16,40,128]{2,1,0:T(8,128)(2,1)S(1)}, u32[]{:S(2)}, u32[]{:S(2)}) %collective-permute-start.10) | collective-permute-done | bytes 163872 | tf_op jit(solution)/shard_map/ppermute | solution.py:415
  52.0 1.1 %join.4.refs_0_ = bf16[40,40,128]{2,1,0:T(8,128)(2,1)} custom-call(bf16[16,40,128]{2,1,0:T(8,128)(2,1)S(1)} %collective-permute-done.10.sum_ref, f32[40,40,128]{2,1,0:T(8,128)S(1)} %get-tuple-element.38.own_ref, bf16[40,40,128]{2,1,0:T(8,128)(2,1)S(1)} %get-tuple-element.39.psum_ref, ...), custom_call_target="tpu_custom_call", output_to_operand_aliasing={{}: (5, {})} | custom-call | bytes 3542400 | tf_op jit(solution)/shard_map/join/pallas_call | solution.py:455
  53.1 0.0 collective-permute-done.9.sum_ref
  53.1 1.0 %join.5 = bf16[40,40,128]{2,1,0:T(8,128)(2,1)} custom-call(bf16[8,40,128]{2,1,0:T(8,128)(2,1)S(1)} %collective-permute-done.9.sum_ref, f32[40,40,128]{2,1,0:T(8,128)S(1)} %get-tuple-element.38.own_ref, bf16[40,40,128]{2,1,0:T(8,128)(2,1)S(1)} %get-tuple-element.39.psum_ref, ...), custom_call_target="tpu_custom_call", output_to_operand_aliasing={{}: (5, {})} | custom-call | bytes 1771200 | tf_op jit(solution)/shard_map/join/pallas_call | solution.py:455
Async XLA Ops:
  1.4 5.7 %collective-permute-start = (bf16[48,128]{1,0:T(8,128)(2,1)S(1)}, bf16[48,128]{1,0:T(8,128)(2,1)S(1)}, u32[]{:S(2)}, u32[]{:S(2)}) collective-permute-start(bf16[48,128]{1,0:T(8,128)(2,1)S(1)} %get-tuple-element.24), channel_id=1, source_target_pairs={{0,4},{4,0},{8,12},{12,8},{1,5},{5,1},{9,13},{13,9},{2,6},{6,2},{1... | collective-permute-start | bytes 36872 | tf_op jit(solution)/shard_map/ppermute | solution.py:497
  1.9 2.6 %copy-start.3 = (s32[160]{0:T(256)S(1)}, s32[160]{0:T(256)}, u32[]{:S(2)}) copy-start(s32[160]{0:T(256)} %ids_ref.1) | copy-start | bytes 1924
  2.0 5.2 %collective-permute-start.1 = (bf16[48,128]{1,0:T(8,128)(2,1)S(1)}, bf16[48,128]{1,0:T(8,128)(2,1)S(1)}, u32[]{:S(2)}, u32[]{:S(2)}) collective-permute-start(bf16[48,128]{1,0:T(8,128)(2,1)S(1)} %get-tuple-element.25), channel_id=1, source_target_pairs={{0,8},{4,12},{8,0},{12,4},{1,9},{5,13},{9,1},{13,5},{2,10},{6,14},... | collective-permute-start | bytes 36872 | tf_op jit(solution)/shard_map/ppermute | solution.py:497
  4.5 3.1 %copy-start = (bf16[128,512]{1,0:T(8,128)(2,1)S(1)}, bf16[128,512]{1,0:T(8,128)(2,1)}, u32[]{:S(2)}) copy-start(bf16[128,512]{1,0:T(8,128)(2,1)} %win_ref.1) | copy-start | bytes 393220
  4.5 3.1 %collective-permute-start.2 = (bf16[48,128]{1,0:T(8,128)(2,1)S(1)}, bf16[48,128]{1,0:T(8,128)(2,1)S(1)}, u32[]{:S(2)}, u32[]{:S(2)}) collective-permute-start(bf16[48,128]{1,0:T(8,128)(2,1)S(1)} %get-tuple-element.26), channel_id=1, source_target_pairs={{0,12},{4,8},{8,4},{12,0},{1,13},{5,9},{9,5},{13,1},{2,14},{6,10},... | collective-permute-start | bytes 36872 | tf_op jit(solution)/shard_map/ppermute | solution.py:497
  11.6 15.7 %collective-permute-start.3 = (bf16[40,40,128]{2,1,0:T(8,128)(2,1)S(1)}, bf16[40,40,128]{2,1,0:T(8,128)(2,1)S(1)}, u32[]{:S(2)}, u32[]{:S(2)}) collective-permute-start(bf16[40,40,128]{2,1,0:T(8,128)(2,1)S(1)} %get-tuple-element.31.refs_0_), channel_id=1, source_target_pairs={{0,8},{1,4},{2,10},{3,6},{4,1},{5,13},{6,3},{7,15},{8,0},{9,12},{1... | collective-permute-start | bytes 1228808 | tf_op jit(solution)/shard_map/ppermute | solution.py:415
  12.9 14.4 %collective-permute-start.4 = (bf16[40,40,128]{2,1,0:T(8,128)(2,1)S(1)}, bf16[40,40,128]{2,1,0:T(8,128)(2,1)S(1)}, u32[]{:S(2)}, u32[]{:S(2)}) collective-permute-start(bf16[40,40,128]{2,1,0:T(8,128)(2,1)S(1)} %get-tuple-element.31.refs_0_), channel_id=1, source_target_pairs={{0,4},{1,8},{2,6},{3,10},{4,13},{5,1},{6,15},{7,3},{8,12},{9,0},{1... | collective-permute-start | bytes 1228808 | tf_op jit(solution)/shard_map/ppermute | solution.py:415
  13.7 13.5 %collective-permute-start.5 = (bf16[16,40,128]{2,1,0:T(8,128)(2,1)S(1)}, bf16[16,40,128]{2,1,0:T(8,128)(2,1)S(1)}, u32[]{:S(2)}, u32[]{:S(2)}) collective-permute-start(bf16[16,40,128]{2,1,0:T(8,128)(2,1)S(1)} %get-tuple-element.33.refs_5_), channel_id=1, source_target_pairs={{0,1},{1,0},{2,3},{3,2},{4,5},{5,4},{6,7},{7,6},{8,9},{9,8},{10,11... | collective-permute-start | bytes 491528 | tf_op jit(solution)/shard_map/ppermute | solution.py:415
  27.3 1.7 %collective-permute-start.6 = (bf16[40,40,128]{2,1,0:T(8,128)(2,1)S(1)}, bf16[40,40,128]{2,1,0:T(8,128)(2,1)S(1)}, u32[]{:S(2)}, u32[]{:S(2)}) collective-permute-start(bf16[40,40,128]{2,1,0:T(8,128)(2,1)S(1)} %collective-permute-done.3.refs_1_), channel_id=1, source_target_pairs={{0,4},{1,5},{2,6},{3,7},{4,0},{5,1},{6,2},{7,3},{8,12},{9,13},{10,... | collective-permute-start | bytes 1228808 | tf_op jit(solution)/shard_map/ppermute | solution.py:415
  27.3 2.3 %collective-permute-start.7 = (bf16[40,40,128]{2,1,0:T(8,128)(2,1)S(1)}, bf16[40,40,128]{2,1,0:T(8,128)(2,1)S(1)}, u32[]{:S(2)}, u32[]{:S(2)}) collective-permute-start(bf16[40,40,128]{2,1,0:T(8,128)(2,1)S(1)} %collective-permute-done.4.refs_3_), channel_id=1, source_target_pairs={{0,4},{1,5},{2,6},{3,7},{4,0},{5,1},{6,2},{7,3},{8,12},{9,13},{10,... | collective-permute-start | bytes 1228808 | tf_op jit(solution)/shard_map/ppermute | solution.py:415
  27.8 9.7 %collective-permute-start.8 = (bf16[24,40,128]{2,1,0:T(8,128)(2,1)S(1)}, bf16[24,40,128]{2,1,0:T(8,128)(2,1)S(1)}, u32[]{:S(2)}, u32[]{:S(2)}) collective-permute-start(bf16[24,40,128]{2,1,0:T(8,128)(2,1)S(1)} %get-tuple-element.36.refs_5_.refs_6_), channel_id=1, source_target_pairs={{0,1},{1,0},{2,3},{3,2},{4,5},{5,4},{6,7},{7,6},{8,9},{9,8},{10,11... | collective-permute-start | bytes 737288 | tf_op jit(solution)/shard_map/ppermute | solution.py:415
  31.7 17.4 %collective-permute-start.11 = (bf16[16,40,128]{2,1,0:T(8,128)(2,1)S(1)}, bf16[16,40,128]{2,1,0:T(8,128)(2,1)S(1)}, u32[]{:S(2)}, u32[]{:S(2)}) collective-permute-start(bf16[16,40,128]{2,1,0:T(8,128)(2,1)S(1)} %send_sums.5), channel_id=1, source_target_pairs={{0,2},{1,3},{2,0},{3,1},{4,6},{5,7},{6,4},{7,5},{8,10},{9,11},{10,... | collective-permute-start | bytes 491528 | tf_op jit(solution)/shard_map/ppermute | solution.py:415
  39.5 4.1 %copy-start.2 = (bf16[128,128]{1,0:T(8,128)(2,1)S(1)}, bf16[128,128]{1,0:T(8,128)(2,1)}, u32[]{:S(2)}) copy-start(bf16[128,128]{1,0:T(8,128)(2,1)} %refs_10_.1) | copy-start | bytes 98308
  39.5 12.5 %collective-permute-start.10 = (bf16[16,40,128]{2,1,0:T(8,128)(2,1)S(1)}, bf16[16,40,128]{2,1,0:T(8,128)(2,1)S(1)}, u32[]{:S(2)}, u32[]{:S(2)}) collective-permute-start(bf16[16,40,128]{2,1,0:T(8,128)(2,1)S(1)} %send_sums.4), channel_id=1, source_target_pairs={{0,2},{1,3},{2,0},{3,1},{4,6},{5,7},{6,4},{7,5},{8,10},{9,11},{10,... | collective-permute-start | bytes 491528 | tf_op jit(solution)/shard_map/ppermute | solution.py:415
  42.4 6.7 %copy-start.1 = (bf16[128,128]{1,0:T(8,128)(2,1)S(1)}, bf16[128,128]{1,0:T(8,128)(2,1)}, u32[]{:S(2)}) copy-start(bf16[128,128]{1,0:T(8,128)(2,1)} %w_ref.5) | copy-start | bytes 98308
  42.4 10.7 %collective-permute-start.9 = (bf16[8,40,128]{2,1,0:T(8,128)(2,1)S(1)}, bf16[8,40,128]{2,1,0:T(8,128)(2,1)S(1)}, u32[]{:S(2)}, u32[]{:S(2)}) collective-permute-start(bf16[8,40,128]{2,1,0:T(8,128)(2,1)S(1)} %send_sums.3), channel_id=1, source_target_pairs={{0,2},{1,3},{2,0},{3,1},{4,6},{5,7},{6,4},{7,5},{8,10},{9,11},{10,... | collective-permute-start | bytes 245768 | tf_op jit(solution)/shard_map/ppermute | solution.py:415

commit v6 on v5

--- a/solution.py
+++ b/solution.py
@@ -49,8 +49,9 @@
 
 
 def align_body(own_i, own_j, count, x_hbm, w_hbm, *refs):
-    outs, (x_ref, w_ref, y_ref, sem) = refs[:count], refs[count:]
-    copies = fetch([(x_hbm, x_ref), (w_hbm, w_ref)], sem)
+    later, outs, refs = refs[:4], refs[4 : 4 + count], refs[4 + count :]
+    brought, (x_ref, w_ref, y_ref, sem) = refs[:4], refs[4:]
+    copies = fetch([(x_hbm, x_ref), (w_hbm, w_ref), *zip(later, brought)], sem)
     seqs, residues, depth = x_ref.shape
     width = w_ref.shape[0] // 2
     height, lanes = outs[0].shape
@@ -64,25 +65,25 @@
         normed, w_ref[...], (((1,), (1,)), ((), ())), preferred_element_type=f32
     )
     start = pl.multiple_of(z * own_j, 8)
-    extent = max(own_i, own_j)
 
     def tall(v):
-        gap = extent - v.shape[0]
+        gap = height - v.shape[0]
         return jnp.concatenate([v, jnp.zeros((gap, v.shape[1]), f32)], axis=0) if gap else v
 
     right = [tall(y_ref[pl.ds(s * residues + start, own_j), width:]) for s in range(seqs)]
     gap = lanes - 2 * seqs * width
-    right += [jnp.zeros((extent, gap), f32)] if gap else []
+    right += [jnp.zeros((height, gap), f32)] if gap else []
     for d, out in enumerate(outs):
         first = pl.multiple_of((me ^ d) * own_i, 8)
         left = [tall(y_ref[pl.ds(s * residues + first, own_i), :width]) for s in range(seqs)]
-        out[pl.ds(0, extent), :] = jnp.concatenate(left + right, axis=1).astype(bf16)
-
-
-def prepare_body(seqs, couple_hbm, ids_ref, valid_hbm, bias_hbm, avg_hbm, base_ref, mask_ref, wq_ref, pick_ref,
-                 couple_ref, valid_ref, bias_ref, avg_ref, wf_ref, idc_ref, sem):
-    sources = (avg_hbm, valid_hbm, bias_hbm, couple_hbm)
-    copies = fetch(list(zip(sources, (avg_ref, valid_ref, bias_ref, couple_ref))), sem)
+        out[...] = jnp.concatenate(left + right, axis=1).astype(bf16)
+    for copy in copies[2:]:
+        copy.wait()
+
+
+def prepare_body(seqs, couple_ref, ids_hbm, valid_ref, bias_ref, avg_ref, base_ref, mask_ref, wq_ref, pick_ref,
+                 wf_ref, idc_ref, ids_ref, sem):
+    (copy,) = fetch([(ids_hbm, ids_ref)], sem)
     own_i, own_j, chans = couple_ref.shape
     pairs, width, _ = wq_ref.shape
     blocks, lanes, _ = pick_ref.shape
@@ -101,15 +102,13 @@
         return carry
 
     lax.fori_loop(0, blocks, pick, 0)
-    for j in range(own_j):
-        idc_ref[pl.ds(j, 1), :] = jnp.full((1, chans), ids_ref[z0 + j], jnp.int32)
-    copies[0].wait()
     wf_ref[...] = avg_ref[...].astype(f32)
     for h in range(pairs):
         both = [wf_ref[pl.ds(2 * h + d, width, stride=width), :] for d in range(2)]
         wq_ref[h] = jnp.concatenate(both, axis=1).astype(bf16)
-    for copy in copies[1:]:
-        copy.wait()
+    copy.wait()
+    for j in range(own_j):
+        idc_ref[pl.ds(j, 1), :] = jnp.full((1, chans), ids_ref[z0 + j], jnp.int32)
     idc = idc_ref[...]
     valid_t = valid_ref[...].astype(f32).T
     lane = lax.broadcasted_iota(jnp.int32, valid_t.shape, 1)
@@ -144,10 +143,9 @@
             xl_ref[pl.ds(r * seqs + s, own_i, stride=total), :] = moved[:, :128]
     lhs = xl_ref[:, :width].astype(bf16)
 
-    rmat = jnp.zeros((own_j, width * total), f32)
-    for r in range(blocks):
-        rmat += jnp.dot(msgs[r][pl.ds(0, own_j), :], pick_ref[r], preferred_element_type=f32)
-    rmat = rmat.astype(bf16)
+    joined = jnp.concatenate([msg[...] for msg in msgs], axis=1)
+    picks = pick_ref[...].reshape(blocks * lanes, width * total)
+    rmat = jnp.dot(joined, picks, preferred_element_type=f32)[:own_j].astype(bf16)
 
     def expand(h, carry):
         out = jnp.dot(lhs, wq_ref[h], preferred_element_type=f32)
@@ -158,7 +156,7 @@
         t_ref[:, where, chans:] = block[half:]
         return carry
 
-    lax.fori_loop(0, width // 2, expand, 0, unroll=4)
+    lax.fori_loop(0, width // 2, expand, 0, unroll=16 if turned else 4)
 
     step = 4 if half % 4 == 0 else 1
 
@@ -303,21 +301,25 @@
     with_right(True, rights, use)
 
 
-def join_body(first, sum_ref, own_ref, psum_ref, gate_ref, w_ref, *refs):
-    out_hbm, done_ref, sem = refs[-3:]
+def join_body(first, parts, own_ref, psum_ref, gate_ref, w_ref, *refs):
+    sums, (out_hbm, done_ref, sem) = refs[:parts], refs[-3:]
     count, extent, chans = done_ref.shape
     group = 8
-
-    def rows(b, carry):
-        some = pl.ds(b * group, group)
-        all_ = pl.ds(first + b * group, group)
-        mixed = own_ref[all_] + sum_ref[some].astype(f32)
-        normed = standardize(mixed).reshape(group * extent, -1).astype(bf16)
-        update = jnp.dot(normed, w_ref[...], preferred_element_type=f32).reshape(group, extent, -1)
-        done_ref[some] = (psum_ref[all_].astype(f32) + gate_ref[all_] * update).astype(bf16)
-        return carry
-
-    lax.fori_loop(0, count // group, rows, 0, unroll=True)
+    at = 0
+    for sum_ref in sums:
+        start = at
+
+        def rows(b, carry):
+            here = pl.ds(start + b * group, group)
+            there = pl.ds(first + start + b * group, group)
+            mixed = own_ref[there] + sum_ref[pl.ds(b * group, group)].astype(f32)
+            normed = standardize(mixed).reshape(group * extent, -1).astype(bf16)
+            update = jnp.dot(normed, w_ref[...], preferred_element_type=f32).reshape(group, extent, -1)
+            done_ref[here] = (psum_ref[there].astype(f32) + gate_ref[there] * update).astype(bf16)
+            return carry
+
+        lax.fori_loop(0, sum_ref.shape[0] // group, rows, 0, unroll=True)
+        at += sum_ref.shape[0]
     copy = pltpu.make_async_copy(done_ref, out_hbm.at[pl.ds(first, count)], sem)
     copy.start()
     copy.wait()
@@ -451,18 +453,18 @@
         name="keep_sums",
     )(*rights, *lefts, *mets, norm, w_gate)
     out = []
-    for part, (_, _, first, n) in zip(sums, chunks):
+    for first, n, parts in ((0, 16, sums[:1]), (16, own_i - 16, sums[1:])):
         out = [pl.pallas_call(
-            functools.partial(join_body, first),
+            functools.partial(join_body, first, len(parts)),
             out_shape=jax.ShapeDtypeStruct((own_i, own_j, chans), bf16),
-            in_specs=[VMEM] * 5 + [HBM] * len(out),
+            in_specs=[VMEM] * (4 + len(parts)) + [HBM] * len(out),
             out_specs=HBM,
             scratch_shapes=[pltpu.VMEM((n, own_j, chans), bf16), pltpu.SemaphoreType.DMA],
-            input_output_aliases={5: 0} if out else {},
+            input_output_aliases={4 + len(parts): 0} if out else {},
             compiler_params=limit(8),
             cost_estimate=cost(0.06 * n),
             name="join",
-        )(part, own, psum, gate, w_final, *out)]
+        )(own, psum, gate, w_final, *parts, *out)]
     return out[0]
 
 
@@ -478,21 +480,23 @@
     paired = rows == 4 and cols == 4 and own_i == own_j and own_i % 8 == 0 and own_i > 32
     scale = 1 if paired else 8
 
-    msgs = pl.pallas_call(
+    later = (average, valid, bias, couple)
+    *msgs, average, valid, bias, couple = pl.pallas_call(
         functools.partial(align_body, own_i, own_j, rows),
-        out_shape=[jax.ShapeDtypeStruct((height, lanes), bf16)] * rows,
-        in_specs=[HBM] * 2,
-        out_specs=[VMEM] * rows,
+        out_shape=[jax.ShapeDtypeStruct((height, lanes), bf16)] * rows
+        + [jax.ShapeDtypeStruct(x.shape, x.dtype) for x in later],
+        in_specs=[HBM] * 6,
+        out_specs=[VMEM] * (rows + 4),
         scratch_shapes=[
             pltpu.VMEM(homolog.shape, bf16),
             pltpu.VMEM((2 * width, depth), bf16),
             pltpu.VMEM((own_seqs * residues, 2 * width), f32),
-            pltpu.SemaphoreType.DMA((2,)),
+            pltpu.SemaphoreType.DMA((6,)),
         ],
         compiler_params=limit(8, scale),
         cost_estimate=cost(1.5),
         name="align",
-    )(hold(homolog), hold(factors.T))
+    )(hold(homolog), hold(factors.T), *map(hold, later))
     msgs = [msgs[0]] + [
         lax.ppermute(msg, "row", [(r, r ^ d) for r in range(rows)])
         for d, msg in enumerate(msgs) if d
@@ -504,21 +508,18 @@
                    jax.ShapeDtypeStruct((own_i, own_j, tri), bf16),
                    jax.ShapeDtypeStruct((width // 2, width, 2 * chans), bf16),
                    jax.ShapeDtypeStruct((rows, lanes, width * total), bf16)],
-        in_specs=[HBM, SMEM, HBM, HBM, HBM],
+        in_specs=[VMEM, HBM, VMEM, VMEM, VMEM],
         out_specs=[VMEM] * 4,
         scratch_shapes=[
-            pltpu.VMEM(couple.shape, bf16),
-            pltpu.VMEM(valid.shape, jnp.int32),
-            pltpu.VMEM(bias.shape, f32),
-            pltpu.VMEM(average.shape, bf16),
             pltpu.VMEM(average.shape, f32),
             pltpu.VMEM((own_j, chans), jnp.int32),
-            pltpu.SemaphoreType.DMA((4,)),
+            pltpu.SMEM(ids.shape, jnp.int32),
+            pltpu.SemaphoreType.DMA((1,)),
         ],
         compiler_params=limit(8, scale),
-        cost_estimate=cost(2.5),
+        cost_estimate=cost(2),
         name="prepare",
-    )(hold(couple), ids, hold(valid), hold(bias), hold(average))
+    )(couple, hold(ids), valid, bias, average)
 
     extents = (own_j, own_i) if paired else (own_i, own_j)
     psum, norm, right = pl.pallas_call(

time: 54.2 us -> 53.6 us (0.989)
  Pallas kernels: 21.8 us -> 19.3 us
  waiting for transfers between devices: 18.4 us -> 20.4 us
    pallas_call x1, Pallas kernels: 2.54 us -> 1.51 us  [shards(): pl.pallas_call(functools.partial(prepare_body, own_seqs), out_shape=[jax....]
    ppermute x3, waiting for transfers between devices: 0.49 us -> 1.53 us  [shards(): lax.ppermute(msg, 'row', [(r, r ^ d) for r in range(rows)])]
    ppermute x9, waiting for transfers between devices: 17.9 us -> 18.9 us  [move(): return lax.ppermute(value, ('row', 'col'), pairs)]
    pallas_call x3 -> x2, Pallas kernels: 3.09 us -> 2.22 us  [paired_plan(): pl.pallas_call(functools.partial(join_body, first, len(parts)), out_shape...]
    pallas_call x1, Pallas kernels: 3.9 us -> 3.21 us  [shards(): pl.pallas_call(functools.partial(pair_body, own_seqs, width, rows, paired...]
  transfers between devices with their start and end apart: 12 -> 12, of which waited for: 6 -> 7; matrix products, arithmetic and copies ran while one was open for 0% -> 0% of each run, Pallas kernels for 29% -> 25%
where the time goes in v6:
time: 53.6 us; the launch traced here: 53.5 us
  waiting for transfers between devices  20.4 us (38%)
  Pallas kernels  19.3 us (36%)
  starting transfers between devices  13.6 us (25%)
    ppermute x9, waiting for transfers between devices, move(): return lax.ppermute(value, ('row', 'col'), pairs)  18.9 us
    ppermute x9, starting transfers between devices, move(): return lax.ppermute(value, ('row', 'col'), pairs)  10.5 us
    pallas_call x1, Pallas kernels, paired_plan(): pl.pallas_call(functools.partial(keep_body, cuts), out_shape=[jax.ShapeDt...  5.36 us
    pallas_call x3, Pallas kernels, paired_plan(): pl.pallas_call(functools.partial(send_body, first), out_shape=jax.ShapeDt...  5.16 us
    pallas_call x1, Pallas kernels, shards(): pl.pallas_call(functools.partial(pair_body, own_seqs, width, rows, paired...  3.21 us
    ppermute x3, starting transfers between devices, shards(): lax.ppermute(msg, 'row', [(r, r ^ d) for r in range(rows)])  3.15 us
    pallas_call x2, Pallas kernels, paired_plan(): pl.pallas_call(functools.partial(join_body, first, len(parts)), out_shape...  2.22 us
    ppermute x3, waiting for transfers between devices, shards(): lax.ppermute(msg, 'row', [(r, r ^ d) for r in range(rows)])  1.53 us
  transfers between devices with their start and end apart: 12, of which 7 were waited for; matrix products, arithmetic and copies ran while one was open for 0% of the time, Pallas kernels for 25%

profile of v6, /device:TPU:0, one launch (start us, length us, event | category | flops | bytes accessed | tf_op | source)
XLA Modules:
  0.0 53.5 jit_solution(16891248715468203023)
XLA Ops:
  0.0 1.5 %align.1 = (bf16[48,128]{1,0:T(8,128)(2,1)S(1)}, bf16[48,128]{1,0:T(8,128)(2,1)S(1)}, bf16[48,128]{1,0:T(8,128)(2,1)S(1)}, bf16[48,128]{1,0:T(8,128)(2,1)S(1)}, ...) custom-call(bf16[2,160,256]{2,1,0:T(8,128)(2,1)} %x_hbm.1, ...), custom_call_target="tpu_custom_call" | custom-call | bytes 5535000 | tf_op jit(solution)/shard_map/align/pallas_call | solution.py:484
  1.5 0.5 collective-permute-start
  2.0 2.6 %collective-permute-start.1 = (bf16[48,128]{1,0:T(8,128)(2,1)S(1)}, bf16[48,128]{1,0:T(8,128)(2,1)S(1)}, u32[]{:S(2)}, u32[]{:S(2)}) collective-permute-start(bf16[48,128]{1,0:T(8,128)(2,1)S(1)} %get-tuple-element.29), channel_id=1, source_target_pairs={{0,8},{4,12},{8,0},{12,4},{1,9},{5,13},{9,1},{13,5},{2,10},{6,14},... | collective-permute-start | bytes 36872 | tf_op jit(solution)/shard_map/ppermute | solution.py:501
  4.6 0.1 collective-permute-start.2
  4.6 0.0 copy-start
  4.6 1.5 %prepare.1 = (f32[40,40,128]{2,1,0:T(8,128)S(1)}, bf16[40,40,128]{2,1,0:T(8,128)(2,1)S(1)}, bf16[16,32,256]{2,1,0:T(8,128)(2,1)S(1)}, bf16[4,128,256]{2,1,0:T(8,128)(2,1)S(1)}) custom-call(bf16[40,40,128]{2,1,0:T(8,128)(2,1)S(1)} %get-tuple-element.31.couple_ref, s32[160]{0:T(256)} %ids_hbm.1, s32[40,40]{1,0:T(8,128)S(1)} %get-tuple-element.32.valid_ref, ...), custom_call_target="tpu_custom_call" | custom-call | bytes 7380000 | tf_op jit(solution)/shard_map/prepare/pallas_call | solution.py:505
  6.1 0.0 collective-permute-done.refs_1_
  6.2 0.1 collective-permute-done.1.refs_2_
  6.2 1.4 %collective-permute-done.2.refs_3_ = bf16[48,128]{1,0:T(8,128)(2,1)S(1)} collective-permute-done((bf16[48,128]{1,0:T(8,128)(2,1)S(1)}, bf16[48,128]{1,0:T(8,128)(2,1)S(1)}, u32[]{:S(2)}, u32[]{:S(2)}) %collective-permute-start.2) | collective-permute-done | bytes 12320 | tf_op jit(solution)/shard_map/ppermute | solution.py:501
  7.7 0.0 copy-done
  7.7 3.2 %pair.1 = (bf16[40,40,128]{2,1,0:T(8,128)(2,1)S(1)}, bf16[1600,128]{1,0:T(8,128)(2,1)S(1)}, bf16[40,40,128]{2,1,0:T(8,128)(2,1)S(1)}) custom-call(bf16[48,128]{1,0:T(8,128)(2,1)S(1)} %get-tuple-element.27.refs_0_, bf16[48,128]{1,0:T(8,128)(2,1)S(1)} %collective-permute-done.refs_1_, bf16[48,128]{1,0:T(8,128)(2,1)S(1)} %collective-permute-done.1.refs_2_, ...), custom_call_target="tpu_custom_call" | custom-call | bytes 16605000 | tf_op jit(solution)/shard_map/pair/pallas_call | solution.py:525
  10.9 0.6 %collective-permute-start.3 = (bf16[40,40,128]{2,1,0:T(8,128)(2,1)S(1)}, bf16[40,40,128]{2,1,0:T(8,128)(2,1)S(1)}, u32[]{:S(2)}, u32[]{:S(2)}) collective-permute-start(bf16[40,40,128]{2,1,0:T(8,128)(2,1)S(1)} %get-tuple-element.39.refs_0_), channel_id=1, source_target_pairs={{0,8},{1,4},{2,10},{3,6},{4,1},{5,13},{6,3},{7,15},{8,0},{9,12},{1... | collective-permute-start | bytes 1228808 | tf_op jit(solution)/shard_map/ppermute | solution.py:417
  11.5 1.1 %collective-permute-start.4 = (bf16[40,40,128]{2,1,0:T(8,128)(2,1)S(1)}, bf16[40,40,128]{2,1,0:T(8,128)(2,1)S(1)}, u32[]{:S(2)}, u32[]{:S(2)}) collective-permute-start(bf16[40,40,128]{2,1,0:T(8,128)(2,1)S(1)} %get-tuple-element.39.refs_0_), channel_id=1, source_target_pairs={{0,4},{1,8},{2,6},{3,10},{4,13},{5,1},{6,15},{7,3},{8,12},{9,0},{1... | collective-permute-start | bytes 1228808 | tf_op jit(solution)/shard_map/ppermute | solution.py:417
  12.7 0.4 left.1
  13.0 1.9 %collective-permute-start.5 = (bf16[16,40,128]{2,1,0:T(8,128)(2,1)S(1)}, bf16[16,40,128]{2,1,0:T(8,128)(2,1)S(1)}, u32[]{:S(2)}, u32[]{:S(2)}) collective-permute-start(bf16[16,40,128]{2,1,0:T(8,128)(2,1)S(1)} %get-tuple-element.41.refs_5_), channel_id=1, source_target_pairs={{0,1},{1,0},{2,3},{3,2},{4,5},{5,4},{6,7},{7,6},{8,9},{9,8},{10,11... | collective-permute-start | bytes 491528 | tf_op jit(solution)/shard_map/ppermute | solution.py:417
  14.9 11.7 %collective-permute-done.5.refs_7_.refs_6_ = bf16[16,40,128]{2,1,0:T(8,128)(2,1)S(1)} collective-permute-done((bf16[16,40,128]{2,1,0:T(8,128)(2,1)S(1)}, bf16[16,40,128]{2,1,0:T(8,128)(2,1)S(1)}, u32[]{:S(2)}, u32[]{:S(2)}) %collective-permute-start.5) | collective-permute-done | bytes 163872 | tf_op jit(solution)/shard_map/ppermute | solution.py:417
  26.6 0.0 collective-permute-done.3.refs_1_
  26.6 0.0 collective-permute-done.4.refs_3_
  26.6 0.0 collective-permute-start.6
  26.6 0.5 collective-permute-start.7
  27.1 0.6 %collective-permute-start.8 = (bf16[24,40,128]{2,1,0:T(8,128)(2,1)S(1)}, bf16[24,40,128]{2,1,0:T(8,128)(2,1)S(1)}, u32[]{:S(2)}, u32[]{:S(2)}) collective-permute-start(bf16[24,40,128]{2,1,0:T(8,128)(2,1)S(1)} %get-tuple-element.44.refs_6_.refs_5_), channel_id=1, source_target_pairs={{0,1},{1,0},{2,3},{3,2},{4,5},{5,4},{6,7},{7,6},{8,9},{9,8},{10,11... | collective-permute-start | bytes 737288 | tf_op jit(solution)/shard_map/ppermute | solution.py:417
  27.7 0.6 %collective-permute-done.6.refs_2_ = bf16[40,40,128]{2,1,0:T(8,128)(2,1)S(1)} collective-permute-done((bf16[40,40,128]{2,1,0:T(8,128)(2,1)S(1)}, bf16[40,40,128]{2,1,0:T(8,128)(2,1)S(1)}, u32[]{:S(2)}, u32[]{:S(2)}) %collective-permute-start.6) | collective-permute-done | bytes 409632 | tf_op jit(solution)/shard_map/ppermute | solution.py:417
  28.3 0.6 %collective-permute-done.7.refs_4_ = bf16[40,40,128]{2,1,0:T(8,128)(2,1)S(1)} collective-permute-done((bf16[40,40,128]{2,1,0:T(8,128)(2,1)S(1)}, bf16[40,40,128]{2,1,0:T(8,128)(2,1)S(1)}, u32[]{:S(2)}, u32[]{:S(2)}) %collective-permute-start.7) | collective-permute-done | bytes 409632 | tf_op jit(solution)/shard_map/ppermute | solution.py:417
  28.9 2.1 %send_sums.5 = bf16[16,40,128]{2,1,0:T(8,128)(2,1)S(1)} custom-call(bf16[40,40,128]{2,1,0:T(8,128)(2,1)S(1)} %get-tuple-element.39.refs_0_, bf16[40,40,128]{2,1,0:T(8,128)(2,1)S(1)} %collective-permute-done.3.refs_1_, bf16[40,40,128]{2,1,0:T(8,128)(2,1)S(1)} %collective-permute-done.6.refs_2_, bf16[40,40,128]{2,1,0:T(8,128)(2,1)S(1)} %collective-permute-done.4.refs_3_, ...), custom_call_target="tpu_custom_call" | custom-call | bytes 8560800 | tf_op jit(solution)/shard_map/send_sums/pallas_call | solution.py:432
  31.0 2.7 %collective-permute-start.11 = (bf16[16,40,128]{2,1,0:T(8,128)(2,1)S(1)}, bf16[16,40,128]{2,1,0:T(8,128)(2,1)S(1)}, u32[]{:S(2)}, u32[]{:S(2)}) collective-permute-start(bf16[16,40,128]{2,1,0:T(8,128)(2,1)S(1)} %send_sums.5), channel_id=1, source_target_pairs={{0,2},{1,3},{2,0},{3,1},{4,6},{5,7},{6,4},{7,5},{8,10},{9,11},{10,... | collective-permute-start | bytes 491528 | tf_op jit(solution)/shard_map/ppermute | solution.py:417
  33.6 3.1 %collective-permute-done.8.refs_8_.refs_6_ = bf16[24,40,128]{2,1,0:T(8,128)(2,1)S(1)} collective-permute-done((bf16[24,40,128]{2,1,0:T(8,128)(2,1)S(1)}, bf16[24,40,128]{2,1,0:T(8,128)(2,1)S(1)}, u32[]{:S(2)}, u32[]{:S(2)}) %collective-permute-start.8) | collective-permute-done | bytes 245792 | tf_op jit(solution)/shard_map/ppermute | solution.py:417
  36.8 2.1 %send_sums.3 = bf16[16,40,128]{2,1,0:T(8,128)(2,1)S(1)} custom-call(bf16[40,40,128]{2,1,0:T(8,128)(2,1)S(1)} %get-tuple-element.39.refs_0_, bf16[40,40,128]{2,1,0:T(8,128)(2,1)S(1)} %collective-permute-done.3.refs_1_, bf16[40,40,128]{2,1,0:T(8,128)(2,1)S(1)} %collective-permute-done.6.refs_2_, bf16[40,40,128]{2,1,0:T(8,128)(2,1)S(1)} %collective-permute-done.4.refs_3_, ...), custom_call_target="tpu_custom_call" | custom-call | bytes 8560800 | tf_op jit(solution)/shard_map/send_sums/pallas_call | solution.py:432
  38.9 0.0 copy-start.2
  38.9 1.8 %collective-permute-start.9 = (bf16[16,40,128]{2,1,0:T(8,128)(2,1)S(1)}, bf16[16,40,128]{2,1,0:T(8,128)(2,1)S(1)}, u32[]{:S(2)}, u32[]{:S(2)}) collective-permute-start(bf16[16,40,128]{2,1,0:T(8,128)(2,1)S(1)} %send_sums.3), channel_id=1, source_target_pairs={{0,2},{1,3},{2,0},{3,1},{4,6},{5,7},{6,4},{7,5},{8,10},{9,11},{10,... | collective-permute-start | bytes 491528 | tf_op jit(solution)/shard_map/ppermute | solution.py:417
  40.6 1.0 %send_sums.4 = bf16[8,40,128]{2,1,0:T(8,128)(2,1)S(1)} custom-call(bf16[40,40,128]{2,1,0:T(8,128)(2,1)S(1)} %get-tuple-element.39.refs_0_, bf16[40,40,128]{2,1,0:T(8,128)(2,1)S(1)} %collective-permute-done.3.refs_1_, bf16[40,40,128]{2,1,0:T(8,128)(2,1)S(1)} %collective-permute-done.6.refs_2_, bf16[40,40,128]{2,1,0:T(8,128)(2,1)S(1)} %collective-permute-done.4.refs_3_, ...), custom_call_target="tpu_custom_call" | custom-call | bytes 5018400 | tf_op jit(solution)/shard_map/send_sums/pallas_call | solution.py:432
  41.7 0.0 copy-start.1
  41.7 1.3 %collective-permute-start.10 = (bf16[8,40,128]{2,1,0:T(8,128)(2,1)S(1)}, bf16[8,40,128]{2,1,0:T(8,128)(2,1)S(1)}, u32[]{:S(2)}, u32[]{:S(2)}) collective-permute-start(bf16[8,40,128]{2,1,0:T(8,128)(2,1)S(1)} %send_sums.4), channel_id=1, source_target_pairs={{0,2},{1,3},{2,0},{3,1},{4,6},{5,7},{6,4},{7,5},{8,10},{9,11},{10,... | collective-permute-start | bytes 245768 | tf_op jit(solution)/shard_map/ppermute | solution.py:417
  43.0 0.0 copy-done.2
  43.0 5.4 %keep_sums.1 = (f32[40,40,128]{2,1,0:T(8,128)S(1)}, f32[40,40,128]{2,1,0:T(8,128)S(1)}) custom-call(bf16[40,40,128]{2,1,0:T(8,128)(2,1)S(1)} %get-tuple-element.39.refs_0_, bf16[40,40,128]{2,1,0:T(8,128)(2,1)S(1)} %collective-permute-done.3.refs_1_, bf16[40,40,128]{2,1,0:T(8,128)(2,1)S(1)} %collective-permute-done.6.refs_2_, ...), custom_call_target="tpu_custom_call" | custom-call | bytes 22140000 | tf_op jit(solution)/shard_map/keep_sums/pallas_call | solution.py:444
  48.4 0.0 collective-permute-done.11.refs_0_
  48.4 0.0 copy-done.1
  48.4 1.1 %join.2.refs_2_ = bf16[40,40,128]{2,1,0:T(8,128)(2,1)} custom-call(f32[40,40,128]{2,1,0:T(8,128)S(1)} %get-tuple-element.46.own_ref, bf16[40,40,128]{2,1,0:T(8,128)(2,1)S(1)} %get-tuple-element.47.psum_ref, f32[40,40,128]{2,1,0:T(8,128)S(1)} %get-tuple-element.48.gate_ref, bf16[128,128]{1,0:T(8,128)(2,1)S(1)} %copy-done.1, ...), custom_call_target="tpu_custom_call" | custom-call | bytes 3542400 | tf_op jit(solution)/shard_map/join/pallas_call | solution.py:457
  49.4 2.9 %collective-permute-done.10.refs_1_ = bf16[8,40,128]{2,1,0:T(8,128)(2,1)S(1)} collective-permute-done((bf16[8,40,128]{2,1,0:T(8,128)(2,1)S(1)}, bf16[8,40,128]{2,1,0:T(8,128)(2,1)S(1)}, u32[]{:S(2)}, u32[]{:S(2)}) %collective-permute-start.10) | collective-permute-done | bytes 81952 | tf_op jit(solution)/shard_map/ppermute | solution.py:417
  52.3 0.0 collective-permute-done.9.refs_0_
  52.3 1.2 %join.3 = bf16[40,40,128]{2,1,0:T(8,128)(2,1)} custom-call(f32[40,40,128]{2,1,0:T(8,128)S(1)} %get-tuple-element.46.own_ref, bf16[40,40,128]{2,1,0:T(8,128)(2,1)S(1)} %get-tuple-element.47.psum_ref, f32[40,40,128]{2,1,0:T(8,128)S(1)} %get-tuple-element.48.gate_ref, bf16[128,128]{1,0:T(8,128)(2,1)S(1)} %copy-done.1, ...), custom_call_target="tpu_custom_call", output_to_operand_aliasing={{}: (6, {})} | custom-call | bytes 5313600 | tf_op jit(solution)/shard_map/join/pallas_call | solution.py:457
Async XLA Ops:
  1.5 4.7 %collective-permute-start = (bf16[48,128]{1,0:T(8,128)(2,1)S(1)}, bf16[48,128]{1,0:T(8,128)(2,1)S(1)}, u32[]{:S(2)}, u32[]{:S(2)}) collective-permute-start(bf16[48,128]{1,0:T(8,128)(2,1)S(1)} %get-tuple-element.28), channel_id=1, source_target_pairs={{0,4},{4,0},{8,12},{12,8},{1,5},{5,1},{9,13},{13,9},{2,6},{6,2},{1... | collective-permute-start | bytes 36872 | tf_op jit(solution)/shard_map/ppermute | solution.py:501
  2.0 4.2 %collective-permute-start.1 = (bf16[48,128]{1,0:T(8,128)(2,1)S(1)}, bf16[48,128]{1,0:T(8,128)(2,1)S(1)}, u32[]{:S(2)}, u32[]{:S(2)}) collective-permute-start(bf16[48,128]{1,0:T(8,128)(2,1)S(1)} %get-tuple-element.29), channel_id=1, source_target_pairs={{0,8},{4,12},{8,0},{12,4},{1,9},{5,13},{9,1},{13,5},{2,10},{6,14},... | collective-permute-start | bytes 36872 | tf_op jit(solution)/shard_map/ppermute | solution.py:501
  4.6 3.1 %collective-permute-start.2 = (bf16[48,128]{1,0:T(8,128)(2,1)S(1)}, bf16[48,128]{1,0:T(8,128)(2,1)S(1)}, u32[]{:S(2)}, u32[]{:S(2)}) collective-permute-start(bf16[48,128]{1,0:T(8,128)(2,1)S(1)} %get-tuple-element.30), channel_id=1, source_target_pairs={{0,12},{4,8},{8,4},{12,0},{1,13},{5,9},{9,5},{13,1},{2,14},{6,10},... | collective-permute-start | bytes 36872 | tf_op jit(solution)/shard_map/ppermute | solution.py:501
  4.6 3.1 %copy-start = (bf16[128,512]{1,0:T(8,128)(2,1)S(1)}, bf16[128,512]{1,0:T(8,128)(2,1)}, u32[]{:S(2)}) copy-start(bf16[128,512]{1,0:T(8,128)(2,1)} %win_ref.1) | copy-start | bytes 393220
  10.9 15.7 %collective-permute-start.3 = (bf16[40,40,128]{2,1,0:T(8,128)(2,1)S(1)}, bf16[40,40,128]{2,1,0:T(8,128)(2,1)S(1)}, u32[]{:S(2)}, u32[]{:S(2)}) collective-permute-start(bf16[40,40,128]{2,1,0:T(8,128)(2,1)S(1)} %get-tuple-element.39.refs_0_), channel_id=1, source_target_pairs={{0,8},{1,4},{2,10},{3,6},{4,1},{5,13},{6,3},{7,15},{8,0},{9,12},{1... | collective-permute-start | bytes 1228808 | tf_op jit(solution)/shard_map/ppermute | solution.py:417
  11.5 15.0 %collective-permute-start.4 = (bf16[40,40,128]{2,1,0:T(8,128)(2,1)S(1)}, bf16[40,40,128]{2,1,0:T(8,128)(2,1)S(1)}, u32[]{:S(2)}, u32[]{:S(2)}) collective-permute-start(bf16[40,40,128]{2,1,0:T(8,128)(2,1)S(1)} %get-tuple-element.39.refs_0_), channel_id=1, source_target_pairs={{0,4},{1,8},{2,6},{3,10},{4,13},{5,1},{6,15},{7,3},{8,12},{9,0},{1... | collective-permute-start | bytes 1228808 | tf_op jit(solution)/shard_map/ppermute | solution.py:417
  13.0 13.6 %collective-permute-start.5 = (bf16[16,40,128]{2,1,0:T(8,128)(2,1)S(1)}, bf16[16,40,128]{2,1,0:T(8,128)(2,1)S(1)}, u32[]{:S(2)}, u32[]{:S(2)}) collective-permute-start(bf16[16,40,128]{2,1,0:T(8,128)(2,1)S(1)} %get-tuple-element.41.refs_5_), channel_id=1, source_target_pairs={{0,1},{1,0},{2,3},{3,2},{4,5},{5,4},{6,7},{7,6},{8,9},{9,8},{10,11... | collective-permute-start | bytes 491528 | tf_op jit(solution)/shard_map/ppermute | solution.py:417
  26.6 1.7 %collective-permute-start.6 = (bf16[40,40,128]{2,1,0:T(8,128)(2,1)S(1)}, bf16[40,40,128]{2,1,0:T(8,128)(2,1)S(1)}, u32[]{:S(2)}, u32[]{:S(2)}) collective-permute-start(bf16[40,40,128]{2,1,0:T(8,128)(2,1)S(1)} %collective-permute-done.3.refs_1_), channel_id=1, source_target_pairs={{0,4},{1,5},{2,6},{3,7},{4,0},{5,1},{6,2},{7,3},{8,12},{9,13},{10,... | collective-permute-start | bytes 1228808 | tf_op jit(solution)/shard_map/ppermute | solution.py:417
  26.6 2.3 %collective-permute-start.7 = (bf16[40,40,128]{2,1,0:T(8,128)(2,1)S(1)}, bf16[40,40,128]{2,1,0:T(8,128)(2,1)S(1)}, u32[]{:S(2)}, u32[]{:S(2)}) collective-permute-start(bf16[40,40,128]{2,1,0:T(8,128)(2,1)S(1)} %collective-permute-done.4.refs_3_), channel_id=1, source_target_pairs={{0,4},{1,5},{2,6},{3,7},{4,0},{5,1},{6,2},{7,3},{8,12},{9,13},{10,... | collective-permute-start | bytes 1228808 | tf_op jit(solution)/shard_map/ppermute | solution.py:417
  27.1 9.7 %collective-permute-start.8 = (bf16[24,40,128]{2,1,0:T(8,128)(2,1)S(1)}, bf16[24,40,128]{2,1,0:T(8,128)(2,1)S(1)}, u32[]{:S(2)}, u32[]{:S(2)}) collective-permute-start(bf16[24,40,128]{2,1,0:T(8,128)(2,1)S(1)} %get-tuple-element.44.refs_6_.refs_5_), channel_id=1, source_target_pairs={{0,1},{1,0},{2,3},{3,2},{4,5},{5,4},{6,7},{7,6},{8,9},{9,8},{10,11... | collective-permute-start | bytes 737288 | tf_op jit(solution)/shard_map/ppermute | solution.py:417
  31.0 17.4 %collective-permute-start.11 = (bf16[16,40,128]{2,1,0:T(8,128)(2,1)S(1)}, bf16[16,40,128]{2,1,0:T(8,128)(2,1)S(1)}, u32[]{:S(2)}, u32[]{:S(2)}) collective-permute-start(bf16[16,40,128]{2,1,0:T(8,128)(2,1)S(1)} %send_sums.5), channel_id=1, source_target_pairs={{0,2},{1,3},{2,0},{3,1},{4,6},{5,7},{6,4},{7,5},{8,10},{9,11},{10,... | collective-permute-start | bytes 491528 | tf_op jit(solution)/shard_map/ppermute | solution.py:417
  38.9 4.1 %copy-start.2 = (bf16[128,128]{1,0:T(8,128)(2,1)S(1)}, bf16[128,128]{1,0:T(8,128)(2,1)}, u32[]{:S(2)}) copy-start(bf16[128,128]{1,0:T(8,128)(2,1)} %refs_10_.1) | copy-start | bytes 98308
  38.9 13.4 %collective-permute-start.9 = (bf16[16,40,128]{2,1,0:T(8,128)(2,1)S(1)}, bf16[16,40,128]{2,1,0:T(8,128)(2,1)S(1)}, u32[]{:S(2)}, u32[]{:S(2)}) collective-permute-start(bf16[16,40,128]{2,1,0:T(8,128)(2,1)S(1)} %send_sums.3), channel_id=1, source_target_pairs={{0,2},{1,3},{2,0},{3,1},{4,6},{5,7},{6,4},{7,5},{8,10},{9,11},{10,... | collective-permute-start | bytes 491528 | tf_op jit(solution)/shard_map/ppermute | solution.py:417
  41.7 6.7 %copy-start.1 = (bf16[128,128]{1,0:T(8,128)(2,1)S(1)}, bf16[128,128]{1,0:T(8,128)(2,1)}, u32[]{:S(2)}) copy-start(bf16[128,128]{1,0:T(8,128)(2,1)} %w_ref.3) | copy-start | bytes 98308
  41.7 10.6 %collective-permute-start.10 = (bf16[8,40,128]{2,1,0:T(8,128)(2,1)S(1)}, bf16[8,40,128]{2,1,0:T(8,128)(2,1)S(1)}, u32[]{:S(2)}, u32[]{:S(2)}) collective-permute-start(bf16[8,40,128]{2,1,0:T(8,128)(2,1)S(1)} %send_sums.4), channel_id=1, source_target_pairs={{0,2},{1,3},{2,0},{3,1},{4,6},{5,7},{6,4},{7,5},{8,10},{9,11},{10,... | collective-permute-start | bytes 245768 | tf_op jit(solution)/shard_map/ppermute | solution.py:417

commit v7 on v6

--- a/solution.py
+++ b/solution.py
@@ -427,7 +427,7 @@
     rights = (right, got, p_got, far, p_far)
 
     sums = []
-    chunks = ((0, 0, 0, 16), (1, 0, 16, 16), (1, 16, 32, own_i - 32))
+    chunks = [(n, m, 0, 8) for n, left in enumerate(lefts) for m in range(0, left.shape[0], 8)]
     for at, first, _, n in chunks:
         part = pl.pallas_call(
             functools.partial(send_body, first),
@@ -453,7 +453,8 @@
         name="keep_sums",
     )(*rights, *lefts, *mets, norm, w_gate)
     out = []
-    for first, n, parts in ((0, 16, sums[:1]), (16, own_i - 16, sums[1:])):
+    for first, n in ((0, 16), (16, own_i - 16)):
+        parts = sums[first // 8 : (first + n) // 8]
         out = [pl.pallas_call(
             functools.partial(join_body, first, len(parts)),
             out_shape=jax.ShapeDtypeStruct((own_i, own_j, chans), bf16),
@@ -497,10 +498,8 @@
         cost_estimate=cost(1.5),
         name="align",
     )(hold(homolog), hold(factors.T), *map(hold, later))
-    msgs = [msgs[0]] + [
-        lax.ppermute(msg, "row", [(r, r ^ d) for r in range(rows)])
-        for d, msg in enumerate(msgs) if d
-    ]
+    for d in reversed(range(1, rows)):
+        msgs[d] = lax.ppermute(msgs[d], "row", [(r, r ^ d) for r in range(rows)])
 
     base, mask, wq, pick = pl.pallas_call(
         functools.partial(prepare_body, own_seqs),
@@ -539,7 +538,7 @@
         name="pair",
     )(*msgs, base, mask, wq, pick, w_in)
 
-    cuts = [16, own_i - 16] if paired else [own_i]
+    cuts = [8, 16, own_i - 24] if paired else [own_i]
     lefts = pl.pallas_call(
         left_body,
         out_shape=[jax.ShapeDtypeStruct((n, own_j, tri), bf16) for n in cuts],

time: 53.6 us -> 53.3 us (level)
  waiting for transfers between devices: 20.4 us -> 15.6 us
  starting transfers between devices: 13.6 us -> 18.1 us
    ppermute x9 -> x12, waiting for transfers between devices: 18.9 us -> 14 us  [move(): return lax.ppermute(value, ('row', 'col'), pairs)]
    ppermute x9 -> x12, starting transfers between devices: 10.5 us -> 14.9 us  [move(): return lax.ppermute(value, ('row', 'col'), pairs)]
    pallas_call x3 -> x5, Pallas kernels: 5.16 us -> 5.2 us  [paired_plan(): pl.pallas_call(functools.partial(send_body, first), out_shape=jax.ShapeDt...]
  transfers between devices with their start and end apart: 12 -> 15, of which waited for: 7 -> 6; matrix products, arithmetic and copies ran while one was open for 0% -> 0% of each run, Pallas kernels for 25% -> 25%
where the time goes in v7:
time: 53.3 us; the launch traced here: 53.1 us
  Pallas kernels  19.3 us (36%)
  starting transfers between devices  18.1 us (34%)
  waiting for transfers between devices  15.6 us (29%)
    ppermute x12, starting transfers between devices, move(): return lax.ppermute(value, ('row', 'col'), pairs)  14.9 us
    ppermute x12, waiting for transfers between devices, move(): return lax.ppermute(value, ('row', 'col'), pairs)  14 us
    pallas_call x1, Pallas kernels, paired_plan(): pl.pallas_call(functools.partial(keep_body, cuts), out_shape=[jax.ShapeDt...  5.36 us
    pallas_call x5, Pallas kernels, paired_plan(): pl.pallas_call(functools.partial(send_body, first), out_shape=jax.ShapeDt...  5.2 us
    pallas_call x1, Pallas kernels, shards(): pl.pallas_call(functools.partial(pair_body, own_seqs, width, rows, paired...  3.21 us
    ppermute x3, starting transfers between devices, shards(): msgs[d] = lax.ppermute(msgs[d], 'row', [(r, r ^ d) for r in range(rows)])  3.15 us
    pallas_call x2, Pallas kernels, paired_plan(): pl.pallas_call(functools.partial(join_body, first, len(parts)), out_shape...  2.22 us
    ppermute x3, waiting for transfers between devices, shards(): msgs[d] = lax.ppermute(msgs[d], 'row', [(r, r ^ d) for r in range(rows)])  1.53 us
  transfers between devices with their start and end apart: 15, of which 6 were waited for; matrix products, arithmetic and copies ran while one was open for 0% of the time, Pallas kernels for 25%

profile of v7, /device:TPU:0, one launch (start us, length us, event | category | flops | bytes accessed | tf_op | source)
XLA Modules:
  0.0 53.1 jit_solution(7042892735140328286)
XLA Ops:
  0.0 1.5 %align.1 = (bf16[48,128]{1,0:T(8,128)(2,1)S(1)}, bf16[48,128]{1,0:T(8,128)(2,1)S(1)}, bf16[48,128]{1,0:T(8,128)(2,1)S(1)}, bf16[48,128]{1,0:T(8,128)(2,1)S(1)}, ...) custom-call(bf16[2,160,256]{2,1,0:T(8,128)(2,1)} %x_hbm.1, ...), custom_call_target="tpu_custom_call" | custom-call | bytes 5535000 | tf_op jit(solution)/shard_map/align/pallas_call | solution.py:485
  1.5 0.5 collective-permute-start
  2.0 2.6 %collective-permute-start.1 = (bf16[48,128]{1,0:T(8,128)(2,1)S(1)}, bf16[48,128]{1,0:T(8,128)(2,1)S(1)}, u32[]{:S(2)}, u32[]{:S(2)}) collective-permute-start(bf16[48,128]{1,0:T(8,128)(2,1)S(1)} %get-tuple-element.30), channel_id=1, source_target_pairs={{0,8},{4,12},{8,0},{12,4},{1,9},{5,13},{9,1},{13,5},{2,10},{6,14},... | collective-permute-start | bytes 36872 | tf_op jit(solution)/shard_map/ppermute | solution.py:502
  4.6 0.1 collective-permute-start.2
  4.6 0.0 copy-start
  4.6 1.5 %prepare.1 = (f32[40,40,128]{2,1,0:T(8,128)S(1)}, bf16[40,40,128]{2,1,0:T(8,128)(2,1)S(1)}, bf16[16,32,256]{2,1,0:T(8,128)(2,1)S(1)}, bf16[4,128,256]{2,1,0:T(8,128)(2,1)S(1)}) custom-call(bf16[40,40,128]{2,1,0:T(8,128)(2,1)S(1)} %get-tuple-element.32.couple_ref, s32[160]{0:T(256)} %ids_hbm.1, s32[40,40]{1,0:T(8,128)S(1)} %get-tuple-element.33.valid_ref, ...), custom_call_target="tpu_custom_call" | custom-call | bytes 7380000 | tf_op jit(solution)/shard_map/prepare/pallas_call | solution.py:504
  6.1 0.0 collective-permute-done.refs_1_
  6.2 0.1 collective-permute-done.1.refs_2_
  6.2 1.4 %collective-permute-done.2.refs_3_ = bf16[48,128]{1,0:T(8,128)(2,1)S(1)} collective-permute-done((bf16[48,128]{1,0:T(8,128)(2,1)S(1)}, bf16[48,128]{1,0:T(8,128)(2,1)S(1)}, u32[]{:S(2)}, u32[]{:S(2)}) %collective-permute-start.2) | collective-permute-done | bytes 12320 | tf_op jit(solution)/shard_map/ppermute | solution.py:502
  7.7 0.0 copy-done
  7.7 3.2 %pair.1 = (bf16[40,40,128]{2,1,0:T(8,128)(2,1)S(1)}, bf16[1600,128]{1,0:T(8,128)(2,1)S(1)}, bf16[40,40,128]{2,1,0:T(8,128)(2,1)S(1)}) custom-call(bf16[48,128]{1,0:T(8,128)(2,1)S(1)} %get-tuple-element.28.refs_0_, bf16[48,128]{1,0:T(8,128)(2,1)S(1)} %collective-permute-done.refs_1_, bf16[48,128]{1,0:T(8,128)(2,1)S(1)} %collective-permute-done.1.refs_2_, ...), custom_call_target="tpu_custom_call" | custom-call | bytes 16605000 | tf_op jit(solution)/shard_map/pair/pallas_call | solution.py:524
  10.9 0.6 %collective-permute-start.3 = (bf16[40,40,128]{2,1,0:T(8,128)(2,1)S(1)}, bf16[40,40,128]{2,1,0:T(8,128)(2,1)S(1)}, u32[]{:S(2)}, u32[]{:S(2)}) collective-permute-start(bf16[40,40,128]{2,1,0:T(8,128)(2,1)S(1)} %get-tuple-element.40.refs_0_), channel_id=1, source_target_pairs={{0,8},{1,4},{2,10},{3,6},{4,1},{5,13},{6,3},{7,15},{8,0},{9,12},{1... | collective-permute-start | bytes 1228808 | tf_op jit(solution)/shard_map/ppermute | solution.py:417
  11.5 1.1 %collective-permute-start.4 = (bf16[40,40,128]{2,1,0:T(8,128)(2,1)S(1)}, bf16[40,40,128]{2,1,0:T(8,128)(2,1)S(1)}, u32[]{:S(2)}, u32[]{:S(2)}) collective-permute-start(bf16[40,40,128]{2,1,0:T(8,128)(2,1)S(1)} %get-tuple-element.40.refs_0_), channel_id=1, source_target_pairs={{0,4},{1,8},{2,6},{3,10},{4,13},{5,1},{6,15},{7,3},{8,12},{9,0},{1... | collective-permute-start | bytes 1228808 | tf_op jit(solution)/shard_map/ppermute | solution.py:417
  12.7 0.4 left.1
  13.0 1.9 %collective-permute-start.5 = (bf16[8,40,128]{2,1,0:T(8,128)(2,1)S(1)}, bf16[8,40,128]{2,1,0:T(8,128)(2,1)S(1)}, u32[]{:S(2)}, u32[]{:S(2)}) collective-permute-start(bf16[8,40,128]{2,1,0:T(8,128)(2,1)S(1)} %get-tuple-element.42.refs_5_), channel_id=1, source_target_pairs={{0,1},{1,0},{2,3},{3,2},{4,5},{5,4},{6,7},{7,6},{8,9},{9,8},{10,11... | collective-permute-start | bytes 245768 | tf_op jit(solution)/shard_map/ppermute | solution.py:417
  14.9 9.9 %collective-permute-done.5.refs_8_.refs_6_ = bf16[8,40,128]{2,1,0:T(8,128)(2,1)S(1)} collective-permute-done((bf16[8,40,128]{2,1,0:T(8,128)(2,1)S(1)}, bf16[8,40,128]{2,1,0:T(8,128)(2,1)S(1)}, u32[]{:S(2)}, u32[]{:S(2)}) %collective-permute-start.5) | collective-permute-done | bytes 81952 | tf_op jit(solution)/shard_map/ppermute | solution.py:417
  24.8 0.0 collective-permute-done.3.refs_1_
  24.8 0.0 collective-permute-done.4.refs_3_
  24.8 0.0 collective-permute-start.6
  24.8 0.5 collective-permute-start.7
  25.4 0.6 %collective-permute-start.8 = (bf16[16,40,128]{2,1,0:T(8,128)(2,1)S(1)}, bf16[16,40,128]{2,1,0:T(8,128)(2,1)S(1)}, u32[]{:S(2)}, u32[]{:S(2)}) collective-permute-start(bf16[16,40,128]{2,1,0:T(8,128)(2,1)S(1)} %get-tuple-element.45.refs_6_.refs_5_), channel_id=1, source_target_pairs={{0,1},{1,0},{2,3},{3,2},{4,5},{5,4},{6,7},{7,6},{8,9},{9,8},{10,11... | collective-permute-start | bytes 491528 | tf_op jit(solution)/shard_map/ppermute | solution.py:417
  26.0 1.4 %collective-permute-start.9 = (bf16[16,40,128]{2,1,0:T(8,128)(2,1)S(1)}, bf16[16,40,128]{2,1,0:T(8,128)(2,1)S(1)}, u32[]{:S(2)}, u32[]{:S(2)}) collective-permute-start(bf16[16,40,128]{2,1,0:T(8,128)(2,1)S(1)} %get-tuple-element.46.refs_7_.refs_5_), channel_id=1, source_target_pairs={{0,1},{1,0},{2,3},{3,2},{4,5},{5,4},{6,7},{7,6},{8,9},{9,8},{10,11... | collective-permute-start | bytes 491528 | tf_op jit(solution)/shard_map/ppermute | solution.py:417
  27.4 0.0 collective-permute-done.6.refs_2_
  27.4 0.0 collective-permute-done.7.refs_4_
  27.4 1.0 %send_sums.8 = bf16[8,40,128]{2,1,0:T(8,128)(2,1)S(1)} custom-call(bf16[40,40,128]{2,1,0:T(8,128)(2,1)S(1)} %get-tuple-element.40.refs_0_, bf16[40,40,128]{2,1,0:T(8,128)(2,1)S(1)} %collective-permute-done.3.refs_1_, bf16[40,40,128]{2,1,0:T(8,128)(2,1)S(1)} %collective-permute-done.6.refs_2_, bf16[40,40,128]{2,1,0:T(8,128)(2,1)S(1)} %collective-permute-done.4.refs_3_, ...), custom_call_target="tpu_custom_call" | custom-call | bytes 5018400 | tf_op jit(solution)/shard_map/send_sums/pallas_call | solution.py:432
  28.4 2.7 %collective-permute-start.13 = (bf16[8,40,128]{2,1,0:T(8,128)(2,1)S(1)}, bf16[8,40,128]{2,1,0:T(8,128)(2,1)S(1)}, u32[]{:S(2)}, u32[]{:S(2)}) collective-permute-start(bf16[8,40,128]{2,1,0:T(8,128)(2,1)S(1)} %send_sums.8), channel_id=1, source_target_pairs={{0,2},{1,3},{2,0},{3,1},{4,6},{5,7},{6,4},{7,5},{8,10},{9,11},{10,... | collective-permute-start | bytes 245768 | tf_op jit(solution)/shard_map/ppermute | solution.py:417
  31.1 3.1 %collective-permute-done.8.refs_9_.refs_6_ = bf16[16,40,128]{2,1,0:T(8,128)(2,1)S(1)} collective-permute-done((bf16[16,40,128]{2,1,0:T(8,128)(2,1)S(1)}, bf16[16,40,128]{2,1,0:T(8,128)(2,1)S(1)}, u32[]{:S(2)}, u32[]{:S(2)}) %collective-permute-start.8) | collective-permute-done | bytes 163872 | tf_op jit(solution)/shard_map/ppermute | solution.py:417
  34.2 1.0 %send_sums.9 = bf16[8,40,128]{2,1,0:T(8,128)(2,1)S(1)} custom-call(bf16[40,40,128]{2,1,0:T(8,128)(2,1)S(1)} %get-tuple-element.40.refs_0_, bf16[40,40,128]{2,1,0:T(8,128)(2,1)S(1)} %collective-permute-done.3.refs_1_, bf16[40,40,128]{2,1,0:T(8,128)(2,1)S(1)} %collective-permute-done.6.refs_2_, bf16[40,40,128]{2,1,0:T(8,128)(2,1)S(1)} %collective-permute-done.4.refs_3_, ...), custom_call_target="tpu_custom_call" | custom-call | bytes 5018400 | tf_op jit(solution)/shard_map/send_sums/pallas_call | solution.py:432
  35.2 0.9 %collective-permute-start.14 = (bf16[8,40,128]{2,1,0:T(8,128)(2,1)S(1)}, bf16[8,40,128]{2,1,0:T(8,128)(2,1)S(1)}, u32[]{:S(2)}, u32[]{:S(2)}) collective-permute-start(bf16[8,40,128]{2,1,0:T(8,128)(2,1)S(1)} %send_sums.9), channel_id=1, source_target_pairs={{0,2},{1,3},{2,0},{3,1},{4,6},{5,7},{6,4},{7,5},{8,10},{9,11},{10,... | collective-permute-start | bytes 245768 | tf_op jit(solution)/shard_map/ppermute | solution.py:417
  36.1 1.0 %send_sums.5 = bf16[8,40,128]{2,1,0:T(8,128)(2,1)S(1)} custom-call(bf16[40,40,128]{2,1,0:T(8,128)(2,1)S(1)} %get-tuple-element.40.refs_0_, bf16[40,40,128]{2,1,0:T(8,128)(2,1)S(1)} %collective-permute-done.3.refs_1_, bf16[40,40,128]{2,1,0:T(8,128)(2,1)S(1)} %collective-permute-done.6.refs_2_, bf16[40,40,128]{2,1,0:T(8,128)(2,1)S(1)} %collective-permute-done.4.refs_3_, ...), custom_call_target="tpu_custom_call" | custom-call | bytes 5018400 | tf_op jit(solution)/shard_map/send_sums/pallas_call | solution.py:432
  37.2 2.2 %collective-permute-start.10 = (bf16[8,40,128]{2,1,0:T(8,128)(2,1)S(1)}, bf16[8,40,128]{2,1,0:T(8,128)(2,1)S(1)}, u32[]{:S(2)}, u32[]{:S(2)}) collective-permute-start(bf16[8,40,128]{2,1,0:T(8,128)(2,1)S(1)} %send_sums.5), channel_id=1, source_target_pairs={{0,2},{1,3},{2,0},{3,1},{4,6},{5,7},{6,4},{7,5},{8,10},{9,11},{10,... | collective-permute-start | bytes 245768 | tf_op jit(solution)/shard_map/ppermute | solution.py:417
  39.3 0.0 collective-permute-done.9.refs_10_.refs_6_
  39.3 1.0 %send_sums.6 = bf16[8,40,128]{2,1,0:T(8,128)(2,1)S(1)} custom-call(bf16[40,40,128]{2,1,0:T(8,128)(2,1)S(1)} %get-tuple-element.40.refs_0_, bf16[40,40,128]{2,1,0:T(8,128)(2,1)S(1)} %collective-permute-done.3.refs_1_, bf16[40,40,128]{2,1,0:T(8,128)(2,1)S(1)} %collective-permute-done.6.refs_2_, bf16[40,40,128]{2,1,0:T(8,128)(2,1)S(1)} %collective-permute-done.4.refs_3_, ...), custom_call_target="tpu_custom_call" | custom-call | bytes 5018400 | tf_op jit(solution)/shard_map/send_sums/pallas_call | solution.py:432
  40.4 0.0 copy-start.2
  40.4 0.9 %collective-permute-start.11 = (bf16[8,40,128]{2,1,0:T(8,128)(2,1)S(1)}, bf16[8,40,128]{2,1,0:T(8,128)(2,1)S(1)}, u32[]{:S(2)}, u32[]{:S(2)}) collective-permute-start(bf16[8,40,128]{2,1,0:T(8,128)(2,1)S(1)} %send_sums.6), channel_id=1, source_target_pairs={{0,2},{1,3},{2,0},{3,1},{4,6},{5,7},{6,4},{7,5},{8,10},{9,11},{10,... | collective-permute-start | bytes 245768 | tf_op jit(solution)/shard_map/ppermute | solution.py:417
  41.3 1.0 %send_sums.7 = bf16[8,40,128]{2,1,0:T(8,128)(2,1)S(1)} custom-call(bf16[40,40,128]{2,1,0:T(8,128)(2,1)S(1)} %get-tuple-element.40.refs_0_, bf16[40,40,128]{2,1,0:T(8,128)(2,1)S(1)} %collective-permute-done.3.refs_1_, bf16[40,40,128]{2,1,0:T(8,128)(2,1)S(1)} %collective-permute-done.6.refs_2_, bf16[40,40,128]{2,1,0:T(8,128)(2,1)S(1)} %collective-permute-done.4.refs_3_, ...), custom_call_target="tpu_custom_call" | custom-call | bytes 5018400 | tf_op jit(solution)/shard_map/send_sums/pallas_call | solution.py:432
  42.3 0.0 copy-start.1
  42.3 2.2 %collective-permute-start.12 = (bf16[8,40,128]{2,1,0:T(8,128)(2,1)S(1)}, bf16[8,40,128]{2,1,0:T(8,128)(2,1)S(1)}, u32[]{:S(2)}, u32[]{:S(2)}) collective-permute-start(bf16[8,40,128]{2,1,0:T(8,128)(2,1)S(1)} %send_sums.7), channel_id=1, source_target_pairs={{0,2},{1,3},{2,0},{3,1},{4,6},{5,7},{6,4},{7,5},{8,10},{9,11},{10,... | collective-permute-start | bytes 245768 | tf_op jit(solution)/shard_map/ppermute | solution.py:417
  44.5 0.0 copy-done.2
  44.5 5.4 %keep_sums.1 = (f32[40,40,128]{2,1,0:T(8,128)S(1)}, f32[40,40,128]{2,1,0:T(8,128)S(1)}) custom-call(bf16[40,40,128]{2,1,0:T(8,128)(2,1)S(1)} %get-tuple-element.40.refs_0_, bf16[40,40,128]{2,1,0:T(8,128)(2,1)S(1)} %collective-permute-done.3.refs_1_, bf16[40,40,128]{2,1,0:T(8,128)(2,1)S(1)} %collective-permute-done.6.refs_2_, ...), custom_call_target="tpu_custom_call" | custom-call | bytes 22140000 | tf_op jit(solution)/shard_map/keep_sums/pallas_call | solution.py:444
  49.9 0.0 collective-permute-done.13.refs_0_
  49.9 0.0 collective-permute-done.14.refs_1_
  49.9 0.0 copy-done.1
  49.9 1.1 %join.2.refs_3_ = bf16[40,40,128]{2,1,0:T(8,128)(2,1)} custom-call(f32[40,40,128]{2,1,0:T(8,128)S(1)} %get-tuple-element.48.own_ref, bf16[40,40,128]{2,1,0:T(8,128)(2,1)S(1)} %get-tuple-element.49.psum_ref, f32[40,40,128]{2,1,0:T(8,128)S(1)} %get-tuple-element.50.gate_ref, bf16[128,128]{1,0:T(8,128)(2,1)S(1)} %copy-done.1, ...), custom_call_target="tpu_custom_call" | custom-call | bytes 3542400 | tf_op jit(solution)/shard_map/join/pallas_call | solution.py:458
  51.0 0.0 collective-permute-done.10.refs_0_
  51.0 0.1 collective-permute-done.11.refs_1_
  51.1 0.9 %collective-permute-done.12.refs_2_ = bf16[8,40,128]{2,1,0:T(8,128)(2,1)S(1)} collective-permute-done((bf16[8,40,128]{2,1,0:T(8,128)(2,1)S(1)}, bf16[8,40,128]{2,1,0:T(8,128)(2,1)S(1)}, u32[]{:S(2)}, u32[]{:S(2)}) %collective-permute-start.12) | collective-permute-done | bytes 81952 | tf_op jit(solution)/shard_map/ppermute | solution.py:417
  52.0 1.2 %join.3 = bf16[40,40,128]{2,1,0:T(8,128)(2,1)} custom-call(f32[40,40,128]{2,1,0:T(8,128)S(1)} %get-tuple-element.48.own_ref, bf16[40,40,128]{2,1,0:T(8,128)(2,1)S(1)} %get-tuple-element.49.psum_ref, f32[40,40,128]{2,1,0:T(8,128)S(1)} %get-tuple-element.50.gate_ref, bf16[128,128]{1,0:T(8,128)(2,1)S(1)} %copy-done.1, ...), custom_call_target="tpu_custom_call", output_to_operand_aliasing={{}: (7, {})} | custom-call | bytes 5313600 | tf_op jit(solution)/shard_map/join/pallas_call | solution.py:458
Async XLA Ops:
  1.5 4.7 %collective-permute-start = (bf16[48,128]{1,0:T(8,128)(2,1)S(1)}, bf16[48,128]{1,0:T(8,128)(2,1)S(1)}, u32[]{:S(2)}, u32[]{:S(2)}) collective-permute-start(bf16[48,128]{1,0:T(8,128)(2,1)S(1)} %get-tuple-element.29), channel_id=1, source_target_pairs={{0,4},{4,0},{8,12},{12,8},{1,5},{5,1},{9,13},{13,9},{2,6},{6,2},{1... | collective-permute-start | bytes 36872 | tf_op jit(solution)/shard_map/ppermute | solution.py:502
  2.0 4.2 %collective-permute-start.1 = (bf16[48,128]{1,0:T(8,128)(2,1)S(1)}, bf16[48,128]{1,0:T(8,128)(2,1)S(1)}, u32[]{:S(2)}, u32[]{:S(2)}) collective-permute-start(bf16[48,128]{1,0:T(8,128)(2,1)S(1)} %get-tuple-element.30), channel_id=1, source_target_pairs={{0,8},{4,12},{8,0},{12,4},{1,9},{5,13},{9,1},{13,5},{2,10},{6,14},... | collective-permute-start | bytes 36872 | tf_op jit(solution)/shard_map/ppermute | solution.py:502
  4.6 3.1 %collective-permute-start.2 = (bf16[48,128]{1,0:T(8,128)(2,1)S(1)}, bf16[48,128]{1,0:T(8,128)(2,1)S(1)}, u32[]{:S(2)}, u32[]{:S(2)}) collective-permute-start(bf16[48,128]{1,0:T(8,128)(2,1)S(1)} %get-tuple-element.31), channel_id=1, source_target_pairs={{0,12},{4,8},{8,4},{12,0},{1,13},{5,9},{9,5},{13,1},{2,14},{6,10},... | collective-permute-start | bytes 36872 | tf_op jit(solution)/shard_map/ppermute | solution.py:502
  4.6 3.1 %copy-start = (bf16[128,512]{1,0:T(8,128)(2,1)S(1)}, bf16[128,512]{1,0:T(8,128)(2,1)}, u32[]{:S(2)}) copy-start(bf16[128,512]{1,0:T(8,128)(2,1)} %win_ref.1) | copy-start | bytes 393220
  10.9 13.9 %collective-permute-start.3 = (bf16[40,40,128]{2,1,0:T(8,128)(2,1)S(1)}, bf16[40,40,128]{2,1,0:T(8,128)(2,1)S(1)}, u32[]{:S(2)}, u32[]{:S(2)}) collective-permute-start(bf16[40,40,128]{2,1,0:T(8,128)(2,1)S(1)} %get-tuple-element.40.refs_0_), channel_id=1, source_target_pairs={{0,8},{1,4},{2,10},{3,6},{4,1},{5,13},{6,3},{7,15},{8,0},{9,12},{1... | collective-permute-start | bytes 1228808 | tf_op jit(solution)/shard_map/ppermute | solution.py:417
  11.5 13.3 %collective-permute-start.4 = (bf16[40,40,128]{2,1,0:T(8,128)(2,1)S(1)}, bf16[40,40,128]{2,1,0:T(8,128)(2,1)S(1)}, u32[]{:S(2)}, u32[]{:S(2)}) collective-permute-start(bf16[40,40,128]{2,1,0:T(8,128)(2,1)S(1)} %get-tuple-element.40.refs_0_), channel_id=1, source_target_pairs={{0,4},{1,8},{2,6},{3,10},{4,13},{5,1},{6,15},{7,3},{8,12},{9,0},{1... | collective-permute-start | bytes 1228808 | tf_op jit(solution)/shard_map/ppermute | solution.py:417
  13.0 11.8 %collective-permute-start.5 = (bf16[8,40,128]{2,1,0:T(8,128)(2,1)S(1)}, bf16[8,40,128]{2,1,0:T(8,128)(2,1)S(1)}, u32[]{:S(2)}, u32[]{:S(2)}) collective-permute-start(bf16[8,40,128]{2,1,0:T(8,128)(2,1)S(1)} %get-tuple-element.42.refs_5_), channel_id=1, source_target_pairs={{0,1},{1,0},{2,3},{3,2},{4,5},{5,4},{6,7},{7,6},{8,9},{9,8},{10,11... | collective-permute-start | bytes 245768 | tf_op jit(solution)/shard_map/ppermute | solution.py:417
  24.8 2.5 %collective-permute-start.6 = (bf16[40,40,128]{2,1,0:T(8,128)(2,1)S(1)}, bf16[40,40,128]{2,1,0:T(8,128)(2,1)S(1)}, u32[]{:S(2)}, u32[]{:S(2)}) collective-permute-start(bf16[40,40,128]{2,1,0:T(8,128)(2,1)S(1)} %collective-permute-done.3.refs_1_), channel_id=1, source_target_pairs={{0,4},{1,5},{2,6},{3,7},{4,0},{5,1},{6,2},{7,3},{8,12},{9,13},{10,... | collective-permute-start | bytes 1228808 | tf_op jit(solution)/shard_map/ppermute | solution.py:417
  24.8 2.5 %collective-permute-start.7 = (bf16[40,40,128]{2,1,0:T(8,128)(2,1)S(1)}, bf16[40,40,128]{2,1,0:T(8,128)(2,1)S(1)}, u32[]{:S(2)}, u32[]{:S(2)}) collective-permute-start(bf16[40,40,128]{2,1,0:T(8,128)(2,1)S(1)} %collective-permute-done.4.refs_3_), channel_id=1, source_target_pairs={{0,4},{1,5},{2,6},{3,7},{4,0},{5,1},{6,2},{7,3},{8,12},{9,13},{10,... | collective-permute-start | bytes 1228808 | tf_op jit(solution)/shard_map/ppermute | solution.py:417
  25.4 8.8 %collective-permute-start.8 = (bf16[16,40,128]{2,1,0:T(8,128)(2,1)S(1)}, bf16[16,40,128]{2,1,0:T(8,128)(2,1)S(1)}, u32[]{:S(2)}, u32[]{:S(2)}) collective-permute-start(bf16[16,40,128]{2,1,0:T(8,128)(2,1)S(1)} %get-tuple-element.45.refs_6_.refs_5_), channel_id=1, source_target_pairs={{0,1},{1,0},{2,3},{3,2},{4,5},{5,4},{6,7},{7,6},{8,9},{9,8},{10,11... | collective-permute-start | bytes 491528 | tf_op jit(solution)/shard_map/ppermute | solution.py:417
  26.0 13.4 %collective-permute-start.9 = (bf16[16,40,128]{2,1,0:T(8,128)(2,1)S(1)}, bf16[16,40,128]{2,1,0:T(8,128)(2,1)S(1)}, u32[]{:S(2)}, u32[]{:S(2)}) collective-permute-start(bf16[16,40,128]{2,1,0:T(8,128)(2,1)S(1)} %get-tuple-element.46.refs_7_.refs_5_), channel_id=1, source_target_pairs={{0,1},{1,0},{2,3},{3,2},{4,5},{5,4},{6,7},{7,6},{8,9},{9,8},{10,11... | collective-permute-start | bytes 491528 | tf_op jit(solution)/shard_map/ppermute | solution.py:417
  28.4 21.4 %collective-permute-start.13 = (bf16[8,40,128]{2,1,0:T(8,128)(2,1)S(1)}, bf16[8,40,128]{2,1,0:T(8,128)(2,1)S(1)}, u32[]{:S(2)}, u32[]{:S(2)}) collective-permute-start(bf16[8,40,128]{2,1,0:T(8,128)(2,1)S(1)} %send_sums.8), channel_id=1, source_target_pairs={{0,2},{1,3},{2,0},{3,1},{4,6},{5,7},{6,4},{7,5},{8,10},{9,11},{10,... | collective-permute-start | bytes 245768 | tf_op jit(solution)/shard_map/ppermute | solution.py:417
  35.2 14.7 %collective-permute-start.14 = (bf16[8,40,128]{2,1,0:T(8,128)(2,1)S(1)}, bf16[8,40,128]{2,1,0:T(8,128)(2,1)S(1)}, u32[]{:S(2)}, u32[]{:S(2)}) collective-permute-start(bf16[8,40,128]{2,1,0:T(8,128)(2,1)S(1)} %send_sums.9), channel_id=1, source_target_pairs={{0,2},{1,3},{2,0},{3,1},{4,6},{5,7},{6,4},{7,5},{8,10},{9,11},{10,... | collective-permute-start | bytes 245768 | tf_op jit(solution)/shard_map/ppermute | solution.py:417
  37.2 13.8 %collective-permute-start.10 = (bf16[8,40,128]{2,1,0:T(8,128)(2,1)S(1)}, bf16[8,40,128]{2,1,0:T(8,128)(2,1)S(1)}, u32[]{:S(2)}, u32[]{:S(2)}) collective-permute-start(bf16[8,40,128]{2,1,0:T(8,128)(2,1)S(1)} %send_sums.5), channel_id=1, source_target_pairs={{0,2},{1,3},{2,0},{3,1},{4,6},{5,7},{6,4},{7,5},{8,10},{9,11},{10,... | collective-permute-start | bytes 245768 | tf_op jit(solution)/shard_map/ppermute | solution.py:417
  40.4 4.1 %copy-start.2 = (bf16[128,128]{1,0:T(8,128)(2,1)S(1)}, bf16[128,128]{1,0:T(8,128)(2,1)}, u32[]{:S(2)}) copy-start(bf16[128,128]{1,0:T(8,128)(2,1)} %refs_12_.1) | copy-start | bytes 98308
  40.4 10.7 %collective-permute-start.11 = (bf16[8,40,128]{2,1,0:T(8,128)(2,1)S(1)}, bf16[8,40,128]{2,1,0:T(8,128)(2,1)S(1)}, u32[]{:S(2)}, u32[]{:S(2)}) collective-permute-start(bf16[8,40,128]{2,1,0:T(8,128)(2,1)S(1)} %send_sums.6), channel_id=1, source_target_pairs={{0,2},{1,3},{2,0},{3,1},{4,6},{5,7},{6,4},{7,5},{8,10},{9,11},{10,... | collective-permute-start | bytes 245768 | tf_op jit(solution)/shard_map/ppermute | solution.py:417
  42.3 7.6 %copy-start.1 = (bf16[128,128]{1,0:T(8,128)(2,1)S(1)}, bf16[128,128]{1,0:T(8,128)(2,1)}, u32[]{:S(2)}) copy-start(bf16[128,128]{1,0:T(8,128)(2,1)} %w_ref.3) | copy-start | bytes 98308
  42.3 9.6 %collective-permute-start.12 = (bf16[8,40,128]{2,1,0:T(8,128)(2,1)S(1)}, bf16[8,40,128]{2,1,0:T(8,128)(2,1)S(1)}, u32[]{:S(2)}, u32[]{:S(2)}) collective-permute-start(bf16[8,40,128]{2,1,0:T(8,128)(2,1)S(1)} %send_sums.7), channel_id=1, source_target_pairs={{0,2},{1,3},{2,0},{3,1},{4,6},{5,7},{6,4},{7,5},{8,10},{9,11},{10,... | collective-permute-start | bytes 245768 | tf_op jit(solution)/shard_map/ppermute | solution.py:417

commit v8 on v6

--- a/solution.py
+++ b/solution.py
@@ -268,26 +268,21 @@
     with_right(False, rights, use)
 
 
-def keep_body(cuts, *refs):
-    rights, refs = refs[:5], refs[5:]
-    lefts, mets = refs[:cuts], refs[cuts : 2 * cuts]
-    norm_ref, wgate_ref, o_ref, gate_ref, lf_ref = refs[2 * cuts :]
-    own_i, depth, chans = o_ref.shape
-    at = 0
-    for l_ref, m_ref in zip(lefts, mets):
-        n = l_ref.shape[0]
-        lf_ref[pl.ds(at, n), pl.ds(0, depth), :] = l_ref[...].astype(f32)
-        lf_ref[pl.ds(at, n), pl.ds(depth, depth), :] = m_ref[...].astype(f32)
-        at += n
+def keep_body(first, *refs):
+    rights, (l_ref, m_ref, norm_ref, wgate_ref, o_ref, gate_ref, lf_ref) = refs[:5], refs[5:]
+    count, depth, chans = o_ref.shape
     group = 8
+    lf_ref[:, pl.ds(0, depth), :] = l_ref[...].astype(f32)
+    lf_ref[:, pl.ds(depth, depth), :] = m_ref[...].astype(f32)
 
     def gates(b, carry):
-        flat = norm_ref[pl.ds(pl.multiple_of(b * group * depth, 16), group * depth), :]
+        at = pl.multiple_of((first + b * group) * depth, 16)
+        flat = norm_ref[pl.ds(at, group * depth), :]
         gate = sigmoid(jnp.dot(flat, wgate_ref[...], preferred_element_type=f32))
         gate_ref[pl.ds(b * group, group)] = gate.reshape(group, depth, -1)
         return carry
 
-    lax.fori_loop(0, own_i // group, gates, 0, unroll=True)
+    lax.fori_loop(0, count // group, gates, 0, unroll=True)
 
     def use(halves):
         def rows(b, carry):
@@ -296,7 +291,7 @@
                 o_ref[b * group + t] = acc[t]
             return carry
 
-        lax.fori_loop(0, own_i // group, rows, 0)
+        lax.fori_loop(0, count // group, rows, 0)
 
     with_right(True, rights, use)
 
@@ -312,10 +307,10 @@
         def rows(b, carry):
             here = pl.ds(start + b * group, group)
             there = pl.ds(first + start + b * group, group)
-            mixed = own_ref[there] + sum_ref[pl.ds(b * group, group)].astype(f32)
+            mixed = own_ref[here] + sum_ref[pl.ds(b * group, group)].astype(f32)
             normed = standardize(mixed).reshape(group * extent, -1).astype(bf16)
             update = jnp.dot(normed, w_ref[...], preferred_element_type=f32).reshape(group, extent, -1)
-            done_ref[here] = (psum_ref[there].astype(f32) + gate_ref[there] * update).astype(bf16)
+            done_ref[here] = (psum_ref[there].astype(f32) + gate_ref[here] * update).astype(bf16)
             return carry
 
         lax.fori_loop(0, sum_ref.shape[0] // group, rows, 0, unroll=True)
@@ -420,42 +415,59 @@
     keeper = lambda r, z: r % 2 == z % 2
     got = move(right, every, lambda r, z: (r ^ 2, z) if keeper(r, z) else (r ^ 1, z ^ 1))
     far = move(right, every, lambda r, z: (r ^ 1, z) if keeper(r, z) else (r ^ 2, z ^ 1))
-    mets = [move(left, every, lambda r, z: (r, z ^ 1)) for left in lefts]
+    mets = [move(left, every, lambda r, z: (r, z ^ 1)) for left in lefts[:2]]
     got, far, mets[0] = lax.optimization_barrier((got, far, mets[0]))
     p_got = move(got, every, lambda r, z: (r ^ 1, z))
     p_far = move(far, every, lambda r, z: (r ^ 1, z))
     rights = (right, got, p_got, far, p_far)
 
-    sums = []
-    chunks = ((0, 0, 0, 16), (1, 0, 16, 16), (1, 16, 32, own_i - 32))
-    for at, first, _, n in chunks:
+    def send(left, met, first):
         part = pl.pallas_call(
             functools.partial(send_body, first),
-            out_shape=jax.ShapeDtypeStruct((n, own_j, tri), bf16),
+            out_shape=jax.ShapeDtypeStruct((8, own_j, tri), bf16),
             in_specs=[VMEM] * 7,
             out_specs=VMEM,
+            scratch_shapes=[pltpu.VMEM((8, 2 * own_j, tri), f32)],
+            compiler_params=limit(8),
+            cost_estimate=cost(1),
+            name="send_sums",
+        )(*rights, left, met)
+        return part, move(part, every, lambda r, z: (r, z ^ 2))
+
+    def keep(left, met, first):
+        n = left.shape[0]
+        return pl.pallas_call(
+            functools.partial(keep_body, first),
+            out_shape=[jax.ShapeDtypeStruct((n, own_j, tri), f32),
+                       jax.ShapeDtypeStruct((n, own_j, chans), f32)],
+            in_specs=[VMEM] * 9,
+            out_specs=[VMEM] * 2,
             scratch_shapes=[pltpu.VMEM((n, 2 * own_j, tri), f32)],
-            compiler_params=limit(8),
-            cost_estimate=cost(0.12 * n + 0.4),
-            name="send_sums",
-        )(*rights, lefts[at], mets[at])
-        sums.append(move(part, every, lambda r, z: (r, z ^ 2)))
-
-    own, gate = pl.pallas_call(
-        functools.partial(keep_body, cuts),
-        out_shape=[jax.ShapeDtypeStruct((own_i, own_j, tri), f32),
-                   jax.ShapeDtypeStruct((own_i, own_j, chans), f32)],
-        in_specs=[VMEM] * (5 + 2 * cuts + 2),
-        out_specs=[VMEM] * 2,
-        scratch_shapes=[pltpu.VMEM((own_i, 2 * own_j, tri), f32)],
-        compiler_params=limit(12),
-        cost_estimate=cost(6),
-        name="keep_sums",
-    )(*rights, *lefts, *mets, norm, w_gate)
+            compiler_params=limit(12),
+            cost_estimate=cost(0.13 * n),
+            name="keep_sums",
+        )(*rights, left, met, norm, w_gate)
+
+    sums, kept = [], []
+    at = 0
+    for n, left in enumerate(lefts):
+        met = mets[n]
+        if kept:
+            met, _ = lax.optimization_barrier((met, kept[-1][0]))
+        parts = [send(left, met, m) for m in range(0, left.shape[0], 8)]
+        sums.append([there for _, there in parts])
+        if len(mets) < cuts:
+            later, _ = lax.optimization_barrier((lefts[n + 2], parts[0][0]))
+            mets.append(move(later, every, lambda r, z: (r, z ^ 1)))
+        kept.append(keep(left, met, at))
+        at += left.shape[0]
+
     out = []
-    for first, n, parts in ((0, 16, sums[:1]), (16, own_i - 16, sums[1:])):
+    at = 0
+    for (own, gate), parts in zip(kept, sums):
+        n = own.shape[0]
         out = [pl.pallas_call(
-            functools.partial(join_body, first, len(parts)),
+            functools.partial(join_body, at, len(parts)),
             out_shape=jax.ShapeDtypeStruct((own_i, own_j, chans), bf16),
             in_specs=[VMEM] * (4 + len(parts)) + [HBM] * len(out),
             out_specs=HBM,
@@ -465,6 +477,7 @@
             cost_estimate=cost(0.06 * n),
             name="join",
         )(own, psum, gate, w_final, *parts, *out)]
+        at += n
     return out[0]
 
 
@@ -498,8 +511,8 @@
         name="align",
     )(hold(homolog), hold(factors.T), *map(hold, later))
     msgs = [msgs[0]] + [
-        lax.ppermute(msg, "row", [(r, r ^ d) for r in range(rows)])
-        for d, msg in enumerate(msgs) if d
+        lax.ppermute(msgs[d], "row", [(r, r ^ d) for r in range(rows)])
+        for d in reversed(range(1, rows))
     ]
 
     base, mask, wq, pick = pl.pallas_call(
@@ -539,7 +552,7 @@
         name="pair",
     )(*msgs, base, mask, wq, pick, w_in)
 
-    cuts = [16, own_i - 16] if paired else [own_i]
+    cuts = [8, 16, own_i - 24] if paired else [own_i]
     lefts = pl.pallas_call(
         left_body,
         out_shape=[jax.ShapeDtypeStruct((n, own_j, tri), bf16) for n in cuts],

time: 53.6 us -> 53.7 us (level)
  waiting for transfers between devices: 20.4 us -> 15.1 us
  starting transfers between devices: 13.6 us -> 17.8 us
  Pallas kernels: 19.3 us -> 20.5 us
    ppermute x9 -> x12, waiting for transfers between devices: 18.9 us -> 13.6 us  [move(): return lax.ppermute(value, ('row', 'col'), pairs)]
    ppermute x9 -> x12, starting transfers between devices: 10.5 us -> 14.6 us  [move(): return lax.ppermute(value, ('row', 'col'), pairs)]
    pallas_call x6 -> x11, Pallas kernels: 12.7 us -> 14 us  [the longest x3 5.66 us: keep(): pl.pallas_call(functools.partial(keep_body, first), out_shape=[jax.ShapeD...]
  transfers between devices with their start and end apart: 12 -> 15, of which waited for: 7 -> 6; matrix products, arithmetic and copies ran while one was open for 0% -> 0% of each run, Pallas kernels for 25% -> 28%
where the time goes in v8:
time: 53.7 us; the launch traced here: 53.6 us
  Pallas kernels  20.5 us (38%)
  starting transfers between devices  17.8 us (33%)
  waiting for transfers between devices  15.1 us (28%)
    ppermute x12, starting transfers between devices, move(): return lax.ppermute(value, ('row', 'col'), pairs)  14.6 us
    ppermute x12, waiting for transfers between devices, move(): return lax.ppermute(value, ('row', 'col'), pairs)  13.6 us
    pallas_call x3, Pallas kernels, keep(): pl.pallas_call(functools.partial(keep_body, first), out_shape=[jax.ShapeD...  5.66 us
    pallas_call x5, Pallas kernels, send(): pl.pallas_call(functools.partial(send_body, first), out_shape=jax.ShapeDt...  5.21 us
    pallas_call x1, Pallas kernels, shards(): pl.pallas_call(functools.partial(pair_body, own_seqs, width, rows, paired...  3.21 us
    ppermute x3, starting transfers between devices, shards(): lax.ppermute(msgs[d], 'row', [(r, r ^ d) for r in range(rows)])  3.12 us
    pallas_call x3, Pallas kernels, paired_plan(): pl.pallas_call(functools.partial(join_body, at, len(parts)), out_shape=ja...  3.09 us
    pallas_call x1, Pallas kernels, shards(): pl.pallas_call(functools.partial(prepare_body, own_seqs), out_shape=[jax....  1.51 us
  transfers between devices with their start and end apart: 15, of which 6 were waited for; matrix products, arithmetic and copies ran while one was open for 0% of the time, Pallas kernels for 28%

profile of v8, /device:TPU:0, one launch (start us, length us, event | category | flops | bytes accessed | tf_op | source)
XLA Modules:
  0.0 53.6 jit_solution(4079271371066040398)
XLA Ops:
  0.0 1.5 %align.1 = (bf16[48,128]{1,0:T(8,128)(2,1)S(1)}, bf16[48,128]{1,0:T(8,128)(2,1)S(1)}, bf16[48,128]{1,0:T(8,128)(2,1)S(1)}, bf16[48,128]{1,0:T(8,128)(2,1)S(1)}, ...) custom-call(bf16[2,160,256]{2,1,0:T(8,128)(2,1)} %x_hbm.1, ...), custom_call_target="tpu_custom_call" | custom-call | bytes 5535000 | tf_op jit(solution)/shard_map/align/pallas_call | solution.py:497
  1.5 2.4 %collective-permute-start = (bf16[48,128]{1,0:T(8,128)(2,1)S(1)}, bf16[48,128]{1,0:T(8,128)(2,1)S(1)}, u32[]{:S(2)}, u32[]{:S(2)}) collective-permute-start(bf16[48,128]{1,0:T(8,128)(2,1)S(1)} %get-tuple-element.36), channel_id=1, source_target_pairs={{0,12},{4,8},{8,4},{12,0},{1,13},{5,9},{9,5},{13,1},{2,14},{6,10},... | collective-permute-start | bytes 36872 | tf_op jit(solution)/shard_map/ppermute | solution.py:514
  3.9 0.6 %collective-permute-start.1 = (bf16[48,128]{1,0:T(8,128)(2,1)S(1)}, bf16[48,128]{1,0:T(8,128)(2,1)S(1)}, u32[]{:S(2)}, u32[]{:S(2)}) collective-permute-start(bf16[48,128]{1,0:T(8,128)(2,1)S(1)} %get-tuple-element.37), channel_id=1, source_target_pairs={{0,8},{4,12},{8,0},{12,4},{1,9},{5,13},{9,1},{13,5},{2,10},{6,14},... | collective-permute-start | bytes 36872 | tf_op jit(solution)/shard_map/ppermute | solution.py:514
  4.6 0.0 collective-permute-start.2
  4.6 0.0 copy-start
  4.6 1.5 %prepare.1 = (f32[40,40,128]{2,1,0:T(8,128)S(1)}, bf16[40,40,128]{2,1,0:T(8,128)(2,1)S(1)}, bf16[16,32,256]{2,1,0:T(8,128)(2,1)S(1)}, bf16[4,128,256]{2,1,0:T(8,128)(2,1)S(1)}) custom-call(bf16[40,40,128]{2,1,0:T(8,128)(2,1)S(1)} %get-tuple-element.39.couple_ref, s32[160]{0:T(256)} %ids_hbm.1, s32[40,40]{1,0:T(8,128)S(1)} %get-tuple-element.40.valid_ref, ...), custom_call_target="tpu_custom_call" | custom-call | bytes 7380000 | tf_op jit(solution)/shard_map/prepare/pallas_call | solution.py:518
  6.1 0.0 collective-permute-done.refs_1_
  6.1 1.5 %collective-permute-done.1.refs_2_ = bf16[48,128]{1,0:T(8,128)(2,1)S(1)} collective-permute-done((bf16[48,128]{1,0:T(8,128)(2,1)S(1)}, bf16[48,128]{1,0:T(8,128)(2,1)S(1)}, u32[]{:S(2)}, u32[]{:S(2)}) %collective-permute-start.1) | collective-permute-done | bytes 12320 | tf_op jit(solution)/shard_map/ppermute | solution.py:514
  7.6 0.0 collective-permute-done.2.refs_3_
  7.6 0.0 copy-done
  7.6 3.2 %pair.1 = (bf16[40,40,128]{2,1,0:T(8,128)(2,1)S(1)}, bf16[1600,128]{1,0:T(8,128)(2,1)S(1)}, bf16[40,40,128]{2,1,0:T(8,128)(2,1)S(1)}) custom-call(bf16[48,128]{1,0:T(8,128)(2,1)S(1)} %get-tuple-element.35.refs_0_, bf16[48,128]{1,0:T(8,128)(2,1)S(1)} %collective-permute-done.refs_1_, bf16[48,128]{1,0:T(8,128)(2,1)S(1)} %collective-permute-done.1.refs_2_, ...), custom_call_target="tpu_custom_call" | custom-call | bytes 16605000 | tf_op jit(solution)/shard_map/pair/pallas_call | solution.py:538
  10.8 0.7 %collective-permute-start.3 = (bf16[40,40,128]{2,1,0:T(8,128)(2,1)S(1)}, bf16[40,40,128]{2,1,0:T(8,128)(2,1)S(1)}, u32[]{:S(2)}, u32[]{:S(2)}) collective-permute-start(bf16[40,40,128]{2,1,0:T(8,128)(2,1)S(1)} %get-tuple-element.47.refs_0_), channel_id=1, source_target_pairs={{0,8},{1,4},{2,10},{3,6},{4,1},{5,13},{6,3},{7,15},{8,0},{9,12},{1... | collective-permute-start | bytes 1228808 | tf_op jit(solution)/shard_map/ppermute | solution.py:412
  11.5 1.0 %collective-permute-start.4 = (bf16[40,40,128]{2,1,0:T(8,128)(2,1)S(1)}, bf16[40,40,128]{2,1,0:T(8,128)(2,1)S(1)}, u32[]{:S(2)}, u32[]{:S(2)}) collective-permute-start(bf16[40,40,128]{2,1,0:T(8,128)(2,1)S(1)} %get-tuple-element.47.refs_0_), channel_id=1, source_target_pairs={{0,4},{1,8},{2,6},{3,10},{4,13},{5,1},{6,15},{7,3},{8,12},{9,0},{1... | collective-permute-start | bytes 1228808 | tf_op jit(solution)/shard_map/ppermute | solution.py:412
  12.6 0.4 left.1
  13.0 1.9 %collective-permute-start.5 = (bf16[8,40,128]{2,1,0:T(8,128)(2,1)S(1)}, bf16[8,40,128]{2,1,0:T(8,128)(2,1)S(1)}, u32[]{:S(2)}, u32[]{:S(2)}) collective-permute-start(bf16[8,40,128]{2,1,0:T(8,128)(2,1)S(1)} %get-tuple-element.49.refs_5_), channel_id=1, source_target_pairs={{0,1},{1,0},{2,3},{3,2},{4,5},{5,4},{6,7},{7,6},{8,9},{9,8},{10,11... | collective-permute-start | bytes 245768 | tf_op jit(solution)/shard_map/ppermute | solution.py:412
  14.8 9.7 %collective-permute-done.5.refs_6_ = bf16[8,40,128]{2,1,0:T(8,128)(2,1)S(1)} collective-permute-done((bf16[8,40,128]{2,1,0:T(8,128)(2,1)S(1)}, bf16[8,40,128]{2,1,0:T(8,128)(2,1)S(1)}, u32[]{:S(2)}, u32[]{:S(2)}) %collective-permute-start.5) | collective-permute-done | bytes 81952 | tf_op jit(solution)/shard_map/ppermute | solution.py:412
  24.6 0.0 collective-permute-done.3.refs_1_
  24.6 0.0 collective-permute-done.4.refs_3_
  24.6 0.0 collective-permute-start.6
  24.6 0.5 collective-permute-start.7
  25.1 0.0 copy-start.2
  25.1 0.8 %collective-permute-start.9 = (bf16[16,40,128]{2,1,0:T(8,128)(2,1)S(1)}, bf16[16,40,128]{2,1,0:T(8,128)(2,1)S(1)}, u32[]{:S(2)}, u32[]{:S(2)}) collective-permute-start(bf16[16,40,128]{2,1,0:T(8,128)(2,1)S(1)} %get-tuple-element.55.refs_5_), channel_id=1, source_target_pairs={{0,1},{1,0},{2,3},{3,2},{4,5},{5,4},{6,7},{7,6},{8,9},{9,8},{10,11... | collective-permute-start | bytes 491528 | tf_op jit(solution)/shard_map/ppermute | solution.py:412
  25.9 0.4 collective-permute-done.6.refs_2_
  26.3 0.6 %collective-permute-done.7.refs_4_ = bf16[40,40,128]{2,1,0:T(8,128)(2,1)S(1)} collective-permute-done((bf16[40,40,128]{2,1,0:T(8,128)(2,1)S(1)}, bf16[40,40,128]{2,1,0:T(8,128)(2,1)S(1)}, u32[]{:S(2)}, u32[]{:S(2)}) %collective-permute-start.7) | collective-permute-done | bytes 409632 | tf_op jit(solution)/shard_map/ppermute | solution.py:412
  26.9 1.0 %send_sums.5 = bf16[8,40,128]{2,1,0:T(8,128)(2,1)S(1)} custom-call(bf16[40,40,128]{2,1,0:T(8,128)(2,1)S(1)} %get-tuple-element.47.refs_0_, bf16[40,40,128]{2,1,0:T(8,128)(2,1)S(1)} %collective-permute-done.3.refs_1_, bf16[40,40,128]{2,1,0:T(8,128)(2,1)S(1)} %collective-permute-done.6.refs_2_, bf16[40,40,128]{2,1,0:T(8,128)(2,1)S(1)} %collective-permute-done.4.refs_3_, ...), custom_call_target="tpu_custom_call" | custom-call | bytes 3690000 | tf_op jit(solution)/shard_map/send_sums/pallas_call | solution.py:425
  27.9 1.0 %collective-permute-start.8 = (bf16[16,40,128]{2,1,0:T(8,128)(2,1)S(1)}, bf16[16,40,128]{2,1,0:T(8,128)(2,1)S(1)}, u32[]{:S(2)}, u32[]{:S(2)}) collective-permute-start(bf16[16,40,128]{2,1,0:T(8,128)(2,1)S(1)} %get-tuple-element.54.refs_5_), channel_id=1, source_target_pairs={{0,1},{1,0},{2,3},{3,2},{4,5},{5,4},{6,7},{7,6},{8,9},{9,8},{10,11... | collective-permute-start | bytes 491528 | tf_op jit(solution)/shard_map/ppermute | solution.py:412
  28.9 2.6 %collective-permute-start.14 = (bf16[8,40,128]{2,1,0:T(8,128)(2,1)S(1)}, bf16[8,40,128]{2,1,0:T(8,128)(2,1)S(1)}, u32[]{:S(2)}, u32[]{:S(2)}) collective-permute-start(bf16[8,40,128]{2,1,0:T(8,128)(2,1)S(1)} %send_sums.5), channel_id=1, source_target_pairs={{0,2},{1,3},{2,0},{3,1},{4,6},{5,7},{6,4},{7,5},{8,10},{9,11},{10,... | collective-permute-start | bytes 245768 | tf_op jit(solution)/shard_map/ppermute | solution.py:412
  31.5 0.0 copy-done.2
  31.5 1.2 %keep_sums.3 = (f32[8,40,128]{2,1,0:T(8,128)S(1)}, f32[8,40,128]{2,1,0:T(8,128)S(1)}) custom-call(bf16[40,40,128]{2,1,0:T(8,128)(2,1)S(1)} %get-tuple-element.47.refs_0_, bf16[40,40,128]{2,1,0:T(8,128)(2,1)S(1)} %collective-permute-done.3.refs_1_, bf16[40,40,128]{2,1,0:T(8,128)(2,1)S(1)} %collective-permute-done.6.refs_2_, ...), custom_call_target="tpu_custom_call" | custom-call | bytes 3837600 | tf_op jit(solution)/shard_map/keep_sums/pallas_call | solution.py:439
  32.7 0.0 collective-permute-done.9.refs_6_
  32.7 1.0 %send_sums.9 = bf16[8,40,128]{2,1,0:T(8,128)(2,1)S(1)} custom-call(bf16[40,40,128]{2,1,0:T(8,128)(2,1)S(1)} %get-tuple-element.47.refs_0_, bf16[40,40,128]{2,1,0:T(8,128)(2,1)S(1)} %collective-permute-done.3.refs_1_, bf16[40,40,128]{2,1,0:T(8,128)(2,1)S(1)} %collective-permute-done.6.refs_2_, bf16[40,40,128]{2,1,0:T(8,128)(2,1)S(1)} %collective-permute-done.4.refs_3_, ...), custom_call_target="tpu_custom_call" | custom-call | bytes 3690000 | tf_op jit(solution)/shard_map/send_sums/pallas_call | solution.py:425
  33.8 1.6 %collective-permute-start.13 = (bf16[8,40,128]{2,1,0:T(8,128)(2,1)S(1)}, bf16[8,40,128]{2,1,0:T(8,128)(2,1)S(1)}, u32[]{:S(2)}, u32[]{:S(2)}) collective-permute-start(bf16[8,40,128]{2,1,0:T(8,128)(2,1)S(1)} %send_sums.9), channel_id=1, source_target_pairs={{0,2},{1,3},{2,0},{3,1},{4,6},{5,7},{6,4},{7,5},{8,10},{9,11},{10,... | collective-permute-start | bytes 245768 | tf_op jit(solution)/shard_map/ppermute | solution.py:412
  35.4 1.0 %send_sums.8 = bf16[8,40,128]{2,1,0:T(8,128)(2,1)S(1)} custom-call(bf16[40,40,128]{2,1,0:T(8,128)(2,1)S(1)} %get-tuple-element.47.refs_0_, bf16[40,40,128]{2,1,0:T(8,128)(2,1)S(1)} %collective-permute-done.3.refs_1_, bf16[40,40,128]{2,1,0:T(8,128)(2,1)S(1)} %collective-permute-done.6.refs_2_, bf16[40,40,128]{2,1,0:T(8,128)(2,1)S(1)} %collective-permute-done.4.refs_3_, ...), custom_call_target="tpu_custom_call" | custom-call | bytes 3690000 | tf_op jit(solution)/shard_map/send_sums/pallas_call | solution.py:425
  36.4 1.4 %collective-permute-start.12 = (bf16[8,40,128]{2,1,0:T(8,128)(2,1)S(1)}, bf16[8,40,128]{2,1,0:T(8,128)(2,1)S(1)}, u32[]{:S(2)}, u32[]{:S(2)}) collective-permute-start(bf16[8,40,128]{2,1,0:T(8,128)(2,1)S(1)} %send_sums.8), channel_id=1, source_target_pairs={{0,2},{1,3},{2,0},{3,1},{4,6},{5,7},{6,4},{7,5},{8,10},{9,11},{10,... | collective-permute-start | bytes 245768 | tf_op jit(solution)/shard_map/ppermute | solution.py:412
  37.9 2.2 %keep_sums.4 = (f32[16,40,128]{2,1,0:T(8,128)S(1)}, f32[16,40,128]{2,1,0:T(8,128)S(1)}) custom-call(bf16[40,40,128]{2,1,0:T(8,128)(2,1)S(1)} %get-tuple-element.47.refs_0_, bf16[40,40,128]{2,1,0:T(8,128)(2,1)S(1)} %collective-permute-done.3.refs_1_, bf16[40,40,128]{2,1,0:T(8,128)(2,1)S(1)} %collective-permute-done.6.refs_2_, ...), custom_call_target="tpu_custom_call" | custom-call | bytes 7675200 | tf_op jit(solution)/shard_map/keep_sums/pallas_call | solution.py:439
  40.1 0.0 collective-permute-done.8.refs_6_
  40.1 1.0 %send_sums.7 = bf16[8,40,128]{2,1,0:T(8,128)(2,1)S(1)} custom-call(bf16[40,40,128]{2,1,0:T(8,128)(2,1)S(1)} %get-tuple-element.47.refs_0_, bf16[40,40,128]{2,1,0:T(8,128)(2,1)S(1)} %collective-permute-done.3.refs_1_, bf16[40,40,128]{2,1,0:T(8,128)(2,1)S(1)} %collective-permute-done.6.refs_2_, bf16[40,40,128]{2,1,0:T(8,128)(2,1)S(1)} %collective-permute-done.4.refs_3_, ...), custom_call_target="tpu_custom_call" | custom-call | bytes 3690000 | tf_op jit(solution)/shard_map/send_sums/pallas_call | solution.py:425
  41.2 0.0 copy-start.1
  41.2 1.6 %collective-permute-start.11 = (bf16[8,40,128]{2,1,0:T(8,128)(2,1)S(1)}, bf16[8,40,128]{2,1,0:T(8,128)(2,1)S(1)}, u32[]{:S(2)}, u32[]{:S(2)}) collective-permute-start(bf16[8,40,128]{2,1,0:T(8,128)(2,1)S(1)} %send_sums.7), channel_id=1, source_target_pairs={{0,2},{1,3},{2,0},{3,1},{4,6},{5,7},{6,4},{7,5},{8,10},{9,11},{10,... | collective-permute-start | bytes 245768 | tf_op jit(solution)/shard_map/ppermute | solution.py:412
  42.8 1.0 %send_sums.6 = bf16[8,40,128]{2,1,0:T(8,128)(2,1)S(1)} custom-call(bf16[40,40,128]{2,1,0:T(8,128)(2,1)S(1)} %get-tuple-element.47.refs_0_, bf16[40,40,128]{2,1,0:T(8,128)(2,1)S(1)} %collective-permute-done.3.refs_1_, bf16[40,40,128]{2,1,0:T(8,128)(2,1)S(1)} %collective-permute-done.6.refs_2_, bf16[40,40,128]{2,1,0:T(8,128)(2,1)S(1)} %collective-permute-done.4.refs_3_, ...), custom_call_target="tpu_custom_call" | custom-call | bytes 3690000 | tf_op jit(solution)/shard_map/send_sums/pallas_call | solution.py:425
  43.9 1.4 %collective-permute-start.10 = (bf16[8,40,128]{2,1,0:T(8,128)(2,1)S(1)}, bf16[8,40,128]{2,1,0:T(8,128)(2,1)S(1)}, u32[]{:S(2)}, u32[]{:S(2)}) collective-permute-start(bf16[8,40,128]{2,1,0:T(8,128)(2,1)S(1)} %send_sums.6), channel_id=1, source_target_pairs={{0,2},{1,3},{2,0},{3,1},{4,6},{5,7},{6,4},{7,5},{8,10},{9,11},{10,... | collective-permute-start | bytes 245768 | tf_op jit(solution)/shard_map/ppermute | solution.py:412
  45.3 0.0 collective-permute-done.14.refs_0_
  45.3 0.0 copy-done.1
  45.3 1.0 %join.3.refs_2_ = bf16[40,40,128]{2,1,0:T(8,128)(2,1)} custom-call(f32[8,40,128]{2,1,0:T(8,128)S(1)} %get-tuple-element.56.own_ref, bf16[40,40,128]{2,1,0:T(8,128)(2,1)S(1)} %get-tuple-element.61.psum_ref, f32[8,40,128]{2,1,0:T(8,128)S(1)} %get-tuple-element.64.gate_ref, bf16[128,128]{1,0:T(8,128)(2,1)S(1)} %copy-done.1, ...), custom_call_target="tpu_custom_call" | custom-call | bytes 1771200 | tf_op jit(solution)/shard_map/join/pallas_call | solution.py:469
  46.3 0.0 collective-permute-done.13.refs_1_
  46.3 2.0 %collective-permute-done.12.refs_0_ = bf16[8,40,128]{2,1,0:T(8,128)(2,1)S(1)} collective-permute-done((bf16[8,40,128]{2,1,0:T(8,128)(2,1)S(1)}, bf16[8,40,128]{2,1,0:T(8,128)(2,1)S(1)}, u32[]{:S(2)}, u32[]{:S(2)}) %collective-permute-start.12) | collective-permute-done | bytes 81952 | tf_op jit(solution)/shard_map/ppermute | solution.py:412
  48.3 1.1 %join.4.refs_2_ = bf16[40,40,128]{2,1,0:T(8,128)(2,1)} custom-call(f32[16,40,128]{2,1,0:T(8,128)S(1)} %get-tuple-element.58.own_ref, bf16[40,40,128]{2,1,0:T(8,128)(2,1)S(1)} %get-tuple-element.61.psum_ref, f32[16,40,128]{2,1,0:T(8,128)S(1)} %get-tuple-element.63.gate_ref, bf16[128,128]{1,0:T(8,128)(2,1)S(1)} %copy-done.1, ...), custom_call_target="tpu_custom_call", output_to_operand_aliasing={{}: (6, {})} | custom-call | bytes 3542400 | tf_op jit(solution)/shard_map/join/pallas_call | solution.py:469
  49.4 2.2 %keep_sums.5 = (f32[16,40,128]{2,1,0:T(8,128)S(1)}, f32[16,40,128]{2,1,0:T(8,128)S(1)}) custom-call(bf16[40,40,128]{2,1,0:T(8,128)(2,1)S(1)} %get-tuple-element.47.refs_0_, bf16[40,40,128]{2,1,0:T(8,128)(2,1)S(1)} %collective-permute-done.3.refs_1_, bf16[40,40,128]{2,1,0:T(8,128)(2,1)S(1)} %collective-permute-done.6.refs_2_, ...), custom_call_target="tpu_custom_call" | custom-call | bytes 7675200 | tf_op jit(solution)/shard_map/keep_sums/pallas_call | solution.py:439
  51.6 0.0 collective-permute-done.11.refs_1_
  51.6 0.9 %collective-permute-done.10.refs_0_ = bf16[8,40,128]{2,1,0:T(8,128)(2,1)S(1)} collective-permute-done((bf16[8,40,128]{2,1,0:T(8,128)(2,1)S(1)}, bf16[8,40,128]{2,1,0:T(8,128)(2,1)S(1)}, u32[]{:S(2)}, u32[]{:S(2)}) %collective-permute-start.10) | collective-permute-done | bytes 81952 | tf_op jit(solution)/shard_map/ppermute | solution.py:412
  52.5 1.1 %join.5 = bf16[40,40,128]{2,1,0:T(8,128)(2,1)} custom-call(f32[16,40,128]{2,1,0:T(8,128)S(1)} %get-tuple-element.60.own_ref, bf16[40,40,128]{2,1,0:T(8,128)(2,1)S(1)} %get-tuple-element.61.psum_ref, f32[16,40,128]{2,1,0:T(8,128)S(1)} %get-tuple-element.62.gate_ref, bf16[128,128]{1,0:T(8,128)(2,1)S(1)} %copy-done.1, ...), custom_call_target="tpu_custom_call", output_to_operand_aliasing={{}: (6, {})} | custom-call | bytes 3542400 | tf_op jit(solution)/shard_map/join/pallas_call | solution.py:469
Async XLA Ops:
  1.5 4.6 %collective-permute-start = (bf16[48,128]{1,0:T(8,128)(2,1)S(1)}, bf16[48,128]{1,0:T(8,128)(2,1)S(1)}, u32[]{:S(2)}, u32[]{:S(2)}) collective-permute-start(bf16[48,128]{1,0:T(8,128)(2,1)S(1)} %get-tuple-element.36), channel_id=1, source_target_pairs={{0,12},{4,8},{8,4},{12,0},{1,13},{5,9},{9,5},{13,1},{2,14},{6,10},... | collective-permute-start | bytes 36872 | tf_op jit(solution)/shard_map/ppermute | solution.py:514
  3.9 3.7 %collective-permute-start.1 = (bf16[48,128]{1,0:T(8,128)(2,1)S(1)}, bf16[48,128]{1,0:T(8,128)(2,1)S(1)}, u32[]{:S(2)}, u32[]{:S(2)}) collective-permute-start(bf16[48,128]{1,0:T(8,128)(2,1)S(1)} %get-tuple-element.37), channel_id=1, source_target_pairs={{0,8},{4,12},{8,0},{12,4},{1,9},{5,13},{9,1},{13,5},{2,10},{6,14},... | collective-permute-start | bytes 36872 | tf_op jit(solution)/shard_map/ppermute | solution.py:514
  4.6 3.1 %collective-permute-start.2 = (bf16[48,128]{1,0:T(8,128)(2,1)S(1)}, bf16[48,128]{1,0:T(8,128)(2,1)S(1)}, u32[]{:S(2)}, u32[]{:S(2)}) collective-permute-start(bf16[48,128]{1,0:T(8,128)(2,1)S(1)} %get-tuple-element.38), channel_id=1, source_target_pairs={{0,4},{4,0},{8,12},{12,8},{1,5},{5,1},{9,13},{13,9},{2,6},{6,2},{1... | collective-permute-start | bytes 36872 | tf_op jit(solution)/shard_map/ppermute | solution.py:514
  4.6 3.0 %copy-start = (bf16[128,512]{1,0:T(8,128)(2,1)S(1)}, bf16[128,512]{1,0:T(8,128)(2,1)}, u32[]{:S(2)}) copy-start(bf16[128,512]{1,0:T(8,128)(2,1)} %win_ref.1) | copy-start | bytes 393220
  10.8 13.7 %collective-permute-start.3 = (bf16[40,40,128]{2,1,0:T(8,128)(2,1)S(1)}, bf16[40,40,128]{2,1,0:T(8,128)(2,1)S(1)}, u32[]{:S(2)}, u32[]{:S(2)}) collective-permute-start(bf16[40,40,128]{2,1,0:T(8,128)(2,1)S(1)} %get-tuple-element.47.refs_0_), channel_id=1, source_target_pairs={{0,8},{1,4},{2,10},{3,6},{4,1},{5,13},{6,3},{7,15},{8,0},{9,12},{1... | collective-permute-start | bytes 1228808 | tf_op jit(solution)/shard_map/ppermute | solution.py:412
  11.5 13.0 %collective-permute-start.4 = (bf16[40,40,128]{2,1,0:T(8,128)(2,1)S(1)}, bf16[40,40,128]{2,1,0:T(8,128)(2,1)S(1)}, u32[]{:S(2)}, u32[]{:S(2)}) collective-permute-start(bf16[40,40,128]{2,1,0:T(8,128)(2,1)S(1)} %get-tuple-element.47.refs_0_), channel_id=1, source_target_pairs={{0,4},{1,8},{2,6},{3,10},{4,13},{5,1},{6,15},{7,3},{8,12},{9,0},{1... | collective-permute-start | bytes 1228808 | tf_op jit(solution)/shard_map/ppermute | solution.py:412
  13.0 11.6 %collective-permute-start.5 = (bf16[8,40,128]{2,1,0:T(8,128)(2,1)S(1)}, bf16[8,40,128]{2,1,0:T(8,128)(2,1)S(1)}, u32[]{:S(2)}, u32[]{:S(2)}) collective-permute-start(bf16[8,40,128]{2,1,0:T(8,128)(2,1)S(1)} %get-tuple-element.49.refs_5_), channel_id=1, source_target_pairs={{0,1},{1,0},{2,3},{3,2},{4,5},{5,4},{6,7},{7,6},{8,9},{9,8},{10,11... | collective-permute-start | bytes 245768 | tf_op jit(solution)/shard_map/ppermute | solution.py:412
  24.6 1.7 %collective-permute-start.6 = (bf16[40,40,128]{2,1,0:T(8,128)(2,1)S(1)}, bf16[40,40,128]{2,1,0:T(8,128)(2,1)S(1)}, u32[]{:S(2)}, u32[]{:S(2)}) collective-permute-start(bf16[40,40,128]{2,1,0:T(8,128)(2,1)S(1)} %collective-permute-done.3.refs_1_), channel_id=1, source_target_pairs={{0,4},{1,5},{2,6},{3,7},{4,0},{5,1},{6,2},{7,3},{8,12},{9,13},{10,... | collective-permute-start | bytes 1228808 | tf_op jit(solution)/shard_map/ppermute | solution.py:412
  24.6 2.3 %collective-permute-start.7 = (bf16[40,40,128]{2,1,0:T(8,128)(2,1)S(1)}, bf16[40,40,128]{2,1,0:T(8,128)(2,1)S(1)}, u32[]{:S(2)}, u32[]{:S(2)}) collective-permute-start(bf16[40,40,128]{2,1,0:T(8,128)(2,1)S(1)} %collective-permute-done.4.refs_3_), channel_id=1, source_target_pairs={{0,4},{1,5},{2,6},{3,7},{4,0},{5,1},{6,2},{7,3},{8,12},{9,13},{10,... | collective-permute-start | bytes 1228808 | tf_op jit(solution)/shard_map/ppermute | solution.py:412
  25.1 6.4 %copy-start.2 = (bf16[128,128]{1,0:T(8,128)(2,1)S(1)}, bf16[128,128]{1,0:T(8,128)(2,1)}, u32[]{:S(2)}) copy-start(bf16[128,128]{1,0:T(8,128)(2,1)} %refs_8_.7) | copy-start | bytes 98308
  25.1 7.6 %collective-permute-start.9 = (bf16[16,40,128]{2,1,0:T(8,128)(2,1)S(1)}, bf16[16,40,128]{2,1,0:T(8,128)(2,1)S(1)}, u32[]{:S(2)}, u32[]{:S(2)}) collective-permute-start(bf16[16,40,128]{2,1,0:T(8,128)(2,1)S(1)} %get-tuple-element.55.refs_5_), channel_id=1, source_target_pairs={{0,1},{1,0},{2,3},{3,2},{4,5},{5,4},{6,7},{7,6},{8,9},{9,8},{10,11... | collective-permute-start | bytes 491528 | tf_op jit(solution)/shard_map/ppermute | solution.py:412
  27.9 12.2 %collective-permute-start.8 = (bf16[16,40,128]{2,1,0:T(8,128)(2,1)S(1)}, bf16[16,40,128]{2,1,0:T(8,128)(2,1)S(1)}, u32[]{:S(2)}, u32[]{:S(2)}) collective-permute-start(bf16[16,40,128]{2,1,0:T(8,128)(2,1)S(1)} %get-tuple-element.54.refs_5_), channel_id=1, source_target_pairs={{0,1},{1,0},{2,3},{3,2},{4,5},{5,4},{6,7},{7,6},{8,9},{9,8},{10,11... | collective-permute-start | bytes 491528 | tf_op jit(solution)/shard_map/ppermute | solution.py:412
  28.9 16.4 %collective-permute-start.14 = (bf16[8,40,128]{2,1,0:T(8,128)(2,1)S(1)}, bf16[8,40,128]{2,1,0:T(8,128)(2,1)S(1)}, u32[]{:S(2)}, u32[]{:S(2)}) collective-permute-start(bf16[8,40,128]{2,1,0:T(8,128)(2,1)S(1)} %send_sums.5), channel_id=1, source_target_pairs={{0,2},{1,3},{2,0},{3,1},{4,6},{5,7},{6,4},{7,5},{8,10},{9,11},{10,... | collective-permute-start | bytes 245768 | tf_op jit(solution)/shard_map/ppermute | solution.py:412
  33.8 12.5 %collective-permute-start.13 = (bf16[8,40,128]{2,1,0:T(8,128)(2,1)S(1)}, bf16[8,40,128]{2,1,0:T(8,128)(2,1)S(1)}, u32[]{:S(2)}, u32[]{:S(2)}) collective-permute-start(bf16[8,40,128]{2,1,0:T(8,128)(2,1)S(1)} %send_sums.9), channel_id=1, source_target_pairs={{0,2},{1,3},{2,0},{3,1},{4,6},{5,7},{6,4},{7,5},{8,10},{9,11},{10,... | collective-permute-start | bytes 245768 | tf_op jit(solution)/shard_map/ppermute | solution.py:412
  36.4 11.8 %collective-permute-start.12 = (bf16[8,40,128]{2,1,0:T(8,128)(2,1)S(1)}, bf16[8,40,128]{2,1,0:T(8,128)(2,1)S(1)}, u32[]{:S(2)}, u32[]{:S(2)}) collective-permute-start(bf16[8,40,128]{2,1,0:T(8,128)(2,1)S(1)} %send_sums.8), channel_id=1, source_target_pairs={{0,2},{1,3},{2,0},{3,1},{4,6},{5,7},{6,4},{7,5},{8,10},{9,11},{10,... | collective-permute-start | bytes 245768 | tf_op jit(solution)/shard_map/ppermute | solution.py:412
  41.2 4.1 %copy-start.1 = (bf16[128,128]{1,0:T(8,128)(2,1)S(1)}, bf16[128,128]{1,0:T(8,128)(2,1)}, u32[]{:S(2)}) copy-start(bf16[128,128]{1,0:T(8,128)(2,1)} %w_ref.5) | copy-start | bytes 98308
  41.2 10.4 %collective-permute-start.11 = (bf16[8,40,128]{2,1,0:T(8,128)(2,1)S(1)}, bf16[8,40,128]{2,1,0:T(8,128)(2,1)S(1)}, u32[]{:S(2)}, u32[]{:S(2)}) collective-permute-start(bf16[8,40,128]{2,1,0:T(8,128)(2,1)S(1)} %send_sums.7), channel_id=1, source_target_pairs={{0,2},{1,3},{2,0},{3,1},{4,6},{5,7},{6,4},{7,5},{8,10},{9,11},{10,... | collective-permute-start | bytes 245768 | tf_op jit(solution)/shard_map/ppermute | solution.py:412
  43.9 8.7 %collective-permute-start.10 = (bf16[8,40,128]{2,1,0:T(8,128)(2,1)S(1)}, bf16[8,40,128]{2,1,0:T(8,128)(2,1)S(1)}, u32[]{:S(2)}, u32[]{:S(2)}) collective-permute-start(bf16[8,40,128]{2,1,0:T(8,128)(2,1)S(1)} %send_sums.6), channel_id=1, source_target_pairs={{0,2},{1,3},{2,0},{3,1},{4,6},{5,7},{6,4},{7,5},{8,10},{9,11},{10,... | collective-permute-start | bytes 245768 | tf_op jit(solution)/shard_map/ppermute | solution.py:412

commit v9 on v7

--- a/solution.py
+++ b/solution.py
@@ -420,7 +420,7 @@
     keeper = lambda r, z: r % 2 == z % 2
     got = move(right, every, lambda r, z: (r ^ 2, z) if keeper(r, z) else (r ^ 1, z ^ 1))
     far = move(right, every, lambda r, z: (r ^ 1, z) if keeper(r, z) else (r ^ 2, z ^ 1))
-    mets = [move(left, every, lambda r, z: (r, z ^ 1)) for left in lefts]
+    mets = [move(left, every, lambda r, z: (r, z ^ 1)) for left in lefts[:2]]
     got, far, mets[0] = lax.optimization_barrier((got, far, mets[0]))
     p_got = move(got, every, lambda r, z: (r ^ 1, z))
     p_far = move(far, every, lambda r, z: (r ^ 1, z))
@@ -440,6 +440,9 @@
             name="send_sums",
         )(*rights, lefts[at], mets[at])
         sums.append(move(part, every, lambda r, z: (r, z ^ 2)))
+        if len(mets) < cuts:
+            left, _ = lax.optimization_barrier((lefts[len(mets)], part))
+            mets.append(move(left, every, lambda r, z: (r, z ^ 1)))
 
     own, gate = pl.pallas_call(
         functools.partial(keep_body, cuts),
@@ -498,8 +501,10 @@
         cost_estimate=cost(1.5),
         name="align",
     )(hold(homolog), hold(factors.T), *map(hold, later))
-    for d in reversed(range(1, rows)):
-        msgs[d] = lax.ppermute(msgs[d], "row", [(r, r ^ d) for r in range(rows)])
+    msgs = [msgs[0]] + [
+        lax.ppermute(msgs[d], "row", [(r, r ^ d) for r in range(rows)])
+        for d in reversed(range(1, rows))
+    ]
 
     base, mask, wq, pick = pl.pallas_call(
         functools.partial(prepare_body, own_seqs),

time: 53.3 us -> 53 us (level)
  transfers between devices with their start and end apart: 15 -> 15, of which waited for: 6 -> 8; matrix products, arithmetic and copies ran while one was open for 0% -> 0% of each run, Pallas kernels for 25% -> 25%
where the time goes in v9:
time: 53 us; the launch traced here: 52.9 us
  Pallas kernels  19.3 us (36%)
  starting transfers between devices  17.8 us (34%)
  waiting for transfers between devices  15.6 us (29%)
    ppermute x12, starting transfers between devices, move(): return lax.ppermute(value, ('row', 'col'), pairs)  14.6 us
    ppermute x12, waiting for transfers between devices, move(): return lax.ppermute(value, ('row', 'col'), pairs)  14.1 us
    pallas_call x1, Pallas kernels, paired_plan(): pl.pallas_call(functools.partial(keep_body, cuts), out_shape=[jax.ShapeDt...  5.36 us
    pallas_call x5, Pallas kernels, paired_plan(): pl.pallas_call(functools.partial(send_body, first), out_shape=jax.ShapeDt...  5.2 us
    pallas_call x1, Pallas kernels, shards(): pl.pallas_call(functools.partial(pair_body, own_seqs, width, rows, paired...  3.21 us
    ppermute x3, starting transfers between devices, shards(): lax.ppermute(msgs[d], 'row', [(r, r ^ d) for r in range(rows)])  3.12 us
    pallas_call x2, Pallas kernels, paired_plan(): pl.pallas_call(functools.partial(join_body, first, len(parts)), out_shape...  2.22 us
    pallas_call x1, Pallas kernels, shards(): pl.pallas_call(functools.partial(prepare_body, own_seqs), out_shape=[jax....  1.51 us
  transfers between devices with their start and end apart: 15, of which 8 were waited for; matrix products, arithmetic and copies ran while one was open for 0% of the time, Pallas kernels for 25%

profile of v9, /device:TPU:0, one launch (start us, length us, event | category | flops | bytes accessed | tf_op | source)
XLA Modules:
  0.0 52.9 jit_solution(2748678937448671535)
XLA Ops:
  0.0 1.5 %align.1 = (bf16[48,128]{1,0:T(8,128)(2,1)S(1)}, bf16[48,128]{1,0:T(8,128)(2,1)S(1)}, bf16[48,128]{1,0:T(8,128)(2,1)S(1)}, bf16[48,128]{1,0:T(8,128)(2,1)S(1)}, ...) custom-call(bf16[2,160,256]{2,1,0:T(8,128)(2,1)} %x_hbm.1, ...), custom_call_target="tpu_custom_call" | custom-call | bytes 5535000 | tf_op jit(solution)/shard_map/align/pallas_call | solution.py:488
  1.5 2.4 %collective-permute-start = (bf16[48,128]{1,0:T(8,128)(2,1)S(1)}, bf16[48,128]{1,0:T(8,128)(2,1)S(1)}, u32[]{:S(2)}, u32[]{:S(2)}) collective-permute-start(bf16[48,128]{1,0:T(8,128)(2,1)S(1)} %get-tuple-element.30), channel_id=1, source_target_pairs={{0,12},{4,8},{8,4},{12,0},{1,13},{5,9},{9,5},{13,1},{2,14},{6,10},... | collective-permute-start | bytes 36872 | tf_op jit(solution)/shard_map/ppermute | solution.py:505
  3.9 0.6 %collective-permute-start.1 = (bf16[48,128]{1,0:T(8,128)(2,1)S(1)}, bf16[48,128]{1,0:T(8,128)(2,1)S(1)}, u32[]{:S(2)}, u32[]{:S(2)}) collective-permute-start(bf16[48,128]{1,0:T(8,128)(2,1)S(1)} %get-tuple-element.31), channel_id=1, source_target_pairs={{0,8},{4,12},{8,0},{12,4},{1,9},{5,13},{9,1},{13,5},{2,10},{6,14},... | collective-permute-start | bytes 36872 | tf_op jit(solution)/shard_map/ppermute | solution.py:505
  4.6 0.0 collective-permute-start.2
  4.6 0.0 copy-start
  4.6 1.5 %prepare.1 = (f32[40,40,128]{2,1,0:T(8,128)S(1)}, bf16[40,40,128]{2,1,0:T(8,128)(2,1)S(1)}, bf16[16,32,256]{2,1,0:T(8,128)(2,1)S(1)}, bf16[4,128,256]{2,1,0:T(8,128)(2,1)S(1)}) custom-call(bf16[40,40,128]{2,1,0:T(8,128)(2,1)S(1)} %get-tuple-element.33.couple_ref, s32[160]{0:T(256)} %ids_hbm.1, s32[40,40]{1,0:T(8,128)S(1)} %get-tuple-element.34.valid_ref, ...), custom_call_target="tpu_custom_call" | custom-call | bytes 7380000 | tf_op jit(solution)/shard_map/prepare/pallas_call | solution.py:509
  6.1 0.0 collective-permute-done.refs_1_
  6.1 1.5 %collective-permute-done.1.refs_2_ = bf16[48,128]{1,0:T(8,128)(2,1)S(1)} collective-permute-done((bf16[48,128]{1,0:T(8,128)(2,1)S(1)}, bf16[48,128]{1,0:T(8,128)(2,1)S(1)}, u32[]{:S(2)}, u32[]{:S(2)}) %collective-permute-start.1) | collective-permute-done | bytes 12320 | tf_op jit(solution)/shard_map/ppermute | solution.py:505
  7.6 0.0 collective-permute-done.2.refs_3_
  7.6 0.0 copy-done
  7.6 3.2 %pair.1 = (bf16[40,40,128]{2,1,0:T(8,128)(2,1)S(1)}, bf16[1600,128]{1,0:T(8,128)(2,1)S(1)}, bf16[40,40,128]{2,1,0:T(8,128)(2,1)S(1)}) custom-call(bf16[48,128]{1,0:T(8,128)(2,1)S(1)} %get-tuple-element.29.refs_0_, bf16[48,128]{1,0:T(8,128)(2,1)S(1)} %collective-permute-done.refs_1_, bf16[48,128]{1,0:T(8,128)(2,1)S(1)} %collective-permute-done.1.refs_2_, ...), custom_call_target="tpu_custom_call" | custom-call | bytes 16605000 | tf_op jit(solution)/shard_map/pair/pallas_call | solution.py:529
  10.8 0.7 %collective-permute-start.3 = (bf16[40,40,128]{2,1,0:T(8,128)(2,1)S(1)}, bf16[40,40,128]{2,1,0:T(8,128)(2,1)S(1)}, u32[]{:S(2)}, u32[]{:S(2)}) collective-permute-start(bf16[40,40,128]{2,1,0:T(8,128)(2,1)S(1)} %get-tuple-element.41.refs_0_), channel_id=1, source_target_pairs={{0,8},{1,4},{2,10},{3,6},{4,1},{5,13},{6,3},{7,15},{8,0},{9,12},{1... | collective-permute-start | bytes 1228808 | tf_op jit(solution)/shard_map/ppermute | solution.py:417
  11.5 1.0 %collective-permute-start.4 = (bf16[40,40,128]{2,1,0:T(8,128)(2,1)S(1)}, bf16[40,40,128]{2,1,0:T(8,128)(2,1)S(1)}, u32[]{:S(2)}, u32[]{:S(2)}) collective-permute-start(bf16[40,40,128]{2,1,0:T(8,128)(2,1)S(1)} %get-tuple-element.41.refs_0_), channel_id=1, source_target_pairs={{0,4},{1,8},{2,6},{3,10},{4,13},{5,1},{6,15},{7,3},{8,12},{9,0},{1... | collective-permute-start | bytes 1228808 | tf_op jit(solution)/shard_map/ppermute | solution.py:417
  12.6 0.4 left.1
  13.0 1.9 %collective-permute-start.5 = (bf16[8,40,128]{2,1,0:T(8,128)(2,1)S(1)}, bf16[8,40,128]{2,1,0:T(8,128)(2,1)S(1)}, u32[]{:S(2)}, u32[]{:S(2)}) collective-permute-start(bf16[8,40,128]{2,1,0:T(8,128)(2,1)S(1)} %get-tuple-element.43.refs_5_), channel_id=1, source_target_pairs={{0,1},{1,0},{2,3},{3,2},{4,5},{5,4},{6,7},{7,6},{8,9},{9,8},{10,11... | collective-permute-start | bytes 245768 | tf_op jit(solution)/shard_map/ppermute | solution.py:417
  14.8 9.7 %collective-permute-done.5.refs_6_.refs_8_ = bf16[8,40,128]{2,1,0:T(8,128)(2,1)S(1)} collective-permute-done((bf16[8,40,128]{2,1,0:T(8,128)(2,1)S(1)}, bf16[8,40,128]{2,1,0:T(8,128)(2,1)S(1)}, u32[]{:S(2)}, u32[]{:S(2)}) %collective-permute-start.5) | collective-permute-done | bytes 81952 | tf_op jit(solution)/shard_map/ppermute | solution.py:417
  24.6 0.0 collective-permute-done.3.refs_1_
  24.6 0.0 collective-permute-done.4.refs_3_
  24.6 0.0 collective-permute-start.6
  24.6 0.5 collective-permute-start.7
  25.1 0.8 %collective-permute-start.8 = (bf16[16,40,128]{2,1,0:T(8,128)(2,1)S(1)}, bf16[16,40,128]{2,1,0:T(8,128)(2,1)S(1)}, u32[]{:S(2)}, u32[]{:S(2)}) collective-permute-start(bf16[16,40,128]{2,1,0:T(8,128)(2,1)S(1)} %get-tuple-element.46.refs_6_.refs_5_), channel_id=1, source_target_pairs={{0,1},{1,0},{2,3},{3,2},{4,5},{5,4},{6,7},{7,6},{8,9},{9,8},{10,11... | collective-permute-start | bytes 491528 | tf_op jit(solution)/shard_map/ppermute | solution.py:417
  25.9 0.4 collective-permute-done.6.refs_2_
  26.3 0.6 %collective-permute-done.7.refs_4_ = bf16[40,40,128]{2,1,0:T(8,128)(2,1)S(1)} collective-permute-done((bf16[40,40,128]{2,1,0:T(8,128)(2,1)S(1)}, bf16[40,40,128]{2,1,0:T(8,128)(2,1)S(1)}, u32[]{:S(2)}, u32[]{:S(2)}) %collective-permute-start.7) | collective-permute-done | bytes 409632 | tf_op jit(solution)/shard_map/ppermute | solution.py:417
  26.9 1.0 %send_sums.5 = bf16[8,40,128]{2,1,0:T(8,128)(2,1)S(1)} custom-call(bf16[40,40,128]{2,1,0:T(8,128)(2,1)S(1)} %get-tuple-element.41.refs_0_, bf16[40,40,128]{2,1,0:T(8,128)(2,1)S(1)} %collective-permute-done.3.refs_1_, bf16[40,40,128]{2,1,0:T(8,128)(2,1)S(1)} %collective-permute-done.6.refs_2_, bf16[40,40,128]{2,1,0:T(8,128)(2,1)S(1)} %collective-permute-done.4.refs_3_, ...), custom_call_target="tpu_custom_call" | custom-call | bytes 5018400 | tf_op jit(solution)/shard_map/send_sums/pallas_call | solution.py:432
  27.9 1.0 %collective-permute-start.9 = (bf16[16,40,128]{2,1,0:T(8,128)(2,1)S(1)}, bf16[16,40,128]{2,1,0:T(8,128)(2,1)S(1)}, u32[]{:S(2)}, u32[]{:S(2)}) collective-permute-start(bf16[16,40,128]{2,1,0:T(8,128)(2,1)S(1)} %get-tuple-element.49.refs_7_.refs_5_), channel_id=1, source_target_pairs={{0,1},{1,0},{2,3},{3,2},{4,5},{5,4},{6,7},{7,6},{8,9},{9,8},{10,11... | collective-permute-start | bytes 491528 | tf_op jit(solution)/shard_map/ppermute | solution.py:417
  28.9 2.6 %collective-permute-start.13 = (bf16[8,40,128]{2,1,0:T(8,128)(2,1)S(1)}, bf16[8,40,128]{2,1,0:T(8,128)(2,1)S(1)}, u32[]{:S(2)}, u32[]{:S(2)}) collective-permute-start(bf16[8,40,128]{2,1,0:T(8,128)(2,1)S(1)} %send_sums.5), channel_id=1, source_target_pairs={{0,2},{1,3},{2,0},{3,1},{4,6},{5,7},{6,4},{7,5},{8,10},{9,11},{10,... | collective-permute-start | bytes 245768 | tf_op jit(solution)/shard_map/ppermute | solution.py:417
  31.5 0.2 collective-permute-done.8.refs_9_.refs_6_
  31.7 1.0 %send_sums.9 = bf16[8,40,128]{2,1,0:T(8,128)(2,1)S(1)} custom-call(bf16[40,40,128]{2,1,0:T(8,128)(2,1)S(1)} %get-tuple-element.41.refs_0_, bf16[40,40,128]{2,1,0:T(8,128)(2,1)S(1)} %collective-permute-done.3.refs_1_, bf16[40,40,128]{2,1,0:T(8,128)(2,1)S(1)} %collective-permute-done.6.refs_2_, bf16[40,40,128]{2,1,0:T(8,128)(2,1)S(1)} %collective-permute-done.4.refs_3_, ...), custom_call_target="tpu_custom_call" | custom-call | bytes 5018400 | tf_op jit(solution)/shard_map/send_sums/pallas_call | solution.py:432
  32.7 2.7 %collective-permute-start.14 = (bf16[8,40,128]{2,1,0:T(8,128)(2,1)S(1)}, bf16[8,40,128]{2,1,0:T(8,128)(2,1)S(1)}, u32[]{:S(2)}, u32[]{:S(2)}) collective-permute-start(bf16[8,40,128]{2,1,0:T(8,128)(2,1)S(1)} %send_sums.9), channel_id=1, source_target_pairs={{0,2},{1,3},{2,0},{3,1},{4,6},{5,7},{6,4},{7,5},{8,10},{9,11},{10,... | collective-permute-start | bytes 245768 | tf_op jit(solution)/shard_map/ppermute | solution.py:417
  35.4 1.0 %send_sums.6 = bf16[8,40,128]{2,1,0:T(8,128)(2,1)S(1)} custom-call(bf16[40,40,128]{2,1,0:T(8,128)(2,1)S(1)} %get-tuple-element.41.refs_0_, bf16[40,40,128]{2,1,0:T(8,128)(2,1)S(1)} %collective-permute-done.3.refs_1_, bf16[40,40,128]{2,1,0:T(8,128)(2,1)S(1)} %collective-permute-done.6.refs_2_, bf16[40,40,128]{2,1,0:T(8,128)(2,1)S(1)} %collective-permute-done.4.refs_3_, ...), custom_call_target="tpu_custom_call" | custom-call | bytes 5018400 | tf_op jit(solution)/shard_map/send_sums/pallas_call | solution.py:432
  36.4 0.4 collective-permute-start.10
  36.8 0.6 %collective-permute-done.9.refs_10_.refs_6_ = bf16[16,40,128]{2,1,0:T(8,128)(2,1)S(1)} collective-permute-done((bf16[16,40,128]{2,1,0:T(8,128)(2,1)S(1)}, bf16[16,40,128]{2,1,0:T(8,128)(2,1)S(1)}, u32[]{:S(2)}, u32[]{:S(2)}) %collective-permute-start.9) | collective-permute-done | bytes 163872 | tf_op jit(solution)/shard_map/ppermute | solution.py:417
  37.4 1.0 %send_sums.7 = bf16[8,40,128]{2,1,0:T(8,128)(2,1)S(1)} custom-call(bf16[40,40,128]{2,1,0:T(8,128)(2,1)S(1)} %get-tuple-element.41.refs_0_, bf16[40,40,128]{2,1,0:T(8,128)(2,1)S(1)} %collective-permute-done.3.refs_1_, bf16[40,40,128]{2,1,0:T(8,128)(2,1)S(1)} %collective-permute-done.6.refs_2_, bf16[40,40,128]{2,1,0:T(8,128)(2,1)S(1)} %collective-permute-done.4.refs_3_, ...), custom_call_target="tpu_custom_call" | custom-call | bytes 5018400 | tf_op jit(solution)/shard_map/send_sums/pallas_call | solution.py:432
  38.5 0.0 copy-start.2
  38.5 2.1 %collective-permute-start.11 = (bf16[8,40,128]{2,1,0:T(8,128)(2,1)S(1)}, bf16[8,40,128]{2,1,0:T(8,128)(2,1)S(1)}, u32[]{:S(2)}, u32[]{:S(2)}) collective-permute-start(bf16[8,40,128]{2,1,0:T(8,128)(2,1)S(1)} %send_sums.7), channel_id=1, source_target_pairs={{0,2},{1,3},{2,0},{3,1},{4,6},{5,7},{6,4},{7,5},{8,10},{9,11},{10,... | collective-permute-start | bytes 245768 | tf_op jit(solution)/shard_map/ppermute | solution.py:417
  40.6 1.0 %send_sums.8 = bf16[8,40,128]{2,1,0:T(8,128)(2,1)S(1)} custom-call(bf16[40,40,128]{2,1,0:T(8,128)(2,1)S(1)} %get-tuple-element.41.refs_0_, bf16[40,40,128]{2,1,0:T(8,128)(2,1)S(1)} %collective-permute-done.3.refs_1_, bf16[40,40,128]{2,1,0:T(8,128)(2,1)S(1)} %collective-permute-done.6.refs_2_, bf16[40,40,128]{2,1,0:T(8,128)(2,1)S(1)} %collective-permute-done.4.refs_3_, ...), custom_call_target="tpu_custom_call" | custom-call | bytes 5018400 | tf_op jit(solution)/shard_map/send_sums/pallas_call | solution.py:432
  41.6 0.0 copy-start.1
  41.6 1.0 %collective-permute-start.12 = (bf16[8,40,128]{2,1,0:T(8,128)(2,1)S(1)}, bf16[8,40,128]{2,1,0:T(8,128)(2,1)S(1)}, u32[]{:S(2)}, u32[]{:S(2)}) collective-permute-start(bf16[8,40,128]{2,1,0:T(8,128)(2,1)S(1)} %send_sums.8), channel_id=1, source_target_pairs={{0,2},{1,3},{2,0},{3,1},{4,6},{5,7},{6,4},{7,5},{8,10},{9,11},{10,... | collective-permute-start | bytes 245768 | tf_op jit(solution)/shard_map/ppermute | solution.py:417
  42.6 0.0 copy-done.2
  42.6 5.4 %keep_sums.1 = (f32[40,40,128]{2,1,0:T(8,128)S(1)}, f32[40,40,128]{2,1,0:T(8,128)S(1)}) custom-call(bf16[40,40,128]{2,1,0:T(8,128)(2,1)S(1)} %get-tuple-element.41.refs_0_, bf16[40,40,128]{2,1,0:T(8,128)(2,1)S(1)} %collective-permute-done.3.refs_1_, bf16[40,40,128]{2,1,0:T(8,128)(2,1)S(1)} %collective-permute-done.6.refs_2_, ...), custom_call_target="tpu_custom_call" | custom-call | bytes 22140000 | tf_op jit(solution)/shard_map/keep_sums/pallas_call | solution.py:447
  48.0 0.0 collective-permute-done.13.refs_0_
  48.0 0.0 collective-permute-done.14.refs_1_
  48.0 0.0 copy-done.1
  48.0 1.1 %join.2.refs_3_ = bf16[40,40,128]{2,1,0:T(8,128)(2,1)} custom-call(f32[40,40,128]{2,1,0:T(8,128)S(1)} %get-tuple-element.50.own_ref, bf16[40,40,128]{2,1,0:T(8,128)(2,1)S(1)} %get-tuple-element.51.psum_ref, f32[40,40,128]{2,1,0:T(8,128)S(1)} %get-tuple-element.52.gate_ref, bf16[128,128]{1,0:T(8,128)(2,1)S(1)} %copy-done.1, ...), custom_call_target="tpu_custom_call" | custom-call | bytes 3542400 | tf_op jit(solution)/shard_map/join/pallas_call | solution.py:461
  49.1 0.0 collective-permute-done.10.refs_0_
  49.1 1.7 %collective-permute-done.11.refs_1_ = bf16[8,40,128]{2,1,0:T(8,128)(2,1)S(1)} collective-permute-done((bf16[8,40,128]{2,1,0:T(8,128)(2,1)S(1)}, bf16[8,40,128]{2,1,0:T(8,128)(2,1)S(1)}, u32[]{:S(2)}, u32[]{:S(2)}) %collective-permute-start.11) | collective-permute-done | bytes 81952 | tf_op jit(solution)/shard_map/ppermute | solution.py:417
  50.7 1.0 %collective-permute-done.12.refs_2_ = bf16[8,40,128]{2,1,0:T(8,128)(2,1)S(1)} collective-permute-done((bf16[8,40,128]{2,1,0:T(8,128)(2,1)S(1)}, bf16[8,40,128]{2,1,0:T(8,128)(2,1)S(1)}, u32[]{:S(2)}, u32[]{:S(2)}) %collective-permute-start.12) | collective-permute-done | bytes 81952 | tf_op jit(solution)/shard_map/ppermute | solution.py:417
  51.7 1.2 %join.3 = bf16[40,40,128]{2,1,0:T(8,128)(2,1)} custom-call(f32[40,40,128]{2,1,0:T(8,128)S(1)} %get-tuple-element.50.own_ref, bf16[40,40,128]{2,1,0:T(8,128)(2,1)S(1)} %get-tuple-element.51.psum_ref, f32[40,40,128]{2,1,0:T(8,128)S(1)} %get-tuple-element.52.gate_ref, bf16[128,128]{1,0:T(8,128)(2,1)S(1)} %copy-done.1, ...), custom_call_target="tpu_custom_call", output_to_operand_aliasing={{}: (7, {})} | custom-call | bytes 5313600 | tf_op jit(solution)/shard_map/join/pallas_call | solution.py:461
Async XLA Ops:
  1.5 4.6 %collective-permute-start = (bf16[48,128]{1,0:T(8,128)(2,1)S(1)}, bf16[48,128]{1,0:T(8,128)(2,1)S(1)}, u32[]{:S(2)}, u32[]{:S(2)}) collective-permute-start(bf16[48,128]{1,0:T(8,128)(2,1)S(1)} %get-tuple-element.30), channel_id=1, source_target_pairs={{0,12},{4,8},{8,4},{12,0},{1,13},{5,9},{9,5},{13,1},{2,14},{6,10},... | collective-permute-start | bytes 36872 | tf_op jit(solution)/shard_map/ppermute | solution.py:505
  3.9 3.7 %collective-permute-start.1 = (bf16[48,128]{1,0:T(8,128)(2,1)S(1)}, bf16[48,128]{1,0:T(8,128)(2,1)S(1)}, u32[]{:S(2)}, u32[]{:S(2)}) collective-permute-start(bf16[48,128]{1,0:T(8,128)(2,1)S(1)} %get-tuple-element.31), channel_id=1, source_target_pairs={{0,8},{4,12},{8,0},{12,4},{1,9},{5,13},{9,1},{13,5},{2,10},{6,14},... | collective-permute-start | bytes 36872 | tf_op jit(solution)/shard_map/ppermute | solution.py:505
  4.6 3.1 %collective-permute-start.2 = (bf16[48,128]{1,0:T(8,128)(2,1)S(1)}, bf16[48,128]{1,0:T(8,128)(2,1)S(1)}, u32[]{:S(2)}, u32[]{:S(2)}) collective-permute-start(bf16[48,128]{1,0:T(8,128)(2,1)S(1)} %get-tuple-element.32), channel_id=1, source_target_pairs={{0,4},{4,0},{8,12},{12,8},{1,5},{5,1},{9,13},{13,9},{2,6},{6,2},{1... | collective-permute-start | bytes 36872 | tf_op jit(solution)/shard_map/ppermute | solution.py:505
  4.6 3.0 %copy-start = (bf16[128,512]{1,0:T(8,128)(2,1)S(1)}, bf16[128,512]{1,0:T(8,128)(2,1)}, u32[]{:S(2)}) copy-start(bf16[128,512]{1,0:T(8,128)(2,1)} %win_ref.1) | copy-start | bytes 393220
  10.8 13.7 %collective-permute-start.3 = (bf16[40,40,128]{2,1,0:T(8,128)(2,1)S(1)}, bf16[40,40,128]{2,1,0:T(8,128)(2,1)S(1)}, u32[]{:S(2)}, u32[]{:S(2)}) collective-permute-start(bf16[40,40,128]{2,1,0:T(8,128)(2,1)S(1)} %get-tuple-element.41.refs_0_), channel_id=1, source_target_pairs={{0,8},{1,4},{2,10},{3,6},{4,1},{5,13},{6,3},{7,15},{8,0},{9,12},{1... | collective-permute-start | bytes 1228808 | tf_op jit(solution)/shard_map/ppermute | solution.py:417
  11.5 13.0 %collective-permute-start.4 = (bf16[40,40,128]{2,1,0:T(8,128)(2,1)S(1)}, bf16[40,40,128]{2,1,0:T(8,128)(2,1)S(1)}, u32[]{:S(2)}, u32[]{:S(2)}) collective-permute-start(bf16[40,40,128]{2,1,0:T(8,128)(2,1)S(1)} %get-tuple-element.41.refs_0_), channel_id=1, source_target_pairs={{0,4},{1,8},{2,6},{3,10},{4,13},{5,1},{6,15},{7,3},{8,12},{9,0},{1... | collective-permute-start | bytes 1228808 | tf_op jit(solution)/shard_map/ppermute | solution.py:417
  13.0 11.6 %collective-permute-start.5 = (bf16[8,40,128]{2,1,0:T(8,128)(2,1)S(1)}, bf16[8,40,128]{2,1,0:T(8,128)(2,1)S(1)}, u32[]{:S(2)}, u32[]{:S(2)}) collective-permute-start(bf16[8,40,128]{2,1,0:T(8,128)(2,1)S(1)} %get-tuple-element.43.refs_5_), channel_id=1, source_target_pairs={{0,1},{1,0},{2,3},{3,2},{4,5},{5,4},{6,7},{7,6},{8,9},{9,8},{10,11... | collective-permute-start | bytes 245768 | tf_op jit(solution)/shard_map/ppermute | solution.py:417
  24.6 1.7 %collective-permute-start.6 = (bf16[40,40,128]{2,1,0:T(8,128)(2,1)S(1)}, bf16[40,40,128]{2,1,0:T(8,128)(2,1)S(1)}, u32[]{:S(2)}, u32[]{:S(2)}) collective-permute-start(bf16[40,40,128]{2,1,0:T(8,128)(2,1)S(1)} %collective-permute-done.3.refs_1_), channel_id=1, source_target_pairs={{0,4},{1,5},{2,6},{3,7},{4,0},{5,1},{6,2},{7,3},{8,12},{9,13},{10,... | collective-permute-start | bytes 1228808 | tf_op jit(solution)/shard_map/ppermute | solution.py:417
  24.6 2.3 %collective-permute-start.7 = (bf16[40,40,128]{2,1,0:T(8,128)(2,1)S(1)}, bf16[40,40,128]{2,1,0:T(8,128)(2,1)S(1)}, u32[]{:S(2)}, u32[]{:S(2)}) collective-permute-start(bf16[40,40,128]{2,1,0:T(8,128)(2,1)S(1)} %collective-permute-done.4.refs_3_), channel_id=1, source_target_pairs={{0,4},{1,5},{2,6},{3,7},{4,0},{5,1},{6,2},{7,3},{8,12},{9,13},{10,... | collective-permute-start | bytes 1228808 | tf_op jit(solution)/shard_map/ppermute | solution.py:417
  25.1 6.6 %collective-permute-start.8 = (bf16[16,40,128]{2,1,0:T(8,128)(2,1)S(1)}, bf16[16,40,128]{2,1,0:T(8,128)(2,1)S(1)}, u32[]{:S(2)}, u32[]{:S(2)}) collective-permute-start(bf16[16,40,128]{2,1,0:T(8,128)(2,1)S(1)} %get-tuple-element.46.refs_6_.refs_5_), channel_id=1, source_target_pairs={{0,1},{1,0},{2,3},{3,2},{4,5},{5,4},{6,7},{7,6},{8,9},{9,8},{10,11... | collective-permute-start | bytes 491528 | tf_op jit(solution)/shard_map/ppermute | solution.py:417
  27.9 9.5 %collective-permute-start.9 = (bf16[16,40,128]{2,1,0:T(8,128)(2,1)S(1)}, bf16[16,40,128]{2,1,0:T(8,128)(2,1)S(1)}, u32[]{:S(2)}, u32[]{:S(2)}) collective-permute-start(bf16[16,40,128]{2,1,0:T(8,128)(2,1)S(1)} %get-tuple-element.49.refs_7_.refs_5_), channel_id=1, source_target_pairs={{0,1},{1,0},{2,3},{3,2},{4,5},{5,4},{6,7},{7,6},{8,9},{9,8},{10,11... | collective-permute-start | bytes 491528 | tf_op jit(solution)/shard_map/ppermute | solution.py:417
  28.9 19.0 %collective-permute-start.13 = (bf16[8,40,128]{2,1,0:T(8,128)(2,1)S(1)}, bf16[8,40,128]{2,1,0:T(8,128)(2,1)S(1)}, u32[]{:S(2)}, u32[]{:S(2)}) collective-permute-start(bf16[8,40,128]{2,1,0:T(8,128)(2,1)S(1)} %send_sums.5), channel_id=1, source_target_pairs={{0,2},{1,3},{2,0},{3,1},{4,6},{5,7},{6,4},{7,5},{8,10},{9,11},{10,... | collective-permute-start | bytes 245768 | tf_op jit(solution)/shard_map/ppermute | solution.py:417
  32.7 15.2 %collective-permute-start.14 = (bf16[8,40,128]{2,1,0:T(8,128)(2,1)S(1)}, bf16[8,40,128]{2,1,0:T(8,128)(2,1)S(1)}, u32[]{:S(2)}, u32[]{:S(2)}) collective-permute-start(bf16[8,40,128]{2,1,0:T(8,128)(2,1)S(1)} %send_sums.9), channel_id=1, source_target_pairs={{0,2},{1,3},{2,0},{3,1},{4,6},{5,7},{6,4},{7,5},{8,10},{9,11},{10,... | collective-permute-start | bytes 245768 | tf_op jit(solution)/shard_map/ppermute | solution.py:417
  36.4 12.6 %collective-permute-start.10 = (bf16[8,40,128]{2,1,0:T(8,128)(2,1)S(1)}, bf16[8,40,128]{2,1,0:T(8,128)(2,1)S(1)}, u32[]{:S(2)}, u32[]{:S(2)}) collective-permute-start(bf16[8,40,128]{2,1,0:T(8,128)(2,1)S(1)} %send_sums.6), channel_id=1, source_target_pairs={{0,2},{1,3},{2,0},{3,1},{4,6},{5,7},{6,4},{7,5},{8,10},{9,11},{10,... | collective-permute-start | bytes 245768 | tf_op jit(solution)/shard_map/ppermute | solution.py:417
  38.5 4.1 %copy-start.2 = (bf16[128,128]{1,0:T(8,128)(2,1)S(1)}, bf16[128,128]{1,0:T(8,128)(2,1)}, u32[]{:S(2)}) copy-start(bf16[128,128]{1,0:T(8,128)(2,1)} %refs_12_.1) | copy-start | bytes 98308
  38.5 12.3 %collective-permute-start.11 = (bf16[8,40,128]{2,1,0:T(8,128)(2,1)S(1)}, bf16[8,40,128]{2,1,0:T(8,128)(2,1)S(1)}, u32[]{:S(2)}, u32[]{:S(2)}) collective-permute-start(bf16[8,40,128]{2,1,0:T(8,128)(2,1)S(1)} %send_sums.7), channel_id=1, source_target_pairs={{0,2},{1,3},{2,0},{3,1},{4,6},{5,7},{6,4},{7,5},{8,10},{9,11},{10,... | collective-permute-start | bytes 245768 | tf_op jit(solution)/shard_map/ppermute | solution.py:417
  41.6 6.4 %copy-start.1 = (bf16[128,128]{1,0:T(8,128)(2,1)S(1)}, bf16[128,128]{1,0:T(8,128)(2,1)}, u32[]{:S(2)}) copy-start(bf16[128,128]{1,0:T(8,128)(2,1)} %w_ref.3) | copy-start | bytes 98308
  41.6 10.1 %collective-permute-start.12 = (bf16[8,40,128]{2,1,0:T(8,128)(2,1)S(1)}, bf16[8,40,128]{2,1,0:T(8,128)(2,1)S(1)}, u32[]{:S(2)}, u32[]{:S(2)}) collective-permute-start(bf16[8,40,128]{2,1,0:T(8,128)(2,1)S(1)} %send_sums.8), channel_id=1, source_target_pairs={{0,2},{1,3},{2,0},{3,1},{4,6},{5,7},{6,4},{7,5},{8,10},{9,11},{10,... | collective-permute-start | bytes 245768 | tf_op jit(solution)/shard_map/ppermute | solution.py:417

commit v10 on v9

--- a/solution.py
+++ b/solution.py
@@ -17,6 +17,10 @@
 
 def limit(mib, scale=1):
     return pltpu.CompilerParams(vmem_limit_bytes=min(56, mib * scale) * 1024 * 1024)
+
+
+def aligned(n, m):
+    return n if isinstance(n, int) else pl.multiple_of(n, m)
 
 
 def round_up(n, m):
@@ -151,12 +155,12 @@
         out = jnp.dot(lhs, wq_ref[h], preferred_element_type=f32)
         parts = [out[:, d * chans : (d + 1) * chans].reshape(own_i, total, chans) for d in range(2)]
         block = jnp.concatenate(parts, axis=1).astype(bf16)
-        where = pl.ds(pl.multiple_of(h * 2 * total, 16), 2 * total)
+        where = pl.ds(aligned(h * 2 * total, 16), 2 * total)
         t_ref[:, where, :chans] = block[:half]
         t_ref[:, where, chans:] = block[half:]
         return carry
 
-    lax.fori_loop(0, width // 2, expand, 0, unroll=16 if turned else 4)
+    repeat(width // 2, expand, turned)
 
     step = 4 if half % 4 == 0 else 1
 
@@ -176,23 +180,31 @@
         for side in range(2):
             cut = slice(side * count, (side + 1) * count)
             i0 = b * step + side * half
-            norm_ref[pl.ds(pl.multiple_of(i0 * own_j, 16), count), :] = flat[cut]
+            norm_ref[pl.ds(aligned(i0 * own_j, 16), count), :] = flat[cut]
             mask = mask_ref[pl.ds(i0, step)].astype(f32).reshape(count, tri)
             right = mask * sigmoid(proj[cut, :tri]) * proj[cut, tri:]
             if turned:
-                flat_ref[pl.ds(pl.multiple_of(i0 * own_j, 8), count), :] = right
+                flat_ref[pl.ds(aligned(i0 * own_j, 8), count), :] = right
             else:
                 right_ref[pl.ds(i0, step)] = right.reshape(step, own_j, tri).astype(bf16)
         return carry
 
-    lax.fori_loop(0, half // step, rows, 0, unroll=True)
+    repeat(half // step, rows, turned)
 
     def turn(k, carry):
         right_ref[k] = flat_ref[pl.ds(k, own_i, stride=own_j), :].astype(bf16)
         return carry
 
     if turned:
-        lax.fori_loop(0, own_j, turn, 0, unroll=8)
+        repeat(own_j, turn, True)
+
+
+def repeat(count, body, static):
+    if static:
+        for n in range(count):
+            body(n, 0)
+    else:
+        lax.fori_loop(0, count, body, 0)
 
 
 def left_body(norm_ref, mask_ref, win_ref, *outs):
@@ -213,6 +225,19 @@
 
         lax.fori_loop(0, out.shape[0] // group, rows, 0, unroll=True)
         at += out.shape[0]
+
+
+def gate_body(norm_ref, wgate_ref, gate_ref):
+    own_i, depth, chans = gate_ref.shape
+    group = 8
+
+    def gates(b, carry):
+        flat = norm_ref[pl.ds(pl.multiple_of(b * group * depth, 16), group * depth), :]
+        gate = sigmoid(jnp.dot(flat, wgate_ref[...], preferred_element_type=f32))
+        gate_ref[pl.ds(b * group, group)] = gate.reshape(group, depth, -1)
+        return carry
+
+    lax.fori_loop(0, own_i // group, gates, 0, unroll=True)
 
 
 def contract(lf_ref, halves, i0, group):
@@ -271,7 +296,7 @@
 def keep_body(cuts, *refs):
     rights, refs = refs[:5], refs[5:]
     lefts, mets = refs[:cuts], refs[cuts : 2 * cuts]
-    norm_ref, wgate_ref, o_ref, gate_ref, lf_ref = refs[2 * cuts :]
+    o_ref, lf_ref = refs[2 * cuts :]
     own_i, depth, chans = o_ref.shape
     at = 0
     for l_ref, m_ref in zip(lefts, mets):
@@ -280,14 +305,6 @@
         lf_ref[pl.ds(at, n), pl.ds(depth, depth), :] = m_ref[...].astype(f32)
         at += n
     group = 8
-
-    def gates(b, carry):
-        flat = norm_ref[pl.ds(pl.multiple_of(b * group * depth, 16), group * depth), :]
-        gate = sigmoid(jnp.dot(flat, wgate_ref[...], preferred_element_type=f32))
-        gate_ref[pl.ds(b * group, group)] = gate.reshape(group, depth, -1)
-        return carry
-
-    lax.fori_loop(0, own_i // group, gates, 0, unroll=True)
 
     def use(halves):
         def rows(b, carry):
@@ -421,7 +438,16 @@
     got = move(right, every, lambda r, z: (r ^ 2, z) if keeper(r, z) else (r ^ 1, z ^ 1))
     far = move(right, every, lambda r, z: (r ^ 1, z) if keeper(r, z) else (r ^ 2, z ^ 1))
     mets = [move(left, every, lambda r, z: (r, z ^ 1)) for left in lefts[:2]]
-    got, far, mets[0] = lax.optimization_barrier((got, far, mets[0]))
+    gate = pl.pallas_call(
+        gate_body,
+        out_shape=jax.ShapeDtypeStruct((own_i, own_j, chans), f32),
+        in_specs=[VMEM] * 2,
+        out_specs=VMEM,
+        compiler_params=limit(8),
+        cost_estimate=cost(1),
+        name="gate",
+    )(norm, w_gate)
+    got, far, mets[0], gate = lax.optimization_barrier((got, far, mets[0], gate))
     p_got = move(got, every, lambda r, z: (r ^ 1, z))
     p_far = move(far, every, lambda r, z: (r ^ 1, z))
     rights = (right, got, p_got, far, p_far)
@@ -444,17 +470,16 @@
             left, _ = lax.optimization_barrier((lefts[len(mets)], part))
             mets.append(move(left, every, lambda r, z: (r, z ^ 1)))
 
-    own, gate = pl.pallas_call(
+    own = pl.pallas_call(
         functools.partial(keep_body, cuts),
-        out_shape=[jax.ShapeDtypeStruct((own_i, own_j, tri), f32),
-                   jax.ShapeDtypeStruct((own_i, own_j, chans), f32)],
-        in_specs=[VMEM] * (5 + 2 * cuts + 2),
-        out_specs=[VMEM] * 2,
+        out_shape=jax.ShapeDtypeStruct((own_i, own_j, tri), f32),
+        in_specs=[VMEM] * (5 + 2 * cuts),
+        out_specs=VMEM,
         scratch_shapes=[pltpu.VMEM((own_i, 2 * own_j, tri), f32)],
         compiler_params=limit(12),
         cost_estimate=cost(6),
         name="keep_sums",
-    )(*rights, *lefts, *mets, norm, w_gate)
+    )(*rights, *lefts, *mets)
     out = []
     for first, n in ((0, 16), (16, own_i - 16)):
         parts = sums[first // 8 : (first + n) // 8]

time: 53 us -> 52.9 us (level)
    pallas_call x1 -> x2, Pallas kernels: 5.36 us -> 5.38 us  [the longest x1 5.12 us: paired_plan(): pl.pallas_call(functools.partial(keep_body, cuts), out_shape=jax.ShapeDty...]
  transfers between devices with their start and end apart: 15 -> 15, of which waited for: 8 -> 9; matrix products, arithmetic and copies ran while one was open for 0% -> 0% of each run, Pallas kernels for 25% -> 26%
where the time goes in v10:
time: 52.9 us; the launch traced here: 52.8 us
  Pallas kernels  19.2 us (36%)
  starting transfers between devices  17.7 us (33%)
  waiting for transfers between devices  15.6 us (29%)
    ppermute x12, starting transfers between devices, move(): return lax.ppermute(value, ('row', 'col'), pairs)  14.6 us
    ppermute x12, waiting for transfers between devices, move(): return lax.ppermute(value, ('row', 'col'), pairs)  14.1 us
    pallas_call x5, Pallas kernels, paired_plan(): pl.pallas_call(functools.partial(send_body, first), out_shape=jax.ShapeDt...  5.2 us
    pallas_call x1, Pallas kernels, paired_plan(): pl.pallas_call(functools.partial(keep_body, cuts), out_shape=jax.ShapeDty...  5.12 us
    ppermute x3, starting transfers between devices, shards(): lax.ppermute(msgs[d], 'row', [(r, r ^ d) for r in range(rows)])  3.12 us
    pallas_call x1, Pallas kernels, shards(): pl.pallas_call(functools.partial(pair_body, own_seqs, width, rows, paired...  3.09 us
    pallas_call x2, Pallas kernels, paired_plan(): pl.pallas_call(functools.partial(join_body, first, len(parts)), out_shape...  2.22 us
    pallas_call x1, Pallas kernels, shards(): pl.pallas_call(functools.partial(prepare_body, own_seqs), out_shape=[jax....  1.51 us
  transfers between devices with their start and end apart: 15, of which 9 were waited for; matrix products, arithmetic and copies ran while one was open for 0% of the time, Pallas kernels for 26%

profile of v10, /device:TPU:0, one launch (start us, length us, event | category | flops | bytes accessed | tf_op | source)
XLA Modules:
  0.0 52.8 jit_solution(4376477914727985405)
XLA Ops:
  0.0 1.5 %align.1 = (bf16[48,128]{1,0:T(8,128)(2,1)S(1)}, bf16[48,128]{1,0:T(8,128)(2,1)S(1)}, bf16[48,128]{1,0:T(8,128)(2,1)S(1)}, bf16[48,128]{1,0:T(8,128)(2,1)S(1)}, ...) custom-call(bf16[2,160,256]{2,1,0:T(8,128)(2,1)} %x_hbm.1, ...), custom_call_target="tpu_custom_call" | custom-call | bytes 5535000 | tf_op jit(solution)/shard_map/align/pallas_call | solution.py:513
  1.5 2.4 %collective-permute-start = (bf16[48,128]{1,0:T(8,128)(2,1)S(1)}, bf16[48,128]{1,0:T(8,128)(2,1)S(1)}, u32[]{:S(2)}, u32[]{:S(2)}) collective-permute-start(bf16[48,128]{1,0:T(8,128)(2,1)S(1)} %get-tuple-element.29), channel_id=1, source_target_pairs={{0,12},{4,8},{8,4},{12,0},{1,13},{5,9},{9,5},{13,1},{2,14},{6,10},... | collective-permute-start | bytes 36872 | tf_op jit(solution)/shard_map/ppermute | solution.py:530
  3.9 0.6 %collective-permute-start.1 = (bf16[48,128]{1,0:T(8,128)(2,1)S(1)}, bf16[48,128]{1,0:T(8,128)(2,1)S(1)}, u32[]{:S(2)}, u32[]{:S(2)}) collective-permute-start(bf16[48,128]{1,0:T(8,128)(2,1)S(1)} %get-tuple-element.30), channel_id=1, source_target_pairs={{0,8},{4,12},{8,0},{12,4},{1,9},{5,13},{9,1},{13,5},{2,10},{6,14},... | collective-permute-start | bytes 36872 | tf_op jit(solution)/shard_map/ppermute | solution.py:530
  4.6 0.0 collective-permute-start.2
  4.6 0.0 copy-start
  4.6 1.5 %prepare.1 = (f32[40,40,128]{2,1,0:T(8,128)S(1)}, bf16[40,40,128]{2,1,0:T(8,128)(2,1)S(1)}, bf16[16,32,256]{2,1,0:T(8,128)(2,1)S(1)}, bf16[4,128,256]{2,1,0:T(8,128)(2,1)S(1)}) custom-call(bf16[40,40,128]{2,1,0:T(8,128)(2,1)S(1)} %get-tuple-element.32.couple_ref, s32[160]{0:T(256)} %ids_hbm.1, s32[40,40]{1,0:T(8,128)S(1)} %get-tuple-element.33.valid_ref, ...), custom_call_target="tpu_custom_call" | custom-call | bytes 7380000 | tf_op jit(solution)/shard_map/prepare/pallas_call | solution.py:534
  6.1 0.0 collective-permute-done.refs_1_
  6.1 1.5 %collective-permute-done.1.refs_2_ = bf16[48,128]{1,0:T(8,128)(2,1)S(1)} collective-permute-done((bf16[48,128]{1,0:T(8,128)(2,1)S(1)}, bf16[48,128]{1,0:T(8,128)(2,1)S(1)}, u32[]{:S(2)}, u32[]{:S(2)}) %collective-permute-start.1) | collective-permute-done | bytes 12320 | tf_op jit(solution)/shard_map/ppermute | solution.py:530
  7.6 0.0 collective-permute-done.2.refs_3_
  7.6 0.0 copy-done
  7.6 3.1 %pair.1 = (bf16[40,40,128]{2,1,0:T(8,128)(2,1)S(1)}, bf16[1600,128]{1,0:T(8,128)(2,1)S(1)}, bf16[40,40,128]{2,1,0:T(8,128)(2,1)S(1)}) custom-call(bf16[48,128]{1,0:T(8,128)(2,1)S(1)} %get-tuple-element.28.refs_0_, bf16[48,128]{1,0:T(8,128)(2,1)S(1)} %collective-permute-done.refs_1_, bf16[48,128]{1,0:T(8,128)(2,1)S(1)} %collective-permute-done.1.refs_2_, ...), custom_call_target="tpu_custom_call" | custom-call | bytes 16605000 | tf_op jit(solution)/shard_map/pair/pallas_call | solution.py:554
  10.7 0.7 %collective-permute-start.3 = (bf16[40,40,128]{2,1,0:T(8,128)(2,1)S(1)}, bf16[40,40,128]{2,1,0:T(8,128)(2,1)S(1)}, u32[]{:S(2)}, u32[]{:S(2)}) collective-permute-start(bf16[40,40,128]{2,1,0:T(8,128)(2,1)S(1)} %get-tuple-element.40.refs_0_), channel_id=1, source_target_pairs={{0,8},{1,4},{2,10},{3,6},{4,1},{5,13},{6,3},{7,15},{8,0},{9,12},{1... | collective-permute-start | bytes 1228808 | tf_op jit(solution)/shard_map/ppermute | solution.py:434
  11.4 1.0 %collective-permute-start.4 = (bf16[40,40,128]{2,1,0:T(8,128)(2,1)S(1)}, bf16[40,40,128]{2,1,0:T(8,128)(2,1)S(1)}, u32[]{:S(2)}, u32[]{:S(2)}) collective-permute-start(bf16[40,40,128]{2,1,0:T(8,128)(2,1)S(1)} %get-tuple-element.40.refs_0_), channel_id=1, source_target_pairs={{0,4},{1,8},{2,6},{3,10},{4,13},{5,1},{6,15},{7,3},{8,12},{9,0},{1... | collective-permute-start | bytes 1228808 | tf_op jit(solution)/shard_map/ppermute | solution.py:434
  12.5 0.0 copy-start.2
  12.5 0.4 left.1
  12.8 1.9 %collective-permute-start.5 = (bf16[8,40,128]{2,1,0:T(8,128)(2,1)S(1)}, bf16[8,40,128]{2,1,0:T(8,128)(2,1)S(1)}, u32[]{:S(2)}, u32[]{:S(2)}) collective-permute-start(bf16[8,40,128]{2,1,0:T(8,128)(2,1)S(1)} %get-tuple-element.42.refs_5_), channel_id=1, source_target_pairs={{0,1},{1,0},{2,3},{3,2},{4,5},{5,4},{6,7},{7,6},{8,9},{9,8},{10,11... | collective-permute-start | bytes 245768 | tf_op jit(solution)/shard_map/ppermute | solution.py:434
  14.7 0.0 copy-done.2
  14.7 0.3 gate.1.gate_ref
  15.0 9.4 %collective-permute-done.5.refs_6_.refs_8_ = bf16[8,40,128]{2,1,0:T(8,128)(2,1)S(1)} collective-permute-done((bf16[8,40,128]{2,1,0:T(8,128)(2,1)S(1)}, bf16[8,40,128]{2,1,0:T(8,128)(2,1)S(1)}, u32[]{:S(2)}, u32[]{:S(2)}) %collective-permute-start.5) | collective-permute-done | bytes 81952 | tf_op jit(solution)/shard_map/ppermute | solution.py:434
  24.4 0.0 collective-permute-done.3.refs_1_
  24.4 0.0 collective-permute-done.4.refs_3_
  24.4 0.0 collective-permute-start.6
  24.4 0.5 collective-permute-start.7
  25.0 0.8 %collective-permute-start.8 = (bf16[16,40,128]{2,1,0:T(8,128)(2,1)S(1)}, bf16[16,40,128]{2,1,0:T(8,128)(2,1)S(1)}, u32[]{:S(2)}, u32[]{:S(2)}) collective-permute-start(bf16[16,40,128]{2,1,0:T(8,128)(2,1)S(1)} %get-tuple-element.45.refs_6_.refs_5_), channel_id=1, source_target_pairs={{0,1},{1,0},{2,3},{3,2},{4,5},{5,4},{6,7},{7,6},{8,9},{9,8},{10,11... | collective-permute-start | bytes 491528 | tf_op jit(solution)/shard_map/ppermute | solution.py:434
  25.8 0.4 collective-permute-done.6.refs_2_
  26.2 0.6 %collective-permute-done.7.refs_4_ = bf16[40,40,128]{2,1,0:T(8,128)(2,1)S(1)} collective-permute-done((bf16[40,40,128]{2,1,0:T(8,128)(2,1)S(1)}, bf16[40,40,128]{2,1,0:T(8,128)(2,1)S(1)}, u32[]{:S(2)}, u32[]{:S(2)}) %collective-permute-start.7) | collective-permute-done | bytes 409632 | tf_op jit(solution)/shard_map/ppermute | solution.py:434
  26.8 1.0 %send_sums.5 = bf16[8,40,128]{2,1,0:T(8,128)(2,1)S(1)} custom-call(bf16[40,40,128]{2,1,0:T(8,128)(2,1)S(1)} %get-tuple-element.40.refs_0_, bf16[40,40,128]{2,1,0:T(8,128)(2,1)S(1)} %collective-permute-done.3.refs_1_, bf16[40,40,128]{2,1,0:T(8,128)(2,1)S(1)} %collective-permute-done.6.refs_2_, bf16[40,40,128]{2,1,0:T(8,128)(2,1)S(1)} %collective-permute-done.4.refs_3_, ...), custom_call_target="tpu_custom_call" | custom-call | bytes 5018400 | tf_op jit(solution)/shard_map/send_sums/pallas_call | solution.py:458
  27.8 1.0 %collective-permute-start.9 = (bf16[16,40,128]{2,1,0:T(8,128)(2,1)S(1)}, bf16[16,40,128]{2,1,0:T(8,128)(2,1)S(1)}, u32[]{:S(2)}, u32[]{:S(2)}) collective-permute-start(bf16[16,40,128]{2,1,0:T(8,128)(2,1)S(1)} %get-tuple-element.48.refs_7_.refs_5_), channel_id=1, source_target_pairs={{0,1},{1,0},{2,3},{3,2},{4,5},{5,4},{6,7},{7,6},{8,9},{9,8},{10,11... | collective-permute-start | bytes 491528 | tf_op jit(solution)/shard_map/ppermute | solution.py:434
  28.8 2.6 %collective-permute-start.13 = (bf16[8,40,128]{2,1,0:T(8,128)(2,1)S(1)}, bf16[8,40,128]{2,1,0:T(8,128)(2,1)S(1)}, u32[]{:S(2)}, u32[]{:S(2)}) collective-permute-start(bf16[8,40,128]{2,1,0:T(8,128)(2,1)S(1)} %send_sums.5), channel_id=1, source_target_pairs={{0,2},{1,3},{2,0},{3,1},{4,6},{5,7},{6,4},{7,5},{8,10},{9,11},{10,... | collective-permute-start | bytes 245768 | tf_op jit(solution)/shard_map/ppermute | solution.py:434
  31.4 0.2 collective-permute-done.8.refs_9_.refs_6_
  31.6 1.0 %send_sums.9 = bf16[8,40,128]{2,1,0:T(8,128)(2,1)S(1)} custom-call(bf16[40,40,128]{2,1,0:T(8,128)(2,1)S(1)} %get-tuple-element.40.refs_0_, bf16[40,40,128]{2,1,0:T(8,128)(2,1)S(1)} %collective-permute-done.3.refs_1_, bf16[40,40,128]{2,1,0:T(8,128)(2,1)S(1)} %collective-permute-done.6.refs_2_, bf16[40,40,128]{2,1,0:T(8,128)(2,1)S(1)} %collective-permute-done.4.refs_3_, ...), custom_call_target="tpu_custom_call" | custom-call | bytes 5018400 | tf_op jit(solution)/shard_map/send_sums/pallas_call | solution.py:458
  32.6 2.7 %collective-permute-start.14 = (bf16[8,40,128]{2,1,0:T(8,128)(2,1)S(1)}, bf16[8,40,128]{2,1,0:T(8,128)(2,1)S(1)}, u32[]{:S(2)}, u32[]{:S(2)}) collective-permute-start(bf16[8,40,128]{2,1,0:T(8,128)(2,1)S(1)} %send_sums.9), channel_id=1, source_target_pairs={{0,2},{1,3},{2,0},{3,1},{4,6},{5,7},{6,4},{7,5},{8,10},{9,11},{10,... | collective-permute-start | bytes 245768 | tf_op jit(solution)/shard_map/ppermute | solution.py:434
  35.3 1.0 %send_sums.6 = bf16[8,40,128]{2,1,0:T(8,128)(2,1)S(1)} custom-call(bf16[40,40,128]{2,1,0:T(8,128)(2,1)S(1)} %get-tuple-element.40.refs_0_, bf16[40,40,128]{2,1,0:T(8,128)(2,1)S(1)} %collective-permute-done.3.refs_1_, bf16[40,40,128]{2,1,0:T(8,128)(2,1)S(1)} %collective-permute-done.6.refs_2_, bf16[40,40,128]{2,1,0:T(8,128)(2,1)S(1)} %collective-permute-done.4.refs_3_, ...), custom_call_target="tpu_custom_call" | custom-call | bytes 5018400 | tf_op jit(solution)/shard_map/send_sums/pallas_call | solution.py:458
  36.3 0.4 collective-permute-start.10
  36.7 0.6 %collective-permute-done.9.refs_10_.refs_6_ = bf16[16,40,128]{2,1,0:T(8,128)(2,1)S(1)} collective-permute-done((bf16[16,40,128]{2,1,0:T(8,128)(2,1)S(1)}, bf16[16,40,128]{2,1,0:T(8,128)(2,1)S(1)}, u32[]{:S(2)}, u32[]{:S(2)}) %collective-permute-start.9) | collective-permute-done | bytes 163872 | tf_op jit(solution)/shard_map/ppermute | solution.py:434
  37.3 1.0 %send_sums.7 = bf16[8,40,128]{2,1,0:T(8,128)(2,1)S(1)} custom-call(bf16[40,40,128]{2,1,0:T(8,128)(2,1)S(1)} %get-tuple-element.40.refs_0_, bf16[40,40,128]{2,1,0:T(8,128)(2,1)S(1)} %collective-permute-done.3.refs_1_, bf16[40,40,128]{2,1,0:T(8,128)(2,1)S(1)} %collective-permute-done.6.refs_2_, bf16[40,40,128]{2,1,0:T(8,128)(2,1)S(1)} %collective-permute-done.4.refs_3_, ...), custom_call_target="tpu_custom_call" | custom-call | bytes 5018400 | tf_op jit(solution)/shard_map/send_sums/pallas_call | solution.py:458
  38.3 2.1 %collective-permute-start.11 = (bf16[8,40,128]{2,1,0:T(8,128)(2,1)S(1)}, bf16[8,40,128]{2,1,0:T(8,128)(2,1)S(1)}, u32[]{:S(2)}, u32[]{:S(2)}) collective-permute-start(bf16[8,40,128]{2,1,0:T(8,128)(2,1)S(1)} %send_sums.7), channel_id=1, source_target_pairs={{0,2},{1,3},{2,0},{3,1},{4,6},{5,7},{6,4},{7,5},{8,10},{9,11},{10,... | collective-permute-start | bytes 245768 | tf_op jit(solution)/shard_map/ppermute | solution.py:434
  40.4 1.0 %send_sums.8 = bf16[8,40,128]{2,1,0:T(8,128)(2,1)S(1)} custom-call(bf16[40,40,128]{2,1,0:T(8,128)(2,1)S(1)} %get-tuple-element.40.refs_0_, bf16[40,40,128]{2,1,0:T(8,128)(2,1)S(1)} %collective-permute-done.3.refs_1_, bf16[40,40,128]{2,1,0:T(8,128)(2,1)S(1)} %collective-permute-done.6.refs_2_, bf16[40,40,128]{2,1,0:T(8,128)(2,1)S(1)} %collective-permute-done.4.refs_3_, ...), custom_call_target="tpu_custom_call" | custom-call | bytes 5018400 | tf_op jit(solution)/shard_map/send_sums/pallas_call | solution.py:458
  41.5 0.0 copy-start.1
  41.5 1.0 %collective-permute-start.12 = (bf16[8,40,128]{2,1,0:T(8,128)(2,1)S(1)}, bf16[8,40,128]{2,1,0:T(8,128)(2,1)S(1)}, u32[]{:S(2)}, u32[]{:S(2)}) collective-permute-start(bf16[8,40,128]{2,1,0:T(8,128)(2,1)S(1)} %send_sums.8), channel_id=1, source_target_pairs={{0,2},{1,3},{2,0},{3,1},{4,6},{5,7},{6,4},{7,5},{8,10},{9,11},{10,... | collective-permute-start | bytes 245768 | tf_op jit(solution)/shard_map/ppermute | solution.py:434
  42.4 5.1 %keep_sums.1.own_ref = f32[40,40,128]{2,1,0:T(8,128)S(1)} custom-call(bf16[40,40,128]{2,1,0:T(8,128)(2,1)S(1)} %get-tuple-element.40.refs_0_, bf16[40,40,128]{2,1,0:T(8,128)(2,1)S(1)} %collective-permute-done.3.refs_1_, bf16[40,40,128]{2,1,0:T(8,128)(2,1)S(1)} %collective-permute-done.6.refs_2_, bf16[40,40,128]{2,1,0:T(8,128)(2,1)S(1)} %collective-permute-done.4.refs_3_, ...), custom_call_target="tpu_custom_call" | custom-call | bytes 22140000 | tf_op jit(solution)/shard_map/keep_sums/pallas_call | solution.py:473
  47.6 0.0 collective-permute-done.13.refs_0_
  47.6 0.0 collective-permute-done.14.refs_1_
  47.6 0.0 copy-done.1
  47.6 1.1 %join.2.refs_3_ = bf16[40,40,128]{2,1,0:T(8,128)(2,1)} custom-call(f32[40,40,128]{2,1,0:T(8,128)S(1)} %keep_sums.1.own_ref, bf16[40,40,128]{2,1,0:T(8,128)(2,1)S(1)} %get-tuple-element.49.psum_ref, f32[40,40,128]{2,1,0:T(8,128)S(1)} %gate.1.gate_ref, bf16[128,128]{1,0:T(8,128)(2,1)S(1)} %copy-done.1, ...), custom_call_target="tpu_custom_call" | custom-call | bytes 3542400 | tf_op jit(solution)/shard_map/join/pallas_call | solution.py:486
  48.7 0.2 collective-permute-done.10.refs_0_
  48.9 1.8 %collective-permute-done.11.refs_1_ = bf16[8,40,128]{2,1,0:T(8,128)(2,1)S(1)} collective-permute-done((bf16[8,40,128]{2,1,0:T(8,128)(2,1)S(1)}, bf16[8,40,128]{2,1,0:T(8,128)(2,1)S(1)}, u32[]{:S(2)}, u32[]{:S(2)}) %collective-permute-start.11) | collective-permute-done | bytes 81952 | tf_op jit(solution)/shard_map/ppermute | solution.py:434
  50.6 1.0 %collective-permute-done.12.refs_2_ = bf16[8,40,128]{2,1,0:T(8,128)(2,1)S(1)} collective-permute-done((bf16[8,40,128]{2,1,0:T(8,128)(2,1)S(1)}, bf16[8,40,128]{2,1,0:T(8,128)(2,1)S(1)}, u32[]{:S(2)}, u32[]{:S(2)}) %collective-permute-start.12) | collective-permute-done | bytes 81952 | tf_op jit(solution)/shard_map/ppermute | solution.py:434
  51.6 1.2 %join.3 = bf16[40,40,128]{2,1,0:T(8,128)(2,1)} custom-call(f32[40,40,128]{2,1,0:T(8,128)S(1)} %keep_sums.1.own_ref, bf16[40,40,128]{2,1,0:T(8,128)(2,1)S(1)} %get-tuple-element.49.psum_ref, f32[40,40,128]{2,1,0:T(8,128)S(1)} %gate.1.gate_ref, bf16[128,128]{1,0:T(8,128)(2,1)S(1)} %copy-done.1, ...), custom_call_target="tpu_custom_call", output_to_operand_aliasing={{}: (7, {})} | custom-call | bytes 5313600 | tf_op jit(solution)/shard_map/join/pallas_call | solution.py:486
Async XLA Ops:
  1.5 4.6 %collective-permute-start = (bf16[48,128]{1,0:T(8,128)(2,1)S(1)}, bf16[48,128]{1,0:T(8,128)(2,1)S(1)}, u32[]{:S(2)}, u32[]{:S(2)}) collective-permute-start(bf16[48,128]{1,0:T(8,128)(2,1)S(1)} %get-tuple-element.29), channel_id=1, source_target_pairs={{0,12},{4,8},{8,4},{12,0},{1,13},{5,9},{9,5},{13,1},{2,14},{6,10},... | collective-permute-start | bytes 36872 | tf_op jit(solution)/shard_map/ppermute | solution.py:530
  3.9 3.7 %collective-permute-start.1 = (bf16[48,128]{1,0:T(8,128)(2,1)S(1)}, bf16[48,128]{1,0:T(8,128)(2,1)S(1)}, u32[]{:S(2)}, u32[]{:S(2)}) collective-permute-start(bf16[48,128]{1,0:T(8,128)(2,1)S(1)} %get-tuple-element.30), channel_id=1, source_target_pairs={{0,8},{4,12},{8,0},{12,4},{1,9},{5,13},{9,1},{13,5},{2,10},{6,14},... | collective-permute-start | bytes 36872 | tf_op jit(solution)/shard_map/ppermute | solution.py:530
  4.6 3.1 %collective-permute-start.2 = (bf16[48,128]{1,0:T(8,128)(2,1)S(1)}, bf16[48,128]{1,0:T(8,128)(2,1)S(1)}, u32[]{:S(2)}, u32[]{:S(2)}) collective-permute-start(bf16[48,128]{1,0:T(8,128)(2,1)S(1)} %get-tuple-element.31), channel_id=1, source_target_pairs={{0,4},{4,0},{8,12},{12,8},{1,5},{5,1},{9,13},{13,9},{2,6},{6,2},{1... | collective-permute-start | bytes 36872 | tf_op jit(solution)/shard_map/ppermute | solution.py:530
  4.6 3.0 %copy-start = (bf16[128,512]{1,0:T(8,128)(2,1)S(1)}, bf16[128,512]{1,0:T(8,128)(2,1)}, u32[]{:S(2)}) copy-start(bf16[128,512]{1,0:T(8,128)(2,1)} %win_ref.1) | copy-start | bytes 393220
  10.7 13.7 %collective-permute-start.3 = (bf16[40,40,128]{2,1,0:T(8,128)(2,1)S(1)}, bf16[40,40,128]{2,1,0:T(8,128)(2,1)S(1)}, u32[]{:S(2)}, u32[]{:S(2)}) collective-permute-start(bf16[40,40,128]{2,1,0:T(8,128)(2,1)S(1)} %get-tuple-element.40.refs_0_), channel_id=1, source_target_pairs={{0,8},{1,4},{2,10},{3,6},{4,1},{5,13},{6,3},{7,15},{8,0},{9,12},{1... | collective-permute-start | bytes 1228808 | tf_op jit(solution)/shard_map/ppermute | solution.py:434
  11.4 13.0 %collective-permute-start.4 = (bf16[40,40,128]{2,1,0:T(8,128)(2,1)S(1)}, bf16[40,40,128]{2,1,0:T(8,128)(2,1)S(1)}, u32[]{:S(2)}, u32[]{:S(2)}) collective-permute-start(bf16[40,40,128]{2,1,0:T(8,128)(2,1)S(1)} %get-tuple-element.40.refs_0_), channel_id=1, source_target_pairs={{0,4},{1,8},{2,6},{3,10},{4,13},{5,1},{6,15},{7,3},{8,12},{9,0},{1... | collective-permute-start | bytes 1228808 | tf_op jit(solution)/shard_map/ppermute | solution.py:434
  12.5 2.2 %copy-start.2 = (bf16[128,128]{1,0:T(8,128)(2,1)S(1)}, bf16[128,128]{1,0:T(8,128)(2,1)}, u32[]{:S(2)}) copy-start(bf16[128,128]{1,0:T(8,128)(2,1)} %wgate_ref.1) | copy-start | bytes 98308
  12.8 11.6 %collective-permute-start.5 = (bf16[8,40,128]{2,1,0:T(8,128)(2,1)S(1)}, bf16[8,40,128]{2,1,0:T(8,128)(2,1)S(1)}, u32[]{:S(2)}, u32[]{:S(2)}) collective-permute-start(bf16[8,40,128]{2,1,0:T(8,128)(2,1)S(1)} %get-tuple-element.42.refs_5_), channel_id=1, source_target_pairs={{0,1},{1,0},{2,3},{3,2},{4,5},{5,4},{6,7},{7,6},{8,9},{9,8},{10,11... | collective-permute-start | bytes 245768 | tf_op jit(solution)/shard_map/ppermute | solution.py:434
  24.4 1.7 %collective-permute-start.6 = (bf16[40,40,128]{2,1,0:T(8,128)(2,1)S(1)}, bf16[40,40,128]{2,1,0:T(8,128)(2,1)S(1)}, u32[]{:S(2)}, u32[]{:S(2)}) collective-permute-start(bf16[40,40,128]{2,1,0:T(8,128)(2,1)S(1)} %collective-permute-done.3.refs_1_), channel_id=1, source_target_pairs={{0,4},{1,5},{2,6},{3,7},{4,0},{5,1},{6,2},{7,3},{8,12},{9,13},{10,... | collective-permute-start | bytes 1228808 | tf_op jit(solution)/shard_map/ppermute | solution.py:434
  24.4 2.3 %collective-permute-start.7 = (bf16[40,40,128]{2,1,0:T(8,128)(2,1)S(1)}, bf16[40,40,128]{2,1,0:T(8,128)(2,1)S(1)}, u32[]{:S(2)}, u32[]{:S(2)}) collective-permute-start(bf16[40,40,128]{2,1,0:T(8,128)(2,1)S(1)} %collective-permute-done.4.refs_3_), channel_id=1, source_target_pairs={{0,4},{1,5},{2,6},{3,7},{4,0},{5,1},{6,2},{7,3},{8,12},{9,13},{10,... | collective-permute-start | bytes 1228808 | tf_op jit(solution)/shard_map/ppermute | solution.py:434
  25.0 6.6 %collective-permute-start.8 = (bf16[16,40,128]{2,1,0:T(8,128)(2,1)S(1)}, bf16[16,40,128]{2,1,0:T(8,128)(2,1)S(1)}, u32[]{:S(2)}, u32[]{:S(2)}) collective-permute-start(bf16[16,40,128]{2,1,0:T(8,128)(2,1)S(1)} %get-tuple-element.45.refs_6_.refs_5_), channel_id=1, source_target_pairs={{0,1},{1,0},{2,3},{3,2},{4,5},{5,4},{6,7},{7,6},{8,9},{9,8},{10,11... | collective-permute-start | bytes 491528 | tf_op jit(solution)/shard_map/ppermute | solution.py:434
  27.8 9.5 %collective-permute-start.9 = (bf16[16,40,128]{2,1,0:T(8,128)(2,1)S(1)}, bf16[16,40,128]{2,1,0:T(8,128)(2,1)S(1)}, u32[]{:S(2)}, u32[]{:S(2)}) collective-permute-start(bf16[16,40,128]{2,1,0:T(8,128)(2,1)S(1)} %get-tuple-element.48.refs_7_.refs_5_), channel_id=1, source_target_pairs={{0,1},{1,0},{2,3},{3,2},{4,5},{5,4},{6,7},{7,6},{8,9},{9,8},{10,11... | collective-permute-start | bytes 491528 | tf_op jit(solution)/shard_map/ppermute | solution.py:434
  28.8 18.8 %collective-permute-start.13 = (bf16[8,40,128]{2,1,0:T(8,128)(2,1)S(1)}, bf16[8,40,128]{2,1,0:T(8,128)(2,1)S(1)}, u32[]{:S(2)}, u32[]{:S(2)}) collective-permute-start(bf16[8,40,128]{2,1,0:T(8,128)(2,1)S(1)} %send_sums.5), channel_id=1, source_target_pairs={{0,2},{1,3},{2,0},{3,1},{4,6},{5,7},{6,4},{7,5},{8,10},{9,11},{10,... | collective-permute-start | bytes 245768 | tf_op jit(solution)/shard_map/ppermute | solution.py:434
  32.6 15.0 %collective-permute-start.14 = (bf16[8,40,128]{2,1,0:T(8,128)(2,1)S(1)}, bf16[8,40,128]{2,1,0:T(8,128)(2,1)S(1)}, u32[]{:S(2)}, u32[]{:S(2)}) collective-permute-start(bf16[8,40,128]{2,1,0:T(8,128)(2,1)S(1)} %send_sums.9), channel_id=1, source_target_pairs={{0,2},{1,3},{2,0},{3,1},{4,6},{5,7},{6,4},{7,5},{8,10},{9,11},{10,... | collective-permute-start | bytes 245768 | tf_op jit(solution)/shard_map/ppermute | solution.py:434
  36.3 12.5 %collective-permute-start.10 = (bf16[8,40,128]{2,1,0:T(8,128)(2,1)S(1)}, bf16[8,40,128]{2,1,0:T(8,128)(2,1)S(1)}, u32[]{:S(2)}, u32[]{:S(2)}) collective-permute-start(bf16[8,40,128]{2,1,0:T(8,128)(2,1)S(1)} %send_sums.6), channel_id=1, source_target_pairs={{0,2},{1,3},{2,0},{3,1},{4,6},{5,7},{6,4},{7,5},{8,10},{9,11},{10,... | collective-permute-start | bytes 245768 | tf_op jit(solution)/shard_map/ppermute | solution.py:434
  38.3 12.3 %collective-permute-start.11 = (bf16[8,40,128]{2,1,0:T(8,128)(2,1)S(1)}, bf16[8,40,128]{2,1,0:T(8,128)(2,1)S(1)}, u32[]{:S(2)}, u32[]{:S(2)}) collective-permute-start(bf16[8,40,128]{2,1,0:T(8,128)(2,1)S(1)} %send_sums.7), channel_id=1, source_target_pairs={{0,2},{1,3},{2,0},{3,1},{4,6},{5,7},{6,4},{7,5},{8,10},{9,11},{10,... | collective-permute-start | bytes 245768 | tf_op jit(solution)/shard_map/ppermute | solution.py:434
  41.5 6.1 %copy-start.1 = (bf16[128,128]{1,0:T(8,128)(2,1)S(1)}, bf16[128,128]{1,0:T(8,128)(2,1)}, u32[]{:S(2)}) copy-start(bf16[128,128]{1,0:T(8,128)(2,1)} %w_ref.3) | copy-start | bytes 98308
  41.5 10.1 %collective-permute-start.12 = (bf16[8,40,128]{2,1,0:T(8,128)(2,1)S(1)}, bf16[8,40,128]{2,1,0:T(8,128)(2,1)S(1)}, u32[]{:S(2)}, u32[]{:S(2)}) collective-permute-start(bf16[8,40,128]{2,1,0:T(8,128)(2,1)S(1)} %send_sums.8), channel_id=1, source_target_pairs={{0,2},{1,3},{2,0},{3,1},{4,6},{5,7},{6,4},{7,5},{8,10},{9,11},{10,... | collective-permute-start | bytes 245768 | tf_op jit(solution)/shard_map/ppermute | solution.py:434

commit v11 on v9

--- a/solution.py
+++ b/solution.py
@@ -125,11 +125,11 @@
     lax.fori_loop(0, own_i, rows, 0, unroll=8)
 
 
-def pair_body(seqs, width, blocks, turned, *refs):
+def pair_body(seqs, width, blocks, *refs):
     msgs = refs[:blocks]
     base_ref, mask_ref, wq_ref, pick_ref, win_ref = refs[blocks : blocks + 5]
     psum_ref, norm_ref, right_ref = refs[blocks + 5 : blocks + 8]
-    xl_ref, t_ref, flat_ref = refs[blocks + 8 :]
+    xl_ref, t_ref = refs[blocks + 8 :]
     own_i, own_j, chans = base_ref.shape
     height, lanes = msgs[0].shape
     total = seqs * blocks
@@ -156,7 +156,7 @@
         t_ref[:, where, chans:] = block[half:]
         return carry
 
-    lax.fori_loop(0, width // 2, expand, 0, unroll=16 if turned else 4)
+    lax.fori_loop(0, width // 2, expand, 0)
 
     step = 4 if half % 4 == 0 else 1
 
@@ -179,20 +179,10 @@
             norm_ref[pl.ds(pl.multiple_of(i0 * own_j, 16), count), :] = flat[cut]
             mask = mask_ref[pl.ds(i0, step)].astype(f32).reshape(count, tri)
             right = mask * sigmoid(proj[cut, :tri]) * proj[cut, tri:]
-            if turned:
-                flat_ref[pl.ds(pl.multiple_of(i0 * own_j, 8), count), :] = right
-            else:
-                right_ref[pl.ds(i0, step)] = right.reshape(step, own_j, tri).astype(bf16)
-        return carry
-
-    lax.fori_loop(0, half // step, rows, 0, unroll=True)
-
-    def turn(k, carry):
-        right_ref[k] = flat_ref[pl.ds(k, own_i, stride=own_j), :].astype(bf16)
-        return carry
-
-    if turned:
-        lax.fori_loop(0, own_j, turn, 0, unroll=8)
+            right_ref[pl.ds(i0, step)] = right.reshape(step, own_j, tri).astype(bf16)
+        return carry
+
+    lax.fori_loop(0, half // step, rows, 0)
 
 
 def left_body(norm_ref, mask_ref, win_ref, *outs):
@@ -234,71 +224,199 @@
     return acc
 
 
-def with_right(own_pair, refs, use):
-    own, got, p_got, far, p_far = refs
-    r, z = lax.axis_index("row"), lax.axis_index("col")
-    keeper = (r % 2) == (z % 2)
-    near = ((r // 2) == (z // 2)) == own_pair
-    table = [
-        (near & keeper, own, p_got),
-        (near & ~keeper, far, got),
-        (~near & keeper, got, far),
-        (~near & ~keeper, p_got, p_far),
-    ]
-    for cond, a, b in table:
-        pl.when(cond)(functools.partial(use, (a, b)))
-
-
-def send_body(first, *refs):
-    rights, (l_ref, m_ref, o_ref, lf_ref) = refs[:5], refs[5:]
+def sums_body(first, right0_ref, right1_ref, l_ref, m_ref, o_ref, lf_ref):
     count, depth = o_ref.shape[0], l_ref.shape[1]
     group = 8
     lf_ref[:, pl.ds(0, depth), :] = l_ref[pl.ds(first, count)].astype(f32)
     lf_ref[:, pl.ds(depth, depth), :] = m_ref[pl.ds(first, count)].astype(f32)
 
-    def use(halves):
-        def rows(b, carry):
-            acc = contract(lf_ref, halves, b * group, group)
-            for t in range(group):
-                o_ref[b * group + t] = acc[t].astype(bf16)
-            return carry
-
-        lax.fori_loop(0, count // group, rows, 0)
-
-    with_right(False, rights, use)
-
-
-def keep_body(cuts, *refs):
-    rights, refs = refs[:5], refs[5:]
-    lefts, mets = refs[:cuts], refs[cuts : 2 * cuts]
-    norm_ref, wgate_ref, o_ref, gate_ref, lf_ref = refs[2 * cuts :]
-    own_i, depth, chans = o_ref.shape
-    at = 0
-    for l_ref, m_ref in zip(lefts, mets):
-        n = l_ref.shape[0]
-        lf_ref[pl.ds(at, n), pl.ds(0, depth), :] = l_ref[...].astype(f32)
-        lf_ref[pl.ds(at, n), pl.ds(depth, depth), :] = m_ref[...].astype(f32)
-        at += n
-    group = 8
-
-    def gates(b, carry):
-        flat = norm_ref[pl.ds(pl.multiple_of(b * group * depth, 16), group * depth), :]
+    def rows(b, carry):
+        acc = contract(lf_ref, (right0_ref, right1_ref), b * group, group)
+        for t in range(group):
+            o_ref[b * group + t] = acc[t].astype(o_ref.dtype)
+        return carry
+
+    lax.fori_loop(0, count // group, rows, 0)
+
+
+def open_body(x_hbm, w_hbm, valid_hbm, couple_hbm, *refs):
+    later, outs, brought = refs[:5], refs[5:9], refs[9:14]
+    block_ref, longer_ref, x_ref, w_ref, valid_ref, y_ref, sem = refs[14:]
+    own_i, own_j, chans = couple_hbm.shape
+    copies = fetch([(x_hbm, x_ref), (w_hbm, w_ref), (valid_hbm, valid_ref),
+                    (couple_hbm, block_ref.at[pl.ds(0, own_i)]),
+                    (couple_hbm, longer_ref.at[pl.ds(0, own_i)]), *zip(later, brought)], sem)
+    seqs, residues, depth = x_ref.shape
+    width = w_ref.shape[0] // 2
+    height, lanes = outs[0].shape
+    me = lax.axis_index("row")
+    z = lax.axis_index("col")
+    copies[0].wait()
+    x = x_ref[...].astype(f32).reshape(seqs * residues, depth)
+    normed = standardize(x).astype(bf16)
+    copies[1].wait()
+    y_ref[...] = lax.dot_general(
+        normed, w_ref[...], (((1,), (1,)), ((), ())), preferred_element_type=f32
+    )
+
+    def cut(start, lane):
+        start = pl.multiple_of(start * own_i, 8)
+        return [y_ref[pl.ds(s * residues + start, own_i), lane : lane + width] for s in range(seqs)]
+
+    empty = jnp.zeros((own_i, seqs * width), f32)
+    shared = cut(z, 0) + cut(z ^ 2, 0) + [empty] + cut(z, width) + cut(z ^ 1, width)
+    below = jnp.zeros((height - own_i, lanes), f32)
+    for d, out in enumerate(outs):
+        rows = jnp.concatenate(cut(me ^ d, 0) + shared, axis=1)
+        out[...] = jnp.concatenate([rows, below], axis=0).astype(bf16)
+    copies[2].wait()
+    mask = valid_ref[...].astype(f32).T
+    mask = jnp.concatenate([mask, jnp.zeros((own_j, chans - own_i), f32)], axis=1)
+    block_ref[own_i] = mask.astype(bf16)
+    for n in range(own_i, longer_ref.shape[0]):
+        longer_ref[n] = mask.astype(bf16)
+    for copy in copies[3:]:
+        copy.wait()
+
+
+def ready_body(seqs, avg_ref, ids_hbm, wq_ref, pick_ref, idt_ref, wf_ref, ids_ref, sem):
+    (copy,) = fetch([(ids_hbm, ids_ref)], sem)
+    pairs, width, _ = wq_ref.shape
+    kinds, blocks, lanes, _ = pick_ref.shape
+    total = blocks * seqs
+    row = lax.broadcasted_iota(jnp.int32, pick_ref.shape[2:], 0)
+    col = lax.broadcasted_iota(jnp.int32, pick_ref.shape[2:], 1)
+    for n in range(kinds):
+        unit = row - n * seqs * width
+        place = lax.rem(unit, width) * total + lax.div(unit, width)
+        place = jnp.where((unit >= 0) & (unit < seqs * width), col - place, -1)
+        for r in range(blocks):
+            pick_ref[n, r] = jnp.where(place == r * seqs, 1.0, 0.0).astype(bf16)
+    wf_ref[...] = avg_ref[...].astype(f32)
+    for h in range(pairs):
+        both = [wf_ref[pl.ds(2 * h + d, width, stride=width), :] for d in range(2)]
+        wq_ref[h] = jnp.concatenate(both, axis=1).astype(bf16)
+    copy.wait()
+
+    def spread(n, carry):
+        idt_ref[pl.ds(n, 1), :] = jnp.full((1, idt_ref.shape[1]), ids_ref[n], jnp.int32)
+        return carry
+
+    lax.fori_loop(0, idt_ref.shape[0], spread, 0, unroll=8)
+
+
+def mix_body(seqs, width, own_i, sets, blocks, *refs):
+    msgs, (wq_ref, pick_ref), outs, xl_ref = refs[:blocks], refs[blocks : blocks + 2], refs[blocks + 2 : -1], refs[-1]
+    total = seqs * blocks
+    half = own_i // 2
+    chans = wq_ref.shape[2] // 2
+    for t_ref, n in zip(outs, sets):
+        group = n // 2 * 128
+        for r in range(blocks):
+            m = msgs[r][pl.ds(0, own_i), group : group + 128].astype(f32)
+            for s in range(seqs):
+                lane = (n % 2) * seqs * width + s * width
+                moved = pltpu.roll(m, 128 - lane, 1) if lane else m
+                xl_ref[pl.ds(r * seqs + s, own_i, stride=total), :] = moved
+        lhs = xl_ref[:, :width].astype(bf16)
+        for h in range(width // 2):
+            out = jnp.dot(lhs, wq_ref[h], preferred_element_type=f32)
+            parts = [out[:, d * chans : (d + 1) * chans].reshape(own_i, total, chans) for d in range(2)]
+            block = jnp.concatenate(parts, axis=1).astype(bf16)
+            where = pl.ds(h * 2 * total, 2 * total)
+            t_ref[:, where, :chans] = block[:half]
+            t_ref[:, where, chans:] = block[half:]
+    if len(outs) > len(sets):
+        joined = jnp.concatenate([msg[:, 256:384] for msg in msgs], axis=1)
+        for n in range(pick_ref.shape[0]):
+            picks = pick_ref[n].reshape(blocks * 128, width * total)
+            right = jnp.dot(joined, picks, preferred_element_type=f32)[:own_i]
+            outs[-1][n] = (right * (1.0 / total)).astype(bf16)
+
+
+def block_norms(block_ref, t_ref, right, row0, col0, idt_ref, bias_ref, use):
+    half, terms, _ = t_ref.shape
+    own_i, own_j, chans = 2 * half, right.shape[0], bias_ref.shape[1]
+    idc = idt_ref[pl.ds(pl.multiple_of(col0, 8), own_j), :]
+    step = 4
+    for b in range(half // step):
+        rows, psums = [[], []], [[], []]
+        for i in range(b * step, b * step + step):
+            both = jnp.dot(right, t_ref[i], preferred_element_type=f32)
+            for side in range(2):
+                at = i + side * half
+                same = idc == idt_ref[pl.ds(row0 + at, 1), :]
+                base = block_ref[at].astype(f32) + jnp.where(same, bias_ref[0:1, :], bias_ref[1:2, :])
+                rows[side].append(at)
+                psums[side].append((base + both[:, side * chans : (side + 1) * chans]).astype(bf16))
+        rows, psums = rows[0] + rows[1], psums[0] + psums[1]
+        flat = jnp.concatenate([standardize(p.astype(f32)) for p in psums], axis=0).astype(bf16)
+        use(rows, psums, flat)
+
+
+def gated(block_ref, rows, flat, w_ref):
+    own_j = block_ref.shape[1]
+    tri = w_ref.shape[1] // 2
+    mask = block_ref[block_ref.shape[0] - 1].astype(f32)
+    proj = jnp.dot(flat, w_ref[...], preferred_element_type=f32)
+    both = sigmoid(proj[:, :tri]) * proj[:, tri:]
+    return [mask[:, at : at + 1] * both[n * own_j : (n + 1) * own_j] for n, at in enumerate(rows)]
+
+
+def own_body(block_ref, t_ref, right_ref, idt_ref, bias_ref, win_ref, wgate_ref, psum_ref, gate_ref, left_ref):
+    own_i, own_j, chans = psum_ref.shape
+    r, z = lax.axis_index("row"), lax.axis_index("col")
+    w_left = win_ref.at[:, pl.ds(0, win_ref.shape[1] // 2)]
+
+    def use(rows, psums, flat):
+        lefts = gated(block_ref, rows, flat, w_left)
         gate = sigmoid(jnp.dot(flat, wgate_ref[...], preferred_element_type=f32))
-        gate_ref[pl.ds(b * group, group)] = gate.reshape(group, depth, -1)
-        return carry
-
-    lax.fori_loop(0, own_i // group, gates, 0, unroll=True)
-
-    def use(halves):
-        def rows(b, carry):
-            acc = contract(lf_ref, halves, b * group, group)
-            for t in range(group):
-                o_ref[b * group + t] = acc[t]
-            return carry
-
-        lax.fori_loop(0, own_i // group, rows, 0)
-
-    with_right(True, rights, use)
+        for n, at in enumerate(rows):
+            psum_ref[at] = psums[n]
+            gate_ref[at] = gate[n * own_j : (n + 1) * own_j]
+            left_ref[at] = lefts[n].astype(bf16)
+
+    block_norms(block_ref, t_ref, right_ref[0], r * own_i, z * own_j, idt_ref, bias_ref, use)
+
+
+def met_body(block_ref, t_ref, right_ref, idt_ref, bias_ref, win_ref, left_ref):
+    own_i, own_j, _ = left_ref.shape
+    r, z = lax.axis_index("row"), lax.axis_index("col")
+    w_left = win_ref.at[:, pl.ds(0, win_ref.shape[1] // 2)]
+
+    def use(rows, psums, flat):
+        for at, left in zip(rows, gated(block_ref, rows, flat, w_left)):
+            left_ref[at] = left.astype(bf16)
+
+    block_norms(block_ref, t_ref, right_ref[1], r * own_i, (z ^ 1) * own_j, idt_ref, bias_ref, use)
+
+
+def right_body(own_pair, h, a_ref, b_ref, c_ref, d_ref, t_ref, right_ref, idt_ref, bias_ref, win_ref, out_ref,
+               block_ref, flat_ref, sem):
+    own_j, own_i, tri = out_ref.shape
+    r, z = lax.axis_index("row"), lax.axis_index("col")
+    keeper = (r % 2) == (z % 2)
+    near = ((r // 2) == (z // 2)) == own_pair
+    table = [(near & keeper, a_ref), (near & ~keeper, b_ref), (~near & keeper, c_ref), (~near & ~keeper, d_ref)]
+    for cond, src in table:
+
+        @pl.when(cond)
+        def _():
+            pltpu.make_async_copy(src.at[pl.ds(0, block_ref.shape[0])], block_ref, sem).start()
+
+    pltpu.make_async_copy(a_ref.at[pl.ds(0, block_ref.shape[0])], block_ref, sem).wait()
+    side = win_ref.shape[1] // 2
+    w_right = win_ref.at[:, pl.ds(side, side)]
+
+    def use(rows, psums, flat):
+        for at, right in zip(rows, gated(block_ref, rows, flat, w_right)):
+            flat_ref[pl.ds(at * own_j, own_j), :] = right
+
+    row0 = (z if own_pair else z ^ 2) * own_i
+    col0 = (z ^ h) * own_j
+    block_norms(block_ref, t_ref, right_ref[h], row0, col0, idt_ref, bias_ref, use)
+    for k in range(own_j):
+        out_ref[k] = flat_ref[pl.ds(k, own_i, stride=own_j), :].astype(bf16)
 
 
 def join_body(first, parts, own_ref, psum_ref, gate_ref, w_ref, *refs):
@@ -405,62 +523,130 @@
     )(summed, psum, norm, w_gate, w_final)
 
 
-def paired_plan(lefts, right, psum, norm, w_gate, w_final):
-    own_i, own_j, chans = psum.shape
+def paired_plan(homolog, couple, ids, valid, bias, factors, average, w_in, w_gate, w_final):
+    seqs, residues, depth = homolog.shape
+    own_i, own_j, chans = couple.shape
+    width = factors.shape[1] // 2
     tri = w_final.shape[0]
-    cuts = len(lefts)
+    total = seqs * 4
     cells = [(r, z) for r in range(4) for z in range(4)]
-
-    def move(value, where, step):
-        pairs = [(r * 4 + z, step(r, z)) for r, z in cells if where(r, z)]
+    struct = jax.ShapeDtypeStruct
+
+    def move(value, step):
+        pairs = [(r * 4 + z, step(r, z)) for r, z in cells]
         pairs = [(src, r * 4 + z) for src, (r, z) in pairs]
         return lax.ppermute(value, ("row", "col"), pairs)
 
-    every = lambda r, z: True
+    def call(body, us, out_shape, scratch, *args, mib=12):
+        return pl.pallas_call(
+            body,
+            out_shape=out_shape,
+            in_specs=[VMEM] * len(args),
+            out_specs=[VMEM] * len(out_shape) if isinstance(out_shape, list) else VMEM,
+            scratch_shapes=scratch,
+            compiler_params=limit(mib),
+            cost_estimate=cost(us),
+            name=getattr(body, "func", body).__name__.removesuffix("_body"),
+        )(*args)
+
     keeper = lambda r, z: r % 2 == z % 2
-    got = move(right, every, lambda r, z: (r ^ 2, z) if keeper(r, z) else (r ^ 1, z ^ 1))
-    far = move(right, every, lambda r, z: (r ^ 1, z) if keeper(r, z) else (r ^ 2, z ^ 1))
-    mets = [move(left, every, lambda r, z: (r, z ^ 1)) for left in lefts[:2]]
-    got, far, mets[0] = lax.optimization_barrier((got, far, mets[0]))
-    p_got = move(got, every, lambda r, z: (r ^ 1, z))
-    p_far = move(far, every, lambda r, z: (r ^ 1, z))
-    rights = (right, got, p_got, far, p_far)
-
-    sums = []
-    chunks = [(n, m, 0, 8) for n, left in enumerate(lefts) for m in range(0, left.shape[0], 8)]
-    for at, first, _, n in chunks:
-        part = pl.pallas_call(
-            functools.partial(send_body, first),
-            out_shape=jax.ShapeDtypeStruct((n, own_j, tri), bf16),
-            in_specs=[VMEM] * 7,
-            out_specs=VMEM,
-            scratch_shapes=[pltpu.VMEM((n, 2 * own_j, tri), f32)],
-            compiler_params=limit(8),
-            cost_estimate=cost(0.12 * n + 0.4),
-            name="send_sums",
-        )(*rights, lefts[at], mets[at])
-        sums.append(move(part, every, lambda r, z: (r, z ^ 2)))
-        if len(mets) < cuts:
-            left, _ = lax.optimization_barrier((lefts[len(mets)], part))
-            mets.append(move(left, every, lambda r, z: (r, z ^ 1)))
-
-    own, gate = pl.pallas_call(
-        functools.partial(keep_body, cuts),
-        out_shape=[jax.ShapeDtypeStruct((own_i, own_j, tri), f32),
-                   jax.ShapeDtypeStruct((own_i, own_j, chans), f32)],
-        in_specs=[VMEM] * (5 + 2 * cuts + 2),
-        out_specs=[VMEM] * 2,
-        scratch_shapes=[pltpu.VMEM((own_i, 2 * own_j, tri), f32)],
-        compiler_params=limit(12),
-        cost_estimate=cost(6),
-        name="keep_sums",
-    )(*rights, *lefts, *mets, norm, w_gate)
+    beside = lambda r, z: (r ^ 1, z)
+    height, lanes = round_up(own_i, 16), 384
+    block = struct((own_i + 1, own_j, chans), bf16)
+    longer = struct((own_i + 2, own_j, chans), bf16)
+    later = (average, bias, w_in, w_gate, w_final)
+    *msgs, average, bias, w_in, w_gate, w_final, own, own_z = pl.pallas_call(
+        open_body,
+        out_shape=[struct((height, lanes), bf16)] * 4 + [struct(x.shape, x.dtype) for x in later] + [block, longer],
+        in_specs=[HBM] * 9,
+        out_specs=[VMEM] * 11,
+        scratch_shapes=[
+            pltpu.VMEM(homolog.shape, bf16),
+            pltpu.VMEM((2 * width, depth), bf16),
+            pltpu.VMEM(valid.shape, jnp.int32),
+            pltpu.VMEM((seqs * residues, 2 * width), f32),
+            pltpu.SemaphoreType.DMA((10,)),
+        ],
+        compiler_params=limit(8),
+        cost_estimate=cost(1.5),
+        name="open",
+    )(*map(hold, (homolog, factors.T, valid, couple) + later))
+    msgs = [msgs[0]] + [
+        lax.ppermute(msgs[d], "row", [(r, r ^ d) for r in range(4)]) for d in (1, 2, 3)
+    ]
+    far = move(own, lambda r, z: (r ^ 2, z) if keeper(r, z) else (r ^ 3, z ^ 1))
+    met = move(own_z, lambda r, z: (r, z ^ 1))
+
+    wq, pick, idt = pl.pallas_call(
+        functools.partial(ready_body, seqs),
+        out_shape=[struct((width // 2, width, 2 * chans), bf16),
+                   struct((2, 4, 128, width * total), bf16),
+                   struct((residues, 128), jnp.int32)],
+        in_specs=[VMEM, HBM],
+        out_specs=[VMEM] * 3,
+        scratch_shapes=[
+            pltpu.VMEM(average.shape, f32),
+            pltpu.SMEM(ids.shape, jnp.int32),
+            pltpu.SemaphoreType.DMA((1,)),
+        ],
+        compiler_params=limit(8),
+        cost_estimate=cost(1.5),
+        name="ready",
+    )(average, hold(ids))
+
+    raw, _ = lax.optimization_barrier((own, idt))
+    p_own = move(raw, beside)
+    t_shape = struct((own_i // 2, width * total, 2 * chans), bf16)
+    xl = [pltpu.VMEM((own_i * total, 128), f32)]
+    t_own, t_send, right = call(
+        functools.partial(mix_body, seqs, width, own_i, (0, 2), 4), 2.4,
+        [t_shape, t_shape, struct((2, own_j, width * total), bf16)], xl, *msgs, wq, pick,
+    )
+    left_shape = struct((own_i, own_j, tri), bf16)
+    psum, gate, left = call(
+        own_body, 2.4,
+        [struct(couple.shape, bf16), struct(couple.shape, f32), left_shape], [],
+        own, t_own, right, idt, bias, w_in, w_gate,
+    )
+
+    def make_right(own_pair, h, t, blocks):
+        return call(
+            functools.partial(right_body, own_pair, h), 1.8,
+            struct((own_j, own_i, tri), bf16),
+            [pltpu.VMEM(block.shape, bf16), pltpu.VMEM((own_i * own_j, tri), f32), pltpu.SemaphoreType.DMA],
+            *blocks, t, right, idt, bias, w_in,
+        )
+
+    far, *_ = lax.optimization_barrier((far, psum))
+    p_far = move(far, beside)
+    here = (own, p_own, far, p_far)
+    send0 = make_right(False, 0, t_send, here)
+    met, *_ = lax.optimization_barrier((met, send0))
+    p_met = move(met, beside)
+    there = (met, p_met, p_far, far)
+    met_left = call(met_body, 1.8, left_shape, [], met, t_own, right, idt, bias, w_in)
+    send1 = make_right(False, 1, t_send, there)
+
+    def sums(rights, first, n, dtype):
+        return call(
+            functools.partial(sums_body, first), 0.13 * n, struct((n, own_j, tri), dtype),
+            [pltpu.VMEM((n, 2 * own_j, tri), f32)], *rights, left, met_left,
+        )
+
+    chunks = [(0, 16), (16, 16), (32, own_i - 32)]
+    leaving = [sums((send0, send1), first, n, bf16) for first, n in chunks]
+    came = [move(part, lambda r, z: (r, z ^ 2)) for part in leaving]
+
+    msgs, _ = lax.optimization_barrier((msgs, leaving[-1]))
+    t_keep = call(functools.partial(mix_body, seqs, width, own_i, (1,), 4), 1.2, [t_shape], xl, *msgs, wq, pick)[0]
+    rights = make_right(True, 0, t_keep, here), make_right(True, 1, t_keep, there)
+    kept = sums(rights, 0, own_i, f32)
+
     out = []
-    for first, n in ((0, 16), (16, own_i - 16)):
-        parts = sums[first // 8 : (first + n) // 8]
+    for first, n, parts in ((0, 16, came[:1]), (16, own_i - 16, came[1:])):
         out = [pl.pallas_call(
             functools.partial(join_body, first, len(parts)),
-            out_shape=jax.ShapeDtypeStruct((own_i, own_j, chans), bf16),
+            out_shape=struct(couple.shape, bf16),
             in_specs=[VMEM] * (4 + len(parts)) + [HBM] * len(out),
             out_specs=HBM,
             scratch_shapes=[pltpu.VMEM((n, own_j, chans), bf16), pltpu.SemaphoreType.DMA],
@@ -468,7 +654,7 @@
             compiler_params=limit(8),
             cost_estimate=cost(0.06 * n),
             name="join",
-        )(own, psum, gate, w_final, *parts, *out)]
+        )(kept, psum, gate, w_final, *parts, *out)]
     return out[0]
 
 
@@ -481,8 +667,10 @@
     total = own_seqs * rows
     lanes = round_up(2 * own_seqs * width, 128)
     height = round_up(max(own_i, own_j), 16)
-    paired = rows == 4 and cols == 4 and own_i == own_j and own_i % 8 == 0 and own_i > 32
-    scale = 1 if paired else 8
+    paired = (rows, cols, own_seqs * width, chans, tri) == (4, 4, 64, 128, 128)
+    if paired and own_i == own_j == 40:
+        return paired_plan(homolog, couple, ids, valid, bias, factors, average, w_in, w_gate, w_final)
+    scale = 8
 
     later = (average, valid, bias, couple)
     *msgs, average, valid, bias, couple = pl.pallas_call(
@@ -525,9 +713,9 @@
         name="prepare",
     )(couple, hold(ids), valid, bias, average)
 
-    extents = (own_j, own_i) if paired else (own_i, own_j)
+    extents = (own_i, own_j)
     psum, norm, right = pl.pallas_call(
-        functools.partial(pair_body, own_seqs, width, rows, paired),
+        functools.partial(pair_body, own_seqs, width, rows),
         out_shape=[jax.ShapeDtypeStruct((own_i, own_j, chans), bf16),
                    jax.ShapeDtypeStruct((own_i * own_j, chans), bf16),
                    jax.ShapeDtypeStruct(extents + (tri,), bf16)],
@@ -536,14 +724,13 @@
         scratch_shapes=[
             pltpu.VMEM((own_i * total, 128), f32),
             pltpu.VMEM((own_i // 2, width * total, 2 * chans), bf16),
-            pltpu.VMEM((own_i * own_j, tri), f32),
         ],
         compiler_params=limit(16, scale),
         cost_estimate=cost(4.5),
         name="pair",
     )(*msgs, base, mask, wq, pick, w_in)
 
-    cuts = [8, 16, own_i - 24] if paired else [own_i]
+    cuts = [own_i]
     lefts = pl.pallas_call(
         left_body,
         out_shape=[jax.ShapeDtypeStruct((n, own_j, tri), bf16) for n in cuts],
@@ -553,8 +740,6 @@
         cost_estimate=cost(1),
         name="left",
     )(norm, mask, w_in)
-    if paired:
-        return paired_plan(lefts, right, psum, norm, w_gate, w_final)
     return gathered_plan(lefts[0], right, psum, norm, w_gate, w_final)
 
 

time: 53 us -> 55.9 us (1.055)
  Pallas kernels: 19.3 us -> 32.9 us
  waiting for transfers between devices: 15.6 us -> 8.9 us
  starting transfers between devices: 17.8 us -> 13.6 us
    pallas_call x10 -> x14, Pallas kernels: 17.1 us -> 30.7 us  [the longest x12 28.2 us: call(): pl.pallas_call(body, out_shape=out_shape, in_specs=[VMEM] * len(args), ou...]
    ppermute x12 -> x8, waiting for transfers between devices: 14.1 us -> 1.4 us  [move(): return lax.ppermute(value, ('row', 'col'), pairs)]
    ppermute x3, waiting for transfers between devices: 1.5 us -> 7.5 us  [paired_plan(): lax.ppermute(msgs[d], 'row', [(r, r ^ d) for r in range(4)])]
    ppermute x12 -> x8, starting transfers between devices: 14.6 us -> 11.1 us  [move(): return lax.ppermute(value, ('row', 'col'), pairs)]
    ppermute x3, starting transfers between devices: 3.12 us -> 2.48 us  [paired_plan(): lax.ppermute(msgs[d], 'row', [(r, r ^ d) for r in range(4)])]
  transfers between devices with their start and end apart: 15 -> 11, of which waited for: 8 -> 2; matrix products, arithmetic and copies ran while one was open for 0% -> 0% of each run, Pallas kernels for 25% -> 46%
where the time goes in v11:
time: 55.9 us; the launch traced here: 55.7 us
  Pallas kernels  32.9 us (59%)
  starting transfers between devices  13.6 us (24%)
  waiting for transfers between devices  8.9 us (16%)
    pallas_call x12, Pallas kernels, call(): pl.pallas_call(body, out_shape=out_shape, in_specs=[VMEM] * len(args), ou...  28.2 us
    ppermute x8, starting transfers between devices, move(): return lax.ppermute(value, ('row', 'col'), pairs)  11.1 us
    ppermute x3, waiting for transfers between devices, paired_plan(): lax.ppermute(msgs[d], 'row', [(r, r ^ d) for r in range(4)])  7.5 us
    ppermute x3, starting transfers between devices, paired_plan(): lax.ppermute(msgs[d], 'row', [(r, r ^ d) for r in range(4)])  2.48 us
    pallas_call x2, Pallas kernels, paired_plan(): pl.pallas_call(functools.partial(join_body, first, len(parts)), out_shape...  2.24 us
    pallas_call x1, Pallas kernels, paired_plan(): pl.pallas_call(open_body, out_shape=[struct((height, lanes), bf16)] * 4 +...  1.59 us
    ppermute x8, waiting for transfers between devices, move(): return lax.ppermute(value, ('row', 'col'), pairs)  1.4 us
  transfers between devices with their start and end apart: 11, of which 2 were waited for; matrix products, arithmetic and copies ran while one was open for 0% of the time, Pallas kernels for 46%

profile of v11, /device:TPU:0, one launch (start us, length us, event | category | flops | bytes accessed | tf_op | source)
XLA Modules:
  0.0 55.7 jit_solution(16111244732295228581)
XLA Ops:
  0.0 1.6 %open.1 = (bf16[48,384]{1,0:T(8,128)(2,1)S(1)}, bf16[48,384]{1,0:T(8,128)(2,1)S(1)}, bf16[48,384]{1,0:T(8,128)(2,1)S(1)}, bf16[48,384]{1,0:T(8,128)(2,1)S(1)}, b...) custom-call(bf16[2,160,256]{2,1,0:T(8,128)(2,1)} %x_hbm.1, ...), custom_call_target="tpu_custom_call" | custom-call | bytes 5535000 | tf_op jit(solution)/shard_map/open/pallas_call | solution.py:558
  1.6 3.0 %collective-permute-start.1 = (bf16[41,40,128]{2,1,0:T(8,128)(2,1)S(1)}, bf16[41,40,128]{2,1,0:T(8,128)(2,1)S(1)}, u32[]{:S(2)}, u32[]{:S(2)}) collective-permute-start(bf16[41,40,128]{2,1,0:T(8,128)(2,1)S(1)} %get-tuple-element.35.block_ref.a_ref), channel_id=1, source_target_pairs={{0,8},{1,12},{2,10},{3,14},{4,9},{5,13},{6,11},{7,15},{8,0},{9,4},... | collective-permute-start | bytes 1259528 | tf_op jit(solution)/shard_map/ppermute | solution.py:538
  4.6 1.1 %collective-permute-start.2 = (bf16[48,384]{1,0:T(8,128)(2,1)S(1)}, bf16[48,384]{1,0:T(8,128)(2,1)S(1)}, u32[]{:S(2)}, u32[]{:S(2)}) collective-permute-start(bf16[48,384]{1,0:T(8,128)(2,1)S(1)} %get-tuple-element.37), channel_id=1, source_target_pairs={{0,4},{4,0},{8,12},{12,8},{1,5},{5,1},{9,13},{13,9},{2,6},{6,2},{1... | collective-permute-start | bytes 110600 | tf_op jit(solution)/shard_map/ppermute | solution.py:575
  5.7 0.5 collective-permute-start.3
  6.3 0.8 %collective-permute-start.4 = (bf16[48,384]{1,0:T(8,128)(2,1)S(1)}, bf16[48,384]{1,0:T(8,128)(2,1)S(1)}, u32[]{:S(2)}, u32[]{:S(2)}) collective-permute-start(bf16[48,384]{1,0:T(8,128)(2,1)S(1)} %get-tuple-element.39), channel_id=1, source_target_pairs={{0,12},{4,8},{8,4},{12,0},{1,13},{5,9},{9,5},{13,1},{2,14},{6,10},... | collective-permute-start | bytes 110600 | tf_op jit(solution)/shard_map/ppermute | solution.py:575
  7.1 0.3 collective-permute-start.6
  7.4 0.9 %ready.1 = (bf16[16,32,256]{2,1,0:T(8,128)(2,1)S(1)}, bf16[2,4,128,256]{3,2,1,0:T(8,128)(2,1)S(1)}, s32[160,128]{1,0:T(8,128)S(1)}) custom-call(bf16[1024,128]{1,0:T(8,128)(2,1)S(1)} %get-tuple-element.33.avg_ref, s32[160]{0:T(256)} %ids_hbm.1), custom_call_target="tpu_custom_call" | custom-call | bytes 5535000 | tf_op jit(solution)/shard_map/ready/pallas_call | solution.py:580
  8.3 0.0 collective-permute-done.2.refs_1_
  8.3 0.6 %collective-permute-start = (bf16[41,40,128]{2,1,0:T(8,128)(2,1)S(1)}, bf16[41,40,128]{2,1,0:T(8,128)(2,1)S(1)}, u32[]{:S(2)}, u32[]{:S(2)}) collective-permute-start(bf16[41,40,128]{2,1,0:T(8,128)(2,1)S(1)} %get-tuple-element.35.block_ref.a_ref), channel_id=1, source_target_pairs={{0,4},{1,5},{2,6},{3,7},{4,0},{5,1},{6,2},{7,3},{8,12},{9,13},{10,... | collective-permute-start | bytes 1259528 | tf_op jit(solution)/shard_map/ppermute | solution.py:538
  8.8 7.5 %collective-permute-done.3.refs_2_ = bf16[48,384]{1,0:T(8,128)(2,1)S(1)} collective-permute-done((bf16[48,384]{1,0:T(8,128)(2,1)S(1)}, bf16[48,384]{1,0:T(8,128)(2,1)S(1)}, u32[]{:S(2)}, u32[]{:S(2)}) %collective-permute-start.3) | collective-permute-done | bytes 36896 | tf_op jit(solution)/shard_map/ppermute | solution.py:575
  16.3 0.0 collective-permute-done.4.refs_3_
  16.3 1.6 %mix.2 = (bf16[20,256,256]{2,1,0:T(8,128)(2,1)S(1)}, bf16[20,256,256]{2,1,0:T(8,128)(2,1)S(1)}, bf16[2,40,256]{2,1,0:T(8,128)(2,1)S(1)}) custom-call(bf16[48,384]{1,0:T(8,128)(2,1)S(1)} %get-tuple-element.53.refs_0_, bf16[48,384]{1,0:T(8,128)(2,1)S(1)} %collective-permute-done.2.refs_1_, bf16[48,384]{1,0:T(8,128)(2,1)S(1)} %collective-permute-done.3.refs_2_, ...), custom_call_target="tpu_custom_call" | custom-call | bytes 8856000 | tf_op jit(solution)/shard_map/mix/pallas_call | solution.py:541
  17.9 2.4 %own.1 = (bf16[40,40,128]{2,1,0:T(8,128)(2,1)S(1)}, f32[40,40,128]{2,1,0:T(8,128)S(1)}, bf16[40,40,128]{2,1,0:T(8,128)(2,1)S(1)}) custom-call(bf16[41,40,128]{2,1,0:T(8,128)(2,1)S(1)} %get-tuple-element.35.block_ref.a_ref, bf16[20,256,256]{2,1,0:T(8,128)(2,1)S(1)} %get-tuple-element.42.t_ref, bf16[2,40,256]{2,1,0:T(8,128)(2,1)S(1)} %get-tuple-element.43.right_ref, ...), custom_call_target="tpu_custom_call" | custom-call | bytes 8856000 | tf_op jit(solution)/shard_map/own/pallas_call | solution.py:541
  20.3 0.0 collective-permute-done.1.c_ref.d_ref
  20.3 0.6 %collective-permute-start.5 = (bf16[41,40,128]{2,1,0:T(8,128)(2,1)S(1)}, bf16[41,40,128]{2,1,0:T(8,128)(2,1)S(1)}, u32[]{:S(2)}, u32[]{:S(2)}) collective-permute-start(bf16[41,40,128]{2,1,0:T(8,128)(2,1)S(1)} %collective-permute-done.1.c_ref.d_ref), channel_id=1, source_target_pairs={{0,4},{1,5},{2,6},{3,7},{4,0},{5,1},{6,2},{7,3},{8,12},{9,13},{10,... | collective-permute-start | bytes 1259528 | tf_op jit(solution)/shard_map/ppermute | solution.py:538
  20.9 0.0 collective-permute-done.b_ref
  20.9 1.4 %collective-permute-done.5.d_ref.c_ref = bf16[41,40,128]{2,1,0:T(8,128)(2,1)S(1)} collective-permute-done((bf16[41,40,128]{2,1,0:T(8,128)(2,1)S(1)}, bf16[41,40,128]{2,1,0:T(8,128)(2,1)S(1)}, u32[]{:S(2)}, u32[]{:S(2)}) %collective-permute-start.5) | collective-permute-done | bytes 419872 | tf_op jit(solution)/shard_map/ppermute | solution.py:538
  22.3 2.6 %right.4.right0_ref = bf16[40,40,128]{2,1,0:T(8,128)(2,1)S(1)} custom-call(bf16[41,40,128]{2,1,0:T(8,128)(2,1)S(1)} %get-tuple-element.35.block_ref.a_ref, bf16[41,40,128]{2,1,0:T(8,128)(2,1)S(1)} %collective-permute-done.b_ref, bf16[41,40,128]{2,1,0:T(8,128)(2,1)S(1)} %collective-permute-done.1.c_ref.d_ref, ...), custom_call_target="tpu_custom_call" | custom-call | bytes 6642000 | tf_op jit(solution)/shard_map/right/pallas_call | solution.py:541
  24.9 0.0 collective-permute-done.6.a_ref.block_ref
  24.9 0.4 collective-permute-start.7
  25.4 2.3 %met.1.m_ref = bf16[40,40,128]{2,1,0:T(8,128)(2,1)S(1)} custom-call(bf16[42,40,128]{2,1,0:T(8,128)(2,1)S(1)} %collective-permute-done.6.a_ref.block_ref, bf16[20,256,256]{2,1,0:T(8,128)(2,1)S(1)} %get-tuple-element.42.t_ref, bf16[2,40,256]{2,1,0:T(8,128)(2,1)S(1)} %get-tuple-element.43.right_ref, s32[160,128]{1,0:T(8,128)S(1)} %get-tuple-element.34.idt_ref, ...), custom_call_target="tpu_custom_call" | custom-call | bytes 6642000 | tf_op jit(solution)/shard_map/met/pallas_call | solution.py:541
  27.7 0.0 collective-permute-done.7.b_ref
  27.7 2.7 %right.5.right1_ref = bf16[40,40,128]{2,1,0:T(8,128)(2,1)S(1)} custom-call(bf16[42,40,128]{2,1,0:T(8,128)(2,1)S(1)} %collective-permute-done.6.a_ref.block_ref, bf16[42,40,128]{2,1,0:T(8,128)(2,1)S(1)} %collective-permute-done.7.b_ref, bf16[41,40,128]{2,1,0:T(8,128)(2,1)S(1)} %collective-permute-done.5.d_ref.c_ref, ...), custom_call_target="tpu_custom_call" | custom-call | bytes 6642000 | tf_op jit(solution)/shard_map/right/pallas_call | solution.py:541
  30.4 2.1 %sums.7 = bf16[16,40,128]{2,1,0:T(8,128)(2,1)S(1)} custom-call(bf16[40,40,128]{2,1,0:T(8,128)(2,1)S(1)} %right.4.right0_ref, bf16[40,40,128]{2,1,0:T(8,128)(2,1)S(1)} %right.5.right1_ref, bf16[40,40,128]{2,1,0:T(8,128)(2,1)S(1)} %get-tuple-element.52.l_ref, bf16[40,40,128]{2,1,0:T(8,128)(2,1)S(1)} %met.1.m_ref), custom_call_target="tpu_custom_call" | custom-call | bytes 7675200 | tf_op jit(solution)/shard_map/sums/pallas_call | solution.py:541
  32.4 3.2 %collective-permute-start.10 = (bf16[16,40,128]{2,1,0:T(8,128)(2,1)S(1)}, bf16[16,40,128]{2,1,0:T(8,128)(2,1)S(1)}, u32[]{:S(2)}, u32[]{:S(2)}) collective-permute-start(bf16[16,40,128]{2,1,0:T(8,128)(2,1)S(1)} %sums.7), channel_id=1, source_target_pairs={{0,2},{1,3},{2,0},{3,1},{4,6},{5,7},{6,4},{7,5},{8,10},{9,11},{10,... | collective-permute-start | bytes 491528 | tf_op jit(solution)/shard_map/ppermute | solution.py:538
  35.6 2.1 %sums.6 = bf16[16,40,128]{2,1,0:T(8,128)(2,1)S(1)} custom-call(bf16[40,40,128]{2,1,0:T(8,128)(2,1)S(1)} %right.4.right0_ref, bf16[40,40,128]{2,1,0:T(8,128)(2,1)S(1)} %right.5.right1_ref, bf16[40,40,128]{2,1,0:T(8,128)(2,1)S(1)} %get-tuple-element.52.l_ref, bf16[40,40,128]{2,1,0:T(8,128)(2,1)S(1)} %met.1.m_ref), custom_call_target="tpu_custom_call" | custom-call | bytes 7675200 | tf_op jit(solution)/shard_map/sums/pallas_call | solution.py:541
  37.7 0.1 collective-permute-start.8
  37.8 1.0 %sums.4 = bf16[8,40,128]{2,1,0:T(8,128)(2,1)S(1)} custom-call(bf16[40,40,128]{2,1,0:T(8,128)(2,1)S(1)} %right.4.right0_ref, bf16[40,40,128]{2,1,0:T(8,128)(2,1)S(1)} %right.5.right1_ref, bf16[40,40,128]{2,1,0:T(8,128)(2,1)S(1)} %get-tuple-element.52.l_ref, bf16[40,40,128]{2,1,0:T(8,128)(2,1)S(1)} %met.1.m_ref), custom_call_target="tpu_custom_call" | custom-call | bytes 3837600 | tf_op jit(solution)/shard_map/sums/pallas_call | solution.py:541
  38.8 3.0 %collective-permute-start.9 = (bf16[8,40,128]{2,1,0:T(8,128)(2,1)S(1)}, bf16[8,40,128]{2,1,0:T(8,128)(2,1)S(1)}, u32[]{:S(2)}, u32[]{:S(2)}) collective-permute-start(bf16[8,40,128]{2,1,0:T(8,128)(2,1)S(1)} %sums.4), channel_id=1, source_target_pairs={{0,2},{1,3},{2,0},{3,1},{4,6},{5,7},{6,4},{7,5},{8,10},{9,11},{10,... | collective-permute-start | bytes 245768 | tf_op jit(solution)/shard_map/ppermute | solution.py:538
  41.8 0.9 %mix.3.t_ref = bf16[20,256,256]{2,1,0:T(8,128)(2,1)S(1)} custom-call(bf16[48,384]{1,0:T(8,128)(2,1)S(1)} %get-tuple-element.53.refs_0_, bf16[48,384]{1,0:T(8,128)(2,1)S(1)} %collective-permute-done.2.refs_1_, bf16[48,384]{1,0:T(8,128)(2,1)S(1)} %collective-permute-done.3.refs_2_, bf16[48,384]{1,0:T(8,128)(2,1)S(1)} %collective-permute-done.4.refs_3_, ...), custom_call_target="tpu_custom_call" | custom-call | bytes 4428000 | tf_op jit(solution)/shard_map/mix/pallas_call | solution.py:541
  42.7 2.8 %right.7.right1_ref = bf16[40,40,128]{2,1,0:T(8,128)(2,1)S(1)} custom-call(bf16[42,40,128]{2,1,0:T(8,128)(2,1)S(1)} %collective-permute-done.6.a_ref.block_ref, bf16[42,40,128]{2,1,0:T(8,128)(2,1)S(1)} %collective-permute-done.7.b_ref, bf16[41,40,128]{2,1,0:T(8,128)(2,1)S(1)} %collective-permute-done.5.d_ref.c_ref, ...), custom_call_target="tpu_custom_call" | custom-call | bytes 6642000 | tf_op jit(solution)/shard_map/right/pallas_call | solution.py:541
  45.5 2.7 %right.6.right0_ref = bf16[40,40,128]{2,1,0:T(8,128)(2,1)S(1)} custom-call(bf16[41,40,128]{2,1,0:T(8,128)(2,1)S(1)} %get-tuple-element.35.block_ref.a_ref, bf16[41,40,128]{2,1,0:T(8,128)(2,1)S(1)} %collective-permute-done.b_ref, bf16[41,40,128]{2,1,0:T(8,128)(2,1)S(1)} %collective-permute-done.1.c_ref.d_ref, ...), custom_call_target="tpu_custom_call" | custom-call | bytes 6642000 | tf_op jit(solution)/shard_map/right/pallas_call | solution.py:541
  48.2 5.1 %sums.5.own_ref = f32[40,40,128]{2,1,0:T(8,128)S(1)} custom-call(bf16[40,40,128]{2,1,0:T(8,128)(2,1)S(1)} %right.6.right0_ref, bf16[40,40,128]{2,1,0:T(8,128)(2,1)S(1)} %right.7.right1_ref, bf16[40,40,128]{2,1,0:T(8,128)(2,1)S(1)} %get-tuple-element.52.l_ref, bf16[40,40,128]{2,1,0:T(8,128)(2,1)S(1)} %met.1.m_ref), custom_call_target="tpu_custom_call" | custom-call | bytes 19188000 | tf_op jit(solution)/shard_map/sums/pallas_call | solution.py:541
  53.3 0.0 collective-permute-done.10.refs_0_
  53.3 1.1 %join.2.refs_2_ = bf16[40,40,128]{2,1,0:T(8,128)(2,1)} custom-call(f32[40,40,128]{2,1,0:T(8,128)S(1)} %sums.5.own_ref, bf16[40,40,128]{2,1,0:T(8,128)(2,1)S(1)} %get-tuple-element.47.psum_ref, f32[40,40,128]{2,1,0:T(8,128)S(1)} %get-tuple-element.57.gate_ref, bf16[128,128]{1,0:T(8,128)(2,1)S(1)} %get-tuple-element.58.w_ref, ...), custom_call_target="tpu_custom_call" | custom-call | bytes 3542400 | tf_op jit(solution)/shard_map/join/pallas_call | solution.py:647
  54.4 0.0 collective-permute-done.9.refs_1_
  54.4 0.0 collective-permute-done.8.refs_0_
  54.4 1.2 %join.3 = bf16[40,40,128]{2,1,0:T(8,128)(2,1)} custom-call(f32[40,40,128]{2,1,0:T(8,128)S(1)} %sums.5.own_ref, bf16[40,40,128]{2,1,0:T(8,128)(2,1)S(1)} %get-tuple-element.47.psum_ref, f32[40,40,128]{2,1,0:T(8,128)S(1)} %get-tuple-element.57.gate_ref, bf16[128,128]{1,0:T(8,128)(2,1)S(1)} %get-tuple-element.58.w_ref, ...), custom_call_target="tpu_custom_call", output_to_operand_aliasing={{}: (6, {})} | custom-call | bytes 5313600 | tf_op jit(solution)/shard_map/join/pallas_call | solution.py:647
Async XLA Ops:
  1.6 18.7 %collective-permute-start.1 = (bf16[41,40,128]{2,1,0:T(8,128)(2,1)S(1)}, bf16[41,40,128]{2,1,0:T(8,128)(2,1)S(1)}, u32[]{:S(2)}, u32[]{:S(2)}) collective-permute-start(bf16[41,40,128]{2,1,0:T(8,128)(2,1)S(1)} %get-tuple-element.35.block_ref.a_ref), channel_id=1, source_target_pairs={{0,8},{1,12},{2,10},{3,14},{4,9},{5,13},{6,11},{7,15},{8,0},{9,4},... | collective-permute-start | bytes 1259528 | tf_op jit(solution)/shard_map/ppermute | solution.py:538
  4.6 3.7 %collective-permute-start.2 = (bf16[48,384]{1,0:T(8,128)(2,1)S(1)}, bf16[48,384]{1,0:T(8,128)(2,1)S(1)}, u32[]{:S(2)}, u32[]{:S(2)}) collective-permute-start(bf16[48,384]{1,0:T(8,128)(2,1)S(1)} %get-tuple-element.37), channel_id=1, source_target_pairs={{0,4},{4,0},{8,12},{12,8},{1,5},{5,1},{9,13},{13,9},{2,6},{6,2},{1... | collective-permute-start | bytes 110600 | tf_op jit(solution)/shard_map/ppermute | solution.py:575
  5.7 10.6 %collective-permute-start.3 = (bf16[48,384]{1,0:T(8,128)(2,1)S(1)}, bf16[48,384]{1,0:T(8,128)(2,1)S(1)}, u32[]{:S(2)}, u32[]{:S(2)}) collective-permute-start(bf16[48,384]{1,0:T(8,128)(2,1)S(1)} %get-tuple-element.38), channel_id=1, source_target_pairs={{0,8},{4,12},{8,0},{12,4},{1,9},{5,13},{9,1},{13,5},{2,10},{6,14},... | collective-permute-start | bytes 110600 | tf_op jit(solution)/shard_map/ppermute | solution.py:575
  6.3 10.1 %collective-permute-start.4 = (bf16[48,384]{1,0:T(8,128)(2,1)S(1)}, bf16[48,384]{1,0:T(8,128)(2,1)S(1)}, u32[]{:S(2)}, u32[]{:S(2)}) collective-permute-start(bf16[48,384]{1,0:T(8,128)(2,1)S(1)} %get-tuple-element.39), channel_id=1, source_target_pairs={{0,12},{4,8},{8,4},{12,0},{1,13},{5,9},{9,5},{13,1},{2,14},{6,10},... | collective-permute-start | bytes 110600 | tf_op jit(solution)/shard_map/ppermute | solution.py:575
  7.1 17.8 %collective-permute-start.6 = (bf16[42,40,128]{2,1,0:T(8,128)(2,1)S(1)}, bf16[42,40,128]{2,1,0:T(8,128)(2,1)S(1)}, u32[]{:S(2)}, u32[]{:S(2)}) collective-permute-start(bf16[42,40,128]{2,1,0:T(8,128)(2,1)S(1)} %get-tuple-element.50), channel_id=1, source_target_pairs={{0,1},{1,0},{2,3},{3,2},{4,5},{5,4},{6,7},{7,6},{8,9},{9,8},{10,11... | collective-permute-start | bytes 1290248 | tf_op jit(solution)/shard_map/ppermute | solution.py:538
  8.3 12.7 %collective-permute-start = (bf16[41,40,128]{2,1,0:T(8,128)(2,1)S(1)}, bf16[41,40,128]{2,1,0:T(8,128)(2,1)S(1)}, u32[]{:S(2)}, u32[]{:S(2)}) collective-permute-start(bf16[41,40,128]{2,1,0:T(8,128)(2,1)S(1)} %get-tuple-element.35.block_ref.a_ref), channel_id=1, source_target_pairs={{0,4},{1,5},{2,6},{3,7},{4,0},{5,1},{6,2},{7,3},{8,12},{9,13},{10,... | collective-permute-start | bytes 1259528 | tf_op jit(solution)/shard_map/ppermute | solution.py:538
  20.3 2.0 %collective-permute-start.5 = (bf16[41,40,128]{2,1,0:T(8,128)(2,1)S(1)}, bf16[41,40,128]{2,1,0:T(8,128)(2,1)S(1)}, u32[]{:S(2)}, u32[]{:S(2)}) collective-permute-start(bf16[41,40,128]{2,1,0:T(8,128)(2,1)S(1)} %collective-permute-done.1.c_ref.d_ref), channel_id=1, source_target_pairs={{0,4},{1,5},{2,6},{3,7},{4,0},{5,1},{6,2},{7,3},{8,12},{9,13},{10,... | collective-permute-start | bytes 1259528 | tf_op jit(solution)/shard_map/ppermute | solution.py:538
  24.9 2.8 %collective-permute-start.7 = (bf16[42,40,128]{2,1,0:T(8,128)(2,1)S(1)}, bf16[42,40,128]{2,1,0:T(8,128)(2,1)S(1)}, u32[]{:S(2)}, u32[]{:S(2)}) collective-permute-start(bf16[42,40,128]{2,1,0:T(8,128)(2,1)S(1)} %collective-permute-done.6.a_ref.block_ref), channel_id=1, source_target_pairs={{0,4},{1,5},{2,6},{3,7},{4,0},{5,1},{6,2},{7,3},{8,12},{9,13},{10,... | collective-permute-start | bytes 1290248 | tf_op jit(solution)/shard_map/ppermute | solution.py:538
  32.4 20.9 %collective-permute-start.10 = (bf16[16,40,128]{2,1,0:T(8,128)(2,1)S(1)}, bf16[16,40,128]{2,1,0:T(8,128)(2,1)S(1)}, u32[]{:S(2)}, u32[]{:S(2)}) collective-permute-start(bf16[16,40,128]{2,1,0:T(8,128)(2,1)S(1)} %sums.7), channel_id=1, source_target_pairs={{0,2},{1,3},{2,0},{3,1},{4,6},{5,7},{6,4},{7,5},{8,10},{9,11},{10,... | collective-permute-start | bytes 491528 | tf_op jit(solution)/shard_map/ppermute | solution.py:538
  37.7 16.7 %collective-permute-start.8 = (bf16[16,40,128]{2,1,0:T(8,128)(2,1)S(1)}, bf16[16,40,128]{2,1,0:T(8,128)(2,1)S(1)}, u32[]{:S(2)}, u32[]{:S(2)}) collective-permute-start(bf16[16,40,128]{2,1,0:T(8,128)(2,1)S(1)} %sums.6), channel_id=1, source_target_pairs={{0,2},{1,3},{2,0},{3,1},{4,6},{5,7},{6,4},{7,5},{8,10},{9,11},{10,... | collective-permute-start | bytes 491528 | tf_op jit(solution)/shard_map/ppermute | solution.py:538
  38.8 15.6 %collective-permute-start.9 = (bf16[8,40,128]{2,1,0:T(8,128)(2,1)S(1)}, bf16[8,40,128]{2,1,0:T(8,128)(2,1)S(1)}, u32[]{:S(2)}, u32[]{:S(2)}) collective-permute-start(bf16[8,40,128]{2,1,0:T(8,128)(2,1)S(1)} %sums.4), channel_id=1, source_target_pairs={{0,2},{1,3},{2,0},{3,1},{4,6},{5,7},{6,4},{7,5},{8,10},{9,11},{10,... | collective-permute-start | bytes 245768 | tf_op jit(solution)/shard_map/ppermute | solution.py:538

commit v12 on v11

--- a/solution.py
+++ b/solution.py
@@ -224,28 +224,41 @@
     return acc
 
 
-def sums_body(first, right0_ref, right1_ref, l_ref, m_ref, o_ref, lf_ref):
+def sums_body(own_pair, first, own_ref, p_own, met_ref, p_met, far_ref, p_far, l_ref, m_ref, o_ref, lf_ref):
     count, depth = o_ref.shape[0], l_ref.shape[1]
     group = 8
     lf_ref[:, pl.ds(0, depth), :] = l_ref[pl.ds(first, count)].astype(f32)
     lf_ref[:, pl.ds(depth, depth), :] = m_ref[pl.ds(first, count)].astype(f32)
 
-    def rows(b, carry):
-        acc = contract(lf_ref, (right0_ref, right1_ref), b * group, group)
-        for t in range(group):
-            o_ref[b * group + t] = acc[t].astype(o_ref.dtype)
-        return carry
-
-    lax.fori_loop(0, count // group, rows, 0)
+    def use(halves):
+        def rows(b, carry):
+            acc = contract(lf_ref, halves, b * group, group)
+            for t in range(group):
+                o_ref[b * group + t] = acc[t].astype(o_ref.dtype)
+            return carry
+
+        lax.fori_loop(0, count // group, rows, 0)
+
+    r, z = lax.axis_index("row"), lax.axis_index("col")
+    keeper = (r % 2) == (z % 2)
+    near = ((r // 2) == (z // 2)) == own_pair
+    table = [
+        (near & keeper, own_ref, met_ref),
+        (near & ~keeper, p_own, p_met),
+        (~near & keeper, far_ref, p_far),
+        (~near & ~keeper, p_far, far_ref),
+    ]
+    for cond, a, b in table:
+        pl.when(cond)(functools.partial(use, (a, b)))
 
 
 def open_body(x_hbm, w_hbm, valid_hbm, couple_hbm, *refs):
     later, outs, brought = refs[:5], refs[5:9], refs[9:14]
-    block_ref, longer_ref, x_ref, w_ref, valid_ref, y_ref, sem = refs[14:]
+    block_ref, x_ref, w_ref, valid_ref, y_ref, sem = refs[14:]
     own_i, own_j, chans = couple_hbm.shape
     copies = fetch([(x_hbm, x_ref), (w_hbm, w_ref), (valid_hbm, valid_ref),
                     (couple_hbm, block_ref.at[pl.ds(0, own_i)]),
-                    (couple_hbm, longer_ref.at[pl.ds(0, own_i)]), *zip(later, brought)], sem)
+                    *zip(later, brought)], sem)
     seqs, residues, depth = x_ref.shape
     width = w_ref.shape[0] // 2
     height, lanes = outs[0].shape
@@ -264,7 +277,7 @@
         return [y_ref[pl.ds(s * residues + start, own_i), lane : lane + width] for s in range(seqs)]
 
     empty = jnp.zeros((own_i, seqs * width), f32)
-    shared = cut(z, 0) + cut(z ^ 2, 0) + [empty] + cut(z, width) + cut(z ^ 1, width)
+    shared = [empty] + cut(z, width) + cut(z ^ 1, width)
     below = jnp.zeros((height - own_i, lanes), f32)
     for d, out in enumerate(outs):
         rows = jnp.concatenate(cut(me ^ d, 0) + shared, axis=1)
@@ -272,9 +285,8 @@
     copies[2].wait()
     mask = valid_ref[...].astype(f32).T
     mask = jnp.concatenate([mask, jnp.zeros((own_j, chans - own_i), f32)], axis=1)
-    block_ref[own_i] = mask.astype(bf16)
-    for n in range(own_i, longer_ref.shape[0]):
-        longer_ref[n] = mask.astype(bf16)
+    for n in range(own_i, block_ref.shape[0]):
+        block_ref[n] = mask.astype(bf16)
     for copy in copies[3:]:
         copy.wait()
 
@@ -305,33 +317,27 @@
     lax.fori_loop(0, idt_ref.shape[0], spread, 0, unroll=8)
 
 
-def mix_body(seqs, width, own_i, sets, blocks, *refs):
-    msgs, (wq_ref, pick_ref), outs, xl_ref = refs[:blocks], refs[blocks : blocks + 2], refs[blocks + 2 : -1], refs[-1]
-    total = seqs * blocks
-    half = own_i // 2
-    chans = wq_ref.shape[2] // 2
-    for t_ref, n in zip(outs, sets):
-        group = n // 2 * 128
-        for r in range(blocks):
-            m = msgs[r][pl.ds(0, own_i), group : group + 128].astype(f32)
-            for s in range(seqs):
-                lane = (n % 2) * seqs * width + s * width
-                moved = pltpu.roll(m, 128 - lane, 1) if lane else m
-                xl_ref[pl.ds(r * seqs + s, own_i, stride=total), :] = moved
-        lhs = xl_ref[:, :width].astype(bf16)
-        for h in range(width // 2):
-            out = jnp.dot(lhs, wq_ref[h], preferred_element_type=f32)
-            parts = [out[:, d * chans : (d + 1) * chans].reshape(own_i, total, chans) for d in range(2)]
-            block = jnp.concatenate(parts, axis=1).astype(bf16)
-            where = pl.ds(h * 2 * total, 2 * total)
-            t_ref[:, where, :chans] = block[:half]
-            t_ref[:, where, chans:] = block[half:]
-    if len(outs) > len(sets):
-        joined = jnp.concatenate([msg[:, 256:384] for msg in msgs], axis=1)
-        for n in range(pick_ref.shape[0]):
-            picks = pick_ref[n].reshape(blocks * 128, width * total)
-            right = jnp.dot(joined, picks, preferred_element_type=f32)[:own_i]
-            outs[-1][n] = (right * (1.0 / total)).astype(bf16)
+def mix_body(seqs, width, *refs):
+    msgs, (wq_ref, pick_ref, t_ref, right_ref, xl_ref) = refs[:4], refs[4:]
+    half, terms, both = t_ref.shape
+    chans, own_i, total = both // 2, 2 * half, seqs * 4
+    for r in range(4):
+        m = msgs[r][pl.ds(0, own_i), :128].astype(f32)
+        for s in range(seqs):
+            moved = pltpu.roll(m, 128 - s * width, 1) if s else m
+            xl_ref[pl.ds(r * seqs + s, own_i, stride=total), :] = moved
+    lhs = xl_ref[:, :width].astype(bf16)
+    joined = jnp.concatenate([msg[:, 128:] for msg in msgs], axis=1)
+    for n in range(2):
+        right = jnp.dot(joined, pick_ref[n].reshape(512, terms), preferred_element_type=f32)[:own_i]
+        right_ref[n] = (right * (1.0 / total)).astype(bf16)
+    for h in range(width // 2):
+        out = jnp.dot(lhs, wq_ref[h], preferred_element_type=f32)
+        parts = [out[:, d * chans : (d + 1) * chans].reshape(own_i, total, chans) for d in range(2)]
+        block = jnp.concatenate(parts, axis=1).astype(bf16)
+        where = pl.ds(h * 2 * total, 2 * total)
+        t_ref[:, where, :chans] = block[:half]
+        t_ref[:, where, chans:] = block[half:]
 
 
 def block_norms(block_ref, t_ref, right, row0, col0, idt_ref, bias_ref, use):
@@ -363,58 +369,51 @@
     return [mask[:, at : at + 1] * both[n * own_j : (n + 1) * own_j] for n, at in enumerate(rows)]
 
 
-def own_body(block_ref, t_ref, right_ref, idt_ref, bias_ref, win_ref, wgate_ref, psum_ref, gate_ref, left_ref):
+def own_body(block_ref, t_ref, right_ref, idt_ref, bias_ref, win_ref, psum_ref, norm_ref, out_ref, flat_ref):
     own_i, own_j, chans = psum_ref.shape
     r, z = lax.axis_index("row"), lax.axis_index("col")
+    side = win_ref.shape[1] // 2
+    w_right = win_ref.at[:, pl.ds(side, side)]
+
+    def use(rows, psums, flat):
+        rights = gated(block_ref, rows, flat, w_right)
+        for n, at in enumerate(rows):
+            psum_ref[at] = psums[n]
+            norm_ref[pl.ds(at * own_j, own_j), :] = flat[n * own_j : (n + 1) * own_j]
+            flat_ref[pl.ds(at * own_j, own_j), :] = rights[n]
+
+    block_norms(block_ref, t_ref, right_ref[0], r * own_i, z * own_j, idt_ref, bias_ref, use)
+    for k in range(own_j):
+        out_ref[k] = flat_ref[pl.ds(k, own_i, stride=own_j), :].astype(bf16)
+
+
+def rest_body(block_ref, norm_ref, win_ref, wgate_ref, left_ref, gate_ref):
+    own_i, own_j, _ = left_ref.shape
     w_left = win_ref.at[:, pl.ds(0, win_ref.shape[1] // 2)]
+    group = 8
+    for i in range(0, own_i, group):
+        flat = norm_ref[pl.ds(i * own_j, group * own_j), :]
+        rows = list(range(i, i + group))
+        gate = sigmoid(jnp.dot(flat, wgate_ref[...], preferred_element_type=f32))
+        for n, left in enumerate(gated(block_ref, rows, flat, w_left)):
+            left_ref[i + n] = left.astype(bf16)
+            gate_ref[i + n] = gate[n * own_j : (n + 1) * own_j]
+
+
+def met_body(block_ref, t_ref, right_ref, idt_ref, bias_ref, win_ref, left_ref, out_ref, flat_ref):
+    own_i, own_j, _ = left_ref.shape
+    r, z = lax.axis_index("row"), lax.axis_index("col")
+    side = win_ref.shape[1] // 2
+    w_left, w_right = win_ref.at[:, pl.ds(0, side)], win_ref.at[:, pl.ds(side, side)]
 
     def use(rows, psums, flat):
         lefts = gated(block_ref, rows, flat, w_left)
-        gate = sigmoid(jnp.dot(flat, wgate_ref[...], preferred_element_type=f32))
+        rights = gated(block_ref, rows, flat, w_right)
         for n, at in enumerate(rows):
-            psum_ref[at] = psums[n]
-            gate_ref[at] = gate[n * own_j : (n + 1) * own_j]
             left_ref[at] = lefts[n].astype(bf16)
-
-    block_norms(block_ref, t_ref, right_ref[0], r * own_i, z * own_j, idt_ref, bias_ref, use)
-
-
-def met_body(block_ref, t_ref, right_ref, idt_ref, bias_ref, win_ref, left_ref):
-    own_i, own_j, _ = left_ref.shape
-    r, z = lax.axis_index("row"), lax.axis_index("col")
-    w_left = win_ref.at[:, pl.ds(0, win_ref.shape[1] // 2)]
-
-    def use(rows, psums, flat):
-        for at, left in zip(rows, gated(block_ref, rows, flat, w_left)):
-            left_ref[at] = left.astype(bf16)
+            flat_ref[pl.ds(at * own_j, own_j), :] = rights[n]
 
     block_norms(block_ref, t_ref, right_ref[1], r * own_i, (z ^ 1) * own_j, idt_ref, bias_ref, use)
-
-
-def right_body(own_pair, h, a_ref, b_ref, c_ref, d_ref, t_ref, right_ref, idt_ref, bias_ref, win_ref, out_ref,
-               block_ref, flat_ref, sem):
-    own_j, own_i, tri = out_ref.shape
-    r, z = lax.axis_index("row"), lax.axis_index("col")
-    keeper = (r % 2) == (z % 2)
-    near = ((r // 2) == (z // 2)) == own_pair
-    table = [(near & keeper, a_ref), (near & ~keeper, b_ref), (~near & keeper, c_ref), (~near & ~keeper, d_ref)]
-    for cond, src in table:
-
-        @pl.when(cond)
-        def _():
-            pltpu.make_async_copy(src.at[pl.ds(0, block_ref.shape[0])], block_ref, sem).start()
-
-    pltpu.make_async_copy(a_ref.at[pl.ds(0, block_ref.shape[0])], block_ref, sem).wait()
-    side = win_ref.shape[1] // 2
-    w_right = win_ref.at[:, pl.ds(side, side)]
-
-    def use(rows, psums, flat):
-        for at, right in zip(rows, gated(block_ref, rows, flat, w_right)):
-            flat_ref[pl.ds(at * own_j, own_j), :] = right
-
-    row0 = (z if own_pair else z ^ 2) * own_i
-    col0 = (z ^ h) * own_j
-    block_norms(block_ref, t_ref, right_ref[h], row0, col0, idt_ref, bias_ref, use)
     for k in range(own_j):
         out_ref[k] = flat_ref[pl.ds(k, own_i, stride=own_j), :].astype(bf16)
 
@@ -551,21 +550,20 @@
 
     keeper = lambda r, z: r % 2 == z % 2
     beside = lambda r, z: (r ^ 1, z)
-    height, lanes = round_up(own_i, 16), 384
+    height, lanes = round_up(own_i, 16), 256
     block = struct((own_i + 1, own_j, chans), bf16)
-    longer = struct((own_i + 2, own_j, chans), bf16)
     later = (average, bias, w_in, w_gate, w_final)
-    *msgs, average, bias, w_in, w_gate, w_final, own, own_z = pl.pallas_call(
+    *msgs, average, bias, w_in, w_gate, w_final, raw = pl.pallas_call(
         open_body,
-        out_shape=[struct((height, lanes), bf16)] * 4 + [struct(x.shape, x.dtype) for x in later] + [block, longer],
+        out_shape=[struct((height, lanes), bf16)] * 4 + [struct(x.shape, x.dtype) for x in later] + [block],
         in_specs=[HBM] * 9,
-        out_specs=[VMEM] * 11,
+        out_specs=[VMEM] * 10,
         scratch_shapes=[
             pltpu.VMEM(homolog.shape, bf16),
             pltpu.VMEM((2 * width, depth), bf16),
             pltpu.VMEM(valid.shape, jnp.int32),
             pltpu.VMEM((seqs * residues, 2 * width), f32),
-            pltpu.SemaphoreType.DMA((10,)),
+            pltpu.SemaphoreType.DMA((9,)),
         ],
         compiler_params=limit(8),
         cost_estimate=cost(1.5),
@@ -574,8 +572,7 @@
     msgs = [msgs[0]] + [
         lax.ppermute(msgs[d], "row", [(r, r ^ d) for r in range(4)]) for d in (1, 2, 3)
     ]
-    far = move(own, lambda r, z: (r ^ 2, z) if keeper(r, z) else (r ^ 3, z ^ 1))
-    met = move(own_z, lambda r, z: (r, z ^ 1))
+    met = move(raw, lambda r, z: (r, z ^ 1))
 
     wq, pick, idt = pl.pallas_call(
         functools.partial(ready_body, seqs),
@@ -594,56 +591,39 @@
         name="ready",
     )(average, hold(ids))
 
-    raw, _ = lax.optimization_barrier((own, idt))
-    p_own = move(raw, beside)
-    t_shape = struct((own_i // 2, width * total, 2 * chans), bf16)
-    xl = [pltpu.VMEM((own_i * total, 128), f32)]
-    t_own, t_send, right = call(
-        functools.partial(mix_body, seqs, width, own_i, (0, 2), 4), 2.4,
-        [t_shape, t_shape, struct((2, own_j, width * total), bf16)], xl, *msgs, wq, pick,
+    t, mixed = call(
+        functools.partial(mix_body, seqs, width), 1,
+        [struct((own_i // 2, width * total, 2 * chans), bf16), struct((2, own_j, width * total), bf16)],
+        [pltpu.VMEM((own_i * total, 128), f32)], *msgs, wq, pick,
     )
-    left_shape = struct((own_i, own_j, tri), bf16)
-    psum, gate, left = call(
-        own_body, 2.4,
-        [struct(couple.shape, bf16), struct(couple.shape, f32), left_shape], [],
-        own, t_own, right, idt, bias, w_in, w_gate,
+    square = struct((own_i, own_j, tri), bf16)
+    flat = [pltpu.VMEM((own_i * own_j, tri), f32)]
+    psum, norm, right = call(
+        own_body, 2.4, [square, struct((own_i * own_j, chans), bf16), square], flat,
+        raw, t, mixed, idt, bias, w_in,
     )
-
-    def make_right(own_pair, h, t, blocks):
+    far = move(right, lambda r, z: (r ^ 2, z) if keeper(r, z) else (r ^ 3, z ^ 1))
+    p_own = move(right, beside)
+    left, gate = call(rest_body, 0.6, [square, struct(couple.shape, f32)], [], raw, norm, w_in, w_gate)
+    met, *_ = lax.optimization_barrier((met, left))
+    met_left, met_right = call(met_body, 3, [square, square], flat, met, t, mixed, idt, bias, w_in)
+    p_met = move(met_right, beside)
+    far, *_ = lax.optimization_barrier((far, met_left))
+    p_far = move(far, beside)
+
+    def sums(own_pair, first, n, dtype):
         return call(
-            functools.partial(right_body, own_pair, h), 1.8,
-            struct((own_j, own_i, tri), bf16),
-            [pltpu.VMEM(block.shape, bf16), pltpu.VMEM((own_i * own_j, tri), f32), pltpu.SemaphoreType.DMA],
-            *blocks, t, right, idt, bias, w_in,
+            functools.partial(sums_body, own_pair, first), 0.13 * n, struct((n, own_j, tri), dtype),
+            [pltpu.VMEM((n, 2 * own_j, tri), f32)],
+            right, p_own, met_right, p_met, far, p_far, left, met_left,
         )
 
-    far, *_ = lax.optimization_barrier((far, psum))
-    p_far = move(far, beside)
-    here = (own, p_own, far, p_far)
-    send0 = make_right(False, 0, t_send, here)
-    met, *_ = lax.optimization_barrier((met, send0))
-    p_met = move(met, beside)
-    there = (met, p_met, p_far, far)
-    met_left = call(met_body, 1.8, left_shape, [], met, t_own, right, idt, bias, w_in)
-    send1 = make_right(False, 1, t_send, there)
-
-    def sums(rights, first, n, dtype):
-        return call(
-            functools.partial(sums_body, first), 0.13 * n, struct((n, own_j, tri), dtype),
-            [pltpu.VMEM((n, 2 * own_j, tri), f32)], *rights, left, met_left,
-        )
-
-    chunks = [(0, 16), (16, 16), (32, own_i - 32)]
-    leaving = [sums((send0, send1), first, n, bf16) for first, n in chunks]
-    came = [move(part, lambda r, z: (r, z ^ 2)) for part in leaving]
-
-    msgs, _ = lax.optimization_barrier((msgs, leaving[-1]))
-    t_keep = call(functools.partial(mix_body, seqs, width, own_i, (1,), 4), 1.2, [t_shape], xl, *msgs, wq, pick)[0]
-    rights = make_right(True, 0, t_keep, here), make_right(True, 1, t_keep, there)
-    kept = sums(rights, 0, own_i, f32)
+    came = [move(sums(False, first, 8, bf16), lambda r, z: (r, z ^ 2)) for first in range(0, own_i, 8)]
+    kept = sums(True, 0, own_i, f32)
 
     out = []
-    for first, n, parts in ((0, 16, came[:1]), (16, own_i - 16, came[1:])):
+    for first, n in ((0, 16), (16, own_i - 16)):
+        parts = came[first // 8 : (first + n) // 8]
         out = [pl.pallas_call(
             functools.partial(join_body, first, len(parts)),
             out_shape=struct(couple.shape, bf16),

time: 55.9 us -> 48.9 us (0.87)
  Pallas kernels: 32.9 us -> 21.3 us
  waiting for transfers between devices: 8.9 us -> 11.4 us
  starting transfers between devices: 13.6 us -> 15.8 us
    pallas_call x12 -> x10, Pallas kernels: 28.2 us -> 16.7 us  [call(): pl.pallas_call(body, out_shape=out_shape, in_specs=[VMEM] * len(args), ou...]
    ppermute x8 -> x10, waiting for transfers between devices: 1.4 us -> 10.9 us  [move(): return lax.ppermute(value, ('row', 'col'), pairs)]
    ppermute x3, waiting for transfers between devices: 7.5 us -> 0.48 us  [paired_plan(): lax.ppermute(msgs[d], 'row', [(r, r ^ d) for r in range(4)])]
    ppermute x8 -> x10, starting transfers between devices: 11.1 us -> 12.6 us  [move(): return lax.ppermute(value, ('row', 'col'), pairs)]
    ppermute x3, starting transfers between devices: 2.48 us -> 3.15 us  [paired_plan(): lax.ppermute(msgs[d], 'row', [(r, r ^ d) for r in range(4)])]
  transfers between devices with their start and end apart: 11 -> 13, of which waited for: 2 -> 6; matrix products, arithmetic and copies ran while one was open for 0% -> 0% of each run, Pallas kernels for 46% -> 36%
where the time goes in v12:
time: 48.9 us; the launch traced here: 48.7 us
  Pallas kernels  21.3 us (44%)
  starting transfers between devices  15.8 us (32%)
  waiting for transfers between devices  11.4 us (23%)
    pallas_call x10, Pallas kernels, call(): pl.pallas_call(body, out_shape=out_shape, in_specs=[VMEM] * len(args), ou...  16.7 us
    ppermute x10, starting transfers between devices, move(): return lax.ppermute(value, ('row', 'col'), pairs)  12.6 us
    ppermute x10, waiting for transfers between devices, move(): return lax.ppermute(value, ('row', 'col'), pairs)  10.9 us
    ppermute x3, starting transfers between devices, paired_plan(): lax.ppermute(msgs[d], 'row', [(r, r ^ d) for r in range(4)])  3.15 us
    pallas_call x2, Pallas kernels, paired_plan(): pl.pallas_call(functools.partial(join_body, first, len(parts)), out_shape...  2.22 us
    pallas_call x1, Pallas kernels, paired_plan(): pl.pallas_call(open_body, out_shape=[struct((height, lanes), bf16)] * 4 +...  1.58 us
  transfers between devices with their start and end apart: 13, of which 6 were waited for; matrix products, arithmetic and copies ran while one was open for 0% of the time, Pallas kernels for 36%

profile of v12, /device:TPU:0, one launch (start us, length us, event | category | flops | bytes accessed | tf_op | source)
XLA Modules:
  0.0 48.7 jit_solution(14065832375121483486)
XLA Ops:
  0.0 1.6 %open.1 = (bf16[48,256]{1,0:T(8,128)(2,1)S(1)}, bf16[48,256]{1,0:T(8,128)(2,1)S(1)}, bf16[48,256]{1,0:T(8,128)(2,1)S(1)}, bf16[48,256]{1,0:T(8,128)(2,1)S(1)}, b...) custom-call(bf16[2,160,256]{2,1,0:T(8,128)(2,1)} %x_hbm.1, ...), custom_call_target="tpu_custom_call" | custom-call | bytes 5535000 | tf_op jit(solution)/shard_map/open/pallas_call | solution.py:556
  1.6 0.5 %collective-permute-start = (bf16[48,256]{1,0:T(8,128)(2,1)S(1)}, bf16[48,256]{1,0:T(8,128)(2,1)S(1)}, u32[]{:S(2)}, u32[]{:S(2)}) collective-permute-start(bf16[48,256]{1,0:T(8,128)(2,1)S(1)} %get-tuple-element.31), channel_id=1, source_target_pairs={{0,4},{4,0},{8,12},{12,8},{1,5},{5,1},{9,13},{13,9},{2,6},{6,2},{1... | collective-permute-start | bytes 73736 | tf_op jit(solution)/shard_map/ppermute | solution.py:573
  2.1 2.6 %collective-permute-start.1 = (bf16[48,256]{1,0:T(8,128)(2,1)S(1)}, bf16[48,256]{1,0:T(8,128)(2,1)S(1)}, u32[]{:S(2)}, u32[]{:S(2)}) collective-permute-start(bf16[48,256]{1,0:T(8,128)(2,1)S(1)} %get-tuple-element.32), channel_id=1, source_target_pairs={{0,8},{4,12},{8,0},{12,4},{1,9},{5,13},{9,1},{13,5},{2,10},{6,14},... | collective-permute-start | bytes 73736 | tf_op jit(solution)/shard_map/ppermute | solution.py:573
  4.7 0.1 collective-permute-start.2
  4.7 1.8 %collective-permute-start.4 = (bf16[41,40,128]{2,1,0:T(8,128)(2,1)S(1)}, bf16[41,40,128]{2,1,0:T(8,128)(2,1)S(1)}, u32[]{:S(2)}, u32[]{:S(2)}) collective-permute-start(bf16[41,40,128]{2,1,0:T(8,128)(2,1)S(1)} %get-tuple-element.29.block_ref), channel_id=1, source_target_pairs={{0,1},{1,0},{2,3},{3,2},{4,5},{5,4},{6,7},{7,6},{8,9},{9,8},{10,11... | collective-permute-start | bytes 1259528 | tf_op jit(solution)/shard_map/ppermute | solution.py:537
  6.5 0.9 %ready.1 = (bf16[16,32,256]{2,1,0:T(8,128)(2,1)S(1)}, bf16[2,4,128,256]{3,2,1,0:T(8,128)(2,1)S(1)}, s32[160,128]{1,0:T(8,128)S(1)}) custom-call(bf16[1024,128]{1,0:T(8,128)(2,1)S(1)} %get-tuple-element.34.avg_ref, s32[160]{0:T(256)} %ids_hbm.1), custom_call_target="tpu_custom_call" | custom-call | bytes 5535000 | tf_op jit(solution)/shard_map/ready/pallas_call | solution.py:577
  7.4 0.0 collective-permute-done.refs_1_
  7.4 0.0 collective-permute-done.1.refs_2_
  7.4 0.5 collective-permute-done.2.refs_3_
  7.9 0.9 %mix.1 = (bf16[20,256,256]{2,1,0:T(8,128)(2,1)S(1)}, bf16[2,40,256]{2,1,0:T(8,128)(2,1)S(1)}) custom-call(bf16[48,256]{1,0:T(8,128)(2,1)S(1)} %get-tuple-element.30.refs_0_, bf16[48,256]{1,0:T(8,128)(2,1)S(1)} %collective-permute-done.refs_1_, bf16[48,256]{1,0:T(8,128)(2,1)S(1)} %collective-permute-done.1.refs_2_, ...), custom_call_target="tpu_custom_call" | custom-call | bytes 3690000 | tf_op jit(solution)/shard_map/mix/pallas_call | solution.py:540
  8.8 2.4 %own.1 = (bf16[40,40,128]{2,1,0:T(8,128)(2,1)S(1)}, bf16[1600,128]{1,0:T(8,128)(2,1)S(1)}, bf16[40,40,128]{2,1,0:T(8,128)(2,1)S(1)}) custom-call(bf16[41,40,128]{2,1,0:T(8,128)(2,1)S(1)} %get-tuple-element.29.block_ref, bf16[20,256,256]{2,1,0:T(8,128)(2,1)S(1)} %get-tuple-element.37.t_ref, bf16[2,40,256]{2,1,0:T(8,128)(2,1)S(1)} %get-tuple-element.38.right_ref, ...), custom_call_target="tpu_custom_call" | custom-call | bytes 8856000 | tf_op jit(solution)/shard_map/own/pallas_call | solution.py:540
  11.2 1.1 %collective-permute-start.6 = (bf16[40,40,128]{2,1,0:T(8,128)(2,1)S(1)}, bf16[40,40,128]{2,1,0:T(8,128)(2,1)S(1)}, u32[]{:S(2)}, u32[]{:S(2)}) collective-permute-start(bf16[40,40,128]{2,1,0:T(8,128)(2,1)S(1)} %get-tuple-element.42.own_ref), channel_id=1, source_target_pairs={{0,8},{1,12},{2,10},{3,14},{4,9},{5,13},{6,11},{7,15},{8,0},{9,4},... | collective-permute-start | bytes 1228808 | tf_op jit(solution)/shard_map/ppermute | solution.py:537
  12.3 0.9 %collective-permute-start.3 = (bf16[40,40,128]{2,1,0:T(8,128)(2,1)S(1)}, bf16[40,40,128]{2,1,0:T(8,128)(2,1)S(1)}, u32[]{:S(2)}, u32[]{:S(2)}) collective-permute-start(bf16[40,40,128]{2,1,0:T(8,128)(2,1)S(1)} %get-tuple-element.42.own_ref), channel_id=1, source_target_pairs={{0,4},{1,5},{2,6},{3,7},{4,0},{5,1},{6,2},{7,3},{8,12},{9,13},{10,... | collective-permute-start | bytes 1228808 | tf_op jit(solution)/shard_map/ppermute | solution.py:537
  13.2 0.5 %rest.1 = (bf16[40,40,128]{2,1,0:T(8,128)(2,1)S(1)}, f32[40,40,128]{2,1,0:T(8,128)S(1)}) custom-call(bf16[41,40,128]{2,1,0:T(8,128)(2,1)S(1)} %get-tuple-element.29.block_ref, bf16[1600,128]{1,0:T(8,128)(2,1)S(1)} %get-tuple-element.43.norm_ref, bf16[128,512]{1,0:T(8,128)(2,1)S(1)} %get-tuple-element.41.win_ref, bf16[128,128]{1,0:T(8,128)(2,1)S(1)} %get-tuple-element.44.wgate_ref), custom_call_target="tpu_custom_call" | custom-call | bytes 2214000 | tf_op jit(solution)/shard_map/rest/pallas_call | solution.py:540
  13.7 3.0 %collective-permute-done.4.block_ref = bf16[41,40,128]{2,1,0:T(8,128)(2,1)S(1)} collective-permute-done((bf16[41,40,128]{2,1,0:T(8,128)(2,1)S(1)}, bf16[41,40,128]{2,1,0:T(8,128)(2,1)S(1)}, u32[]{:S(2)}, u32[]{:S(2)}) %collective-permute-start.4) | collective-permute-done | bytes 419872 | tf_op jit(solution)/shard_map/ppermute | solution.py:537
  16.7 2.6 %met.1 = (bf16[40,40,128]{2,1,0:T(8,128)(2,1)S(1)}, bf16[40,40,128]{2,1,0:T(8,128)(2,1)S(1)}) custom-call(bf16[41,40,128]{2,1,0:T(8,128)(2,1)S(1)} %collective-permute-done.4.block_ref, bf16[20,256,256]{2,1,0:T(8,128)(2,1)S(1)} %get-tuple-element.37.t_ref, bf16[2,40,256]{2,1,0:T(8,128)(2,1)S(1)} %get-tuple-element.38.right_ref, ...), custom_call_target="tpu_custom_call" | custom-call | bytes 11070000 | tf_op jit(solution)/shard_map/met/pallas_call | solution.py:540
  19.3 0.1 collective-permute-start.5
  19.4 4.2 %collective-permute-done.6.far_ref = bf16[40,40,128]{2,1,0:T(8,128)(2,1)S(1)} collective-permute-done((bf16[40,40,128]{2,1,0:T(8,128)(2,1)S(1)}, bf16[40,40,128]{2,1,0:T(8,128)(2,1)S(1)}, u32[]{:S(2)}, u32[]{:S(2)}) %collective-permute-start.6) | collective-permute-done | bytes 409632 | tf_op jit(solution)/shard_map/ppermute | solution.py:537
  23.6 0.0 collective-permute-start.7
  23.6 0.0 collective-permute-done.3.p_own
  23.6 0.0 collective-permute-done.5.p_met
  23.6 1.7 %collective-permute-done.7.p_far = bf16[40,40,128]{2,1,0:T(8,128)(2,1)S(1)} collective-permute-done((bf16[40,40,128]{2,1,0:T(8,128)(2,1)S(1)}, bf16[40,40,128]{2,1,0:T(8,128)(2,1)S(1)}, u32[]{:S(2)}, u32[]{:S(2)}) %collective-permute-start.7) | collective-permute-done | bytes 409632 | tf_op jit(solution)/shard_map/ppermute | solution.py:537
  25.4 1.0 %sums.11 = bf16[8,40,128]{2,1,0:T(8,128)(2,1)S(1)} custom-call(bf16[40,40,128]{2,1,0:T(8,128)(2,1)S(1)} %get-tuple-element.42.own_ref, bf16[40,40,128]{2,1,0:T(8,128)(2,1)S(1)} %collective-permute-done.3.p_own, bf16[40,40,128]{2,1,0:T(8,128)(2,1)S(1)} %get-tuple-element.47.met_ref, bf16[40,40,128]{2,1,0:T(8,128)(2,1)S(1)} %collective-permute-done.5.p_met, ...), custom_call_target="tpu_custom_call" | custom-call | bytes 3837600 | tf_op jit(solution)/shard_map/sums/pallas_call | solution.py:540
  26.4 2.7 %collective-permute-start.12 = (bf16[8,40,128]{2,1,0:T(8,128)(2,1)S(1)}, bf16[8,40,128]{2,1,0:T(8,128)(2,1)S(1)}, u32[]{:S(2)}, u32[]{:S(2)}) collective-permute-start(bf16[8,40,128]{2,1,0:T(8,128)(2,1)S(1)} %sums.11), channel_id=1, source_target_pairs={{0,2},{1,3},{2,0},{3,1},{4,6},{5,7},{6,4},{7,5},{8,10},{9,11},{10,... | collective-permute-start | bytes 245768 | tf_op jit(solution)/shard_map/ppermute | solution.py:537
  29.1 1.0 %sums.10 = bf16[8,40,128]{2,1,0:T(8,128)(2,1)S(1)} custom-call(bf16[40,40,128]{2,1,0:T(8,128)(2,1)S(1)} %get-tuple-element.42.own_ref, bf16[40,40,128]{2,1,0:T(8,128)(2,1)S(1)} %collective-permute-done.3.p_own, bf16[40,40,128]{2,1,0:T(8,128)(2,1)S(1)} %get-tuple-element.47.met_ref, bf16[40,40,128]{2,1,0:T(8,128)(2,1)S(1)} %collective-permute-done.5.p_met, ...), custom_call_target="tpu_custom_call" | custom-call | bytes 3837600 | tf_op jit(solution)/shard_map/sums/pallas_call | solution.py:540
  30.1 0.4 collective-permute-start.11
  30.5 1.0 %sums.9 = bf16[8,40,128]{2,1,0:T(8,128)(2,1)S(1)} custom-call(bf16[40,40,128]{2,1,0:T(8,128)(2,1)S(1)} %get-tuple-element.42.own_ref, bf16[40,40,128]{2,1,0:T(8,128)(2,1)S(1)} %collective-permute-done.3.p_own, bf16[40,40,128]{2,1,0:T(8,128)(2,1)S(1)} %get-tuple-element.47.met_ref, bf16[40,40,128]{2,1,0:T(8,128)(2,1)S(1)} %collective-permute-done.5.p_met, ...), custom_call_target="tpu_custom_call" | custom-call | bytes 3837600 | tf_op jit(solution)/shard_map/sums/pallas_call | solution.py:540
  31.6 2.7 %collective-permute-start.10 = (bf16[8,40,128]{2,1,0:T(8,128)(2,1)S(1)}, bf16[8,40,128]{2,1,0:T(8,128)(2,1)S(1)}, u32[]{:S(2)}, u32[]{:S(2)}) collective-permute-start(bf16[8,40,128]{2,1,0:T(8,128)(2,1)S(1)} %sums.9), channel_id=1, source_target_pairs={{0,2},{1,3},{2,0},{3,1},{4,6},{5,7},{6,4},{7,5},{8,10},{9,11},{10,... | collective-permute-start | bytes 245768 | tf_op jit(solution)/shard_map/ppermute | solution.py:537
  34.2 1.0 %sums.8 = bf16[8,40,128]{2,1,0:T(8,128)(2,1)S(1)} custom-call(bf16[40,40,128]{2,1,0:T(8,128)(2,1)S(1)} %get-tuple-element.42.own_ref, bf16[40,40,128]{2,1,0:T(8,128)(2,1)S(1)} %collective-permute-done.3.p_own, bf16[40,40,128]{2,1,0:T(8,128)(2,1)S(1)} %get-tuple-element.47.met_ref, bf16[40,40,128]{2,1,0:T(8,128)(2,1)S(1)} %collective-permute-done.5.p_met, ...), custom_call_target="tpu_custom_call" | custom-call | bytes 3837600 | tf_op jit(solution)/shard_map/sums/pallas_call | solution.py:540
  35.3 0.4 collective-permute-start.9
  35.7 1.0 %sums.7 = bf16[8,40,128]{2,1,0:T(8,128)(2,1)S(1)} custom-call(bf16[40,40,128]{2,1,0:T(8,128)(2,1)S(1)} %get-tuple-element.42.own_ref, bf16[40,40,128]{2,1,0:T(8,128)(2,1)S(1)} %collective-permute-done.3.p_own, bf16[40,40,128]{2,1,0:T(8,128)(2,1)S(1)} %get-tuple-element.47.met_ref, bf16[40,40,128]{2,1,0:T(8,128)(2,1)S(1)} %collective-permute-done.5.p_met, ...), custom_call_target="tpu_custom_call" | custom-call | bytes 3837600 | tf_op jit(solution)/shard_map/sums/pallas_call | solution.py:540
  36.7 2.7 %collective-permute-start.8 = (bf16[8,40,128]{2,1,0:T(8,128)(2,1)S(1)}, bf16[8,40,128]{2,1,0:T(8,128)(2,1)S(1)}, u32[]{:S(2)}, u32[]{:S(2)}) collective-permute-start(bf16[8,40,128]{2,1,0:T(8,128)(2,1)S(1)} %sums.7), channel_id=1, source_target_pairs={{0,2},{1,3},{2,0},{3,1},{4,6},{5,7},{6,4},{7,5},{8,10},{9,11},{10,... | collective-permute-start | bytes 245768 | tf_op jit(solution)/shard_map/ppermute | solution.py:537
  39.4 5.1 %sums.6.own_ref = f32[40,40,128]{2,1,0:T(8,128)S(1)} custom-call(bf16[40,40,128]{2,1,0:T(8,128)(2,1)S(1)} %get-tuple-element.42.own_ref, bf16[40,40,128]{2,1,0:T(8,128)(2,1)S(1)} %collective-permute-done.3.p_own, bf16[40,40,128]{2,1,0:T(8,128)(2,1)S(1)} %get-tuple-element.47.met_ref, bf16[40,40,128]{2,1,0:T(8,128)(2,1)S(1)} %collective-permute-done.5.p_met, ...), custom_call_target="tpu_custom_call" | custom-call | bytes 19188000 | tf_op jit(solution)/shard_map/sums/pallas_call | solution.py:540
  44.5 0.0 collective-permute-done.12.refs_1_
  44.6 0.0 collective-permute-done.11.refs_0_
  44.6 1.1 %join.2.refs_3_ = bf16[40,40,128]{2,1,0:T(8,128)(2,1)} custom-call(f32[40,40,128]{2,1,0:T(8,128)S(1)} %sums.6.own_ref, bf16[40,40,128]{2,1,0:T(8,128)(2,1)S(1)} %get-tuple-element.50.psum_ref, f32[40,40,128]{2,1,0:T(8,128)S(1)} %get-tuple-element.51.gate_ref, bf16[128,128]{1,0:T(8,128)(2,1)S(1)} %get-tuple-element.52.w_ref, ...), custom_call_target="tpu_custom_call" | custom-call | bytes 3542400 | tf_op jit(solution)/shard_map/join/pallas_call | solution.py:627
  45.6 0.0 collective-permute-done.10.refs_2_
  45.6 0.2 collective-permute-done.9.refs_1_
  45.8 1.8 %collective-permute-done.8.refs_0_ = bf16[8,40,128]{2,1,0:T(8,128)(2,1)S(1)} collective-permute-done((bf16[8,40,128]{2,1,0:T(8,128)(2,1)S(1)}, bf16[8,40,128]{2,1,0:T(8,128)(2,1)S(1)}, u32[]{:S(2)}, u32[]{:S(2)}) %collective-permute-start.8) | collective-permute-done | bytes 81952 | tf_op jit(solution)/shard_map/ppermute | solution.py:537
  47.6 1.2 %join.3 = bf16[40,40,128]{2,1,0:T(8,128)(2,1)} custom-call(f32[40,40,128]{2,1,0:T(8,128)S(1)} %sums.6.own_ref, bf16[40,40,128]{2,1,0:T(8,128)(2,1)S(1)} %get-tuple-element.50.psum_ref, f32[40,40,128]{2,1,0:T(8,128)S(1)} %get-tuple-element.51.gate_ref, bf16[128,128]{1,0:T(8,128)(2,1)S(1)} %get-tuple-element.52.w_ref, ...), custom_call_target="tpu_custom_call", output_to_operand_aliasing={{}: (7, {})} | custom-call | bytes 5313600 | tf_op jit(solution)/shard_map/join/pallas_call | solution.py:627
Async XLA Ops:
  1.6 5.8 %collective-permute-start = (bf16[48,256]{1,0:T(8,128)(2,1)S(1)}, bf16[48,256]{1,0:T(8,128)(2,1)S(1)}, u32[]{:S(2)}, u32[]{:S(2)}) collective-permute-start(bf16[48,256]{1,0:T(8,128)(2,1)S(1)} %get-tuple-element.31), channel_id=1, source_target_pairs={{0,4},{4,0},{8,12},{12,8},{1,5},{5,1},{9,13},{13,9},{2,6},{6,2},{1... | collective-permute-start | bytes 73736 | tf_op jit(solution)/shard_map/ppermute | solution.py:573
  2.1 5.3 %collective-permute-start.1 = (bf16[48,256]{1,0:T(8,128)(2,1)S(1)}, bf16[48,256]{1,0:T(8,128)(2,1)S(1)}, u32[]{:S(2)}, u32[]{:S(2)}) collective-permute-start(bf16[48,256]{1,0:T(8,128)(2,1)S(1)} %get-tuple-element.32), channel_id=1, source_target_pairs={{0,8},{4,12},{8,0},{12,4},{1,9},{5,13},{9,1},{13,5},{2,10},{6,14},... | collective-permute-start | bytes 73736 | tf_op jit(solution)/shard_map/ppermute | solution.py:573
  4.7 3.3 %collective-permute-start.2 = (bf16[48,256]{1,0:T(8,128)(2,1)S(1)}, bf16[48,256]{1,0:T(8,128)(2,1)S(1)}, u32[]{:S(2)}, u32[]{:S(2)}) collective-permute-start(bf16[48,256]{1,0:T(8,128)(2,1)S(1)} %get-tuple-element.33), channel_id=1, source_target_pairs={{0,12},{4,8},{8,4},{12,0},{1,13},{5,9},{9,5},{13,1},{2,14},{6,10},... | collective-permute-start | bytes 73736 | tf_op jit(solution)/shard_map/ppermute | solution.py:573
  4.7 12.0 %collective-permute-start.4 = (bf16[41,40,128]{2,1,0:T(8,128)(2,1)S(1)}, bf16[41,40,128]{2,1,0:T(8,128)(2,1)S(1)}, u32[]{:S(2)}, u32[]{:S(2)}) collective-permute-start(bf16[41,40,128]{2,1,0:T(8,128)(2,1)S(1)} %get-tuple-element.29.block_ref), channel_id=1, source_target_pairs={{0,1},{1,0},{2,3},{3,2},{4,5},{5,4},{6,7},{7,6},{8,9},{9,8},{10,11... | collective-permute-start | bytes 1259528 | tf_op jit(solution)/shard_map/ppermute | solution.py:537
  11.2 12.4 %collective-permute-start.6 = (bf16[40,40,128]{2,1,0:T(8,128)(2,1)S(1)}, bf16[40,40,128]{2,1,0:T(8,128)(2,1)S(1)}, u32[]{:S(2)}, u32[]{:S(2)}) collective-permute-start(bf16[40,40,128]{2,1,0:T(8,128)(2,1)S(1)} %get-tuple-element.42.own_ref), channel_id=1, source_target_pairs={{0,8},{1,12},{2,10},{3,14},{4,9},{5,13},{6,11},{7,15},{8,0},{9,4},... | collective-permute-start | bytes 1228808 | tf_op jit(solution)/shard_map/ppermute | solution.py:537
  12.3 11.3 %collective-permute-start.3 = (bf16[40,40,128]{2,1,0:T(8,128)(2,1)S(1)}, bf16[40,40,128]{2,1,0:T(8,128)(2,1)S(1)}, u32[]{:S(2)}, u32[]{:S(2)}) collective-permute-start(bf16[40,40,128]{2,1,0:T(8,128)(2,1)S(1)} %get-tuple-element.42.own_ref), channel_id=1, source_target_pairs={{0,4},{1,5},{2,6},{3,7},{4,0},{5,1},{6,2},{7,3},{8,12},{9,13},{10,... | collective-permute-start | bytes 1228808 | tf_op jit(solution)/shard_map/ppermute | solution.py:537
  19.3 4.3 %collective-permute-start.5 = (bf16[40,40,128]{2,1,0:T(8,128)(2,1)S(1)}, bf16[40,40,128]{2,1,0:T(8,128)(2,1)S(1)}, u32[]{:S(2)}, u32[]{:S(2)}) collective-permute-start(bf16[40,40,128]{2,1,0:T(8,128)(2,1)S(1)} %get-tuple-element.47.met_ref), channel_id=1, source_target_pairs={{0,4},{1,5},{2,6},{3,7},{4,0},{5,1},{6,2},{7,3},{8,12},{9,13},{10,... | collective-permute-start | bytes 1228808 | tf_op jit(solution)/shard_map/ppermute | solution.py:537
  23.6 1.7 %collective-permute-start.7 = (bf16[40,40,128]{2,1,0:T(8,128)(2,1)S(1)}, bf16[40,40,128]{2,1,0:T(8,128)(2,1)S(1)}, u32[]{:S(2)}, u32[]{:S(2)}) collective-permute-start(bf16[40,40,128]{2,1,0:T(8,128)(2,1)S(1)} %collective-permute-done.6.far_ref), channel_id=1, source_target_pairs={{0,4},{1,5},{2,6},{3,7},{4,0},{5,1},{6,2},{7,3},{8,12},{9,13},{10,... | collective-permute-start | bytes 1228808 | tf_op jit(solution)/shard_map/ppermute | solution.py:537
  26.4 18.1 %collective-permute-start.12 = (bf16[8,40,128]{2,1,0:T(8,128)(2,1)S(1)}, bf16[8,40,128]{2,1,0:T(8,128)(2,1)S(1)}, u32[]{:S(2)}, u32[]{:S(2)}) collective-permute-start(bf16[8,40,128]{2,1,0:T(8,128)(2,1)S(1)} %sums.11), channel_id=1, source_target_pairs={{0,2},{1,3},{2,0},{3,1},{4,6},{5,7},{6,4},{7,5},{8,10},{9,11},{10,... | collective-permute-start | bytes 245768 | tf_op jit(solution)/shard_map/ppermute | solution.py:537
  30.1 14.4 %collective-permute-start.11 = (bf16[8,40,128]{2,1,0:T(8,128)(2,1)S(1)}, bf16[8,40,128]{2,1,0:T(8,128)(2,1)S(1)}, u32[]{:S(2)}, u32[]{:S(2)}) collective-permute-start(bf16[8,40,128]{2,1,0:T(8,128)(2,1)S(1)} %sums.10), channel_id=1, source_target_pairs={{0,2},{1,3},{2,0},{3,1},{4,6},{5,7},{6,4},{7,5},{8,10},{9,11},{10,... | collective-permute-start | bytes 245768 | tf_op jit(solution)/shard_map/ppermute | solution.py:537
  31.6 14.1 %collective-permute-start.10 = (bf16[8,40,128]{2,1,0:T(8,128)(2,1)S(1)}, bf16[8,40,128]{2,1,0:T(8,128)(2,1)S(1)}, u32[]{:S(2)}, u32[]{:S(2)}) collective-permute-start(bf16[8,40,128]{2,1,0:T(8,128)(2,1)S(1)} %sums.9), channel_id=1, source_target_pairs={{0,2},{1,3},{2,0},{3,1},{4,6},{5,7},{6,4},{7,5},{8,10},{9,11},{10,... | collective-permute-start | bytes 245768 | tf_op jit(solution)/shard_map/ppermute | solution.py:537
  35.3 10.5 %collective-permute-start.9 = (bf16[8,40,128]{2,1,0:T(8,128)(2,1)S(1)}, bf16[8,40,128]{2,1,0:T(8,128)(2,1)S(1)}, u32[]{:S(2)}, u32[]{:S(2)}) collective-permute-start(bf16[8,40,128]{2,1,0:T(8,128)(2,1)S(1)} %sums.8), channel_id=1, source_target_pairs={{0,2},{1,3},{2,0},{3,1},{4,6},{5,7},{6,4},{7,5},{8,10},{9,11},{10,... | collective-permute-start | bytes 245768 | tf_op jit(solution)/shard_map/ppermute | solution.py:537
  36.7 10.8 %collective-permute-start.8 = (bf16[8,40,128]{2,1,0:T(8,128)(2,1)S(1)}, bf16[8,40,128]{2,1,0:T(8,128)(2,1)S(1)}, u32[]{:S(2)}, u32[]{:S(2)}) collective-permute-start(bf16[8,40,128]{2,1,0:T(8,128)(2,1)S(1)} %sums.7), channel_id=1, source_target_pairs={{0,2},{1,3},{2,0},{3,1},{4,6},{5,7},{6,4},{7,5},{8,10},{9,11},{10,... | collective-permute-start | bytes 245768 | tf_op jit(solution)/shard_map/ppermute | solution.py:537

commit v13 on v12

--- a/solution.py
+++ b/solution.py
@@ -224,7 +224,7 @@
     return acc
 
 
-def sums_body(own_pair, first, own_ref, p_own, met_ref, p_met, far_ref, p_far, l_ref, m_ref, o_ref, lf_ref):
+def sums_body(own_pair, first, own_ref, other_ref, p_other, met_ref, p_met, far_ref, p_far, l_ref, m_ref, o_ref, lf_ref):
     count, depth = o_ref.shape[0], l_ref.shape[1]
     group = 8
     lf_ref[:, pl.ds(0, depth), :] = l_ref[pl.ds(first, count)].astype(f32)
@@ -244,9 +244,9 @@
     near = ((r // 2) == (z // 2)) == own_pair
     table = [
         (near & keeper, own_ref, met_ref),
-        (near & ~keeper, p_own, p_met),
-        (~near & keeper, far_ref, p_far),
-        (~near & ~keeper, p_far, far_ref),
+        (near & ~keeper, far_ref, p_met),
+        (~near & keeper, p_other, far_ref),
+        (~near & ~keeper, other_ref, p_far),
     ]
     for cond, a, b in table:
         pl.when(cond)(functools.partial(use, (a, b)))
@@ -276,11 +276,11 @@
         start = pl.multiple_of(start * own_i, 8)
         return [y_ref[pl.ds(s * residues + start, own_i), lane : lane + width] for s in range(seqs)]
 
-    empty = jnp.zeros((own_i, seqs * width), f32)
-    shared = [empty] + cut(z, width) + cut(z ^ 1, width)
+    shared = cut(z, width) + cut(z ^ 1, width)
     below = jnp.zeros((height - own_i, lanes), f32)
     for d, out in enumerate(outs):
-        rows = jnp.concatenate(cut(me ^ d, 0) + shared, axis=1)
+        other = ((me ^ d) // 2 ^ 1) * 2 + z % 2
+        rows = jnp.concatenate(cut(me ^ d, 0) + cut(other, 0) + shared, axis=1)
         out[...] = jnp.concatenate([rows, below], axis=0).astype(bf16)
     copies[2].wait()
     mask = valid_ref[...].astype(f32).T
@@ -317,20 +317,16 @@
     lax.fori_loop(0, idt_ref.shape[0], spread, 0, unroll=8)
 
 
-def mix_body(seqs, width, *refs):
-    msgs, (wq_ref, pick_ref, t_ref, right_ref, xl_ref) = refs[:4], refs[4:]
+def mix_rows(seqs, width, lane0, msgs, wq_ref, t_ref, xl_ref):
     half, terms, both = t_ref.shape
     chans, own_i, total = both // 2, 2 * half, seqs * 4
     for r in range(4):
         m = msgs[r][pl.ds(0, own_i), :128].astype(f32)
         for s in range(seqs):
-            moved = pltpu.roll(m, 128 - s * width, 1) if s else m
+            lane = lane0 + s * width
+            moved = pltpu.roll(m, 128 - lane, 1) if lane else m
             xl_ref[pl.ds(r * seqs + s, own_i, stride=total), :] = moved
     lhs = xl_ref[:, :width].astype(bf16)
-    joined = jnp.concatenate([msg[:, 128:] for msg in msgs], axis=1)
-    for n in range(2):
-        right = jnp.dot(joined, pick_ref[n].reshape(512, terms), preferred_element_type=f32)[:own_i]
-        right_ref[n] = (right * (1.0 / total)).astype(bf16)
     for h in range(width // 2):
         out = jnp.dot(lhs, wq_ref[h], preferred_element_type=f32)
         parts = [out[:, d * chans : (d + 1) * chans].reshape(own_i, total, chans) for d in range(2)]
@@ -338,6 +334,16 @@
         where = pl.ds(h * 2 * total, 2 * total)
         t_ref[:, where, :chans] = block[:half]
         t_ref[:, where, chans:] = block[half:]
+
+
+def mix_body(seqs, width, *refs):
+    msgs, (wq_ref, pick_ref, t_ref, right_ref, xl_ref) = refs[:4], refs[4:]
+    own_j, terms = right_ref.shape[1:]
+    joined = jnp.concatenate([msg[:, 128:] for msg in msgs], axis=1)
+    for n in range(2):
+        right = jnp.dot(joined, pick_ref[n].reshape(512, terms), preferred_element_type=f32)[:own_j]
+        right_ref[n] = (right * (1.0 / (seqs * 4))).astype(bf16)
+    mix_rows(seqs, width, 0, msgs, wq_ref, t_ref, xl_ref)
 
 
 def block_norms(block_ref, t_ref, right, row0, col0, idt_ref, bias_ref, use):
@@ -398,6 +404,26 @@
         for n, left in enumerate(gated(block_ref, rows, flat, w_left)):
             left_ref[i + n] = left.astype(bf16)
             gate_ref[i + n] = gate[n * own_j : (n + 1) * own_j]
+
+
+def other_body(seqs, width, *refs):
+    msgs, refs = refs[:4], refs[4:]
+    wq_ref, block_ref, right_ref, idt_ref, bias_ref, win_ref, out_ref, t_ref, xl_ref, flat_ref = refs
+    own_j, own_i, _ = out_ref.shape
+    r, z = lax.axis_index("row"), lax.axis_index("col")
+    side = win_ref.shape[1] // 2
+    w_right = win_ref.at[:, pl.ds(side, side)]
+
+    def use(rows, psums, flat):
+        for at, right in zip(rows, gated(block_ref, rows, flat, w_right)):
+            flat_ref[pl.ds(at * own_j, own_j), :] = right
+
+    @pl.when((r % 2) != (z % 2))
+    def _():
+        mix_rows(seqs, width, seqs * width, msgs, wq_ref, t_ref, xl_ref)
+        block_norms(block_ref, t_ref, right_ref[0], (r ^ 3) * own_i, z * own_j, idt_ref, bias_ref, use)
+        for k in range(own_j):
+            out_ref[k] = flat_ref[pl.ds(k, own_i, stride=own_j), :].astype(bf16)
 
 
 def met_body(block_ref, t_ref, right_ref, idt_ref, bias_ref, win_ref, left_ref, out_ref, flat_ref):
@@ -573,6 +599,7 @@
         lax.ppermute(msgs[d], "row", [(r, r ^ d) for r in range(4)]) for d in (1, 2, 3)
     ]
     met = move(raw, lambda r, z: (r, z ^ 1))
+    raw_other = move(raw, lambda r, z: (r ^ 3, z) if keeper(r, z) else (r ^ 1, z))
 
     wq, pick, idt = pl.pallas_call(
         functools.partial(ready_body, seqs),
@@ -602,10 +629,15 @@
         own_body, 2.4, [square, struct((own_i * own_j, chans), bf16), square], flat,
         raw, t, mixed, idt, bias, w_in,
     )
-    far = move(right, lambda r, z: (r ^ 2, z) if keeper(r, z) else (r ^ 3, z ^ 1))
-    p_own = move(right, beside)
+    far = move(right, lambda r, z: (r ^ 1, z) if keeper(r, z) else (r ^ 2, z ^ 1))
     left, gate = call(rest_body, 0.6, [square, struct(couple.shape, f32)], [], raw, norm, w_in, w_gate)
-    met, *_ = lax.optimization_barrier((met, left))
+    other = call(
+        functools.partial(other_body, seqs, width), 3, square,
+        [pltpu.VMEM(t.shape, bf16), pltpu.VMEM((own_i * total, 128), f32)] + flat,
+        *msgs, wq, raw_other, mixed, idt, bias, w_in,
+    )
+    p_other = move(other, beside)
+    met, *_ = lax.optimization_barrier((met, other))
     met_left, met_right = call(met_body, 3, [square, square], flat, met, t, mixed, idt, bias, w_in)
     p_met = move(met_right, beside)
     far, *_ = lax.optimization_barrier((far, met_left))
@@ -615,14 +647,14 @@
         return call(
             functools.partial(sums_body, own_pair, first), 0.13 * n, struct((n, own_j, tri), dtype),
             [pltpu.VMEM((n, 2 * own_j, tri), f32)],
-            right, p_own, met_right, p_met, far, p_far, left, met_left,
+            right, other, p_other, met_right, p_met, far, p_far, left, met_left,
         )
 
     came = [move(sums(False, first, 8, bf16), lambda r, z: (r, z ^ 2)) for first in range(0, own_i, 8)]
     kept = sums(True, 0, own_i, f32)
 
     out = []
-    for first, n in ((0, 16), (16, own_i - 16)):
+    for first, n in ((0, 16), (16, 16), (32, own_i - 32)):
         parts = came[first // 8 : (first + n) // 8]
         out = [pl.pallas_call(
             functools.partial(join_body, first, len(parts)),

time: 48.9 us -> 47.9 us (0.980)
  waiting for transfers between devices: 11.4 us -> 5.91 us
  starting transfers between devices: 15.8 us -> 19.1 us
  Pallas kernels: 21.3 us -> 22.4 us
    ppermute x10 -> x11, waiting for transfers between devices: 10.9 us -> 5.79 us  [move(): return lax.ppermute(value, ('row', 'col'), pairs)]
    ppermute x10 -> x11, starting transfers between devices: 12.6 us -> 16 us  [move(): return lax.ppermute(value, ('row', 'col'), pairs)]
    pallas_call x2 -> x3, Pallas kernels: 2.22 us -> 3.1 us  [paired_plan(): pl.pallas_call(functools.partial(join_body, first, len(parts)), out_shape...]
    pallas_call x10 -> x11, Pallas kernels: 16.7 us -> 16.8 us  [call(): pl.pallas_call(body, out_shape=out_shape, in_specs=[VMEM] * len(args), ou...]
  transfers between devices with their start and end apart: 13 -> 14, of which waited for: 6 -> 5; matrix products, arithmetic and copies ran while one was open for 0% -> 0% of each run, Pallas kernels for 36% -> 39%
where the time goes in v13:
time: 47.9 us; the launch traced here: 47.8 us
  Pallas kernels  22.4 us (47%)
  starting transfers between devices  19.1 us (40%)
  waiting for transfers between devices  5.91 us (12%)
    pallas_call x11, Pallas kernels, call(): pl.pallas_call(body, out_shape=out_shape, in_specs=[VMEM] * len(args), ou...  16.8 us
    ppermute x11, starting transfers between devices, move(): return lax.ppermute(value, ('row', 'col'), pairs)  16 us
    ppermute x11, waiting for transfers between devices, move(): return lax.ppermute(value, ('row', 'col'), pairs)  5.79 us
    ppermute x3, starting transfers between devices, paired_plan(): lax.ppermute(msgs[d], 'row', [(r, r ^ d) for r in range(4)])  3.15 us
    pallas_call x3, Pallas kernels, paired_plan(): pl.pallas_call(functools.partial(join_body, first, len(parts)), out_shape...  3.1 us
    pallas_call x1, Pallas kernels, paired_plan(): pl.pallas_call(open_body, out_shape=[struct((height, lanes), bf16)] * 4 +...  1.59 us
  transfers between devices with their start and end apart: 14, of which 5 were waited for; matrix products, arithmetic and copies ran while one was open for 0% of the time, Pallas kernels for 39%

profile of v13, /device:TPU:0, one launch (start us, length us, event | category | flops | bytes accessed | tf_op | source)
XLA Modules:
  0.0 47.8 jit_solution(4000326835483115674)
XLA Ops:
  0.0 1.6 %open.1 = (bf16[48,256]{1,0:T(8,128)(2,1)S(1)}, bf16[48,256]{1,0:T(8,128)(2,1)S(1)}, bf16[48,256]{1,0:T(8,128)(2,1)S(1)}, bf16[48,256]{1,0:T(8,128)(2,1)S(1)}, b...) custom-call(bf16[2,160,256]{2,1,0:T(8,128)(2,1)} %x_hbm.1, ...), custom_call_target="tpu_custom_call" | custom-call | bytes 5535000 | tf_op jit(solution)/shard_map/open/pallas_call | solution.py:582
  1.6 0.5 %collective-permute-start = (bf16[48,256]{1,0:T(8,128)(2,1)S(1)}, bf16[48,256]{1,0:T(8,128)(2,1)S(1)}, u32[]{:S(2)}, u32[]{:S(2)}) collective-permute-start(bf16[48,256]{1,0:T(8,128)(2,1)S(1)} %get-tuple-element.31), channel_id=1, source_target_pairs={{0,4},{4,0},{8,12},{12,8},{1,5},{5,1},{9,13},{13,9},{2,6},{6,2},{1... | collective-permute-start | bytes 73736 | tf_op jit(solution)/shard_map/ppermute | solution.py:599
  2.1 2.6 %collective-permute-start.1 = (bf16[48,256]{1,0:T(8,128)(2,1)S(1)}, bf16[48,256]{1,0:T(8,128)(2,1)S(1)}, u32[]{:S(2)}, u32[]{:S(2)}) collective-permute-start(bf16[48,256]{1,0:T(8,128)(2,1)S(1)} %get-tuple-element.32), channel_id=1, source_target_pairs={{0,8},{4,12},{8,0},{12,4},{1,9},{5,13},{9,1},{13,5},{2,10},{6,14},... | collective-permute-start | bytes 73736 | tf_op jit(solution)/shard_map/ppermute | solution.py:599
  4.7 0.1 collective-permute-start.2
  4.8 1.7 %collective-permute-start.3 = (bf16[41,40,128]{2,1,0:T(8,128)(2,1)S(1)}, bf16[41,40,128]{2,1,0:T(8,128)(2,1)S(1)}, u32[]{:S(2)}, u32[]{:S(2)}) collective-permute-start(bf16[41,40,128]{2,1,0:T(8,128)(2,1)S(1)} %get-tuple-element.29.block_ref), channel_id=1, source_target_pairs={{0,12},{1,5},{2,14},{3,7},{4,0},{5,9},{6,2},{7,11},{8,4},{9,13},{1... | collective-permute-start | bytes 1259528 | tf_op jit(solution)/shard_map/ppermute | solution.py:563
  6.4 0.5 %collective-permute-start.5 = (bf16[41,40,128]{2,1,0:T(8,128)(2,1)S(1)}, bf16[41,40,128]{2,1,0:T(8,128)(2,1)S(1)}, u32[]{:S(2)}, u32[]{:S(2)}) collective-permute-start(bf16[41,40,128]{2,1,0:T(8,128)(2,1)S(1)} %get-tuple-element.29.block_ref), channel_id=1, source_target_pairs={{0,1},{1,0},{2,3},{3,2},{4,5},{5,4},{6,7},{7,6},{8,9},{9,8},{10,11... | collective-permute-start | bytes 1259528 | tf_op jit(solution)/shard_map/ppermute | solution.py:563
  6.9 0.9 %ready.1 = (bf16[16,32,256]{2,1,0:T(8,128)(2,1)S(1)}, bf16[2,4,128,256]{3,2,1,0:T(8,128)(2,1)S(1)}, s32[160,128]{1,0:T(8,128)S(1)}) custom-call(bf16[1024,128]{1,0:T(8,128)(2,1)S(1)} %get-tuple-element.34.avg_ref, s32[160]{0:T(256)} %ids_hbm.1), custom_call_target="tpu_custom_call" | custom-call | bytes 5535000 | tf_op jit(solution)/shard_map/ready/pallas_call | solution.py:604
  7.8 0.0 collective-permute-done.refs_1_
  7.8 0.0 collective-permute-done.1.refs_2_
  7.8 0.1 collective-permute-done.2.refs_3_
  7.9 0.9 %mix.1 = (bf16[20,256,256]{2,1,0:T(8,128)(2,1)S(1)}, bf16[2,40,256]{2,1,0:T(8,128)(2,1)S(1)}) custom-call(bf16[48,256]{1,0:T(8,128)(2,1)S(1)} %get-tuple-element.30.refs_0_, bf16[48,256]{1,0:T(8,128)(2,1)S(1)} %collective-permute-done.refs_1_, bf16[48,256]{1,0:T(8,128)(2,1)S(1)} %collective-permute-done.1.refs_2_, ...), custom_call_target="tpu_custom_call" | custom-call | bytes 3690000 | tf_op jit(solution)/shard_map/mix/pallas_call | solution.py:566
  8.9 2.4 %own.1 = (bf16[40,40,128]{2,1,0:T(8,128)(2,1)S(1)}, bf16[1600,128]{1,0:T(8,128)(2,1)S(1)}, bf16[40,40,128]{2,1,0:T(8,128)(2,1)S(1)}) custom-call(bf16[41,40,128]{2,1,0:T(8,128)(2,1)S(1)} %get-tuple-element.29.block_ref, bf16[20,256,256]{2,1,0:T(8,128)(2,1)S(1)} %get-tuple-element.37.t_ref, bf16[2,40,256]{2,1,0:T(8,128)(2,1)S(1)} %get-tuple-element.38.right_ref.refs_6_, ...), custom_call_target="tpu_custom_call" | custom-call | bytes 8856000 | tf_op jit(solution)/shard_map/own/pallas_call | solution.py:566
  11.2 0.9 %collective-permute-start.7 = (bf16[40,40,128]{2,1,0:T(8,128)(2,1)S(1)}, bf16[40,40,128]{2,1,0:T(8,128)(2,1)S(1)}, u32[]{:S(2)}, u32[]{:S(2)}) collective-permute-start(bf16[40,40,128]{2,1,0:T(8,128)(2,1)S(1)} %get-tuple-element.42.own_ref), channel_id=1, source_target_pairs={{0,4},{1,8},{2,6},{3,10},{4,13},{5,1},{6,15},{7,3},{8,12},{9,0},{1... | collective-permute-start | bytes 1228808 | tf_op jit(solution)/shard_map/ppermute | solution.py:563
  12.2 0.0 collective-permute-done.3.refs_5_
  12.2 4.0 %collective-permute-start.4 = (bf16[40,40,128]{2,1,0:T(8,128)(2,1)S(1)}, bf16[40,40,128]{2,1,0:T(8,128)(2,1)S(1)}, u32[]{:S(2)}, u32[]{:S(2)}) collective-permute-start(bf16[40,40,128]{2,1,0:T(8,128)(2,1)S(1)} %other.1.other_ref), channel_id=1, source_target_pairs={{0,4},{1,5},{2,6},{3,7},{4,0},{5,1},{6,2},{7,3},{8,12},{9,13},{10,... | collective-permute-start | bytes 1228808 | tf_op jit(solution)/shard_map/ppermute | solution.py:563
  16.2 1.8 %collective-permute-done.5.block_ref = bf16[41,40,128]{2,1,0:T(8,128)(2,1)S(1)} collective-permute-done((bf16[41,40,128]{2,1,0:T(8,128)(2,1)S(1)}, bf16[41,40,128]{2,1,0:T(8,128)(2,1)S(1)}, u32[]{:S(2)}, u32[]{:S(2)}) %collective-permute-start.5) | collective-permute-done | bytes 419872 | tf_op jit(solution)/shard_map/ppermute | solution.py:563
  18.0 2.5 %met.1 = (bf16[40,40,128]{2,1,0:T(8,128)(2,1)S(1)}, bf16[40,40,128]{2,1,0:T(8,128)(2,1)S(1)}) custom-call(bf16[41,40,128]{2,1,0:T(8,128)(2,1)S(1)} %collective-permute-done.5.block_ref, bf16[20,256,256]{2,1,0:T(8,128)(2,1)S(1)} %get-tuple-element.37.t_ref, bf16[2,40,256]{2,1,0:T(8,128)(2,1)S(1)} %get-tuple-element.38.right_ref.refs_6_, ...), custom_call_target="tpu_custom_call" | custom-call | bytes 11070000 | tf_op jit(solution)/shard_map/met/pallas_call | solution.py:566
  20.6 0.1 collective-permute-start.6
  20.7 1.8 %collective-permute-done.7.far_ref = bf16[40,40,128]{2,1,0:T(8,128)(2,1)S(1)} collective-permute-done((bf16[40,40,128]{2,1,0:T(8,128)(2,1)S(1)}, bf16[40,40,128]{2,1,0:T(8,128)(2,1)S(1)}, u32[]{:S(2)}, u32[]{:S(2)}) %collective-permute-start.7) | collective-permute-done | bytes 409632 | tf_op jit(solution)/shard_map/ppermute | solution.py:563
  22.4 0.0 collective-permute-start.8
  22.4 0.5 %rest.1 = (bf16[40,40,128]{2,1,0:T(8,128)(2,1)S(1)}, f32[40,40,128]{2,1,0:T(8,128)S(1)}) custom-call(bf16[41,40,128]{2,1,0:T(8,128)(2,1)S(1)} %get-tuple-element.29.block_ref, bf16[1600,128]{1,0:T(8,128)(2,1)S(1)} %get-tuple-element.47.norm_ref, bf16[128,512]{1,0:T(8,128)(2,1)S(1)} %get-tuple-element.41.win_ref.refs_9_, ...), custom_call_target="tpu_custom_call" | custom-call | bytes 2214000 | tf_op jit(solution)/shard_map/rest/pallas_call | solution.py:566
  22.9 0.0 collective-permute-done.6.p_met
  22.9 0.0 collective-permute-done.4.p_other
  22.9 1.2 %collective-permute-done.8.p_far = bf16[40,40,128]{2,1,0:T(8,128)(2,1)S(1)} collective-permute-done((bf16[40,40,128]{2,1,0:T(8,128)(2,1)S(1)}, bf16[40,40,128]{2,1,0:T(8,128)(2,1)S(1)}, u32[]{:S(2)}, u32[]{:S(2)}) %collective-permute-start.8) | collective-permute-done | bytes 409632 | tf_op jit(solution)/shard_map/ppermute | solution.py:563
  24.2 1.0 %sums.10 = bf16[8,40,128]{2,1,0:T(8,128)(2,1)S(1)} custom-call(bf16[40,40,128]{2,1,0:T(8,128)(2,1)S(1)} %get-tuple-element.42.own_ref, bf16[40,40,128]{2,1,0:T(8,128)(2,1)S(1)} %other.1.other_ref, bf16[40,40,128]{2,1,0:T(8,128)(2,1)S(1)} %collective-permute-done.4.p_other, bf16[40,40,128]{2,1,0:T(8,128)(2,1)S(1)} %get-tuple-element.44.met_ref, ...), custom_call_target="tpu_custom_call" | custom-call | bytes 3837600 | tf_op jit(solution)/shard_map/sums/pallas_call | solution.py:566
  25.2 2.7 %collective-permute-start.12 = (bf16[8,40,128]{2,1,0:T(8,128)(2,1)S(1)}, bf16[8,40,128]{2,1,0:T(8,128)(2,1)S(1)}, u32[]{:S(2)}, u32[]{:S(2)}) collective-permute-start(bf16[8,40,128]{2,1,0:T(8,128)(2,1)S(1)} %sums.10), channel_id=1, source_target_pairs={{0,2},{1,3},{2,0},{3,1},{4,6},{5,7},{6,4},{7,5},{8,10},{9,11},{10,... | collective-permute-start | bytes 245768 | tf_op jit(solution)/shard_map/ppermute | solution.py:563
  27.9 1.0 %sums.11 = bf16[8,40,128]{2,1,0:T(8,128)(2,1)S(1)} custom-call(bf16[40,40,128]{2,1,0:T(8,128)(2,1)S(1)} %get-tuple-element.42.own_ref, bf16[40,40,128]{2,1,0:T(8,128)(2,1)S(1)} %other.1.other_ref, bf16[40,40,128]{2,1,0:T(8,128)(2,1)S(1)} %collective-permute-done.4.p_other, bf16[40,40,128]{2,1,0:T(8,128)(2,1)S(1)} %get-tuple-element.44.met_ref, ...), custom_call_target="tpu_custom_call" | custom-call | bytes 3837600 | tf_op jit(solution)/shard_map/sums/pallas_call | solution.py:566
  28.9 0.4 collective-permute-start.13
  29.3 1.0 %sums.8 = bf16[8,40,128]{2,1,0:T(8,128)(2,1)S(1)} custom-call(bf16[40,40,128]{2,1,0:T(8,128)(2,1)S(1)} %get-tuple-element.42.own_ref, bf16[40,40,128]{2,1,0:T(8,128)(2,1)S(1)} %other.1.other_ref, bf16[40,40,128]{2,1,0:T(8,128)(2,1)S(1)} %collective-permute-done.4.p_other, bf16[40,40,128]{2,1,0:T(8,128)(2,1)S(1)} %get-tuple-element.44.met_ref, ...), custom_call_target="tpu_custom_call" | custom-call | bytes 3837600 | tf_op jit(solution)/shard_map/sums/pallas_call | solution.py:566
  30.4 2.7 %collective-permute-start.10 = (bf16[8,40,128]{2,1,0:T(8,128)(2,1)S(1)}, bf16[8,40,128]{2,1,0:T(8,128)(2,1)S(1)}, u32[]{:S(2)}, u32[]{:S(2)}) collective-permute-start(bf16[8,40,128]{2,1,0:T(8,128)(2,1)S(1)} %sums.8), channel_id=1, source_target_pairs={{0,2},{1,3},{2,0},{3,1},{4,6},{5,7},{6,4},{7,5},{8,10},{9,11},{10,... | collective-permute-start | bytes 245768 | tf_op jit(solution)/shard_map/ppermute | solution.py:563
  33.0 1.2 %sums.9 = bf16[8,40,128]{2,1,0:T(8,128)(2,1)S(1)} custom-call(bf16[40,40,128]{2,1,0:T(8,128)(2,1)S(1)} %get-tuple-element.42.own_ref, bf16[40,40,128]{2,1,0:T(8,128)(2,1)S(1)} %other.1.other_ref, bf16[40,40,128]{2,1,0:T(8,128)(2,1)S(1)} %collective-permute-done.4.p_other, bf16[40,40,128]{2,1,0:T(8,128)(2,1)S(1)} %get-tuple-element.44.met_ref, ...), custom_call_target="tpu_custom_call" | custom-call | bytes 3837600 | tf_op jit(solution)/shard_map/sums/pallas_call | solution.py:566
  34.2 0.4 collective-permute-start.11
  34.6 1.0 %sums.7 = bf16[8,40,128]{2,1,0:T(8,128)(2,1)S(1)} custom-call(bf16[40,40,128]{2,1,0:T(8,128)(2,1)S(1)} %get-tuple-element.42.own_ref, bf16[40,40,128]{2,1,0:T(8,128)(2,1)S(1)} %other.1.other_ref, bf16[40,40,128]{2,1,0:T(8,128)(2,1)S(1)} %collective-permute-done.4.p_other, bf16[40,40,128]{2,1,0:T(8,128)(2,1)S(1)} %get-tuple-element.44.met_ref, ...), custom_call_target="tpu_custom_call" | custom-call | bytes 3837600 | tf_op jit(solution)/shard_map/sums/pallas_call | solution.py:566
  35.7 2.7 %collective-permute-start.9 = (bf16[8,40,128]{2,1,0:T(8,128)(2,1)S(1)}, bf16[8,40,128]{2,1,0:T(8,128)(2,1)S(1)}, u32[]{:S(2)}, u32[]{:S(2)}) collective-permute-start(bf16[8,40,128]{2,1,0:T(8,128)(2,1)S(1)} %sums.7), channel_id=1, source_target_pairs={{0,2},{1,3},{2,0},{3,1},{4,6},{5,7},{6,4},{7,5},{8,10},{9,11},{10,... | collective-permute-start | bytes 245768 | tf_op jit(solution)/shard_map/ppermute | solution.py:563
  38.3 5.1 %sums.6.own_ref = f32[40,40,128]{2,1,0:T(8,128)S(1)} custom-call(bf16[40,40,128]{2,1,0:T(8,128)(2,1)S(1)} %get-tuple-element.42.own_ref, bf16[40,40,128]{2,1,0:T(8,128)(2,1)S(1)} %other.1.other_ref, bf16[40,40,128]{2,1,0:T(8,128)(2,1)S(1)} %collective-permute-done.4.p_other, bf16[40,40,128]{2,1,0:T(8,128)(2,1)S(1)} %get-tuple-element.44.met_ref, ...), custom_call_target="tpu_custom_call" | custom-call | bytes 19188000 | tf_op jit(solution)/shard_map/sums/pallas_call | solution.py:566
  43.5 0.0 collective-permute-done.12.refs_0_
  43.5 0.0 collective-permute-done.13.refs_1_
  43.5 1.1 %join.3.refs_2_ = bf16[40,40,128]{2,1,0:T(8,128)(2,1)} custom-call(f32[40,40,128]{2,1,0:T(8,128)S(1)} %sums.6.own_ref, bf16[40,40,128]{2,1,0:T(8,128)(2,1)S(1)} %get-tuple-element.50.psum_ref, f32[40,40,128]{2,1,0:T(8,128)S(1)} %get-tuple-element.51.gate_ref, bf16[128,128]{1,0:T(8,128)(2,1)S(1)} %get-tuple-element.52.w_ref, ...), custom_call_target="tpu_custom_call" | custom-call | bytes 3542400 | tf_op jit(solution)/shard_map/join/pallas_call | solution.py:659
  44.6 0.0 collective-permute-done.10.refs_0_
  44.6 1.0 %collective-permute-done.11.refs_1_ = bf16[8,40,128]{2,1,0:T(8,128)(2,1)S(1)} collective-permute-done((bf16[8,40,128]{2,1,0:T(8,128)(2,1)S(1)}, bf16[8,40,128]{2,1,0:T(8,128)(2,1)S(1)}, u32[]{:S(2)}, u32[]{:S(2)}) %collective-permute-start.11) | collective-permute-done | bytes 81952 | tf_op jit(solution)/shard_map/ppermute | solution.py:563
  45.6 1.1 %join.4.refs_1_ = bf16[40,40,128]{2,1,0:T(8,128)(2,1)} custom-call(f32[40,40,128]{2,1,0:T(8,128)S(1)} %sums.6.own_ref, bf16[40,40,128]{2,1,0:T(8,128)(2,1)S(1)} %get-tuple-element.50.psum_ref, f32[40,40,128]{2,1,0:T(8,128)S(1)} %get-tuple-element.51.gate_ref, bf16[128,128]{1,0:T(8,128)(2,1)S(1)} %get-tuple-element.52.w_ref, ...), custom_call_target="tpu_custom_call", output_to_operand_aliasing={{}: (6, {})} | custom-call | bytes 3542400 | tf_op jit(solution)/shard_map/join/pallas_call | solution.py:659
  46.6 0.0 collective-permute-done.9.refs_0_
  46.6 1.0 %join.5 = bf16[40,40,128]{2,1,0:T(8,128)(2,1)} custom-call(f32[40,40,128]{2,1,0:T(8,128)S(1)} %sums.6.own_ref, bf16[40,40,128]{2,1,0:T(8,128)(2,1)S(1)} %get-tuple-element.50.psum_ref, f32[40,40,128]{2,1,0:T(8,128)S(1)} %get-tuple-element.51.gate_ref, bf16[128,128]{1,0:T(8,128)(2,1)S(1)} %get-tuple-element.52.w_ref, ...), custom_call_target="tpu_custom_call", output_to_operand_aliasing={{}: (5, {})} | custom-call | bytes 1771200 | tf_op jit(solution)/shard_map/join/pallas_call | solution.py:659
  (1 shorter events, 0.0 us)
Async XLA Ops:
  1.6 6.2 %collective-permute-start = (bf16[48,256]{1,0:T(8,128)(2,1)S(1)}, bf16[48,256]{1,0:T(8,128)(2,1)S(1)}, u32[]{:S(2)}, u32[]{:S(2)}) collective-permute-start(bf16[48,256]{1,0:T(8,128)(2,1)S(1)} %get-tuple-element.31), channel_id=1, source_target_pairs={{0,4},{4,0},{8,12},{12,8},{1,5},{5,1},{9,13},{13,9},{2,6},{6,2},{1... | collective-permute-start | bytes 73736 | tf_op jit(solution)/shard_map/ppermute | solution.py:599
  2.1 5.7 %collective-permute-start.1 = (bf16[48,256]{1,0:T(8,128)(2,1)S(1)}, bf16[48,256]{1,0:T(8,128)(2,1)S(1)}, u32[]{:S(2)}, u32[]{:S(2)}) collective-permute-start(bf16[48,256]{1,0:T(8,128)(2,1)S(1)} %get-tuple-element.32), channel_id=1, source_target_pairs={{0,8},{4,12},{8,0},{12,4},{1,9},{5,13},{9,1},{13,5},{2,10},{6,14},... | collective-permute-start | bytes 73736 | tf_op jit(solution)/shard_map/ppermute | solution.py:599
  4.7 3.3 %collective-permute-start.2 = (bf16[48,256]{1,0:T(8,128)(2,1)S(1)}, bf16[48,256]{1,0:T(8,128)(2,1)S(1)}, u32[]{:S(2)}, u32[]{:S(2)}) collective-permute-start(bf16[48,256]{1,0:T(8,128)(2,1)S(1)} %get-tuple-element.33), channel_id=1, source_target_pairs={{0,12},{4,8},{8,4},{12,0},{1,13},{5,9},{9,5},{13,1},{2,14},{6,10},... | collective-permute-start | bytes 73736 | tf_op jit(solution)/shard_map/ppermute | solution.py:599
  4.8 7.4 %collective-permute-start.3 = (bf16[41,40,128]{2,1,0:T(8,128)(2,1)S(1)}, bf16[41,40,128]{2,1,0:T(8,128)(2,1)S(1)}, u32[]{:S(2)}, u32[]{:S(2)}) collective-permute-start(bf16[41,40,128]{2,1,0:T(8,128)(2,1)S(1)} %get-tuple-element.29.block_ref), channel_id=1, source_target_pairs={{0,12},{1,5},{2,14},{3,7},{4,0},{5,9},{6,2},{7,11},{8,4},{9,13},{1... | collective-permute-start | bytes 1259528 | tf_op jit(solution)/shard_map/ppermute | solution.py:563
  6.4 11.6 %collective-permute-start.5 = (bf16[41,40,128]{2,1,0:T(8,128)(2,1)S(1)}, bf16[41,40,128]{2,1,0:T(8,128)(2,1)S(1)}, u32[]{:S(2)}, u32[]{:S(2)}) collective-permute-start(bf16[41,40,128]{2,1,0:T(8,128)(2,1)S(1)} %get-tuple-element.29.block_ref), channel_id=1, source_target_pairs={{0,1},{1,0},{2,3},{3,2},{4,5},{5,4},{6,7},{7,6},{8,9},{9,8},{10,11... | collective-permute-start | bytes 1259528 | tf_op jit(solution)/shard_map/ppermute | solution.py:563
  11.2 11.2 %collective-permute-start.7 = (bf16[40,40,128]{2,1,0:T(8,128)(2,1)S(1)}, bf16[40,40,128]{2,1,0:T(8,128)(2,1)S(1)}, u32[]{:S(2)}, u32[]{:S(2)}) collective-permute-start(bf16[40,40,128]{2,1,0:T(8,128)(2,1)S(1)} %get-tuple-element.42.own_ref), channel_id=1, source_target_pairs={{0,4},{1,8},{2,6},{3,10},{4,13},{5,1},{6,15},{7,3},{8,12},{9,0},{1... | collective-permute-start | bytes 1228808 | tf_op jit(solution)/shard_map/ppermute | solution.py:563
  12.2 10.8 %collective-permute-start.4 = (bf16[40,40,128]{2,1,0:T(8,128)(2,1)S(1)}, bf16[40,40,128]{2,1,0:T(8,128)(2,1)S(1)}, u32[]{:S(2)}, u32[]{:S(2)}) collective-permute-start(bf16[40,40,128]{2,1,0:T(8,128)(2,1)S(1)} %other.1.other_ref), channel_id=1, source_target_pairs={{0,4},{1,5},{2,6},{3,7},{4,0},{5,1},{6,2},{7,3},{8,12},{9,13},{10,... | collective-permute-start | bytes 1228808 | tf_op jit(solution)/shard_map/ppermute | solution.py:563
  20.6 2.3 %collective-permute-start.6 = (bf16[40,40,128]{2,1,0:T(8,128)(2,1)S(1)}, bf16[40,40,128]{2,1,0:T(8,128)(2,1)S(1)}, u32[]{:S(2)}, u32[]{:S(2)}) collective-permute-start(bf16[40,40,128]{2,1,0:T(8,128)(2,1)S(1)} %get-tuple-element.44.met_ref), channel_id=1, source_target_pairs={{0,4},{1,5},{2,6},{3,7},{4,0},{5,1},{6,2},{7,3},{8,12},{9,13},{10,... | collective-permute-start | bytes 1228808 | tf_op jit(solution)/shard_map/ppermute | solution.py:563
  22.4 1.7 %collective-permute-start.8 = (bf16[40,40,128]{2,1,0:T(8,128)(2,1)S(1)}, bf16[40,40,128]{2,1,0:T(8,128)(2,1)S(1)}, u32[]{:S(2)}, u32[]{:S(2)}) collective-permute-start(bf16[40,40,128]{2,1,0:T(8,128)(2,1)S(1)} %collective-permute-done.7.far_ref), channel_id=1, source_target_pairs={{0,4},{1,5},{2,6},{3,7},{4,0},{5,1},{6,2},{7,3},{8,12},{9,13},{10,... | collective-permute-start | bytes 1228808 | tf_op jit(solution)/shard_map/ppermute | solution.py:563
  25.2 18.3 %collective-permute-start.12 = (bf16[8,40,128]{2,1,0:T(8,128)(2,1)S(1)}, bf16[8,40,128]{2,1,0:T(8,128)(2,1)S(1)}, u32[]{:S(2)}, u32[]{:S(2)}) collective-permute-start(bf16[8,40,128]{2,1,0:T(8,128)(2,1)S(1)} %sums.10), channel_id=1, source_target_pairs={{0,2},{1,3},{2,0},{3,1},{4,6},{5,7},{6,4},{7,5},{8,10},{9,11},{10,... | collective-permute-start | bytes 245768 | tf_op jit(solution)/shard_map/ppermute | solution.py:563
  28.9 14.6 %collective-permute-start.13 = (bf16[8,40,128]{2,1,0:T(8,128)(2,1)S(1)}, bf16[8,40,128]{2,1,0:T(8,128)(2,1)S(1)}, u32[]{:S(2)}, u32[]{:S(2)}) collective-permute-start(bf16[8,40,128]{2,1,0:T(8,128)(2,1)S(1)} %sums.11), channel_id=1, source_target_pairs={{0,2},{1,3},{2,0},{3,1},{4,6},{5,7},{6,4},{7,5},{8,10},{9,11},{10,... | collective-permute-start | bytes 245768 | tf_op jit(solution)/shard_map/ppermute | solution.py:563
  30.4 14.2 %collective-permute-start.10 = (bf16[8,40,128]{2,1,0:T(8,128)(2,1)S(1)}, bf16[8,40,128]{2,1,0:T(8,128)(2,1)S(1)}, u32[]{:S(2)}, u32[]{:S(2)}) collective-permute-start(bf16[8,40,128]{2,1,0:T(8,128)(2,1)S(1)} %sums.8), channel_id=1, source_target_pairs={{0,2},{1,3},{2,0},{3,1},{4,6},{5,7},{6,4},{7,5},{8,10},{9,11},{10,... | collective-permute-start | bytes 245768 | tf_op jit(solution)/shard_map/ppermute | solution.py:563
  34.2 11.3 %collective-permute-start.11 = (bf16[8,40,128]{2,1,0:T(8,128)(2,1)S(1)}, bf16[8,40,128]{2,1,0:T(8,128)(2,1)S(1)}, u32[]{:S(2)}, u32[]{:S(2)}) collective-permute-start(bf16[8,40,128]{2,1,0:T(8,128)(2,1)S(1)} %sums.9), channel_id=1, source_target_pairs={{0,2},{1,3},{2,0},{3,1},{4,6},{5,7},{6,4},{7,5},{8,10},{9,11},{10,... | collective-permute-start | bytes 245768 | tf_op jit(solution)/shard_map/ppermute | solution.py:563
  35.7 10.9 %collective-permute-start.9 = (bf16[8,40,128]{2,1,0:T(8,128)(2,1)S(1)}, bf16[8,40,128]{2,1,0:T(8,128)(2,1)S(1)}, u32[]{:S(2)}, u32[]{:S(2)}) collective-permute-start(bf16[8,40,128]{2,1,0:T(8,128)(2,1)S(1)} %sums.7), channel_id=1, source_target_pairs={{0,2},{1,3},{2,0},{3,1},{4,6},{5,7},{6,4},{7,5},{8,10},{9,11},{10,... | collective-permute-start | bytes 245768 | tf_op jit(solution)/shard_map/ppermute | solution.py:563

commit v14 on v13

--- a/solution.py
+++ b/solution.py
@@ -254,11 +254,11 @@
 
 def open_body(x_hbm, w_hbm, valid_hbm, couple_hbm, *refs):
     later, outs, brought = refs[:5], refs[5:9], refs[9:14]
-    block_ref, x_ref, w_ref, valid_ref, y_ref, sem = refs[14:]
+    block_ref, longer_ref, x_ref, w_ref, valid_ref, y_ref, sem = refs[14:]
     own_i, own_j, chans = couple_hbm.shape
     copies = fetch([(x_hbm, x_ref), (w_hbm, w_ref), (valid_hbm, valid_ref),
                     (couple_hbm, block_ref.at[pl.ds(0, own_i)]),
-                    *zip(later, brought)], sem)
+                    (couple_hbm, longer_ref.at[pl.ds(0, own_i)]), *zip(later, brought)], sem)
     seqs, residues, depth = x_ref.shape
     width = w_ref.shape[0] // 2
     height, lanes = outs[0].shape
@@ -285,8 +285,9 @@
     copies[2].wait()
     mask = valid_ref[...].astype(f32).T
     mask = jnp.concatenate([mask, jnp.zeros((own_j, chans - own_i), f32)], axis=1)
-    for n in range(own_i, block_ref.shape[0]):
-        block_ref[n] = mask.astype(bf16)
+    block_ref[own_i] = mask.astype(bf16)
+    for n in range(own_i, longer_ref.shape[0]):
+        longer_ref[n] = mask.astype(bf16)
     for copy in copies[3:]:
         copy.wait()
 
@@ -578,18 +579,19 @@
     beside = lambda r, z: (r ^ 1, z)
     height, lanes = round_up(own_i, 16), 256
     block = struct((own_i + 1, own_j, chans), bf16)
+    longer = struct((own_i + 3, own_j, chans), bf16)
     later = (average, bias, w_in, w_gate, w_final)
-    *msgs, average, bias, w_in, w_gate, w_final, raw = pl.pallas_call(
+    *msgs, average, bias, w_in, w_gate, w_final, raw, raw_z = pl.pallas_call(
         open_body,
-        out_shape=[struct((height, lanes), bf16)] * 4 + [struct(x.shape, x.dtype) for x in later] + [block],
+        out_shape=[struct((height, lanes), bf16)] * 4 + [struct(x.shape, x.dtype) for x in later] + [block, longer],
         in_specs=[HBM] * 9,
-        out_specs=[VMEM] * 10,
+        out_specs=[VMEM] * 11,
         scratch_shapes=[
             pltpu.VMEM(homolog.shape, bf16),
             pltpu.VMEM((2 * width, depth), bf16),
             pltpu.VMEM(valid.shape, jnp.int32),
             pltpu.VMEM((seqs * residues, 2 * width), f32),
-            pltpu.SemaphoreType.DMA((9,)),
+            pltpu.SemaphoreType.DMA((10,)),
         ],
         compiler_params=limit(8),
         cost_estimate=cost(1.5),
@@ -598,7 +600,7 @@
     msgs = [msgs[0]] + [
         lax.ppermute(msgs[d], "row", [(r, r ^ d) for r in range(4)]) for d in (1, 2, 3)
     ]
-    met = move(raw, lambda r, z: (r, z ^ 1))
+    met = move(raw_z, lambda r, z: (r, z ^ 1))
     raw_other = move(raw, lambda r, z: (r ^ 3, z) if keeper(r, z) else (r ^ 1, z))
 
     wq, pick, idt = pl.pallas_call(
@@ -636,11 +638,12 @@
         [pltpu.VMEM(t.shape, bf16), pltpu.VMEM((own_i * total, 128), f32)] + flat,
         *msgs, wq, raw_other, mixed, idt, bias, w_in,
     )
-    p_other = move(other, beside)
     met, *_ = lax.optimization_barrier((met, other))
     met_left, met_right = call(met_body, 3, [square, square], flat, met, t, mixed, idt, bias, w_in)
+    other, *_ = lax.optimization_barrier((other, met_left))
+    p_other = move(other, beside)
     p_met = move(met_right, beside)
-    far, *_ = lax.optimization_barrier((far, met_left))
+    far, p_other, p_met = lax.optimization_barrier((far, p_other, p_met))
     p_far = move(far, beside)
 
     def sums(own_pair, first, n, dtype):

time: 47.9 us -> 50.9 us (1.063)
  waiting for transfers between devices: 5.91 us -> 8.71 us
    ppermute x3, waiting for transfers between devices: 0.12 us -> 4.91 us  [paired_plan(): lax.ppermute(msgs[d], 'row', [(r, r ^ d) for r in range(4)])]
    ppermute x11, waiting for transfers between devices: 5.79 us -> 3.8 us  [move(): return lax.ppermute(value, ('row', 'col'), pairs)]
    ppermute x11, starting transfers between devices: 16 us -> 17.5 us  [move(): return lax.ppermute(value, ('row', 'col'), pairs)]
    ppermute x3, starting transfers between devices: 3.15 us -> 1.86 us  [paired_plan(): lax.ppermute(msgs[d], 'row', [(r, r ^ d) for r in range(4)])]
  transfers between devices with their start and end apart: 14 -> 14, of which waited for: 5 -> 5; matrix products, arithmetic and copies ran while one was open for 0% -> 0% of each run, Pallas kernels for 39% -> 37%
where the time goes in v14:
time: 50.9 us; the launch traced here: 50.8 us
  Pallas kernels  22.4 us (44%)
  starting transfers between devices  19.3 us (38%)
  waiting for transfers between devices  8.71 us (17%)
    ppermute x11, starting transfers between devices, move(): return lax.ppermute(value, ('row', 'col'), pairs)  17.5 us
    pallas_call x11, Pallas kernels, call(): pl.pallas_call(body, out_shape=out_shape, in_specs=[VMEM] * len(args), ou...  16.8 us
    ppermute x3, waiting for transfers between devices, paired_plan(): lax.ppermute(msgs[d], 'row', [(r, r ^ d) for r in range(4)])  4.91 us
    ppermute x11, waiting for transfers between devices, move(): return lax.ppermute(value, ('row', 'col'), pairs)  3.8 us
    pallas_call x3, Pallas kernels, paired_plan(): pl.pallas_call(functools.partial(join_body, first, len(parts)), out_shape...  3.1 us
    ppermute x3, starting transfers between devices, paired_plan(): lax.ppermute(msgs[d], 'row', [(r, r ^ d) for r in range(4)])  1.86 us
    pallas_call x1, Pallas kernels, paired_plan(): pl.pallas_call(open_body, out_shape=[struct((height, lanes), bf16)] * 4 +...  1.6 us
  transfers between devices with their start and end apart: 14, of which 5 were waited for; matrix products, arithmetic and copies ran while one was open for 0% of the time, Pallas kernels for 37%

profile of v14, /device:TPU:0, one launch (start us, length us, event | category | flops | bytes accessed | tf_op | source)
XLA Modules:
  0.0 50.8 jit_solution(3466838095593846007)
XLA Ops:
  0.0 1.6 %open.1 = (bf16[48,256]{1,0:T(8,128)(2,1)S(1)}, bf16[48,256]{1,0:T(8,128)(2,1)S(1)}, bf16[48,256]{1,0:T(8,128)(2,1)S(1)}, bf16[48,256]{1,0:T(8,128)(2,1)S(1)}, b...) custom-call(bf16[2,160,256]{2,1,0:T(8,128)(2,1)} %x_hbm.1, ...), custom_call_target="tpu_custom_call" | custom-call | bytes 5535000 | tf_op jit(solution)/shard_map/open/pallas_call | solution.py:584
  1.6 3.1 %collective-permute-start.4 = (bf16[43,40,128]{2,1,0:T(8,128)(2,1)S(1)}, bf16[43,40,128]{2,1,0:T(8,128)(2,1)S(1)}, u32[]{:S(2)}, u32[]{:S(2)}) collective-permute-start(bf16[43,40,128]{2,1,0:T(8,128)(2,1)S(1)} %get-tuple-element.47), channel_id=1, source_target_pairs={{0,1},{1,0},{2,3},{3,2},{4,5},{5,4},{6,7},{7,6},{8,9},{9,8},{10,11... | collective-permute-start | bytes 1320968 | tf_op jit(solution)/shard_map/ppermute | solution.py:564
  4.7 0.7 %collective-permute-start.3 = (bf16[41,40,128]{2,1,0:T(8,128)(2,1)S(1)}, bf16[41,40,128]{2,1,0:T(8,128)(2,1)S(1)}, u32[]{:S(2)}, u32[]{:S(2)}) collective-permute-start(bf16[41,40,128]{2,1,0:T(8,128)(2,1)S(1)} %get-tuple-element.33.block_ref), channel_id=1, source_target_pairs={{0,12},{1,5},{2,14},{3,7},{4,0},{5,9},{6,2},{7,11},{8,4},{9,13},{1... | collective-permute-start | bytes 1259528 | tf_op jit(solution)/shard_map/ppermute | solution.py:564
  5.4 0.0 collective-permute-start
  5.4 1.3 %collective-permute-start.1 = (bf16[48,256]{1,0:T(8,128)(2,1)S(1)}, bf16[48,256]{1,0:T(8,128)(2,1)S(1)}, u32[]{:S(2)}, u32[]{:S(2)}) collective-permute-start(bf16[48,256]{1,0:T(8,128)(2,1)S(1)} %get-tuple-element.36), channel_id=1, source_target_pairs={{0,8},{4,12},{8,0},{12,4},{1,9},{5,13},{9,1},{13,5},{2,10},{6,14},... | collective-permute-start | bytes 73736 | tf_op jit(solution)/shard_map/ppermute | solution.py:601
  6.7 0.5 %collective-permute-start.2 = (bf16[48,256]{1,0:T(8,128)(2,1)S(1)}, bf16[48,256]{1,0:T(8,128)(2,1)S(1)}, u32[]{:S(2)}, u32[]{:S(2)}) collective-permute-start(bf16[48,256]{1,0:T(8,128)(2,1)S(1)} %get-tuple-element.37), channel_id=1, source_target_pairs={{0,12},{4,8},{8,4},{12,0},{1,13},{5,9},{9,5},{13,1},{2,14},{6,10},... | collective-permute-start | bytes 73736 | tf_op jit(solution)/shard_map/ppermute | solution.py:601
  7.2 0.9 %ready.1 = (bf16[16,32,256]{2,1,0:T(8,128)(2,1)S(1)}, bf16[2,4,128,256]{3,2,1,0:T(8,128)(2,1)S(1)}, s32[160,128]{1,0:T(8,128)S(1)}) custom-call(bf16[1024,128]{1,0:T(8,128)(2,1)S(1)} %get-tuple-element.38.avg_ref, s32[160]{0:T(256)} %ids_hbm.1), custom_call_target="tpu_custom_call" | custom-call | bytes 5535000 | tf_op jit(solution)/shard_map/ready/pallas_call | solution.py:606
  8.1 0.0 collective-permute-done.refs_1_
  8.1 4.9 %collective-permute-done.1.refs_2_ = bf16[48,256]{1,0:T(8,128)(2,1)S(1)} collective-permute-done((bf16[48,256]{1,0:T(8,128)(2,1)S(1)}, bf16[48,256]{1,0:T(8,128)(2,1)S(1)}, u32[]{:S(2)}, u32[]{:S(2)}) %collective-permute-start.1) | collective-permute-done | bytes 24608 | tf_op jit(solution)/shard_map/ppermute | solution.py:601
  13.0 0.0 collective-permute-done.2.refs_3_
  13.0 0.9 %mix.1 = (bf16[20,256,256]{2,1,0:T(8,128)(2,1)S(1)}, bf16[2,40,256]{2,1,0:T(8,128)(2,1)S(1)}) custom-call(bf16[48,256]{1,0:T(8,128)(2,1)S(1)} %get-tuple-element.34.refs_0_, bf16[48,256]{1,0:T(8,128)(2,1)S(1)} %collective-permute-done.refs_1_, bf16[48,256]{1,0:T(8,128)(2,1)S(1)} %collective-permute-done.1.refs_2_, ...), custom_call_target="tpu_custom_call" | custom-call | bytes 3690000 | tf_op jit(solution)/shard_map/mix/pallas_call | solution.py:567
  13.9 2.4 %own.1 = (bf16[40,40,128]{2,1,0:T(8,128)(2,1)S(1)}, bf16[1600,128]{1,0:T(8,128)(2,1)S(1)}, bf16[40,40,128]{2,1,0:T(8,128)(2,1)S(1)}) custom-call(bf16[41,40,128]{2,1,0:T(8,128)(2,1)S(1)} %get-tuple-element.33.block_ref, bf16[20,256,256]{2,1,0:T(8,128)(2,1)S(1)} %get-tuple-element.41.t_ref, bf16[2,40,256]{2,1,0:T(8,128)(2,1)S(1)} %get-tuple-element.42.right_ref.refs_6_, ...), custom_call_target="tpu_custom_call" | custom-call | bytes 8856000 | tf_op jit(solution)/shard_map/own/pallas_call | solution.py:567
  16.3 0.4 collective-permute-start.5
  16.8 0.0 collective-permute-done.3.refs_5_
  16.8 0.0 collective-permute-done.4.block_ref
  16.8 2.5 %met.1 = (bf16[40,40,128]{2,1,0:T(8,128)(2,1)S(1)}, bf16[40,40,128]{2,1,0:T(8,128)(2,1)S(1)}) custom-call(bf16[43,40,128]{2,1,0:T(8,128)(2,1)S(1)} %collective-permute-done.4.block_ref, bf16[20,256,256]{2,1,0:T(8,128)(2,1)S(1)} %get-tuple-element.41.t_ref, bf16[2,40,256]{2,1,0:T(8,128)(2,1)S(1)} %get-tuple-element.42.right_ref.refs_6_, ...), custom_call_target="tpu_custom_call" | custom-call | bytes 11070000 | tf_op jit(solution)/shard_map/met/pallas_call | solution.py:567
  19.3 4.1 %collective-permute-start.6 = (bf16[40,40,128]{2,1,0:T(8,128)(2,1)S(1)}, bf16[40,40,128]{2,1,0:T(8,128)(2,1)S(1)}, u32[]{:S(2)}, u32[]{:S(2)}) collective-permute-start(bf16[40,40,128]{2,1,0:T(8,128)(2,1)S(1)} %other.1.other_ref), channel_id=1, source_target_pairs={{0,4},{1,5},{2,6},{3,7},{4,0},{5,1},{6,2},{7,3},{8,12},{9,13},{10,... | collective-permute-start | bytes 1228808 | tf_op jit(solution)/shard_map/ppermute | solution.py:564
  23.4 0.1 collective-permute-start.7
  23.5 1.8 %collective-permute-done.5.far_ref = bf16[40,40,128]{2,1,0:T(8,128)(2,1)S(1)} collective-permute-done((bf16[40,40,128]{2,1,0:T(8,128)(2,1)S(1)}, bf16[40,40,128]{2,1,0:T(8,128)(2,1)S(1)}, u32[]{:S(2)}, u32[]{:S(2)}) %collective-permute-start.5) | collective-permute-done | bytes 409632 | tf_op jit(solution)/shard_map/ppermute | solution.py:564
  25.2 0.0 collective-permute-done.6.p_other
  25.2 0.1 collective-permute-done.7.p_met
  25.3 0.4 collective-permute-start.8
  25.7 0.5 rest.1
  26.2 0.9 %collective-permute-done.8.p_far = bf16[40,40,128]{2,1,0:T(8,128)(2,1)S(1)} collective-permute-done((bf16[40,40,128]{2,1,0:T(8,128)(2,1)S(1)}, bf16[40,40,128]{2,1,0:T(8,128)(2,1)S(1)}, u32[]{:S(2)}, u32[]{:S(2)}) %collective-permute-start.8) | collective-permute-done | bytes 409632 | tf_op jit(solution)/shard_map/ppermute | solution.py:564
  27.1 1.0 %sums.10 = bf16[8,40,128]{2,1,0:T(8,128)(2,1)S(1)} custom-call(bf16[40,40,128]{2,1,0:T(8,128)(2,1)S(1)} %get-tuple-element.46.own_ref, bf16[40,40,128]{2,1,0:T(8,128)(2,1)S(1)} %other.1.other_ref, bf16[40,40,128]{2,1,0:T(8,128)(2,1)S(1)} %collective-permute-done.6.p_other, bf16[40,40,128]{2,1,0:T(8,128)(2,1)S(1)} %get-tuple-element.51.met_ref, ...), custom_call_target="tpu_custom_call" | custom-call | bytes 3837600 | tf_op jit(solution)/shard_map/sums/pallas_call | solution.py:567
  28.1 2.7 %collective-permute-start.12 = (bf16[8,40,128]{2,1,0:T(8,128)(2,1)S(1)}, bf16[8,40,128]{2,1,0:T(8,128)(2,1)S(1)}, u32[]{:S(2)}, u32[]{:S(2)}) collective-permute-start(bf16[8,40,128]{2,1,0:T(8,128)(2,1)S(1)} %sums.10), channel_id=1, source_target_pairs={{0,2},{1,3},{2,0},{3,1},{4,6},{5,7},{6,4},{7,5},{8,10},{9,11},{10,... | collective-permute-start | bytes 245768 | tf_op jit(solution)/shard_map/ppermute | solution.py:564
  30.8 1.0 %sums.11 = bf16[8,40,128]{2,1,0:T(8,128)(2,1)S(1)} custom-call(bf16[40,40,128]{2,1,0:T(8,128)(2,1)S(1)} %get-tuple-element.46.own_ref, bf16[40,40,128]{2,1,0:T(8,128)(2,1)S(1)} %other.1.other_ref, bf16[40,40,128]{2,1,0:T(8,128)(2,1)S(1)} %collective-permute-done.6.p_other, bf16[40,40,128]{2,1,0:T(8,128)(2,1)S(1)} %get-tuple-element.51.met_ref, ...), custom_call_target="tpu_custom_call" | custom-call | bytes 3837600 | tf_op jit(solution)/shard_map/sums/pallas_call | solution.py:567
  31.8 0.4 collective-permute-start.13
  32.2 1.0 %sums.8 = bf16[8,40,128]{2,1,0:T(8,128)(2,1)S(1)} custom-call(bf16[40,40,128]{2,1,0:T(8,128)(2,1)S(1)} %get-tuple-element.46.own_ref, bf16[40,40,128]{2,1,0:T(8,128)(2,1)S(1)} %other.1.other_ref, bf16[40,40,128]{2,1,0:T(8,128)(2,1)S(1)} %collective-permute-done.6.p_other, bf16[40,40,128]{2,1,0:T(8,128)(2,1)S(1)} %get-tuple-element.51.met_ref, ...), custom_call_target="tpu_custom_call" | custom-call | bytes 3837600 | tf_op jit(solution)/shard_map/sums/pallas_call | solution.py:567
  33.3 2.7 %collective-permute-start.10 = (bf16[8,40,128]{2,1,0:T(8,128)(2,1)S(1)}, bf16[8,40,128]{2,1,0:T(8,128)(2,1)S(1)}, u32[]{:S(2)}, u32[]{:S(2)}) collective-permute-start(bf16[8,40,128]{2,1,0:T(8,128)(2,1)S(1)} %sums.8), channel_id=1, source_target_pairs={{0,2},{1,3},{2,0},{3,1},{4,6},{5,7},{6,4},{7,5},{8,10},{9,11},{10,... | collective-permute-start | bytes 245768 | tf_op jit(solution)/shard_map/ppermute | solution.py:564
  35.9 1.2 %sums.9 = bf16[8,40,128]{2,1,0:T(8,128)(2,1)S(1)} custom-call(bf16[40,40,128]{2,1,0:T(8,128)(2,1)S(1)} %get-tuple-element.46.own_ref, bf16[40,40,128]{2,1,0:T(8,128)(2,1)S(1)} %other.1.other_ref, bf16[40,40,128]{2,1,0:T(8,128)(2,1)S(1)} %collective-permute-done.6.p_other, bf16[40,40,128]{2,1,0:T(8,128)(2,1)S(1)} %get-tuple-element.51.met_ref, ...), custom_call_target="tpu_custom_call" | custom-call | bytes 3837600 | tf_op jit(solution)/shard_map/sums/pallas_call | solution.py:567
  37.2 0.4 collective-permute-start.11
  37.6 1.0 %sums.7 = bf16[8,40,128]{2,1,0:T(8,128)(2,1)S(1)} custom-call(bf16[40,40,128]{2,1,0:T(8,128)(2,1)S(1)} %get-tuple-element.46.own_ref, bf16[40,40,128]{2,1,0:T(8,128)(2,1)S(1)} %other.1.other_ref, bf16[40,40,128]{2,1,0:T(8,128)(2,1)S(1)} %collective-permute-done.6.p_other, bf16[40,40,128]{2,1,0:T(8,128)(2,1)S(1)} %get-tuple-element.51.met_ref, ...), custom_call_target="tpu_custom_call" | custom-call | bytes 3837600 | tf_op jit(solution)/shard_map/sums/pallas_call | solution.py:567
  38.6 2.7 %collective-permute-start.9 = (bf16[8,40,128]{2,1,0:T(8,128)(2,1)S(1)}, bf16[8,40,128]{2,1,0:T(8,128)(2,1)S(1)}, u32[]{:S(2)}, u32[]{:S(2)}) collective-permute-start(bf16[8,40,128]{2,1,0:T(8,128)(2,1)S(1)} %sums.7), channel_id=1, source_target_pairs={{0,2},{1,3},{2,0},{3,1},{4,6},{5,7},{6,4},{7,5},{8,10},{9,11},{10,... | collective-permute-start | bytes 245768 | tf_op jit(solution)/shard_map/ppermute | solution.py:564
  41.3 5.1 %sums.6.own_ref = f32[40,40,128]{2,1,0:T(8,128)S(1)} custom-call(bf16[40,40,128]{2,1,0:T(8,128)(2,1)S(1)} %get-tuple-element.46.own_ref, bf16[40,40,128]{2,1,0:T(8,128)(2,1)S(1)} %other.1.other_ref, bf16[40,40,128]{2,1,0:T(8,128)(2,1)S(1)} %collective-permute-done.6.p_other, bf16[40,40,128]{2,1,0:T(8,128)(2,1)S(1)} %get-tuple-element.51.met_ref, ...), custom_call_target="tpu_custom_call" | custom-call | bytes 19188000 | tf_op jit(solution)/shard_map/sums/pallas_call | solution.py:567
  46.4 0.0 collective-permute-done.12.refs_0_
  46.4 0.0 collective-permute-done.13.refs_1_
  46.4 1.1 %join.3.refs_2_ = bf16[40,40,128]{2,1,0:T(8,128)(2,1)} custom-call(f32[40,40,128]{2,1,0:T(8,128)S(1)} %sums.6.own_ref, bf16[40,40,128]{2,1,0:T(8,128)(2,1)S(1)} %get-tuple-element.58.psum_ref, f32[40,40,128]{2,1,0:T(8,128)S(1)} %get-tuple-element.59.gate_ref, bf16[128,128]{1,0:T(8,128)(2,1)S(1)} %get-tuple-element.60.w_ref, ...), custom_call_target="tpu_custom_call" | custom-call | bytes 3542400 | tf_op jit(solution)/shard_map/join/pallas_call | solution.py:662
  47.5 0.0 collective-permute-done.10.refs_0_
  47.5 1.0 %collective-permute-done.11.refs_1_ = bf16[8,40,128]{2,1,0:T(8,128)(2,1)S(1)} collective-permute-done((bf16[8,40,128]{2,1,0:T(8,128)(2,1)S(1)}, bf16[8,40,128]{2,1,0:T(8,128)(2,1)S(1)}, u32[]{:S(2)}, u32[]{:S(2)}) %collective-permute-start.11) | collective-permute-done | bytes 81952 | tf_op jit(solution)/shard_map/ppermute | solution.py:564
  48.5 1.1 %join.4.refs_1_ = bf16[40,40,128]{2,1,0:T(8,128)(2,1)} custom-call(f32[40,40,128]{2,1,0:T(8,128)S(1)} %sums.6.own_ref, bf16[40,40,128]{2,1,0:T(8,128)(2,1)S(1)} %get-tuple-element.58.psum_ref, f32[40,40,128]{2,1,0:T(8,128)S(1)} %get-tuple-element.59.gate_ref, bf16[128,128]{1,0:T(8,128)(2,1)S(1)} %get-tuple-element.60.w_ref, ...), custom_call_target="tpu_custom_call", output_to_operand_aliasing={{}: (6, {})} | custom-call | bytes 3542400 | tf_op jit(solution)/shard_map/join/pallas_call | solution.py:662
  49.6 0.0 collective-permute-done.9.refs_0_
  49.6 1.0 %join.5 = bf16[40,40,128]{2,1,0:T(8,128)(2,1)} custom-call(f32[40,40,128]{2,1,0:T(8,128)S(1)} %sums.6.own_ref, bf16[40,40,128]{2,1,0:T(8,128)(2,1)S(1)} %get-tuple-element.58.psum_ref, f32[40,40,128]{2,1,0:T(8,128)S(1)} %get-tuple-element.59.gate_ref, bf16[128,128]{1,0:T(8,128)(2,1)S(1)} %get-tuple-element.60.w_ref, ...), custom_call_target="tpu_custom_call", output_to_operand_aliasing={{}: (5, {})} | custom-call | bytes 1771200 | tf_op jit(solution)/shard_map/join/pallas_call | solution.py:662
  (1 shorter events, 0.0 us)
Async XLA Ops:
  1.6 15.2 %collective-permute-start.4 = (bf16[43,40,128]{2,1,0:T(8,128)(2,1)S(1)}, bf16[43,40,128]{2,1,0:T(8,128)(2,1)S(1)}, u32[]{:S(2)}, u32[]{:S(2)}) collective-permute-start(bf16[43,40,128]{2,1,0:T(8,128)(2,1)S(1)} %get-tuple-element.47), channel_id=1, source_target_pairs={{0,1},{1,0},{2,3},{3,2},{4,5},{5,4},{6,7},{7,6},{8,9},{9,8},{10,11... | collective-permute-start | bytes 1320968 | tf_op jit(solution)/shard_map/ppermute | solution.py:564
  4.7 12.1 %collective-permute-start.3 = (bf16[41,40,128]{2,1,0:T(8,128)(2,1)S(1)}, bf16[41,40,128]{2,1,0:T(8,128)(2,1)S(1)}, u32[]{:S(2)}, u32[]{:S(2)}) collective-permute-start(bf16[41,40,128]{2,1,0:T(8,128)(2,1)S(1)} %get-tuple-element.33.block_ref), channel_id=1, source_target_pairs={{0,12},{1,5},{2,14},{3,7},{4,0},{5,9},{6,2},{7,11},{8,4},{9,13},{1... | collective-permute-start | bytes 1259528 | tf_op jit(solution)/shard_map/ppermute | solution.py:564
  5.4 2.7 %collective-permute-start = (bf16[48,256]{1,0:T(8,128)(2,1)S(1)}, bf16[48,256]{1,0:T(8,128)(2,1)S(1)}, u32[]{:S(2)}, u32[]{:S(2)}) collective-permute-start(bf16[48,256]{1,0:T(8,128)(2,1)S(1)} %get-tuple-element.35), channel_id=1, source_target_pairs={{0,4},{4,0},{8,12},{12,8},{1,5},{5,1},{9,13},{13,9},{2,6},{6,2},{1... | collective-permute-start | bytes 73736 | tf_op jit(solution)/shard_map/ppermute | solution.py:601
  5.4 7.7 %collective-permute-start.1 = (bf16[48,256]{1,0:T(8,128)(2,1)S(1)}, bf16[48,256]{1,0:T(8,128)(2,1)S(1)}, u32[]{:S(2)}, u32[]{:S(2)}) collective-permute-start(bf16[48,256]{1,0:T(8,128)(2,1)S(1)} %get-tuple-element.36), channel_id=1, source_target_pairs={{0,8},{4,12},{8,0},{12,4},{1,9},{5,13},{9,1},{13,5},{2,10},{6,14},... | collective-permute-start | bytes 73736 | tf_op jit(solution)/shard_map/ppermute | solution.py:601
  6.7 6.3 %collective-permute-start.2 = (bf16[48,256]{1,0:T(8,128)(2,1)S(1)}, bf16[48,256]{1,0:T(8,128)(2,1)S(1)}, u32[]{:S(2)}, u32[]{:S(2)}) collective-permute-start(bf16[48,256]{1,0:T(8,128)(2,1)S(1)} %get-tuple-element.37), channel_id=1, source_target_pairs={{0,12},{4,8},{8,4},{12,0},{1,13},{5,9},{9,5},{13,1},{2,14},{6,10},... | collective-permute-start | bytes 73736 | tf_op jit(solution)/shard_map/ppermute | solution.py:601
  16.3 8.9 %collective-permute-start.5 = (bf16[40,40,128]{2,1,0:T(8,128)(2,1)S(1)}, bf16[40,40,128]{2,1,0:T(8,128)(2,1)S(1)}, u32[]{:S(2)}, u32[]{:S(2)}) collective-permute-start(bf16[40,40,128]{2,1,0:T(8,128)(2,1)S(1)} %get-tuple-element.46.own_ref), channel_id=1, source_target_pairs={{0,4},{1,8},{2,6},{3,10},{4,13},{5,1},{6,15},{7,3},{8,12},{9,0},{1... | collective-permute-start | bytes 1228808 | tf_op jit(solution)/shard_map/ppermute | solution.py:564
  19.3 5.9 %collective-permute-start.6 = (bf16[40,40,128]{2,1,0:T(8,128)(2,1)S(1)}, bf16[40,40,128]{2,1,0:T(8,128)(2,1)S(1)}, u32[]{:S(2)}, u32[]{:S(2)}) collective-permute-start(bf16[40,40,128]{2,1,0:T(8,128)(2,1)S(1)} %other.1.other_ref), channel_id=1, source_target_pairs={{0,4},{1,5},{2,6},{3,7},{4,0},{5,1},{6,2},{7,3},{8,12},{9,13},{10,... | collective-permute-start | bytes 1228808 | tf_op jit(solution)/shard_map/ppermute | solution.py:564
  23.4 2.0 %collective-permute-start.7 = (bf16[40,40,128]{2,1,0:T(8,128)(2,1)S(1)}, bf16[40,40,128]{2,1,0:T(8,128)(2,1)S(1)}, u32[]{:S(2)}, u32[]{:S(2)}) collective-permute-start(bf16[40,40,128]{2,1,0:T(8,128)(2,1)S(1)} %get-tuple-element.51.met_ref), channel_id=1, source_target_pairs={{0,4},{1,5},{2,6},{3,7},{4,0},{5,1},{6,2},{7,3},{8,12},{9,13},{10,... | collective-permute-start | bytes 1228808 | tf_op jit(solution)/shard_map/ppermute | solution.py:564
  25.3 1.7 %collective-permute-start.8 = (bf16[40,40,128]{2,1,0:T(8,128)(2,1)S(1)}, bf16[40,40,128]{2,1,0:T(8,128)(2,1)S(1)}, u32[]{:S(2)}, u32[]{:S(2)}) collective-permute-start(bf16[40,40,128]{2,1,0:T(8,128)(2,1)S(1)} %collective-permute-done.5.far_ref), channel_id=1, source_target_pairs={{0,4},{1,5},{2,6},{3,7},{4,0},{5,1},{6,2},{7,3},{8,12},{9,13},{10,... | collective-permute-start | bytes 1228808 | tf_op jit(solution)/shard_map/ppermute | solution.py:564
  28.1 18.3 %collective-permute-start.12 = (bf16[8,40,128]{2,1,0:T(8,128)(2,1)S(1)}, bf16[8,40,128]{2,1,0:T(8,128)(2,1)S(1)}, u32[]{:S(2)}, u32[]{:S(2)}) collective-permute-start(bf16[8,40,128]{2,1,0:T(8,128)(2,1)S(1)} %sums.10), channel_id=1, source_target_pairs={{0,2},{1,3},{2,0},{3,1},{4,6},{5,7},{6,4},{7,5},{8,10},{9,11},{10,... | collective-permute-start | bytes 245768 | tf_op jit(solution)/shard_map/ppermute | solution.py:564
  31.8 14.6 %collective-permute-start.13 = (bf16[8,40,128]{2,1,0:T(8,128)(2,1)S(1)}, bf16[8,40,128]{2,1,0:T(8,128)(2,1)S(1)}, u32[]{:S(2)}, u32[]{:S(2)}) collective-permute-start(bf16[8,40,128]{2,1,0:T(8,128)(2,1)S(1)} %sums.11), channel_id=1, source_target_pairs={{0,2},{1,3},{2,0},{3,1},{4,6},{5,7},{6,4},{7,5},{8,10},{9,11},{10,... | collective-permute-start | bytes 245768 | tf_op jit(solution)/shard_map/ppermute | solution.py:564
  33.3 14.2 %collective-permute-start.10 = (bf16[8,40,128]{2,1,0:T(8,128)(2,1)S(1)}, bf16[8,40,128]{2,1,0:T(8,128)(2,1)S(1)}, u32[]{:S(2)}, u32[]{:S(2)}) collective-permute-start(bf16[8,40,128]{2,1,0:T(8,128)(2,1)S(1)} %sums.8), channel_id=1, source_target_pairs={{0,2},{1,3},{2,0},{3,1},{4,6},{5,7},{6,4},{7,5},{8,10},{9,11},{10,... | collective-permute-start | bytes 245768 | tf_op jit(solution)/shard_map/ppermute | solution.py:564
  37.2 11.4 %collective-permute-start.11 = (bf16[8,40,128]{2,1,0:T(8,128)(2,1)S(1)}, bf16[8,40,128]{2,1,0:T(8,128)(2,1)S(1)}, u32[]{:S(2)}, u32[]{:S(2)}) collective-permute-start(bf16[8,40,128]{2,1,0:T(8,128)(2,1)S(1)} %sums.9), channel_id=1, source_target_pairs={{0,2},{1,3},{2,0},{3,1},{4,6},{5,7},{6,4},{7,5},{8,10},{9,11},{10,... | collective-permute-start | bytes 245768 | tf_op jit(solution)/shard_map/ppermute | solution.py:564
  38.6 11.0 %collective-permute-start.9 = (bf16[8,40,128]{2,1,0:T(8,128)(2,1)S(1)}, bf16[8,40,128]{2,1,0:T(8,128)(2,1)S(1)}, u32[]{:S(2)}, u32[]{:S(2)}) collective-permute-start(bf16[8,40,128]{2,1,0:T(8,128)(2,1)S(1)} %sums.7), channel_id=1, source_target_pairs={{0,2},{1,3},{2,0},{3,1},{4,6},{5,7},{6,4},{7,5},{8,10},{9,11},{10,... | collective-permute-start | bytes 245768 | tf_op jit(solution)/shard_map/ppermute | solution.py:564

commit v15 on v14

--- a/solution.py
+++ b/solution.py
@@ -638,12 +638,11 @@
         [pltpu.VMEM(t.shape, bf16), pltpu.VMEM((own_i * total, 128), f32)] + flat,
         *msgs, wq, raw_other, mixed, idt, bias, w_in,
     )
+    p_other = move(other, beside)
     met, *_ = lax.optimization_barrier((met, other))
     met_left, met_right = call(met_body, 3, [square, square], flat, met, t, mixed, idt, bias, w_in)
-    other, *_ = lax.optimization_barrier((other, met_left))
-    p_other = move(other, beside)
     p_met = move(met_right, beside)
-    far, p_other, p_met = lax.optimization_barrier((far, p_other, p_met))
+    far, *_ = lax.optimization_barrier((far, met_left))
     p_far = move(far, beside)
 
     def sums(own_pair, first, n, dtype):

time: 50.9 us -> 46.7 us (0.917)
  waiting for transfers between devices: 8.71 us -> 3.65 us
  starting transfers between devices: 19.3 us -> 20.1 us
    ppermute x3, waiting for transfers between devices: 4.91 us -> 0.61 us  [paired_plan(): lax.ppermute(msgs[d], 'row', [(r, r ^ d) for r in range(4)])]
    ppermute x11, starting transfers between devices: 17.5 us -> 18.3 us  [move(): return lax.ppermute(value, ('row', 'col'), pairs)]
    ppermute x11, waiting for transfers between devices: 3.8 us -> 3.05 us  [move(): return lax.ppermute(value, ('row', 'col'), pairs)]
  transfers between devices with their start and end apart: 14 -> 14, of which waited for: 5 -> 6; matrix products, arithmetic and copies ran while one was open for 0% -> 0% of each run, Pallas kernels for 37% -> 40%
where the time goes in v15:
time: 46.7 us; the launch traced here: 46.5 us
  Pallas kernels  22.4 us (48%)
  starting transfers between devices  20.1 us (43%)
  waiting for transfers between devices  3.65 us (8%)
    ppermute x11, starting transfers between devices, move(): return lax.ppermute(value, ('row', 'col'), pairs)  18.3 us
    pallas_call x11, Pallas kernels, call(): pl.pallas_call(body, out_shape=out_shape, in_specs=[VMEM] * len(args), ou...  16.8 us
    pallas_call x3, Pallas kernels, paired_plan(): pl.pallas_call(functools.partial(join_body, first, len(parts)), out_shape...  3.1 us
    ppermute x11, waiting for transfers between devices, move(): return lax.ppermute(value, ('row', 'col'), pairs)  3.05 us
    ppermute x3, starting transfers between devices, paired_plan(): lax.ppermute(msgs[d], 'row', [(r, r ^ d) for r in range(4)])  1.86 us
    pallas_call x1, Pallas kernels, paired_plan(): pl.pallas_call(open_body, out_shape=[struct((height, lanes), bf16)] * 4 +...  1.6 us
  transfers between devices with their start and end apart: 14, of which 6 were waited for; matrix products, arithmetic and copies ran while one was open for 0% of the time, Pallas kernels for 40%

profile of v15, /device:TPU:0, one launch (start us, length us, event | category | flops | bytes accessed | tf_op | source)
XLA Modules:
  0.0 46.5 jit_solution(8928756821524383948)
XLA Ops:
  0.0 1.6 %open.1 = (bf16[48,256]{1,0:T(8,128)(2,1)S(1)}, bf16[48,256]{1,0:T(8,128)(2,1)S(1)}, bf16[48,256]{1,0:T(8,128)(2,1)S(1)}, bf16[48,256]{1,0:T(8,128)(2,1)S(1)}, b...) custom-call(bf16[2,160,256]{2,1,0:T(8,128)(2,1)} %x_hbm.1, ...), custom_call_target="tpu_custom_call" | custom-call | bytes 5535000 | tf_op jit(solution)/shard_map/open/pallas_call | solution.py:584
  1.6 3.1 %collective-permute-start.5 = (bf16[43,40,128]{2,1,0:T(8,128)(2,1)S(1)}, bf16[43,40,128]{2,1,0:T(8,128)(2,1)S(1)}, u32[]{:S(2)}, u32[]{:S(2)}) collective-permute-start(bf16[43,40,128]{2,1,0:T(8,128)(2,1)S(1)} %get-tuple-element.44), channel_id=1, source_target_pairs={{0,1},{1,0},{2,3},{3,2},{4,5},{5,4},{6,7},{7,6},{8,9},{9,8},{10,11... | collective-permute-start | bytes 1320968 | tf_op jit(solution)/shard_map/ppermute | solution.py:564
  4.7 0.0 collective-permute-start
  4.7 1.5 %collective-permute-start.1 = (bf16[48,256]{1,0:T(8,128)(2,1)S(1)}, bf16[48,256]{1,0:T(8,128)(2,1)S(1)}, u32[]{:S(2)}, u32[]{:S(2)}) collective-permute-start(bf16[48,256]{1,0:T(8,128)(2,1)S(1)} %get-tuple-element.33), channel_id=1, source_target_pairs={{0,8},{4,12},{8,0},{12,4},{1,9},{5,13},{9,1},{13,5},{2,10},{6,14},... | collective-permute-start | bytes 73736 | tf_op jit(solution)/shard_map/ppermute | solution.py:601
  6.2 0.4 collective-permute-start.2
  6.6 1.4 %collective-permute-start.3 = (bf16[41,40,128]{2,1,0:T(8,128)(2,1)S(1)}, bf16[41,40,128]{2,1,0:T(8,128)(2,1)S(1)}, u32[]{:S(2)}, u32[]{:S(2)}) collective-permute-start(bf16[41,40,128]{2,1,0:T(8,128)(2,1)S(1)} %get-tuple-element.30.block_ref), channel_id=1, source_target_pairs={{0,12},{1,5},{2,14},{3,7},{4,0},{5,9},{6,2},{7,11},{8,4},{9,13},{1... | collective-permute-start | bytes 1259528 | tf_op jit(solution)/shard_map/ppermute | solution.py:564
  7.9 0.9 %ready.1 = (bf16[16,32,256]{2,1,0:T(8,128)(2,1)S(1)}, bf16[2,4,128,256]{3,2,1,0:T(8,128)(2,1)S(1)}, s32[160,128]{1,0:T(8,128)S(1)}) custom-call(bf16[1024,128]{1,0:T(8,128)(2,1)S(1)} %get-tuple-element.35.avg_ref, s32[160]{0:T(256)} %ids_hbm.1), custom_call_target="tpu_custom_call" | custom-call | bytes 5535000 | tf_op jit(solution)/shard_map/ready/pallas_call | solution.py:606
  8.8 0.0 collective-permute-done.refs_1_
  8.8 0.0 collective-permute-done.1.refs_2_
  8.8 0.6 %collective-permute-done.2.refs_3_ = bf16[48,256]{1,0:T(8,128)(2,1)S(1)} collective-permute-done((bf16[48,256]{1,0:T(8,128)(2,1)S(1)}, bf16[48,256]{1,0:T(8,128)(2,1)S(1)}, u32[]{:S(2)}, u32[]{:S(2)}) %collective-permute-start.2) | collective-permute-done | bytes 24608 | tf_op jit(solution)/shard_map/ppermute | solution.py:601
  9.4 0.9 %mix.1 = (bf16[20,256,256]{2,1,0:T(8,128)(2,1)S(1)}, bf16[2,40,256]{2,1,0:T(8,128)(2,1)S(1)}) custom-call(bf16[48,256]{1,0:T(8,128)(2,1)S(1)} %get-tuple-element.31.refs_0_, bf16[48,256]{1,0:T(8,128)(2,1)S(1)} %collective-permute-done.refs_1_, bf16[48,256]{1,0:T(8,128)(2,1)S(1)} %collective-permute-done.1.refs_2_, ...), custom_call_target="tpu_custom_call" | custom-call | bytes 3690000 | tf_op jit(solution)/shard_map/mix/pallas_call | solution.py:567
  10.4 2.4 %own.1 = (bf16[40,40,128]{2,1,0:T(8,128)(2,1)S(1)}, bf16[1600,128]{1,0:T(8,128)(2,1)S(1)}, bf16[40,40,128]{2,1,0:T(8,128)(2,1)S(1)}) custom-call(bf16[41,40,128]{2,1,0:T(8,128)(2,1)S(1)} %get-tuple-element.30.block_ref, bf16[20,256,256]{2,1,0:T(8,128)(2,1)S(1)} %get-tuple-element.38.t_ref, bf16[2,40,256]{2,1,0:T(8,128)(2,1)S(1)} %get-tuple-element.39.right_ref.refs_6_, ...), custom_call_target="tpu_custom_call" | custom-call | bytes 8856000 | tf_op jit(solution)/shard_map/own/pallas_call | solution.py:567
  12.7 0.6 %collective-permute-start.7 = (bf16[40,40,128]{2,1,0:T(8,128)(2,1)S(1)}, bf16[40,40,128]{2,1,0:T(8,128)(2,1)S(1)}, u32[]{:S(2)}, u32[]{:S(2)}) collective-permute-start(bf16[40,40,128]{2,1,0:T(8,128)(2,1)S(1)} %get-tuple-element.43.own_ref), channel_id=1, source_target_pairs={{0,4},{1,8},{2,6},{3,10},{4,13},{5,1},{6,15},{7,3},{8,12},{9,0},{1... | collective-permute-start | bytes 1228808 | tf_op jit(solution)/shard_map/ppermute | solution.py:564
  13.3 0.2 collective-permute-done.3.refs_5_
  13.5 4.4 %collective-permute-start.4 = (bf16[40,40,128]{2,1,0:T(8,128)(2,1)S(1)}, bf16[40,40,128]{2,1,0:T(8,128)(2,1)S(1)}, u32[]{:S(2)}, u32[]{:S(2)}) collective-permute-start(bf16[40,40,128]{2,1,0:T(8,128)(2,1)S(1)} %other.1.other_ref), channel_id=1, source_target_pairs={{0,4},{1,5},{2,6},{3,7},{4,0},{5,1},{6,2},{7,3},{8,12},{9,13},{10,... | collective-permute-start | bytes 1228808 | tf_op jit(solution)/shard_map/ppermute | solution.py:564
  17.9 0.0 collective-permute-done.5.block_ref
  17.9 2.5 %met.1 = (bf16[40,40,128]{2,1,0:T(8,128)(2,1)S(1)}, bf16[40,40,128]{2,1,0:T(8,128)(2,1)S(1)}) custom-call(bf16[43,40,128]{2,1,0:T(8,128)(2,1)S(1)} %collective-permute-done.5.block_ref, bf16[20,256,256]{2,1,0:T(8,128)(2,1)S(1)} %get-tuple-element.38.t_ref, bf16[2,40,256]{2,1,0:T(8,128)(2,1)S(1)} %get-tuple-element.39.right_ref.refs_6_, ...), custom_call_target="tpu_custom_call" | custom-call | bytes 11070000 | tf_op jit(solution)/shard_map/met/pallas_call | solution.py:567
  20.4 0.1 collective-permute-start.6
  20.5 1.1 %collective-permute-done.7.far_ref = bf16[40,40,128]{2,1,0:T(8,128)(2,1)S(1)} collective-permute-done((bf16[40,40,128]{2,1,0:T(8,128)(2,1)S(1)}, bf16[40,40,128]{2,1,0:T(8,128)(2,1)S(1)}, u32[]{:S(2)}, u32[]{:S(2)}) %collective-permute-start.7) | collective-permute-done | bytes 409632 | tf_op jit(solution)/shard_map/ppermute | solution.py:564
  21.7 0.0 collective-permute-start.8
  21.7 0.5 %rest.1 = (bf16[40,40,128]{2,1,0:T(8,128)(2,1)S(1)}, f32[40,40,128]{2,1,0:T(8,128)S(1)}) custom-call(bf16[41,40,128]{2,1,0:T(8,128)(2,1)S(1)} %get-tuple-element.30.block_ref, bf16[1600,128]{1,0:T(8,128)(2,1)S(1)} %get-tuple-element.49.norm_ref, bf16[128,512]{1,0:T(8,128)(2,1)S(1)} %get-tuple-element.42.win_ref.refs_9_, ...), custom_call_target="tpu_custom_call" | custom-call | bytes 2214000 | tf_op jit(solution)/shard_map/rest/pallas_call | solution.py:567
  22.2 0.0 collective-permute-done.4.p_other
  22.2 0.1 collective-permute-done.6.p_met
  22.3 1.1 %collective-permute-done.8.p_far = bf16[40,40,128]{2,1,0:T(8,128)(2,1)S(1)} collective-permute-done((bf16[40,40,128]{2,1,0:T(8,128)(2,1)S(1)}, bf16[40,40,128]{2,1,0:T(8,128)(2,1)S(1)}, u32[]{:S(2)}, u32[]{:S(2)}) %collective-permute-start.8) | collective-permute-done | bytes 409632 | tf_op jit(solution)/shard_map/ppermute | solution.py:564
  23.4 1.0 %sums.10 = bf16[8,40,128]{2,1,0:T(8,128)(2,1)S(1)} custom-call(bf16[40,40,128]{2,1,0:T(8,128)(2,1)S(1)} %get-tuple-element.43.own_ref, bf16[40,40,128]{2,1,0:T(8,128)(2,1)S(1)} %other.1.other_ref, bf16[40,40,128]{2,1,0:T(8,128)(2,1)S(1)} %collective-permute-done.4.p_other, bf16[40,40,128]{2,1,0:T(8,128)(2,1)S(1)} %get-tuple-element.46.met_ref, ...), custom_call_target="tpu_custom_call" | custom-call | bytes 3837600 | tf_op jit(solution)/shard_map/sums/pallas_call | solution.py:567
  24.5 2.7 %collective-permute-start.12 = (bf16[8,40,128]{2,1,0:T(8,128)(2,1)S(1)}, bf16[8,40,128]{2,1,0:T(8,128)(2,1)S(1)}, u32[]{:S(2)}, u32[]{:S(2)}) collective-permute-start(bf16[8,40,128]{2,1,0:T(8,128)(2,1)S(1)} %sums.10), channel_id=1, source_target_pairs={{0,2},{1,3},{2,0},{3,1},{4,6},{5,7},{6,4},{7,5},{8,10},{9,11},{10,... | collective-permute-start | bytes 245768 | tf_op jit(solution)/shard_map/ppermute | solution.py:564
  27.1 1.0 %sums.11 = bf16[8,40,128]{2,1,0:T(8,128)(2,1)S(1)} custom-call(bf16[40,40,128]{2,1,0:T(8,128)(2,1)S(1)} %get-tuple-element.43.own_ref, bf16[40,40,128]{2,1,0:T(8,128)(2,1)S(1)} %other.1.other_ref, bf16[40,40,128]{2,1,0:T(8,128)(2,1)S(1)} %collective-permute-done.4.p_other, bf16[40,40,128]{2,1,0:T(8,128)(2,1)S(1)} %get-tuple-element.46.met_ref, ...), custom_call_target="tpu_custom_call" | custom-call | bytes 3837600 | tf_op jit(solution)/shard_map/sums/pallas_call | solution.py:567
  28.2 0.4 collective-permute-start.13
  28.6 1.0 %sums.8 = bf16[8,40,128]{2,1,0:T(8,128)(2,1)S(1)} custom-call(bf16[40,40,128]{2,1,0:T(8,128)(2,1)S(1)} %get-tuple-element.43.own_ref, bf16[40,40,128]{2,1,0:T(8,128)(2,1)S(1)} %other.1.other_ref, bf16[40,40,128]{2,1,0:T(8,128)(2,1)S(1)} %collective-permute-done.4.p_other, bf16[40,40,128]{2,1,0:T(8,128)(2,1)S(1)} %get-tuple-element.46.met_ref, ...), custom_call_target="tpu_custom_call" | custom-call | bytes 3837600 | tf_op jit(solution)/shard_map/sums/pallas_call | solution.py:567
  29.6 2.7 %collective-permute-start.10 = (bf16[8,40,128]{2,1,0:T(8,128)(2,1)S(1)}, bf16[8,40,128]{2,1,0:T(8,128)(2,1)S(1)}, u32[]{:S(2)}, u32[]{:S(2)}) collective-permute-start(bf16[8,40,128]{2,1,0:T(8,128)(2,1)S(1)} %sums.8), channel_id=1, source_target_pairs={{0,2},{1,3},{2,0},{3,1},{4,6},{5,7},{6,4},{7,5},{8,10},{9,11},{10,... | collective-permute-start | bytes 245768 | tf_op jit(solution)/shard_map/ppermute | solution.py:564
  32.3 1.2 %sums.9 = bf16[8,40,128]{2,1,0:T(8,128)(2,1)S(1)} custom-call(bf16[40,40,128]{2,1,0:T(8,128)(2,1)S(1)} %get-tuple-element.43.own_ref, bf16[40,40,128]{2,1,0:T(8,128)(2,1)S(1)} %other.1.other_ref, bf16[40,40,128]{2,1,0:T(8,128)(2,1)S(1)} %collective-permute-done.4.p_other, bf16[40,40,128]{2,1,0:T(8,128)(2,1)S(1)} %get-tuple-element.46.met_ref, ...), custom_call_target="tpu_custom_call" | custom-call | bytes 3837600 | tf_op jit(solution)/shard_map/sums/pallas_call | solution.py:567
  33.5 0.4 collective-permute-start.11
  33.9 1.0 %sums.7 = bf16[8,40,128]{2,1,0:T(8,128)(2,1)S(1)} custom-call(bf16[40,40,128]{2,1,0:T(8,128)(2,1)S(1)} %get-tuple-element.43.own_ref, bf16[40,40,128]{2,1,0:T(8,128)(2,1)S(1)} %other.1.other_ref, bf16[40,40,128]{2,1,0:T(8,128)(2,1)S(1)} %collective-permute-done.4.p_other, bf16[40,40,128]{2,1,0:T(8,128)(2,1)S(1)} %get-tuple-element.46.met_ref, ...), custom_call_target="tpu_custom_call" | custom-call | bytes 3837600 | tf_op jit(solution)/shard_map/sums/pallas_call | solution.py:567
  34.9 2.7 %collective-permute-start.9 = (bf16[8,40,128]{2,1,0:T(8,128)(2,1)S(1)}, bf16[8,40,128]{2,1,0:T(8,128)(2,1)S(1)}, u32[]{:S(2)}, u32[]{:S(2)}) collective-permute-start(bf16[8,40,128]{2,1,0:T(8,128)(2,1)S(1)} %sums.7), channel_id=1, source_target_pairs={{0,2},{1,3},{2,0},{3,1},{4,6},{5,7},{6,4},{7,5},{8,10},{9,11},{10,... | collective-permute-start | bytes 245768 | tf_op jit(solution)/shard_map/ppermute | solution.py:564
  37.6 5.1 %sums.6.own_ref = f32[40,40,128]{2,1,0:T(8,128)S(1)} custom-call(bf16[40,40,128]{2,1,0:T(8,128)(2,1)S(1)} %get-tuple-element.43.own_ref, bf16[40,40,128]{2,1,0:T(8,128)(2,1)S(1)} %other.1.other_ref, bf16[40,40,128]{2,1,0:T(8,128)(2,1)S(1)} %collective-permute-done.4.p_other, bf16[40,40,128]{2,1,0:T(8,128)(2,1)S(1)} %get-tuple-element.46.met_ref, ...), custom_call_target="tpu_custom_call" | custom-call | bytes 19188000 | tf_op jit(solution)/shard_map/sums/pallas_call | solution.py:567
  42.7 0.0 collective-permute-done.12.refs_0_
  42.7 0.0 collective-permute-done.13.refs_1_
  42.8 1.1 %join.3.refs_2_ = bf16[40,40,128]{2,1,0:T(8,128)(2,1)} custom-call(f32[40,40,128]{2,1,0:T(8,128)S(1)} %sums.6.own_ref, bf16[40,40,128]{2,1,0:T(8,128)(2,1)S(1)} %get-tuple-element.52.psum_ref, f32[40,40,128]{2,1,0:T(8,128)S(1)} %get-tuple-element.53.gate_ref, bf16[128,128]{1,0:T(8,128)(2,1)S(1)} %get-tuple-element.54.w_ref, ...), custom_call_target="tpu_custom_call" | custom-call | bytes 3542400 | tf_op jit(solution)/shard_map/join/pallas_call | solution.py:661
  43.8 0.0 collective-permute-done.10.refs_0_
  43.8 0.0 collective-permute-done.11.refs_1_
  43.8 1.1 %join.4.refs_1_ = bf16[40,40,128]{2,1,0:T(8,128)(2,1)} custom-call(f32[40,40,128]{2,1,0:T(8,128)S(1)} %sums.6.own_ref, bf16[40,40,128]{2,1,0:T(8,128)(2,1)S(1)} %get-tuple-element.52.psum_ref, f32[40,40,128]{2,1,0:T(8,128)S(1)} %get-tuple-element.53.gate_ref, bf16[128,128]{1,0:T(8,128)(2,1)S(1)} %get-tuple-element.54.w_ref, ...), custom_call_target="tpu_custom_call", output_to_operand_aliasing={{}: (6, {})} | custom-call | bytes 3542400 | tf_op jit(solution)/shard_map/join/pallas_call | solution.py:661
  44.9 0.5 %collective-permute-done.9.refs_0_ = bf16[8,40,128]{2,1,0:T(8,128)(2,1)S(1)} collective-permute-done((bf16[8,40,128]{2,1,0:T(8,128)(2,1)S(1)}, bf16[8,40,128]{2,1,0:T(8,128)(2,1)S(1)}, u32[]{:S(2)}, u32[]{:S(2)}) %collective-permute-start.9) | collective-permute-done | bytes 81952 | tf_op jit(solution)/shard_map/ppermute | solution.py:564
  45.4 1.0 %join.5 = bf16[40,40,128]{2,1,0:T(8,128)(2,1)} custom-call(f32[40,40,128]{2,1,0:T(8,128)S(1)} %sums.6.own_ref, bf16[40,40,128]{2,1,0:T(8,128)(2,1)S(1)} %get-tuple-element.52.psum_ref, f32[40,40,128]{2,1,0:T(8,128)S(1)} %get-tuple-element.53.gate_ref, bf16[128,128]{1,0:T(8,128)(2,1)S(1)} %get-tuple-element.54.w_ref, ...), custom_call_target="tpu_custom_call", output_to_operand_aliasing={{}: (5, {})} | custom-call | bytes 1771200 | tf_op jit(solution)/shard_map/join/pallas_call | solution.py:661
  (1 shorter events, 0.0 us)
Async XLA Ops:
  1.6 16.3 %collective-permute-start.5 = (bf16[43,40,128]{2,1,0:T(8,128)(2,1)S(1)}, bf16[43,40,128]{2,1,0:T(8,128)(2,1)S(1)}, u32[]{:S(2)}, u32[]{:S(2)}) collective-permute-start(bf16[43,40,128]{2,1,0:T(8,128)(2,1)S(1)} %get-tuple-element.44), channel_id=1, source_target_pairs={{0,1},{1,0},{2,3},{3,2},{4,5},{5,4},{6,7},{7,6},{8,9},{9,8},{10,11... | collective-permute-start | bytes 1320968 | tf_op jit(solution)/shard_map/ppermute | solution.py:564
  4.7 4.1 %collective-permute-start = (bf16[48,256]{1,0:T(8,128)(2,1)S(1)}, bf16[48,256]{1,0:T(8,128)(2,1)S(1)}, u32[]{:S(2)}, u32[]{:S(2)}) collective-permute-start(bf16[48,256]{1,0:T(8,128)(2,1)S(1)} %get-tuple-element.32), channel_id=1, source_target_pairs={{0,4},{4,0},{8,12},{12,8},{1,5},{5,1},{9,13},{13,9},{2,6},{6,2},{1... | collective-permute-start | bytes 73736 | tf_op jit(solution)/shard_map/ppermute | solution.py:601
  4.7 4.1 %collective-permute-start.1 = (bf16[48,256]{1,0:T(8,128)(2,1)S(1)}, bf16[48,256]{1,0:T(8,128)(2,1)S(1)}, u32[]{:S(2)}, u32[]{:S(2)}) collective-permute-start(bf16[48,256]{1,0:T(8,128)(2,1)S(1)} %get-tuple-element.33), channel_id=1, source_target_pairs={{0,8},{4,12},{8,0},{12,4},{1,9},{5,13},{9,1},{13,5},{2,10},{6,14},... | collective-permute-start | bytes 73736 | tf_op jit(solution)/shard_map/ppermute | solution.py:601
  6.2 3.3 %collective-permute-start.2 = (bf16[48,256]{1,0:T(8,128)(2,1)S(1)}, bf16[48,256]{1,0:T(8,128)(2,1)S(1)}, u32[]{:S(2)}, u32[]{:S(2)}) collective-permute-start(bf16[48,256]{1,0:T(8,128)(2,1)S(1)} %get-tuple-element.34), channel_id=1, source_target_pairs={{0,12},{4,8},{8,4},{12,0},{1,13},{5,9},{9,5},{13,1},{2,14},{6,10},... | collective-permute-start | bytes 73736 | tf_op jit(solution)/shard_map/ppermute | solution.py:601
  6.6 7.0 %collective-permute-start.3 = (bf16[41,40,128]{2,1,0:T(8,128)(2,1)S(1)}, bf16[41,40,128]{2,1,0:T(8,128)(2,1)S(1)}, u32[]{:S(2)}, u32[]{:S(2)}) collective-permute-start(bf16[41,40,128]{2,1,0:T(8,128)(2,1)S(1)} %get-tuple-element.30.block_ref), channel_id=1, source_target_pairs={{0,12},{1,5},{2,14},{3,7},{4,0},{5,9},{6,2},{7,11},{8,4},{9,13},{1... | collective-permute-start | bytes 1259528 | tf_op jit(solution)/shard_map/ppermute | solution.py:564
  12.7 8.9 %collective-permute-start.7 = (bf16[40,40,128]{2,1,0:T(8,128)(2,1)S(1)}, bf16[40,40,128]{2,1,0:T(8,128)(2,1)S(1)}, u32[]{:S(2)}, u32[]{:S(2)}) collective-permute-start(bf16[40,40,128]{2,1,0:T(8,128)(2,1)S(1)} %get-tuple-element.43.own_ref), channel_id=1, source_target_pairs={{0,4},{1,8},{2,6},{3,10},{4,13},{5,1},{6,15},{7,3},{8,12},{9,0},{1... | collective-permute-start | bytes 1228808 | tf_op jit(solution)/shard_map/ppermute | solution.py:564
  13.5 8.6 %collective-permute-start.4 = (bf16[40,40,128]{2,1,0:T(8,128)(2,1)S(1)}, bf16[40,40,128]{2,1,0:T(8,128)(2,1)S(1)}, u32[]{:S(2)}, u32[]{:S(2)}) collective-permute-start(bf16[40,40,128]{2,1,0:T(8,128)(2,1)S(1)} %other.1.other_ref), channel_id=1, source_target_pairs={{0,4},{1,5},{2,6},{3,7},{4,0},{5,1},{6,2},{7,3},{8,12},{9,13},{10,... | collective-permute-start | bytes 1228808 | tf_op jit(solution)/shard_map/ppermute | solution.py:564
  20.4 1.8 %collective-permute-start.6 = (bf16[40,40,128]{2,1,0:T(8,128)(2,1)S(1)}, bf16[40,40,128]{2,1,0:T(8,128)(2,1)S(1)}, u32[]{:S(2)}, u32[]{:S(2)}) collective-permute-start(bf16[40,40,128]{2,1,0:T(8,128)(2,1)S(1)} %get-tuple-element.46.met_ref), channel_id=1, source_target_pairs={{0,4},{1,5},{2,6},{3,7},{4,0},{5,1},{6,2},{7,3},{8,12},{9,13},{10,... | collective-permute-start | bytes 1228808 | tf_op jit(solution)/shard_map/ppermute | solution.py:564
  21.7 1.7 %collective-permute-start.8 = (bf16[40,40,128]{2,1,0:T(8,128)(2,1)S(1)}, bf16[40,40,128]{2,1,0:T(8,128)(2,1)S(1)}, u32[]{:S(2)}, u32[]{:S(2)}) collective-permute-start(bf16[40,40,128]{2,1,0:T(8,128)(2,1)S(1)} %collective-permute-done.7.far_ref), channel_id=1, source_target_pairs={{0,4},{1,5},{2,6},{3,7},{4,0},{5,1},{6,2},{7,3},{8,12},{9,13},{10,... | collective-permute-start | bytes 1228808 | tf_op jit(solution)/shard_map/ppermute | solution.py:564
  24.5 18.3 %collective-permute-start.12 = (bf16[8,40,128]{2,1,0:T(8,128)(2,1)S(1)}, bf16[8,40,128]{2,1,0:T(8,128)(2,1)S(1)}, u32[]{:S(2)}, u32[]{:S(2)}) collective-permute-start(bf16[8,40,128]{2,1,0:T(8,128)(2,1)S(1)} %sums.10), channel_id=1, source_target_pairs={{0,2},{1,3},{2,0},{3,1},{4,6},{5,7},{6,4},{7,5},{8,10},{9,11},{10,... | collective-permute-start | bytes 245768 | tf_op jit(solution)/shard_map/ppermute | solution.py:564
  28.2 14.6 %collective-permute-start.13 = (bf16[8,40,128]{2,1,0:T(8,128)(2,1)S(1)}, bf16[8,40,128]{2,1,0:T(8,128)(2,1)S(1)}, u32[]{:S(2)}, u32[]{:S(2)}) collective-permute-start(bf16[8,40,128]{2,1,0:T(8,128)(2,1)S(1)} %sums.11), channel_id=1, source_target_pairs={{0,2},{1,3},{2,0},{3,1},{4,6},{5,7},{6,4},{7,5},{8,10},{9,11},{10,... | collective-permute-start | bytes 245768 | tf_op jit(solution)/shard_map/ppermute | solution.py:564
  29.6 14.2 %collective-permute-start.10 = (bf16[8,40,128]{2,1,0:T(8,128)(2,1)S(1)}, bf16[8,40,128]{2,1,0:T(8,128)(2,1)S(1)}, u32[]{:S(2)}, u32[]{:S(2)}) collective-permute-start(bf16[8,40,128]{2,1,0:T(8,128)(2,1)S(1)} %sums.8), channel_id=1, source_target_pairs={{0,2},{1,3},{2,0},{3,1},{4,6},{5,7},{6,4},{7,5},{8,10},{9,11},{10,... | collective-permute-start | bytes 245768 | tf_op jit(solution)/shard_map/ppermute | solution.py:564
  33.5 10.3 %collective-permute-start.11 = (bf16[8,40,128]{2,1,0:T(8,128)(2,1)S(1)}, bf16[8,40,128]{2,1,0:T(8,128)(2,1)S(1)}, u32[]{:S(2)}, u32[]{:S(2)}) collective-permute-start(bf16[8,40,128]{2,1,0:T(8,128)(2,1)S(1)} %sums.9), channel_id=1, source_target_pairs={{0,2},{1,3},{2,0},{3,1},{4,6},{5,7},{6,4},{7,5},{8,10},{9,11},{10,... | collective-permute-start | bytes 245768 | tf_op jit(solution)/shard_map/ppermute | solution.py:564
  34.9 10.5 %collective-permute-start.9 = (bf16[8,40,128]{2,1,0:T(8,128)(2,1)S(1)}, bf16[8,40,128]{2,1,0:T(8,128)(2,1)S(1)}, u32[]{:S(2)}, u32[]{:S(2)}) collective-permute-start(bf16[8,40,128]{2,1,0:T(8,128)(2,1)S(1)} %sums.7), channel_id=1, source_target_pairs={{0,2},{1,3},{2,0},{3,1},{4,6},{5,7},{6,4},{7,5},{8,10},{9,11},{10,... | collective-permute-start | bytes 245768 | tf_op jit(solution)/shard_map/ppermute | solution.py:564

commit v16 on v15

--- a/solution.py
+++ b/solution.py
@@ -407,9 +407,15 @@
             gate_ref[i + n] = gate[n * own_j : (n + 1) * own_j]
 
 
-def other_body(seqs, width, *refs):
-    msgs, refs = refs[:4], refs[4:]
-    wq_ref, block_ref, right_ref, idt_ref, bias_ref, win_ref, out_ref, t_ref, xl_ref, flat_ref = refs
+def mix_other_body(seqs, width, *refs):
+    msgs, (wq_ref, t_ref, xl_ref) = refs[:4], refs[4:]
+
+    @pl.when((lax.axis_index("row") % 2) != (lax.axis_index("col") % 2))
+    def _():
+        mix_rows(seqs, width, seqs * width, msgs, wq_ref, t_ref, xl_ref)
+
+
+def other_body(block_ref, t_ref, right_ref, idt_ref, bias_ref, win_ref, out_ref, flat_ref):
     own_j, own_i, _ = out_ref.shape
     r, z = lax.axis_index("row"), lax.axis_index("col")
     side = win_ref.shape[1] // 2
@@ -421,13 +427,12 @@
 
     @pl.when((r % 2) != (z % 2))
     def _():
-        mix_rows(seqs, width, seqs * width, msgs, wq_ref, t_ref, xl_ref)
         block_norms(block_ref, t_ref, right_ref[0], (r ^ 3) * own_i, z * own_j, idt_ref, bias_ref, use)
         for k in range(own_j):
             out_ref[k] = flat_ref[pl.ds(k, own_i, stride=own_j), :].astype(bf16)
 
 
-def met_body(block_ref, t_ref, right_ref, idt_ref, bias_ref, win_ref, left_ref, out_ref, flat_ref):
+def met_body(block_ref, t_ref, right_ref, idt_ref, bias_ref, win_ref, left_ref, out_ref, flat_ref, norm_ref):
     own_i, own_j, _ = left_ref.shape
     r, z = lax.axis_index("row"), lax.axis_index("col")
     side = win_ref.shape[1] // 2
@@ -435,14 +440,20 @@
 
     def use(rows, psums, flat):
         lefts = gated(block_ref, rows, flat, w_left)
-        rights = gated(block_ref, rows, flat, w_right)
         for n, at in enumerate(rows):
             left_ref[at] = lefts[n].astype(bf16)
-            flat_ref[pl.ds(at * own_j, own_j), :] = rights[n]
+            norm_ref[pl.ds(at * own_j, own_j), :] = flat[n * own_j : (n + 1) * own_j]
 
     block_norms(block_ref, t_ref, right_ref[1], r * own_i, (z ^ 1) * own_j, idt_ref, bias_ref, use)
-    for k in range(own_j):
-        out_ref[k] = flat_ref[pl.ds(k, own_i, stride=own_j), :].astype(bf16)
+
+    @pl.when((r % 2) == (z % 2))
+    def _():
+        for i in range(0, own_i, 8):
+            flat = norm_ref[pl.ds(i * own_j, 8 * own_j), :]
+            for n, right in enumerate(gated(block_ref, list(range(i, i + 8)), flat, w_right)):
+                flat_ref[pl.ds((i + n) * own_j, own_j), :] = right
+        for k in range(own_j):
+            out_ref[k] = flat_ref[pl.ds(k, own_i, stride=own_j), :].astype(bf16)
 
 
 def join_body(first, parts, own_ref, psum_ref, gate_ref, w_ref, *refs):
@@ -601,8 +612,6 @@
         lax.ppermute(msgs[d], "row", [(r, r ^ d) for r in range(4)]) for d in (1, 2, 3)
     ]
     met = move(raw_z, lambda r, z: (r, z ^ 1))
-    raw_other = move(raw, lambda r, z: (r ^ 3, z) if keeper(r, z) else (r ^ 1, z))
-
     wq, pick, idt = pl.pallas_call(
         functools.partial(ready_body, seqs),
         out_shape=[struct((width // 2, width, 2 * chans), bf16),
@@ -620,6 +629,8 @@
         name="ready",
     )(average, hold(ids))
 
+    raw, msgs, idt = lax.optimization_barrier((raw, msgs, idt))
+    raw_other = move(raw, lambda r, z: (r ^ 3, z) if keeper(r, z) else (r ^ 1, z))
     t, mixed = call(
         functools.partial(mix_body, seqs, width), 1,
         [struct((own_i // 2, width * total, 2 * chans), bf16), struct((2, own_j, width * total), bf16)],
@@ -633,16 +644,20 @@
     )
     far = move(right, lambda r, z: (r ^ 1, z) if keeper(r, z) else (r ^ 2, z ^ 1))
     left, gate = call(rest_body, 0.6, [square, struct(couple.shape, f32)], [], raw, norm, w_in, w_gate)
-    other = call(
-        functools.partial(other_body, seqs, width), 3, square,
-        [pltpu.VMEM(t.shape, bf16), pltpu.VMEM((own_i * total, 128), f32)] + flat,
-        *msgs, wq, raw_other, mixed, idt, bias, w_in,
+    msgs, right = lax.optimization_barrier((msgs, right))
+    t_other = call(
+        functools.partial(mix_other_body, seqs, width), 1, struct(t.shape, bf16),
+        [pltpu.VMEM((own_i * total, 128), f32)], *msgs, wq,
     )
+    met, *_ = lax.optimization_barrier((met, t_other))
+    met_left, met_right = call(
+        met_body, 3, [square, square], flat + [pltpu.VMEM(norm.shape, bf16)], met, t, mixed, idt, bias, w_in
+    )
+    p_met = move(met_right, beside)
+    raw_other, *_ = lax.optimization_barrier((raw_other, met_left))
+    other = call(other_body, 2.4, square, flat, raw_other, t_other, mixed, idt, bias, w_in)
     p_other = move(other, beside)
-    met, *_ = lax.optimization_barrier((met, other))
-    met_left, met_right = call(met_body, 3, [square, square], flat, met, t, mixed, idt, bias, w_in)
-    p_met = move(met_right, beside)
-    far, *_ = lax.optimization_barrier((far, met_left))
+    far, other, p_met = lax.optimization_barrier((far, other, p_met))
     p_far = move(far, beside)
 
     def sums(own_pair, first, n, dtype):

time: 46.7 us -> 47.6 us (1.019)
  waiting for transfers between devices: 3.65 us -> 6.77 us
  starting transfers between devices: 20.1 us -> 17.6 us
    ppermute x11, starting transfers between devices: 18.3 us -> 15.8 us  [move(): return lax.ppermute(value, ('row', 'col'), pairs)]
    ppermute x11, waiting for transfers between devices: 3.05 us -> 4.78 us  [move(): return lax.ppermute(value, ('row', 'col'), pairs)]
    ppermute x3, waiting for transfers between devices: 0.61 us -> 1.99 us  [paired_plan(): lax.ppermute(msgs[d], 'row', [(r, r ^ d) for r in range(4)])]
    pallas_call x11 -> x12, Pallas kernels: 16.8 us -> 17.1 us  [call(): pl.pallas_call(body, out_shape=out_shape, in_specs=[VMEM] * len(args), ou...]
  transfers between devices with their start and end apart: 14 -> 14, of which waited for: 6 -> 7; matrix products, arithmetic and copies ran while one was open for 0% -> 0% of each run, Pallas kernels for 40% -> 40%
where the time goes in v16:
time: 47.6 us; the launch traced here: 47.4 us
  Pallas kernels  22.7 us (48%)
  starting transfers between devices  17.6 us (37%)
  waiting for transfers between devices  6.77 us (14%)
    pallas_call x12, Pallas kernels, call(): pl.pallas_call(body, out_shape=out_shape, in_specs=[VMEM] * len(args), ou...  17.1 us
    ppermute x11, starting transfers between devices, move(): return lax.ppermute(value, ('row', 'col'), pairs)  15.8 us
    ppermute x11, waiting for transfers between devices, move(): return lax.ppermute(value, ('row', 'col'), pairs)  4.78 us
    pallas_call x3, Pallas kernels, paired_plan(): pl.pallas_call(functools.partial(join_body, first, len(parts)), out_shape...  3.1 us
    ppermute x3, waiting for transfers between devices, paired_plan(): lax.ppermute(msgs[d], 'row', [(r, r ^ d) for r in range(4)])  1.99 us
    ppermute x3, starting transfers between devices, paired_plan(): lax.ppermute(msgs[d], 'row', [(r, r ^ d) for r in range(4)])  1.86 us
    pallas_call x1, Pallas kernels, paired_plan(): pl.pallas_call(open_body, out_shape=[struct((height, lanes), bf16)] * 4 +...  1.6 us
  transfers between devices with their start and end apart: 14, of which 7 were waited for; matrix products, arithmetic and copies ran while one was open for 0% of the time, Pallas kernels for 40%

profile of v16, /device:TPU:0, one launch (start us, length us, event | category | flops | bytes accessed | tf_op | source)
XLA Modules:
  0.0 47.4 jit_solution(4139056914983761503)
XLA Ops:
  0.0 1.6 %open.1 = (bf16[48,256]{1,0:T(8,128)(2,1)S(1)}, bf16[48,256]{1,0:T(8,128)(2,1)S(1)}, bf16[48,256]{1,0:T(8,128)(2,1)S(1)}, bf16[48,256]{1,0:T(8,128)(2,1)S(1)}, b...) custom-call(bf16[2,160,256]{2,1,0:T(8,128)(2,1)} %x_hbm.1, ...), custom_call_target="tpu_custom_call" | custom-call | bytes 5535000 | tf_op jit(solution)/shard_map/open/pallas_call | solution.py:595
  1.6 3.1 %collective-permute-start.5 = (bf16[43,40,128]{2,1,0:T(8,128)(2,1)S(1)}, bf16[43,40,128]{2,1,0:T(8,128)(2,1)S(1)}, u32[]{:S(2)}, u32[]{:S(2)}) collective-permute-start(bf16[43,40,128]{2,1,0:T(8,128)(2,1)S(1)} %get-tuple-element.65), channel_id=1, source_target_pairs={{0,1},{1,0},{2,3},{3,2},{4,5},{5,4},{6,7},{7,6},{8,9},{9,8},{10,11... | collective-permute-start | bytes 1320968 | tf_op jit(solution)/shard_map/ppermute | solution.py:575
  4.7 0.0 collective-permute-start
  4.7 1.5 %collective-permute-start.1 = (bf16[48,256]{1,0:T(8,128)(2,1)S(1)}, bf16[48,256]{1,0:T(8,128)(2,1)S(1)}, u32[]{:S(2)}, u32[]{:S(2)}) collective-permute-start(bf16[48,256]{1,0:T(8,128)(2,1)S(1)} %get-tuple-element.47), channel_id=1, source_target_pairs={{0,8},{4,12},{8,0},{12,4},{1,9},{5,13},{9,1},{13,5},{2,10},{6,14},... | collective-permute-start | bytes 73736 | tf_op jit(solution)/shard_map/ppermute | solution.py:612
  6.2 0.4 collective-permute-start.2
  6.6 0.9 %ready.1 = (bf16[16,32,256]{2,1,0:T(8,128)(2,1)S(1)}, bf16[2,4,128,256]{3,2,1,0:T(8,128)(2,1)S(1)}, s32[160,128]{1,0:T(8,128)S(1)}) custom-call(bf16[1024,128]{1,0:T(8,128)(2,1)S(1)} %get-tuple-element.49.avg_ref, s32[160]{0:T(256)} %ids_hbm.1), custom_call_target="tpu_custom_call" | custom-call | bytes 5535000 | tf_op jit(solution)/shard_map/ready/pallas_call | solution.py:615
  7.5 0.0 collective-permute-done.refs_1_
  7.5 1.1 %collective-permute-done.1.refs_2_ = bf16[48,256]{1,0:T(8,128)(2,1)S(1)} collective-permute-done((bf16[48,256]{1,0:T(8,128)(2,1)S(1)}, bf16[48,256]{1,0:T(8,128)(2,1)S(1)}, u32[]{:S(2)}, u32[]{:S(2)}) %collective-permute-start.1) | collective-permute-done | bytes 24608 | tf_op jit(solution)/shard_map/ppermute | solution.py:612
  8.5 0.9 %collective-permute-done.2.refs_3_ = bf16[48,256]{1,0:T(8,128)(2,1)S(1)} collective-permute-done((bf16[48,256]{1,0:T(8,128)(2,1)S(1)}, bf16[48,256]{1,0:T(8,128)(2,1)S(1)}, u32[]{:S(2)}, u32[]{:S(2)}) %collective-permute-start.2) | collective-permute-done | bytes 24608 | tf_op jit(solution)/shard_map/ppermute | solution.py:612
  9.4 0.8 %collective-permute-start.4 = (bf16[41,40,128]{2,1,0:T(8,128)(2,1)S(1)}, bf16[41,40,128]{2,1,0:T(8,128)(2,1)S(1)}, u32[]{:S(2)}, u32[]{:S(2)}) collective-permute-start(bf16[41,40,128]{2,1,0:T(8,128)(2,1)S(1)} %get-tuple-element.55.block_ref), channel_id=1, source_target_pairs={{0,12},{1,5},{2,14},{3,7},{4,0},{5,9},{6,2},{7,11},{8,4},{9,13},{1... | collective-permute-start | bytes 1259528 | tf_op jit(solution)/shard_map/ppermute | solution.py:575
  10.2 0.9 %mix.1 = (bf16[20,256,256]{2,1,0:T(8,128)(2,1)S(1)}, bf16[2,40,256]{2,1,0:T(8,128)(2,1)S(1)}) custom-call(bf16[48,256]{1,0:T(8,128)(2,1)S(1)} %get-tuple-element.66.refs_0_, bf16[48,256]{1,0:T(8,128)(2,1)S(1)} %collective-permute-done.refs_1_, bf16[48,256]{1,0:T(8,128)(2,1)S(1)} %collective-permute-done.1.refs_2_, ...), custom_call_target="tpu_custom_call" | custom-call | bytes 3690000 | tf_op jit(solution)/shard_map/mix/pallas_call | solution.py:578
  11.2 2.4 %own.1 = (bf16[40,40,128]{2,1,0:T(8,128)(2,1)S(1)}, bf16[1600,128]{1,0:T(8,128)(2,1)S(1)}, bf16[40,40,128]{2,1,0:T(8,128)(2,1)S(1)}) custom-call(bf16[41,40,128]{2,1,0:T(8,128)(2,1)S(1)} %get-tuple-element.55.block_ref, bf16[20,256,256]{2,1,0:T(8,128)(2,1)S(1)} %get-tuple-element.58.t_ref, bf16[2,40,256]{2,1,0:T(8,128)(2,1)S(1)} %get-tuple-element.59.right_ref, ...), custom_call_target="tpu_custom_call" | custom-call | bytes 8856000 | tf_op jit(solution)/shard_map/own/pallas_call | solution.py:578
  13.5 0.1 collective-permute-start.3
  13.6 1.2 %collective-permute-done.5.block_ref = bf16[43,40,128]{2,1,0:T(8,128)(2,1)S(1)} collective-permute-done((bf16[43,40,128]{2,1,0:T(8,128)(2,1)S(1)}, bf16[43,40,128]{2,1,0:T(8,128)(2,1)S(1)}, u32[]{:S(2)}, u32[]{:S(2)}) %collective-permute-start.5) | collective-permute-done | bytes 440352 | tf_op jit(solution)/shard_map/ppermute | solution.py:575
  14.8 2.8 %met.1 = (bf16[40,40,128]{2,1,0:T(8,128)(2,1)S(1)}, bf16[40,40,128]{2,1,0:T(8,128)(2,1)S(1)}) custom-call(bf16[43,40,128]{2,1,0:T(8,128)(2,1)S(1)} %collective-permute-done.5.block_ref, bf16[20,256,256]{2,1,0:T(8,128)(2,1)S(1)} %get-tuple-element.58.t_ref, bf16[2,40,256]{2,1,0:T(8,128)(2,1)S(1)} %get-tuple-element.59.right_ref, ...), custom_call_target="tpu_custom_call" | custom-call | bytes 11070000 | tf_op jit(solution)/shard_map/met/pallas_call | solution.py:578
  17.7 0.2 collective-permute-start.6
  17.9 0.0 collective-permute-done.4.block_ref
  17.9 2.8 %collective-permute-start.7 = (bf16[40,40,128]{2,1,0:T(8,128)(2,1)S(1)}, bf16[40,40,128]{2,1,0:T(8,128)(2,1)S(1)}, u32[]{:S(2)}, u32[]{:S(2)}) collective-permute-start(bf16[40,40,128]{2,1,0:T(8,128)(2,1)S(1)} %other.1.other_ref), channel_id=1, source_target_pairs={{0,4},{1,5},{2,6},{3,7},{4,0},{5,1},{6,2},{7,3},{8,12},{9,13},{10,... | collective-permute-start | bytes 1228808 | tf_op jit(solution)/shard_map/ppermute | solution.py:575
  20.7 1.7 %collective-permute-done.3.far_ref = bf16[40,40,128]{2,1,0:T(8,128)(2,1)S(1)} collective-permute-done((bf16[40,40,128]{2,1,0:T(8,128)(2,1)S(1)}, bf16[40,40,128]{2,1,0:T(8,128)(2,1)S(1)}, u32[]{:S(2)}, u32[]{:S(2)}) %collective-permute-start.3) | collective-permute-done | bytes 409632 | tf_op jit(solution)/shard_map/ppermute | solution.py:575
  22.4 0.0 collective-permute-done.6.p_met
  22.4 0.0 collective-permute-start.8
  22.5 0.5 %rest.1 = (bf16[40,40,128]{2,1,0:T(8,128)(2,1)S(1)}, f32[40,40,128]{2,1,0:T(8,128)S(1)}) custom-call(bf16[41,40,128]{2,1,0:T(8,128)(2,1)S(1)} %get-tuple-element.55.block_ref, bf16[1600,128]{1,0:T(8,128)(2,1)S(1)} %get-tuple-element.77.norm_ref, bf16[128,512]{1,0:T(8,128)(2,1)S(1)} %get-tuple-element.62.win_ref, bf16[128,128]{1,0:T(8,128)(2,1)S(1)} %get-tuple-element.78.wgate_ref), custom_call_target="tpu_custom_call" | custom-call | bytes 2214000 | tf_op jit(solution)/shard_map/rest/pallas_call | solution.py:578
  23.0 0.0 collective-permute-done.7.p_other
  23.0 1.2 %collective-permute-done.8.p_far = bf16[40,40,128]{2,1,0:T(8,128)(2,1)S(1)} collective-permute-done((bf16[40,40,128]{2,1,0:T(8,128)(2,1)S(1)}, bf16[40,40,128]{2,1,0:T(8,128)(2,1)S(1)}, u32[]{:S(2)}, u32[]{:S(2)}) %collective-permute-start.8) | collective-permute-done | bytes 409632 | tf_op jit(solution)/shard_map/ppermute | solution.py:575
  24.2 1.0 %sums.11 = bf16[8,40,128]{2,1,0:T(8,128)(2,1)S(1)} custom-call(bf16[40,40,128]{2,1,0:T(8,128)(2,1)S(1)} %get-tuple-element.64.own_ref, bf16[40,40,128]{2,1,0:T(8,128)(2,1)S(1)} %other.1.other_ref, bf16[40,40,128]{2,1,0:T(8,128)(2,1)S(1)} %collective-permute-done.7.p_other, bf16[40,40,128]{2,1,0:T(8,128)(2,1)S(1)} %get-tuple-element.73.met_ref, ...), custom_call_target="tpu_custom_call" | custom-call | bytes 3837600 | tf_op jit(solution)/shard_map/sums/pallas_call | solution.py:578
  25.2 2.7 %collective-permute-start.13 = (bf16[8,40,128]{2,1,0:T(8,128)(2,1)S(1)}, bf16[8,40,128]{2,1,0:T(8,128)(2,1)S(1)}, u32[]{:S(2)}, u32[]{:S(2)}) collective-permute-start(bf16[8,40,128]{2,1,0:T(8,128)(2,1)S(1)} %sums.11), channel_id=1, source_target_pairs={{0,2},{1,3},{2,0},{3,1},{4,6},{5,7},{6,4},{7,5},{8,10},{9,11},{10,... | collective-permute-start | bytes 245768 | tf_op jit(solution)/shard_map/ppermute | solution.py:575
  27.9 1.0 %sums.10 = bf16[8,40,128]{2,1,0:T(8,128)(2,1)S(1)} custom-call(bf16[40,40,128]{2,1,0:T(8,128)(2,1)S(1)} %get-tuple-element.64.own_ref, bf16[40,40,128]{2,1,0:T(8,128)(2,1)S(1)} %other.1.other_ref, bf16[40,40,128]{2,1,0:T(8,128)(2,1)S(1)} %collective-permute-done.7.p_other, bf16[40,40,128]{2,1,0:T(8,128)(2,1)S(1)} %get-tuple-element.73.met_ref, ...), custom_call_target="tpu_custom_call" | custom-call | bytes 3837600 | tf_op jit(solution)/shard_map/sums/pallas_call | solution.py:578
  28.9 0.4 collective-permute-start.12
  29.4 1.2 %sums.9 = bf16[8,40,128]{2,1,0:T(8,128)(2,1)S(1)} custom-call(bf16[40,40,128]{2,1,0:T(8,128)(2,1)S(1)} %get-tuple-element.64.own_ref, bf16[40,40,128]{2,1,0:T(8,128)(2,1)S(1)} %other.1.other_ref, bf16[40,40,128]{2,1,0:T(8,128)(2,1)S(1)} %collective-permute-done.7.p_other, bf16[40,40,128]{2,1,0:T(8,128)(2,1)S(1)} %get-tuple-element.73.met_ref, ...), custom_call_target="tpu_custom_call" | custom-call | bytes 3837600 | tf_op jit(solution)/shard_map/sums/pallas_call | solution.py:578
  30.6 2.7 %collective-permute-start.11 = (bf16[8,40,128]{2,1,0:T(8,128)(2,1)S(1)}, bf16[8,40,128]{2,1,0:T(8,128)(2,1)S(1)}, u32[]{:S(2)}, u32[]{:S(2)}) collective-permute-start(bf16[8,40,128]{2,1,0:T(8,128)(2,1)S(1)} %sums.9), channel_id=1, source_target_pairs={{0,2},{1,3},{2,0},{3,1},{4,6},{5,7},{6,4},{7,5},{8,10},{9,11},{10,... | collective-permute-start | bytes 245768 | tf_op jit(solution)/shard_map/ppermute | solution.py:575
  33.2 1.0 %sums.8 = bf16[8,40,128]{2,1,0:T(8,128)(2,1)S(1)} custom-call(bf16[40,40,128]{2,1,0:T(8,128)(2,1)S(1)} %get-tuple-element.64.own_ref, bf16[40,40,128]{2,1,0:T(8,128)(2,1)S(1)} %other.1.other_ref, bf16[40,40,128]{2,1,0:T(8,128)(2,1)S(1)} %collective-permute-done.7.p_other, bf16[40,40,128]{2,1,0:T(8,128)(2,1)S(1)} %get-tuple-element.73.met_ref, ...), custom_call_target="tpu_custom_call" | custom-call | bytes 3837600 | tf_op jit(solution)/shard_map/sums/pallas_call | solution.py:578
  34.3 0.4 collective-permute-start.10
  34.7 1.0 %sums.7 = bf16[8,40,128]{2,1,0:T(8,128)(2,1)S(1)} custom-call(bf16[40,40,128]{2,1,0:T(8,128)(2,1)S(1)} %get-tuple-element.64.own_ref, bf16[40,40,128]{2,1,0:T(8,128)(2,1)S(1)} %other.1.other_ref, bf16[40,40,128]{2,1,0:T(8,128)(2,1)S(1)} %collective-permute-done.7.p_other, bf16[40,40,128]{2,1,0:T(8,128)(2,1)S(1)} %get-tuple-element.73.met_ref, ...), custom_call_target="tpu_custom_call" | custom-call | bytes 3837600 | tf_op jit(solution)/shard_map/sums/pallas_call | solution.py:578
  35.7 2.7 %collective-permute-start.9 = (bf16[8,40,128]{2,1,0:T(8,128)(2,1)S(1)}, bf16[8,40,128]{2,1,0:T(8,128)(2,1)S(1)}, u32[]{:S(2)}, u32[]{:S(2)}) collective-permute-start(bf16[8,40,128]{2,1,0:T(8,128)(2,1)S(1)} %sums.7), channel_id=1, source_target_pairs={{0,2},{1,3},{2,0},{3,1},{4,6},{5,7},{6,4},{7,5},{8,10},{9,11},{10,... | collective-permute-start | bytes 245768 | tf_op jit(solution)/shard_map/ppermute | solution.py:575
  38.4 5.1 %sums.6.own_ref = f32[40,40,128]{2,1,0:T(8,128)S(1)} custom-call(bf16[40,40,128]{2,1,0:T(8,128)(2,1)S(1)} %get-tuple-element.64.own_ref, bf16[40,40,128]{2,1,0:T(8,128)(2,1)S(1)} %other.1.other_ref, bf16[40,40,128]{2,1,0:T(8,128)(2,1)S(1)} %collective-permute-done.7.p_other, bf16[40,40,128]{2,1,0:T(8,128)(2,1)S(1)} %get-tuple-element.73.met_ref, ...), custom_call_target="tpu_custom_call" | custom-call | bytes 19188000 | tf_op jit(solution)/shard_map/sums/pallas_call | solution.py:578
  43.5 0.0 collective-permute-done.13.refs_1_
  43.5 0.0 collective-permute-done.12.refs_0_
  43.5 1.1 %join.3.refs_2_ = bf16[40,40,128]{2,1,0:T(8,128)(2,1)} custom-call(f32[40,40,128]{2,1,0:T(8,128)S(1)} %sums.6.own_ref, bf16[40,40,128]{2,1,0:T(8,128)(2,1)S(1)} %get-tuple-element.80.psum_ref, f32[40,40,128]{2,1,0:T(8,128)S(1)} %get-tuple-element.81.gate_ref, bf16[128,128]{1,0:T(8,128)(2,1)S(1)} %get-tuple-element.82.w_ref, ...), custom_call_target="tpu_custom_call" | custom-call | bytes 3542400 | tf_op jit(solution)/shard_map/join/pallas_call | solution.py:676
  44.6 0.0 collective-permute-done.11.refs_1_
  44.6 0.1 collective-permute-done.10.refs_0_
  44.7 1.1 %join.4.refs_1_ = bf16[40,40,128]{2,1,0:T(8,128)(2,1)} custom-call(f32[40,40,128]{2,1,0:T(8,128)S(1)} %sums.6.own_ref, bf16[40,40,128]{2,1,0:T(8,128)(2,1)S(1)} %get-tuple-element.80.psum_ref, f32[40,40,128]{2,1,0:T(8,128)S(1)} %get-tuple-element.81.gate_ref, bf16[128,128]{1,0:T(8,128)(2,1)S(1)} %get-tuple-element.82.w_ref, ...), custom_call_target="tpu_custom_call", output_to_operand_aliasing={{}: (6, {})} | custom-call | bytes 3542400 | tf_op jit(solution)/shard_map/join/pallas_call | solution.py:676
  45.8 0.5 %collective-permute-done.9.refs_0_ = bf16[8,40,128]{2,1,0:T(8,128)(2,1)S(1)} collective-permute-done((bf16[8,40,128]{2,1,0:T(8,128)(2,1)S(1)}, bf16[8,40,128]{2,1,0:T(8,128)(2,1)S(1)}, u32[]{:S(2)}, u32[]{:S(2)}) %collective-permute-start.9) | collective-permute-done | bytes 81952 | tf_op jit(solution)/shard_map/ppermute | solution.py:575
  46.3 1.0 %join.5 = bf16[40,40,128]{2,1,0:T(8,128)(2,1)} custom-call(f32[40,40,128]{2,1,0:T(8,128)S(1)} %sums.6.own_ref, bf16[40,40,128]{2,1,0:T(8,128)(2,1)S(1)} %get-tuple-element.80.psum_ref, f32[40,40,128]{2,1,0:T(8,128)S(1)} %get-tuple-element.81.gate_ref, bf16[128,128]{1,0:T(8,128)(2,1)S(1)} %get-tuple-element.82.w_ref, ...), custom_call_target="tpu_custom_call", output_to_operand_aliasing={{}: (5, {})} | custom-call | bytes 1771200 | tf_op jit(solution)/shard_map/join/pallas_call | solution.py:676
  (2 shorter events, 0.0 us)
Async XLA Ops:
  1.6 13.2 %collective-permute-start.5 = (bf16[43,40,128]{2,1,0:T(8,128)(2,1)S(1)}, bf16[43,40,128]{2,1,0:T(8,128)(2,1)S(1)}, u32[]{:S(2)}, u32[]{:S(2)}) collective-permute-start(bf16[43,40,128]{2,1,0:T(8,128)(2,1)S(1)} %get-tuple-element.65), channel_id=1, source_target_pairs={{0,1},{1,0},{2,3},{3,2},{4,5},{5,4},{6,7},{7,6},{8,9},{9,8},{10,11... | collective-permute-start | bytes 1320968 | tf_op jit(solution)/shard_map/ppermute | solution.py:575
  4.7 2.7 %collective-permute-start = (bf16[48,256]{1,0:T(8,128)(2,1)S(1)}, bf16[48,256]{1,0:T(8,128)(2,1)S(1)}, u32[]{:S(2)}, u32[]{:S(2)}) collective-permute-start(bf16[48,256]{1,0:T(8,128)(2,1)S(1)} %get-tuple-element.46), channel_id=1, source_target_pairs={{0,4},{4,0},{8,12},{12,8},{1,5},{5,1},{9,13},{13,9},{2,6},{6,2},{1... | collective-permute-start | bytes 73736 | tf_op jit(solution)/shard_map/ppermute | solution.py:612
  4.7 3.8 %collective-permute-start.1 = (bf16[48,256]{1,0:T(8,128)(2,1)S(1)}, bf16[48,256]{1,0:T(8,128)(2,1)S(1)}, u32[]{:S(2)}, u32[]{:S(2)}) collective-permute-start(bf16[48,256]{1,0:T(8,128)(2,1)S(1)} %get-tuple-element.47), channel_id=1, source_target_pairs={{0,8},{4,12},{8,0},{12,4},{1,9},{5,13},{9,1},{13,5},{2,10},{6,14},... | collective-permute-start | bytes 73736 | tf_op jit(solution)/shard_map/ppermute | solution.py:612
  6.2 3.3 %collective-permute-start.2 = (bf16[48,256]{1,0:T(8,128)(2,1)S(1)}, bf16[48,256]{1,0:T(8,128)(2,1)S(1)}, u32[]{:S(2)}, u32[]{:S(2)}) collective-permute-start(bf16[48,256]{1,0:T(8,128)(2,1)S(1)} %get-tuple-element.48), channel_id=1, source_target_pairs={{0,12},{4,8},{8,4},{12,0},{1,13},{5,9},{9,5},{13,1},{2,14},{6,10},... | collective-permute-start | bytes 73736 | tf_op jit(solution)/shard_map/ppermute | solution.py:612
  9.4 8.4 %collective-permute-start.4 = (bf16[41,40,128]{2,1,0:T(8,128)(2,1)S(1)}, bf16[41,40,128]{2,1,0:T(8,128)(2,1)S(1)}, u32[]{:S(2)}, u32[]{:S(2)}) collective-permute-start(bf16[41,40,128]{2,1,0:T(8,128)(2,1)S(1)} %get-tuple-element.55.block_ref), channel_id=1, source_target_pairs={{0,12},{1,5},{2,14},{3,7},{4,0},{5,9},{6,2},{7,11},{8,4},{9,13},{1... | collective-permute-start | bytes 1259528 | tf_op jit(solution)/shard_map/ppermute | solution.py:575
  13.5 8.9 %collective-permute-start.3 = (bf16[40,40,128]{2,1,0:T(8,128)(2,1)S(1)}, bf16[40,40,128]{2,1,0:T(8,128)(2,1)S(1)}, u32[]{:S(2)}, u32[]{:S(2)}) collective-permute-start(bf16[40,40,128]{2,1,0:T(8,128)(2,1)S(1)} %get-tuple-element.64.own_ref), channel_id=1, source_target_pairs={{0,4},{1,8},{2,6},{3,10},{4,13},{5,1},{6,15},{7,3},{8,12},{9,0},{1... | collective-permute-start | bytes 1228808 | tf_op jit(solution)/shard_map/ppermute | solution.py:575
  17.7 4.8 %collective-permute-start.6 = (bf16[40,40,128]{2,1,0:T(8,128)(2,1)S(1)}, bf16[40,40,128]{2,1,0:T(8,128)(2,1)S(1)}, u32[]{:S(2)}, u32[]{:S(2)}) collective-permute-start(bf16[40,40,128]{2,1,0:T(8,128)(2,1)S(1)} %get-tuple-element.73.met_ref), channel_id=1, source_target_pairs={{0,4},{1,5},{2,6},{3,7},{4,0},{5,1},{6,2},{7,3},{8,12},{9,13},{10,... | collective-permute-start | bytes 1228808 | tf_op jit(solution)/shard_map/ppermute | solution.py:575
  17.9 5.1 %collective-permute-start.7 = (bf16[40,40,128]{2,1,0:T(8,128)(2,1)S(1)}, bf16[40,40,128]{2,1,0:T(8,128)(2,1)S(1)}, u32[]{:S(2)}, u32[]{:S(2)}) collective-permute-start(bf16[40,40,128]{2,1,0:T(8,128)(2,1)S(1)} %other.1.other_ref), channel_id=1, source_target_pairs={{0,4},{1,5},{2,6},{3,7},{4,0},{5,1},{6,2},{7,3},{8,12},{9,13},{10,... | collective-permute-start | bytes 1228808 | tf_op jit(solution)/shard_map/ppermute | solution.py:575
  22.4 1.7 %collective-permute-start.8 = (bf16[40,40,128]{2,1,0:T(8,128)(2,1)S(1)}, bf16[40,40,128]{2,1,0:T(8,128)(2,1)S(1)}, u32[]{:S(2)}, u32[]{:S(2)}) collective-permute-start(bf16[40,40,128]{2,1,0:T(8,128)(2,1)S(1)} %collective-permute-done.3.far_ref), channel_id=1, source_target_pairs={{0,4},{1,5},{2,6},{3,7},{4,0},{5,1},{6,2},{7,3},{8,12},{9,13},{10,... | collective-permute-start | bytes 1228808 | tf_op jit(solution)/shard_map/ppermute | solution.py:575
  25.2 18.3 %collective-permute-start.13 = (bf16[8,40,128]{2,1,0:T(8,128)(2,1)S(1)}, bf16[8,40,128]{2,1,0:T(8,128)(2,1)S(1)}, u32[]{:S(2)}, u32[]{:S(2)}) collective-permute-start(bf16[8,40,128]{2,1,0:T(8,128)(2,1)S(1)} %sums.11), channel_id=1, source_target_pairs={{0,2},{1,3},{2,0},{3,1},{4,6},{5,7},{6,4},{7,5},{8,10},{9,11},{10,... | collective-permute-start | bytes 245768 | tf_op jit(solution)/shard_map/ppermute | solution.py:575
  28.9 14.6 %collective-permute-start.12 = (bf16[8,40,128]{2,1,0:T(8,128)(2,1)S(1)}, bf16[8,40,128]{2,1,0:T(8,128)(2,1)S(1)}, u32[]{:S(2)}, u32[]{:S(2)}) collective-permute-start(bf16[8,40,128]{2,1,0:T(8,128)(2,1)S(1)} %sums.10), channel_id=1, source_target_pairs={{0,2},{1,3},{2,0},{3,1},{4,6},{5,7},{6,4},{7,5},{8,10},{9,11},{10,... | collective-permute-start | bytes 245768 | tf_op jit(solution)/shard_map/ppermute | solution.py:575
  30.6 14.0 %collective-permute-start.11 = (bf16[8,40,128]{2,1,0:T(8,128)(2,1)S(1)}, bf16[8,40,128]{2,1,0:T(8,128)(2,1)S(1)}, u32[]{:S(2)}, u32[]{:S(2)}) collective-permute-start(bf16[8,40,128]{2,1,0:T(8,128)(2,1)S(1)} %sums.9), channel_id=1, source_target_pairs={{0,2},{1,3},{2,0},{3,1},{4,6},{5,7},{6,4},{7,5},{8,10},{9,11},{10,... | collective-permute-start | bytes 245768 | tf_op jit(solution)/shard_map/ppermute | solution.py:575
  34.3 10.4 %collective-permute-start.10 = (bf16[8,40,128]{2,1,0:T(8,128)(2,1)S(1)}, bf16[8,40,128]{2,1,0:T(8,128)(2,1)S(1)}, u32[]{:S(2)}, u32[]{:S(2)}) collective-permute-start(bf16[8,40,128]{2,1,0:T(8,128)(2,1)S(1)} %sums.8), channel_id=1, source_target_pairs={{0,2},{1,3},{2,0},{3,1},{4,6},{5,7},{6,4},{7,5},{8,10},{9,11},{10,... | collective-permute-start | bytes 245768 | tf_op jit(solution)/shard_map/ppermute | solution.py:575
  35.7 10.6 %collective-permute-start.9 = (bf16[8,40,128]{2,1,0:T(8,128)(2,1)S(1)}, bf16[8,40,128]{2,1,0:T(8,128)(2,1)S(1)}, u32[]{:S(2)}, u32[]{:S(2)}) collective-permute-start(bf16[8,40,128]{2,1,0:T(8,128)(2,1)S(1)} %sums.7), channel_id=1, source_target_pairs={{0,2},{1,3},{2,0},{3,1},{4,6},{5,7},{6,4},{7,5},{8,10},{9,11},{10,... | collective-permute-start | bytes 245768 | tf_op jit(solution)/shard_map/ppermute | solution.py:575

commit v17 on v16

--- a/solution.py
+++ b/solution.py
@@ -612,6 +612,8 @@
         lax.ppermute(msgs[d], "row", [(r, r ^ d) for r in range(4)]) for d in (1, 2, 3)
     ]
     met = move(raw_z, lambda r, z: (r, z ^ 1))
+    raw_other = move(raw, lambda r, z: (r ^ 3, z) if keeper(r, z) else (r ^ 1, z))
+
     wq, pick, idt = pl.pallas_call(
         functools.partial(ready_body, seqs),
         out_shape=[struct((width // 2, width, 2 * chans), bf16),
@@ -629,8 +631,6 @@
         name="ready",
     )(average, hold(ids))
 
-    raw, msgs, idt = lax.optimization_barrier((raw, msgs, idt))
-    raw_other = move(raw, lambda r, z: (r ^ 3, z) if keeper(r, z) else (r ^ 1, z))
     t, mixed = call(
         functools.partial(mix_body, seqs, width), 1,
         [struct((own_i // 2, width * total, 2 * chans), bf16), struct((2, own_j, width * total), bf16)],
@@ -649,15 +649,14 @@
         functools.partial(mix_other_body, seqs, width), 1, struct(t.shape, bf16),
         [pltpu.VMEM((own_i * total, 128), f32)], *msgs, wq,
     )
-    met, *_ = lax.optimization_barrier((met, t_other))
+    other = call(other_body, 2.4, square, flat, raw_other, t_other, mixed, idt, bias, w_in)
+    p_other = move(other, beside)
+    met, *_ = lax.optimization_barrier((met, other))
     met_left, met_right = call(
         met_body, 3, [square, square], flat + [pltpu.VMEM(norm.shape, bf16)], met, t, mixed, idt, bias, w_in
     )
     p_met = move(met_right, beside)
-    raw_other, *_ = lax.optimization_barrier((raw_other, met_left))
-    other = call(other_body, 2.4, square, flat, raw_other, t_other, mixed, idt, bias, w_in)
-    p_other = move(other, beside)
-    far, other, p_met = lax.optimization_barrier((far, other, p_met))
+    far, *_ = lax.optimization_barrier((far, met_left))
     p_far = move(far, beside)
 
     def sums(own_pair, first, n, dtype):

time: 47.6 us -> 47 us (0.987)
  waiting for transfers between devices: 6.77 us -> 4.5 us
  starting transfers between devices: 17.6 us -> 19.3 us
    ppermute x11, starting transfers between devices: 15.8 us -> 17.5 us  [move(): return lax.ppermute(value, ('row', 'col'), pairs)]
    ppermute x3, waiting for transfers between devices: 1.99 us -> 0.61 us  [paired_plan(): lax.ppermute(msgs[d], 'row', [(r, r ^ d) for r in range(4)])]
    ppermute x11, waiting for transfers between devices: 4.78 us -> 3.89 us  [move(): return lax.ppermute(value, ('row', 'col'), pairs)]
  transfers between devices with their start and end apart: 14 -> 14, of which waited for: 7 -> 6; matrix products, arithmetic and copies ran while one was open for 0% -> 0% of each run, Pallas kernels for 40% -> 41%
where the time goes in v17:
time: 47 us; the launch traced here: 46.8 us
  Pallas kernels  22.7 us (48%)
  starting transfers between devices  19.3 us (41%)
  waiting for transfers between devices  4.5 us (10%)
    ppermute x11, starting transfers between devices, move(): return lax.ppermute(value, ('row', 'col'), pairs)  17.5 us
    pallas_call x12, Pallas kernels, call(): pl.pallas_call(body, out_shape=out_shape, in_specs=[VMEM] * len(args), ou...  17.1 us
    ppermute x11, waiting for transfers between devices, move(): return lax.ppermute(value, ('row', 'col'), pairs)  3.89 us
    pallas_call x3, Pallas kernels, paired_plan(): pl.pallas_call(functools.partial(join_body, first, len(parts)), out_shape...  3.1 us
    ppermute x3, starting transfers between devices, paired_plan(): lax.ppermute(msgs[d], 'row', [(r, r ^ d) for r in range(4)])  1.86 us
    pallas_call x1, Pallas kernels, paired_plan(): pl.pallas_call(open_body, out_shape=[struct((height, lanes), bf16)] * 4 +...  1.6 us
  transfers between devices with their start and end apart: 14, of which 6 were waited for; matrix products, arithmetic and copies ran while one was open for 0% of the time, Pallas kernels for 41%

profile of v17, /device:TPU:0, one launch (start us, length us, event | category | flops | bytes accessed | tf_op | source)
XLA Modules:
  0.0 46.8 jit_solution(17727276871911335786)
XLA Ops:
  0.0 1.6 %open.1 = (bf16[48,256]{1,0:T(8,128)(2,1)S(1)}, bf16[48,256]{1,0:T(8,128)(2,1)S(1)}, bf16[48,256]{1,0:T(8,128)(2,1)S(1)}, bf16[48,256]{1,0:T(8,128)(2,1)S(1)}, b...) custom-call(bf16[2,160,256]{2,1,0:T(8,128)(2,1)} %x_hbm.1, ...), custom_call_target="tpu_custom_call" | custom-call | bytes 5535000 | tf_op jit(solution)/shard_map/open/pallas_call | solution.py:595
  1.6 3.1 %collective-permute-start.5 = (bf16[43,40,128]{2,1,0:T(8,128)(2,1)S(1)}, bf16[43,40,128]{2,1,0:T(8,128)(2,1)S(1)}, u32[]{:S(2)}, u32[]{:S(2)}) collective-permute-start(bf16[43,40,128]{2,1,0:T(8,128)(2,1)S(1)} %get-tuple-element.54), channel_id=1, source_target_pairs={{0,1},{1,0},{2,3},{3,2},{4,5},{5,4},{6,7},{7,6},{8,9},{9,8},{10,11... | collective-permute-start | bytes 1320968 | tf_op jit(solution)/shard_map/ppermute | solution.py:575
  4.7 0.0 collective-permute-start
  4.7 1.5 %collective-permute-start.1 = (bf16[48,256]{1,0:T(8,128)(2,1)S(1)}, bf16[48,256]{1,0:T(8,128)(2,1)S(1)}, u32[]{:S(2)}, u32[]{:S(2)}) collective-permute-start(bf16[48,256]{1,0:T(8,128)(2,1)S(1)} %get-tuple-element.37), channel_id=1, source_target_pairs={{0,8},{4,12},{8,0},{12,4},{1,9},{5,13},{9,1},{13,5},{2,10},{6,14},... | collective-permute-start | bytes 73736 | tf_op jit(solution)/shard_map/ppermute | solution.py:612
  6.2 0.4 collective-permute-start.2
  6.6 1.4 %collective-permute-start.3 = (bf16[41,40,128]{2,1,0:T(8,128)(2,1)S(1)}, bf16[41,40,128]{2,1,0:T(8,128)(2,1)S(1)}, u32[]{:S(2)}, u32[]{:S(2)}) collective-permute-start(bf16[41,40,128]{2,1,0:T(8,128)(2,1)S(1)} %get-tuple-element.39.block_ref), channel_id=1, source_target_pairs={{0,12},{1,5},{2,14},{3,7},{4,0},{5,9},{6,2},{7,11},{8,4},{9,13},{1... | collective-permute-start | bytes 1259528 | tf_op jit(solution)/shard_map/ppermute | solution.py:575
  7.9 0.9 %ready.1 = (bf16[16,32,256]{2,1,0:T(8,128)(2,1)S(1)}, bf16[2,4,128,256]{3,2,1,0:T(8,128)(2,1)S(1)}, s32[160,128]{1,0:T(8,128)S(1)}) custom-call(bf16[1024,128]{1,0:T(8,128)(2,1)S(1)} %get-tuple-element.40.avg_ref, s32[160]{0:T(256)} %ids_hbm.1), custom_call_target="tpu_custom_call" | custom-call | bytes 5535000 | tf_op jit(solution)/shard_map/ready/pallas_call | solution.py:617
  8.8 0.0 collective-permute-done.refs_1_
  8.8 0.0 collective-permute-done.1.refs_2_
  8.8 0.6 %collective-permute-done.2.refs_3_ = bf16[48,256]{1,0:T(8,128)(2,1)S(1)} collective-permute-done((bf16[48,256]{1,0:T(8,128)(2,1)S(1)}, bf16[48,256]{1,0:T(8,128)(2,1)S(1)}, u32[]{:S(2)}, u32[]{:S(2)}) %collective-permute-start.2) | collective-permute-done | bytes 24608 | tf_op jit(solution)/shard_map/ppermute | solution.py:612
  9.4 0.9 %mix.1 = (bf16[20,256,256]{2,1,0:T(8,128)(2,1)S(1)}, bf16[2,40,256]{2,1,0:T(8,128)(2,1)S(1)}) custom-call(bf16[48,256]{1,0:T(8,128)(2,1)S(1)} %get-tuple-element.50.refs_0_, bf16[48,256]{1,0:T(8,128)(2,1)S(1)} %collective-permute-done.refs_1_, bf16[48,256]{1,0:T(8,128)(2,1)S(1)} %collective-permute-done.1.refs_2_, ...), custom_call_target="tpu_custom_call" | custom-call | bytes 3690000 | tf_op jit(solution)/shard_map/mix/pallas_call | solution.py:578
  10.4 2.4 %own.1 = (bf16[40,40,128]{2,1,0:T(8,128)(2,1)S(1)}, bf16[1600,128]{1,0:T(8,128)(2,1)S(1)}, bf16[40,40,128]{2,1,0:T(8,128)(2,1)S(1)}) custom-call(bf16[41,40,128]{2,1,0:T(8,128)(2,1)S(1)} %get-tuple-element.39.block_ref, bf16[20,256,256]{2,1,0:T(8,128)(2,1)S(1)} %get-tuple-element.43.t_ref, bf16[2,40,256]{2,1,0:T(8,128)(2,1)S(1)} %get-tuple-element.44.right_ref, ...), custom_call_target="tpu_custom_call" | custom-call | bytes 8856000 | tf_op jit(solution)/shard_map/own/pallas_call | solution.py:578
  12.7 0.6 %collective-permute-start.7 = (bf16[40,40,128]{2,1,0:T(8,128)(2,1)S(1)}, bf16[40,40,128]{2,1,0:T(8,128)(2,1)S(1)}, u32[]{:S(2)}, u32[]{:S(2)}) collective-permute-start(bf16[40,40,128]{2,1,0:T(8,128)(2,1)S(1)} %get-tuple-element.49.own_ref), channel_id=1, source_target_pairs={{0,4},{1,8},{2,6},{3,10},{4,13},{5,1},{6,15},{7,3},{8,12},{9,0},{1... | collective-permute-start | bytes 1228808 | tf_op jit(solution)/shard_map/ppermute | solution.py:575
  13.3 0.2 collective-permute-done.3.block_ref
  13.5 3.6 %collective-permute-start.4 = (bf16[40,40,128]{2,1,0:T(8,128)(2,1)S(1)}, bf16[40,40,128]{2,1,0:T(8,128)(2,1)S(1)}, u32[]{:S(2)}, u32[]{:S(2)}) collective-permute-start(bf16[40,40,128]{2,1,0:T(8,128)(2,1)S(1)} %other.1.other_ref), channel_id=1, source_target_pairs={{0,4},{1,5},{2,6},{3,7},{4,0},{5,1},{6,2},{7,3},{8,12},{9,13},{10,... | collective-permute-start | bytes 1228808 | tf_op jit(solution)/shard_map/ppermute | solution.py:575
  17.1 0.0 collective-permute-done.5.block_ref
  17.1 2.8 %met.1 = (bf16[40,40,128]{2,1,0:T(8,128)(2,1)S(1)}, bf16[40,40,128]{2,1,0:T(8,128)(2,1)S(1)}) custom-call(bf16[43,40,128]{2,1,0:T(8,128)(2,1)S(1)} %collective-permute-done.5.block_ref, bf16[20,256,256]{2,1,0:T(8,128)(2,1)S(1)} %get-tuple-element.43.t_ref, bf16[2,40,256]{2,1,0:T(8,128)(2,1)S(1)} %get-tuple-element.44.right_ref, ...), custom_call_target="tpu_custom_call" | custom-call | bytes 11070000 | tf_op jit(solution)/shard_map/met/pallas_call | solution.py:578
  19.9 0.1 collective-permute-start.6
  20.0 1.7 %collective-permute-done.7.far_ref = bf16[40,40,128]{2,1,0:T(8,128)(2,1)S(1)} collective-permute-done((bf16[40,40,128]{2,1,0:T(8,128)(2,1)S(1)}, bf16[40,40,128]{2,1,0:T(8,128)(2,1)S(1)}, u32[]{:S(2)}, u32[]{:S(2)}) %collective-permute-start.7) | collective-permute-done | bytes 409632 | tf_op jit(solution)/shard_map/ppermute | solution.py:575
  21.7 0.0 collective-permute-start.8
  21.7 0.5 %rest.1 = (bf16[40,40,128]{2,1,0:T(8,128)(2,1)S(1)}, f32[40,40,128]{2,1,0:T(8,128)S(1)}) custom-call(bf16[41,40,128]{2,1,0:T(8,128)(2,1)S(1)} %get-tuple-element.39.block_ref, bf16[1600,128]{1,0:T(8,128)(2,1)S(1)} %get-tuple-element.59.norm_ref, bf16[128,512]{1,0:T(8,128)(2,1)S(1)} %get-tuple-element.47.win_ref, bf16[128,128]{1,0:T(8,128)(2,1)S(1)} %get-tuple-element.60.wgate_ref), custom_call_target="tpu_custom_call" | custom-call | bytes 2214000 | tf_op jit(solution)/shard_map/rest/pallas_call | solution.py:578
  22.2 0.0 collective-permute-done.4.p_other
  22.2 0.0 collective-permute-done.6.p_met
  22.2 1.2 %collective-permute-done.8.p_far = bf16[40,40,128]{2,1,0:T(8,128)(2,1)S(1)} collective-permute-done((bf16[40,40,128]{2,1,0:T(8,128)(2,1)S(1)}, bf16[40,40,128]{2,1,0:T(8,128)(2,1)S(1)}, u32[]{:S(2)}, u32[]{:S(2)}) %collective-permute-start.8) | collective-permute-done | bytes 409632 | tf_op jit(solution)/shard_map/ppermute | solution.py:575
  23.4 1.0 %sums.10 = bf16[8,40,128]{2,1,0:T(8,128)(2,1)S(1)} custom-call(bf16[40,40,128]{2,1,0:T(8,128)(2,1)S(1)} %get-tuple-element.49.own_ref, bf16[40,40,128]{2,1,0:T(8,128)(2,1)S(1)} %other.1.other_ref, bf16[40,40,128]{2,1,0:T(8,128)(2,1)S(1)} %collective-permute-done.4.p_other, bf16[40,40,128]{2,1,0:T(8,128)(2,1)S(1)} %get-tuple-element.56.met_ref, ...), custom_call_target="tpu_custom_call" | custom-call | bytes 3837600 | tf_op jit(solution)/shard_map/sums/pallas_call | solution.py:578
  24.5 2.7 %collective-permute-start.12 = (bf16[8,40,128]{2,1,0:T(8,128)(2,1)S(1)}, bf16[8,40,128]{2,1,0:T(8,128)(2,1)S(1)}, u32[]{:S(2)}, u32[]{:S(2)}) collective-permute-start(bf16[8,40,128]{2,1,0:T(8,128)(2,1)S(1)} %sums.10), channel_id=1, source_target_pairs={{0,2},{1,3},{2,0},{3,1},{4,6},{5,7},{6,4},{7,5},{8,10},{9,11},{10,... | collective-permute-start | bytes 245768 | tf_op jit(solution)/shard_map/ppermute | solution.py:575
  27.1 1.0 %sums.11 = bf16[8,40,128]{2,1,0:T(8,128)(2,1)S(1)} custom-call(bf16[40,40,128]{2,1,0:T(8,128)(2,1)S(1)} %get-tuple-element.49.own_ref, bf16[40,40,128]{2,1,0:T(8,128)(2,1)S(1)} %other.1.other_ref, bf16[40,40,128]{2,1,0:T(8,128)(2,1)S(1)} %collective-permute-done.4.p_other, bf16[40,40,128]{2,1,0:T(8,128)(2,1)S(1)} %get-tuple-element.56.met_ref, ...), custom_call_target="tpu_custom_call" | custom-call | bytes 3837600 | tf_op jit(solution)/shard_map/sums/pallas_call | solution.py:578
  28.2 0.4 collective-permute-start.13
  28.6 1.2 %sums.8 = bf16[8,40,128]{2,1,0:T(8,128)(2,1)S(1)} custom-call(bf16[40,40,128]{2,1,0:T(8,128)(2,1)S(1)} %get-tuple-element.49.own_ref, bf16[40,40,128]{2,1,0:T(8,128)(2,1)S(1)} %other.1.other_ref, bf16[40,40,128]{2,1,0:T(8,128)(2,1)S(1)} %collective-permute-done.4.p_other, bf16[40,40,128]{2,1,0:T(8,128)(2,1)S(1)} %get-tuple-element.56.met_ref, ...), custom_call_target="tpu_custom_call" | custom-call | bytes 3837600 | tf_op jit(solution)/shard_map/sums/pallas_call | solution.py:578
  29.8 2.7 %collective-permute-start.10 = (bf16[8,40,128]{2,1,0:T(8,128)(2,1)S(1)}, bf16[8,40,128]{2,1,0:T(8,128)(2,1)S(1)}, u32[]{:S(2)}, u32[]{:S(2)}) collective-permute-start(bf16[8,40,128]{2,1,0:T(8,128)(2,1)S(1)} %sums.8), channel_id=1, source_target_pairs={{0,2},{1,3},{2,0},{3,1},{4,6},{5,7},{6,4},{7,5},{8,10},{9,11},{10,... | collective-permute-start | bytes 245768 | tf_op jit(solution)/shard_map/ppermute | solution.py:575
  32.5 1.0 %sums.9 = bf16[8,40,128]{2,1,0:T(8,128)(2,1)S(1)} custom-call(bf16[40,40,128]{2,1,0:T(8,128)(2,1)S(1)} %get-tuple-element.49.own_ref, bf16[40,40,128]{2,1,0:T(8,128)(2,1)S(1)} %other.1.other_ref, bf16[40,40,128]{2,1,0:T(8,128)(2,1)S(1)} %collective-permute-done.4.p_other, bf16[40,40,128]{2,1,0:T(8,128)(2,1)S(1)} %get-tuple-element.56.met_ref, ...), custom_call_target="tpu_custom_call" | custom-call | bytes 3837600 | tf_op jit(solution)/shard_map/sums/pallas_call | solution.py:578
  33.5 0.4 collective-permute-start.11
  33.9 1.0 %sums.7 = bf16[8,40,128]{2,1,0:T(8,128)(2,1)S(1)} custom-call(bf16[40,40,128]{2,1,0:T(8,128)(2,1)S(1)} %get-tuple-element.49.own_ref, bf16[40,40,128]{2,1,0:T(8,128)(2,1)S(1)} %other.1.other_ref, bf16[40,40,128]{2,1,0:T(8,128)(2,1)S(1)} %collective-permute-done.4.p_other, bf16[40,40,128]{2,1,0:T(8,128)(2,1)S(1)} %get-tuple-element.56.met_ref, ...), custom_call_target="tpu_custom_call" | custom-call | bytes 3837600 | tf_op jit(solution)/shard_map/sums/pallas_call | solution.py:578
  34.9 2.7 %collective-permute-start.9 = (bf16[8,40,128]{2,1,0:T(8,128)(2,1)S(1)}, bf16[8,40,128]{2,1,0:T(8,128)(2,1)S(1)}, u32[]{:S(2)}, u32[]{:S(2)}) collective-permute-start(bf16[8,40,128]{2,1,0:T(8,128)(2,1)S(1)} %sums.7), channel_id=1, source_target_pairs={{0,2},{1,3},{2,0},{3,1},{4,6},{5,7},{6,4},{7,5},{8,10},{9,11},{10,... | collective-permute-start | bytes 245768 | tf_op jit(solution)/shard_map/ppermute | solution.py:575
  37.6 5.1 %sums.6.own_ref = f32[40,40,128]{2,1,0:T(8,128)S(1)} custom-call(bf16[40,40,128]{2,1,0:T(8,128)(2,1)S(1)} %get-tuple-element.49.own_ref, bf16[40,40,128]{2,1,0:T(8,128)(2,1)S(1)} %other.1.other_ref, bf16[40,40,128]{2,1,0:T(8,128)(2,1)S(1)} %collective-permute-done.4.p_other, bf16[40,40,128]{2,1,0:T(8,128)(2,1)S(1)} %get-tuple-element.56.met_ref, ...), custom_call_target="tpu_custom_call" | custom-call | bytes 19188000 | tf_op jit(solution)/shard_map/sums/pallas_call | solution.py:578
  42.7 0.0 collective-permute-done.12.refs_0_
  42.7 0.0 collective-permute-done.13.refs_1_
  42.8 1.1 %join.3.refs_2_ = bf16[40,40,128]{2,1,0:T(8,128)(2,1)} custom-call(f32[40,40,128]{2,1,0:T(8,128)S(1)} %sums.6.own_ref, bf16[40,40,128]{2,1,0:T(8,128)(2,1)S(1)} %get-tuple-element.62.psum_ref, f32[40,40,128]{2,1,0:T(8,128)S(1)} %get-tuple-element.63.gate_ref, bf16[128,128]{1,0:T(8,128)(2,1)S(1)} %get-tuple-element.64.w_ref, ...), custom_call_target="tpu_custom_call" | custom-call | bytes 3542400 | tf_op jit(solution)/shard_map/join/pallas_call | solution.py:675
  43.8 0.0 collective-permute-done.10.refs_0_
  43.8 0.2 collective-permute-done.11.refs_1_
  44.1 1.1 %join.4.refs_1_ = bf16[40,40,128]{2,1,0:T(8,128)(2,1)} custom-call(f32[40,40,128]{2,1,0:T(8,128)S(1)} %sums.6.own_ref, bf16[40,40,128]{2,1,0:T(8,128)(2,1)S(1)} %get-tuple-element.62.psum_ref, f32[40,40,128]{2,1,0:T(8,128)S(1)} %get-tuple-element.63.gate_ref, bf16[128,128]{1,0:T(8,128)(2,1)S(1)} %get-tuple-element.64.w_ref, ...), custom_call_target="tpu_custom_call", output_to_operand_aliasing={{}: (6, {})} | custom-call | bytes 3542400 | tf_op jit(solution)/shard_map/join/pallas_call | solution.py:675
  45.1 0.6 %collective-permute-done.9.refs_0_ = bf16[8,40,128]{2,1,0:T(8,128)(2,1)S(1)} collective-permute-done((bf16[8,40,128]{2,1,0:T(8,128)(2,1)S(1)}, bf16[8,40,128]{2,1,0:T(8,128)(2,1)S(1)}, u32[]{:S(2)}, u32[]{:S(2)}) %collective-permute-start.9) | collective-permute-done | bytes 81952 | tf_op jit(solution)/shard_map/ppermute | solution.py:575
  45.7 1.0 %join.5 = bf16[40,40,128]{2,1,0:T(8,128)(2,1)} custom-call(f32[40,40,128]{2,1,0:T(8,128)S(1)} %sums.6.own_ref, bf16[40,40,128]{2,1,0:T(8,128)(2,1)S(1)} %get-tuple-element.62.psum_ref, f32[40,40,128]{2,1,0:T(8,128)S(1)} %get-tuple-element.63.gate_ref, bf16[128,128]{1,0:T(8,128)(2,1)S(1)} %get-tuple-element.64.w_ref, ...), custom_call_target="tpu_custom_call", output_to_operand_aliasing={{}: (5, {})} | custom-call | bytes 1771200 | tf_op jit(solution)/shard_map/join/pallas_call | solution.py:675
  (2 shorter events, 0.0 us)
Async XLA Ops:
  1.6 15.5 %collective-permute-start.5 = (bf16[43,40,128]{2,1,0:T(8,128)(2,1)S(1)}, bf16[43,40,128]{2,1,0:T(8,128)(2,1)S(1)}, u32[]{:S(2)}, u32[]{:S(2)}) collective-permute-start(bf16[43,40,128]{2,1,0:T(8,128)(2,1)S(1)} %get-tuple-element.54), channel_id=1, source_target_pairs={{0,1},{1,0},{2,3},{3,2},{4,5},{5,4},{6,7},{7,6},{8,9},{9,8},{10,11... | collective-permute-start | bytes 1320968 | tf_op jit(solution)/shard_map/ppermute | solution.py:575
  4.7 4.1 %collective-permute-start = (bf16[48,256]{1,0:T(8,128)(2,1)S(1)}, bf16[48,256]{1,0:T(8,128)(2,1)S(1)}, u32[]{:S(2)}, u32[]{:S(2)}) collective-permute-start(bf16[48,256]{1,0:T(8,128)(2,1)S(1)} %get-tuple-element.36), channel_id=1, source_target_pairs={{0,4},{4,0},{8,12},{12,8},{1,5},{5,1},{9,13},{13,9},{2,6},{6,2},{1... | collective-permute-start | bytes 73736 | tf_op jit(solution)/shard_map/ppermute | solution.py:612
  4.7 4.1 %collective-permute-start.1 = (bf16[48,256]{1,0:T(8,128)(2,1)S(1)}, bf16[48,256]{1,0:T(8,128)(2,1)S(1)}, u32[]{:S(2)}, u32[]{:S(2)}) collective-permute-start(bf16[48,256]{1,0:T(8,128)(2,1)S(1)} %get-tuple-element.37), channel_id=1, source_target_pairs={{0,8},{4,12},{8,0},{12,4},{1,9},{5,13},{9,1},{13,5},{2,10},{6,14},... | collective-permute-start | bytes 73736 | tf_op jit(solution)/shard_map/ppermute | solution.py:612
  6.2 3.3 %collective-permute-start.2 = (bf16[48,256]{1,0:T(8,128)(2,1)S(1)}, bf16[48,256]{1,0:T(8,128)(2,1)S(1)}, u32[]{:S(2)}, u32[]{:S(2)}) collective-permute-start(bf16[48,256]{1,0:T(8,128)(2,1)S(1)} %get-tuple-element.38), channel_id=1, source_target_pairs={{0,12},{4,8},{8,4},{12,0},{1,13},{5,9},{9,5},{13,1},{2,14},{6,10},... | collective-permute-start | bytes 73736 | tf_op jit(solution)/shard_map/ppermute | solution.py:612
  6.6 7.0 %collective-permute-start.3 = (bf16[41,40,128]{2,1,0:T(8,128)(2,1)S(1)}, bf16[41,40,128]{2,1,0:T(8,128)(2,1)S(1)}, u32[]{:S(2)}, u32[]{:S(2)}) collective-permute-start(bf16[41,40,128]{2,1,0:T(8,128)(2,1)S(1)} %get-tuple-element.39.block_ref), channel_id=1, source_target_pairs={{0,12},{1,5},{2,14},{3,7},{4,0},{5,9},{6,2},{7,11},{8,4},{9,13},{1... | collective-permute-start | bytes 1259528 | tf_op jit(solution)/shard_map/ppermute | solution.py:575
  12.7 8.9 %collective-permute-start.7 = (bf16[40,40,128]{2,1,0:T(8,128)(2,1)S(1)}, bf16[40,40,128]{2,1,0:T(8,128)(2,1)S(1)}, u32[]{:S(2)}, u32[]{:S(2)}) collective-permute-start(bf16[40,40,128]{2,1,0:T(8,128)(2,1)S(1)} %get-tuple-element.49.own_ref), channel_id=1, source_target_pairs={{0,4},{1,8},{2,6},{3,10},{4,13},{5,1},{6,15},{7,3},{8,12},{9,0},{1... | collective-permute-start | bytes 1228808 | tf_op jit(solution)/shard_map/ppermute | solution.py:575
  13.5 8.6 %collective-permute-start.4 = (bf16[40,40,128]{2,1,0:T(8,128)(2,1)S(1)}, bf16[40,40,128]{2,1,0:T(8,128)(2,1)S(1)}, u32[]{:S(2)}, u32[]{:S(2)}) collective-permute-start(bf16[40,40,128]{2,1,0:T(8,128)(2,1)S(1)} %other.1.other_ref), channel_id=1, source_target_pairs={{0,4},{1,5},{2,6},{3,7},{4,0},{5,1},{6,2},{7,3},{8,12},{9,13},{10,... | collective-permute-start | bytes 1228808 | tf_op jit(solution)/shard_map/ppermute | solution.py:575
  19.9 2.3 %collective-permute-start.6 = (bf16[40,40,128]{2,1,0:T(8,128)(2,1)S(1)}, bf16[40,40,128]{2,1,0:T(8,128)(2,1)S(1)}, u32[]{:S(2)}, u32[]{:S(2)}) collective-permute-start(bf16[40,40,128]{2,1,0:T(8,128)(2,1)S(1)} %get-tuple-element.56.met_ref), channel_id=1, source_target_pairs={{0,4},{1,5},{2,6},{3,7},{4,0},{5,1},{6,2},{7,3},{8,12},{9,13},{10,... | collective-permute-start | bytes 1228808 | tf_op jit(solution)/shard_map/ppermute | solution.py:575
  21.7 1.7 %collective-permute-start.8 = (bf16[40,40,128]{2,1,0:T(8,128)(2,1)S(1)}, bf16[40,40,128]{2,1,0:T(8,128)(2,1)S(1)}, u32[]{:S(2)}, u32[]{:S(2)}) collective-permute-start(bf16[40,40,128]{2,1,0:T(8,128)(2,1)S(1)} %collective-permute-done.7.far_ref), channel_id=1, source_target_pairs={{0,4},{1,5},{2,6},{3,7},{4,0},{5,1},{6,2},{7,3},{8,12},{9,13},{10,... | collective-permute-start | bytes 1228808 | tf_op jit(solution)/shard_map/ppermute | solution.py:575
  24.5 18.3 %collective-permute-start.12 = (bf16[8,40,128]{2,1,0:T(8,128)(2,1)S(1)}, bf16[8,40,128]{2,1,0:T(8,128)(2,1)S(1)}, u32[]{:S(2)}, u32[]{:S(2)}) collective-permute-start(bf16[8,40,128]{2,1,0:T(8,128)(2,1)S(1)} %sums.10), channel_id=1, source_target_pairs={{0,2},{1,3},{2,0},{3,1},{4,6},{5,7},{6,4},{7,5},{8,10},{9,11},{10,... | collective-permute-start | bytes 245768 | tf_op jit(solution)/shard_map/ppermute | solution.py:575
  28.2 14.6 %collective-permute-start.13 = (bf16[8,40,128]{2,1,0:T(8,128)(2,1)S(1)}, bf16[8,40,128]{2,1,0:T(8,128)(2,1)S(1)}, u32[]{:S(2)}, u32[]{:S(2)}) collective-permute-start(bf16[8,40,128]{2,1,0:T(8,128)(2,1)S(1)} %sums.11), channel_id=1, source_target_pairs={{0,2},{1,3},{2,0},{3,1},{4,6},{5,7},{6,4},{7,5},{8,10},{9,11},{10,... | collective-permute-start | bytes 245768 | tf_op jit(solution)/shard_map/ppermute | solution.py:575
  29.8 14.0 %collective-permute-start.10 = (bf16[8,40,128]{2,1,0:T(8,128)(2,1)S(1)}, bf16[8,40,128]{2,1,0:T(8,128)(2,1)S(1)}, u32[]{:S(2)}, u32[]{:S(2)}) collective-permute-start(bf16[8,40,128]{2,1,0:T(8,128)(2,1)S(1)} %sums.8), channel_id=1, source_target_pairs={{0,2},{1,3},{2,0},{3,1},{4,6},{5,7},{6,4},{7,5},{8,10},{9,11},{10,... | collective-permute-start | bytes 245768 | tf_op jit(solution)/shard_map/ppermute | solution.py:575
  33.5 10.6 %collective-permute-start.11 = (bf16[8,40,128]{2,1,0:T(8,128)(2,1)S(1)}, bf16[8,40,128]{2,1,0:T(8,128)(2,1)S(1)}, u32[]{:S(2)}, u32[]{:S(2)}) collective-permute-start(bf16[8,40,128]{2,1,0:T(8,128)(2,1)S(1)} %sums.9), channel_id=1, source_target_pairs={{0,2},{1,3},{2,0},{3,1},{4,6},{5,7},{6,4},{7,5},{8,10},{9,11},{10,... | collective-permute-start | bytes 245768 | tf_op jit(solution)/shard_map/ppermute | solution.py:575
  34.9 10.8 %collective-permute-start.9 = (bf16[8,40,128]{2,1,0:T(8,128)(2,1)S(1)}, bf16[8,40,128]{2,1,0:T(8,128)(2,1)S(1)}, u32[]{:S(2)}, u32[]{:S(2)}) collective-permute-start(bf16[8,40,128]{2,1,0:T(8,128)(2,1)S(1)} %sums.7), channel_id=1, source_target_pairs={{0,2},{1,3},{2,0},{3,1},{4,6},{5,7},{6,4},{7,5},{8,10},{9,11},{10,... | collective-permute-start | bytes 245768 | tf_op jit(solution)/shard_map/ppermute | solution.py:575

commit v18 on v17

--- a/solution.py
+++ b/solution.py
@@ -590,7 +590,7 @@
     beside = lambda r, z: (r ^ 1, z)
     height, lanes = round_up(own_i, 16), 256
     block = struct((own_i + 1, own_j, chans), bf16)
-    longer = struct((own_i + 3, own_j, chans), bf16)
+    longer = struct((own_i + 2, own_j, chans), bf16)
     later = (average, bias, w_in, w_gate, w_final)
     *msgs, average, bias, w_in, w_gate, w_final, raw, raw_z = pl.pallas_call(
         open_body,

time: 47 us -> 47.9 us (1.019)
  waiting for transfers between devices: 4.5 us -> 6.03 us
  starting transfers between devices: 19.3 us -> 18.6 us
    ppermute x11, waiting for transfers between devices: 3.89 us -> 6.03 us  [move(): return lax.ppermute(value, ('row', 'col'), pairs)]
    ppermute x11, starting transfers between devices: 17.5 us -> 15.5 us  [move(): return lax.ppermute(value, ('row', 'col'), pairs)]
    ppermute x3, starting transfers between devices: 1.86 us -> 3.15 us  [paired_plan(): lax.ppermute(msgs[d], 'row', [(r, r ^ d) for r in range(4)])]
    ppermute x3, waiting for transfers between devices: 0.61 us -> 0.01 us  [paired_plan(): lax.ppermute(msgs[d], 'row', [(r, r ^ d) for r in range(4)])]
  transfers between devices with their start and end apart: 14 -> 14, of which waited for: 6 -> 5; matrix products, arithmetic and copies ran while one was open for 0% -> 0% of each run, Pallas kernels for 41% -> 40%
where the time goes in v18:
time: 47.9 us; the launch traced here: 47.7 us
  Pallas kernels  22.7 us (47%)
  starting transfers between devices  18.6 us (39%)
  waiting for transfers between devices  6.03 us (13%)
    pallas_call x12, Pallas kernels, call(): pl.pallas_call(body, out_shape=out_shape, in_specs=[VMEM] * len(args), ou...  17.1 us
    ppermute x11, starting transfers between devices, move(): return lax.ppermute(value, ('row', 'col'), pairs)  15.5 us
    ppermute x11, waiting for transfers between devices, move(): return lax.ppermute(value, ('row', 'col'), pairs)  6.03 us
    ppermute x3, starting transfers between devices, paired_plan(): lax.ppermute(msgs[d], 'row', [(r, r ^ d) for r in range(4)])  3.15 us
    pallas_call x3, Pallas kernels, paired_plan(): pl.pallas_call(functools.partial(join_body, first, len(parts)), out_shape...  3.1 us
    pallas_call x1, Pallas kernels, paired_plan(): pl.pallas_call(open_body, out_shape=[struct((height, lanes), bf16)] * 4 +...  1.6 us
  transfers between devices with their start and end apart: 14, of which 5 were waited for; matrix products, arithmetic and copies ran while one was open for 0% of the time, Pallas kernels for 40%

profile of v18, /device:TPU:0, one launch (start us, length us, event | category | flops | bytes accessed | tf_op | source)
XLA Modules:
  0.0 47.7 jit_solution(2402325985574632248)
XLA Ops:
  0.0 1.6 %open.1 = (bf16[48,256]{1,0:T(8,128)(2,1)S(1)}, bf16[48,256]{1,0:T(8,128)(2,1)S(1)}, bf16[48,256]{1,0:T(8,128)(2,1)S(1)}, bf16[48,256]{1,0:T(8,128)(2,1)S(1)}, b...) custom-call(bf16[2,160,256]{2,1,0:T(8,128)(2,1)} %x_hbm.1, ...), custom_call_target="tpu_custom_call" | custom-call | bytes 5535000 | tf_op jit(solution)/shard_map/open/pallas_call | solution.py:595
  1.6 0.5 %collective-permute-start = (bf16[48,256]{1,0:T(8,128)(2,1)S(1)}, bf16[48,256]{1,0:T(8,128)(2,1)S(1)}, u32[]{:S(2)}, u32[]{:S(2)}) collective-permute-start(bf16[48,256]{1,0:T(8,128)(2,1)S(1)} %get-tuple-element.36), channel_id=1, source_target_pairs={{0,4},{4,0},{8,12},{12,8},{1,5},{5,1},{9,13},{13,9},{2,6},{6,2},{1... | collective-permute-start | bytes 73736 | tf_op jit(solution)/shard_map/ppermute | solution.py:612
  2.1 2.6 %collective-permute-start.1 = (bf16[48,256]{1,0:T(8,128)(2,1)S(1)}, bf16[48,256]{1,0:T(8,128)(2,1)S(1)}, u32[]{:S(2)}, u32[]{:S(2)}) collective-permute-start(bf16[48,256]{1,0:T(8,128)(2,1)S(1)} %get-tuple-element.37), channel_id=1, source_target_pairs={{0,8},{4,12},{8,0},{12,4},{1,9},{5,13},{9,1},{13,5},{2,10},{6,14},... | collective-permute-start | bytes 73736 | tf_op jit(solution)/shard_map/ppermute | solution.py:612
  4.7 0.1 collective-permute-start.2
  4.8 1.8 %collective-permute-start.5 = (bf16[42,40,128]{2,1,0:T(8,128)(2,1)S(1)}, bf16[42,40,128]{2,1,0:T(8,128)(2,1)S(1)}, u32[]{:S(2)}, u32[]{:S(2)}) collective-permute-start(bf16[42,40,128]{2,1,0:T(8,128)(2,1)S(1)} %get-tuple-element.54), channel_id=1, source_target_pairs={{0,1},{1,0},{2,3},{3,2},{4,5},{5,4},{6,7},{7,6},{8,9},{9,8},{10,11... | collective-permute-start | bytes 1290248 | tf_op jit(solution)/shard_map/ppermute | solution.py:575
  6.6 1.2 %collective-permute-start.3 = (bf16[41,40,128]{2,1,0:T(8,128)(2,1)S(1)}, bf16[41,40,128]{2,1,0:T(8,128)(2,1)S(1)}, u32[]{:S(2)}, u32[]{:S(2)}) collective-permute-start(bf16[41,40,128]{2,1,0:T(8,128)(2,1)S(1)} %get-tuple-element.39.block_ref), channel_id=1, source_target_pairs={{0,12},{1,5},{2,14},{3,7},{4,0},{5,9},{6,2},{7,11},{8,4},{9,13},{1... | collective-permute-start | bytes 1259528 | tf_op jit(solution)/shard_map/ppermute | solution.py:575
  7.7 0.9 %ready.1 = (bf16[16,32,256]{2,1,0:T(8,128)(2,1)S(1)}, bf16[2,4,128,256]{3,2,1,0:T(8,128)(2,1)S(1)}, s32[160,128]{1,0:T(8,128)S(1)}) custom-call(bf16[1024,128]{1,0:T(8,128)(2,1)S(1)} %get-tuple-element.40.avg_ref, s32[160]{0:T(256)} %ids_hbm.1), custom_call_target="tpu_custom_call" | custom-call | bytes 5535000 | tf_op jit(solution)/shard_map/ready/pallas_call | solution.py:617
  8.6 0.0 collective-permute-done.refs_1_
  8.6 0.0 collective-permute-done.1.refs_2_
  8.6 0.0 collective-permute-done.2.refs_3_
  8.7 0.9 %mix.1 = (bf16[20,256,256]{2,1,0:T(8,128)(2,1)S(1)}, bf16[2,40,256]{2,1,0:T(8,128)(2,1)S(1)}) custom-call(bf16[48,256]{1,0:T(8,128)(2,1)S(1)} %get-tuple-element.50.refs_0_, bf16[48,256]{1,0:T(8,128)(2,1)S(1)} %collective-permute-done.refs_1_, bf16[48,256]{1,0:T(8,128)(2,1)S(1)} %collective-permute-done.1.refs_2_, ...), custom_call_target="tpu_custom_call" | custom-call | bytes 3690000 | tf_op jit(solution)/shard_map/mix/pallas_call | solution.py:578
  9.6 2.4 %own.1 = (bf16[40,40,128]{2,1,0:T(8,128)(2,1)S(1)}, bf16[1600,128]{1,0:T(8,128)(2,1)S(1)}, bf16[40,40,128]{2,1,0:T(8,128)(2,1)S(1)}) custom-call(bf16[41,40,128]{2,1,0:T(8,128)(2,1)S(1)} %get-tuple-element.39.block_ref, bf16[20,256,256]{2,1,0:T(8,128)(2,1)S(1)} %get-tuple-element.43.t_ref, bf16[2,40,256]{2,1,0:T(8,128)(2,1)S(1)} %get-tuple-element.44.right_ref, ...), custom_call_target="tpu_custom_call" | custom-call | bytes 8856000 | tf_op jit(solution)/shard_map/own/pallas_call | solution.py:578
  12.0 0.1 collective-permute-start.7
  12.1 1.3 %collective-permute-done.3.block_ref = bf16[41,40,128]{2,1,0:T(8,128)(2,1)S(1)} collective-permute-done((bf16[41,40,128]{2,1,0:T(8,128)(2,1)S(1)}, bf16[41,40,128]{2,1,0:T(8,128)(2,1)S(1)}, u32[]{:S(2)}, u32[]{:S(2)}) %collective-permute-start.3) | collective-permute-done | bytes 419872 | tf_op jit(solution)/shard_map/ppermute | solution.py:575
  13.3 3.6 %collective-permute-start.4 = (bf16[40,40,128]{2,1,0:T(8,128)(2,1)S(1)}, bf16[40,40,128]{2,1,0:T(8,128)(2,1)S(1)}, u32[]{:S(2)}, u32[]{:S(2)}) collective-permute-start(bf16[40,40,128]{2,1,0:T(8,128)(2,1)S(1)} %other.1.other_ref), channel_id=1, source_target_pairs={{0,4},{1,5},{2,6},{3,7},{4,0},{5,1},{6,2},{7,3},{8,12},{9,13},{10,... | collective-permute-start | bytes 1228808 | tf_op jit(solution)/shard_map/ppermute | solution.py:575
  16.9 0.1 collective-permute-done.5.block_ref
  17.0 2.8 %met.1 = (bf16[40,40,128]{2,1,0:T(8,128)(2,1)S(1)}, bf16[40,40,128]{2,1,0:T(8,128)(2,1)S(1)}) custom-call(bf16[42,40,128]{2,1,0:T(8,128)(2,1)S(1)} %collective-permute-done.5.block_ref, bf16[20,256,256]{2,1,0:T(8,128)(2,1)S(1)} %get-tuple-element.43.t_ref, bf16[2,40,256]{2,1,0:T(8,128)(2,1)S(1)} %get-tuple-element.44.right_ref, ...), custom_call_target="tpu_custom_call" | custom-call | bytes 11070000 | tf_op jit(solution)/shard_map/met/pallas_call | solution.py:578
  19.8 0.1 collective-permute-start.6
  19.9 2.6 %collective-permute-done.7.far_ref = bf16[40,40,128]{2,1,0:T(8,128)(2,1)S(1)} collective-permute-done((bf16[40,40,128]{2,1,0:T(8,128)(2,1)S(1)}, bf16[40,40,128]{2,1,0:T(8,128)(2,1)S(1)}, u32[]{:S(2)}, u32[]{:S(2)}) %collective-permute-start.7) | collective-permute-done | bytes 409632 | tf_op jit(solution)/shard_map/ppermute | solution.py:575
  22.5 0.0 collective-permute-start.8
  22.5 0.5 %rest.1 = (bf16[40,40,128]{2,1,0:T(8,128)(2,1)S(1)}, f32[40,40,128]{2,1,0:T(8,128)S(1)}) custom-call(bf16[41,40,128]{2,1,0:T(8,128)(2,1)S(1)} %get-tuple-element.39.block_ref, bf16[1600,128]{1,0:T(8,128)(2,1)S(1)} %get-tuple-element.59.norm_ref, bf16[128,512]{1,0:T(8,128)(2,1)S(1)} %get-tuple-element.47.win_ref, bf16[128,128]{1,0:T(8,128)(2,1)S(1)} %get-tuple-element.60.wgate_ref), custom_call_target="tpu_custom_call" | custom-call | bytes 2214000 | tf_op jit(solution)/shard_map/rest/pallas_call | solution.py:578
  23.0 0.0 collective-permute-done.4.p_other
  23.0 0.0 collective-permute-done.6.p_met
  23.0 1.2 %collective-permute-done.8.p_far = bf16[40,40,128]{2,1,0:T(8,128)(2,1)S(1)} collective-permute-done((bf16[40,40,128]{2,1,0:T(8,128)(2,1)S(1)}, bf16[40,40,128]{2,1,0:T(8,128)(2,1)S(1)}, u32[]{:S(2)}, u32[]{:S(2)}) %collective-permute-start.8) | collective-permute-done | bytes 409632 | tf_op jit(solution)/shard_map/ppermute | solution.py:575
  24.2 1.0 %sums.10 = bf16[8,40,128]{2,1,0:T(8,128)(2,1)S(1)} custom-call(bf16[40,40,128]{2,1,0:T(8,128)(2,1)S(1)} %get-tuple-element.49.own_ref, bf16[40,40,128]{2,1,0:T(8,128)(2,1)S(1)} %other.1.other_ref, bf16[40,40,128]{2,1,0:T(8,128)(2,1)S(1)} %collective-permute-done.4.p_other, bf16[40,40,128]{2,1,0:T(8,128)(2,1)S(1)} %get-tuple-element.56.met_ref, ...), custom_call_target="tpu_custom_call" | custom-call | bytes 3837600 | tf_op jit(solution)/shard_map/sums/pallas_call | solution.py:578
  25.3 2.7 %collective-permute-start.12 = (bf16[8,40,128]{2,1,0:T(8,128)(2,1)S(1)}, bf16[8,40,128]{2,1,0:T(8,128)(2,1)S(1)}, u32[]{:S(2)}, u32[]{:S(2)}) collective-permute-start(bf16[8,40,128]{2,1,0:T(8,128)(2,1)S(1)} %sums.10), channel_id=1, source_target_pairs={{0,2},{1,3},{2,0},{3,1},{4,6},{5,7},{6,4},{7,5},{8,10},{9,11},{10,... | collective-permute-start | bytes 245768 | tf_op jit(solution)/shard_map/ppermute | solution.py:575
  27.9 1.0 %sums.11 = bf16[8,40,128]{2,1,0:T(8,128)(2,1)S(1)} custom-call(bf16[40,40,128]{2,1,0:T(8,128)(2,1)S(1)} %get-tuple-element.49.own_ref, bf16[40,40,128]{2,1,0:T(8,128)(2,1)S(1)} %other.1.other_ref, bf16[40,40,128]{2,1,0:T(8,128)(2,1)S(1)} %collective-permute-done.4.p_other, bf16[40,40,128]{2,1,0:T(8,128)(2,1)S(1)} %get-tuple-element.56.met_ref, ...), custom_call_target="tpu_custom_call" | custom-call | bytes 3837600 | tf_op jit(solution)/shard_map/sums/pallas_call | solution.py:578
  29.0 0.4 collective-permute-start.13
  29.4 1.2 %sums.8 = bf16[8,40,128]{2,1,0:T(8,128)(2,1)S(1)} custom-call(bf16[40,40,128]{2,1,0:T(8,128)(2,1)S(1)} %get-tuple-element.49.own_ref, bf16[40,40,128]{2,1,0:T(8,128)(2,1)S(1)} %other.1.other_ref, bf16[40,40,128]{2,1,0:T(8,128)(2,1)S(1)} %collective-permute-done.4.p_other, bf16[40,40,128]{2,1,0:T(8,128)(2,1)S(1)} %get-tuple-element.56.met_ref, ...), custom_call_target="tpu_custom_call" | custom-call | bytes 3837600 | tf_op jit(solution)/shard_map/sums/pallas_call | solution.py:578
  30.6 2.7 %collective-permute-start.10 = (bf16[8,40,128]{2,1,0:T(8,128)(2,1)S(1)}, bf16[8,40,128]{2,1,0:T(8,128)(2,1)S(1)}, u32[]{:S(2)}, u32[]{:S(2)}) collective-permute-start(bf16[8,40,128]{2,1,0:T(8,128)(2,1)S(1)} %sums.8), channel_id=1, source_target_pairs={{0,2},{1,3},{2,0},{3,1},{4,6},{5,7},{6,4},{7,5},{8,10},{9,11},{10,... | collective-permute-start | bytes 245768 | tf_op jit(solution)/shard_map/ppermute | solution.py:575
  33.3 1.0 %sums.9 = bf16[8,40,128]{2,1,0:T(8,128)(2,1)S(1)} custom-call(bf16[40,40,128]{2,1,0:T(8,128)(2,1)S(1)} %get-tuple-element.49.own_ref, bf16[40,40,128]{2,1,0:T(8,128)(2,1)S(1)} %other.1.other_ref, bf16[40,40,128]{2,1,0:T(8,128)(2,1)S(1)} %collective-permute-done.4.p_other, bf16[40,40,128]{2,1,0:T(8,128)(2,1)S(1)} %get-tuple-element.56.met_ref, ...), custom_call_target="tpu_custom_call" | custom-call | bytes 3837600 | tf_op jit(solution)/shard_map/sums/pallas_call | solution.py:578
  34.3 0.4 collective-permute-start.11
  34.7 1.0 %sums.7 = bf16[8,40,128]{2,1,0:T(8,128)(2,1)S(1)} custom-call(bf16[40,40,128]{2,1,0:T(8,128)(2,1)S(1)} %get-tuple-element.49.own_ref, bf16[40,40,128]{2,1,0:T(8,128)(2,1)S(1)} %other.1.other_ref, bf16[40,40,128]{2,1,0:T(8,128)(2,1)S(1)} %collective-permute-done.4.p_other, bf16[40,40,128]{2,1,0:T(8,128)(2,1)S(1)} %get-tuple-element.56.met_ref, ...), custom_call_target="tpu_custom_call" | custom-call | bytes 3837600 | tf_op jit(solution)/shard_map/sums/pallas_call | solution.py:578
  35.8 2.7 %collective-permute-start.9 = (bf16[8,40,128]{2,1,0:T(8,128)(2,1)S(1)}, bf16[8,40,128]{2,1,0:T(8,128)(2,1)S(1)}, u32[]{:S(2)}, u32[]{:S(2)}) collective-permute-start(bf16[8,40,128]{2,1,0:T(8,128)(2,1)S(1)} %sums.7), channel_id=1, source_target_pairs={{0,2},{1,3},{2,0},{3,1},{4,6},{5,7},{6,4},{7,5},{8,10},{9,11},{10,... | collective-permute-start | bytes 245768 | tf_op jit(solution)/shard_map/ppermute | solution.py:575
  38.4 5.1 %sums.6.own_ref = f32[40,40,128]{2,1,0:T(8,128)S(1)} custom-call(bf16[40,40,128]{2,1,0:T(8,128)(2,1)S(1)} %get-tuple-element.49.own_ref, bf16[40,40,128]{2,1,0:T(8,128)(2,1)S(1)} %other.1.other_ref, bf16[40,40,128]{2,1,0:T(8,128)(2,1)S(1)} %collective-permute-done.4.p_other, bf16[40,40,128]{2,1,0:T(8,128)(2,1)S(1)} %get-tuple-element.56.met_ref, ...), custom_call_target="tpu_custom_call" | custom-call | bytes 19188000 | tf_op jit(solution)/shard_map/sums/pallas_call | solution.py:578
  43.5 0.0 collective-permute-done.12.refs_0_
  43.6 0.0 collective-permute-done.13.refs_1_
  43.6 1.1 %join.3.refs_2_ = bf16[40,40,128]{2,1,0:T(8,128)(2,1)} custom-call(f32[40,40,128]{2,1,0:T(8,128)S(1)} %sums.6.own_ref, bf16[40,40,128]{2,1,0:T(8,128)(2,1)S(1)} %get-tuple-element.62.psum_ref, f32[40,40,128]{2,1,0:T(8,128)S(1)} %get-tuple-element.63.gate_ref, bf16[128,128]{1,0:T(8,128)(2,1)S(1)} %get-tuple-element.64.w_ref, ...), custom_call_target="tpu_custom_call" | custom-call | bytes 3542400 | tf_op jit(solution)/shard_map/join/pallas_call | solution.py:675
  44.6 0.0 collective-permute-done.10.refs_0_
  44.6 0.8 %collective-permute-done.11.refs_1_ = bf16[8,40,128]{2,1,0:T(8,128)(2,1)S(1)} collective-permute-done((bf16[8,40,128]{2,1,0:T(8,128)(2,1)S(1)}, bf16[8,40,128]{2,1,0:T(8,128)(2,1)S(1)}, u32[]{:S(2)}, u32[]{:S(2)}) %collective-permute-start.11) | collective-permute-done | bytes 81952 | tf_op jit(solution)/shard_map/ppermute | solution.py:575
  45.5 1.1 %join.4.refs_1_ = bf16[40,40,128]{2,1,0:T(8,128)(2,1)} custom-call(f32[40,40,128]{2,1,0:T(8,128)S(1)} %sums.6.own_ref, bf16[40,40,128]{2,1,0:T(8,128)(2,1)S(1)} %get-tuple-element.62.psum_ref, f32[40,40,128]{2,1,0:T(8,128)S(1)} %get-tuple-element.63.gate_ref, bf16[128,128]{1,0:T(8,128)(2,1)S(1)} %get-tuple-element.64.w_ref, ...), custom_call_target="tpu_custom_call", output_to_operand_aliasing={{}: (6, {})} | custom-call | bytes 3542400 | tf_op jit(solution)/shard_map/join/pallas_call | solution.py:675
  46.6 0.0 collective-permute-done.9.refs_0_
  46.6 1.0 %join.5 = bf16[40,40,128]{2,1,0:T(8,128)(2,1)} custom-call(f32[40,40,128]{2,1,0:T(8,128)S(1)} %sums.6.own_ref, bf16[40,40,128]{2,1,0:T(8,128)(2,1)S(1)} %get-tuple-element.62.psum_ref, f32[40,40,128]{2,1,0:T(8,128)S(1)} %get-tuple-element.63.gate_ref, bf16[128,128]{1,0:T(8,128)(2,1)S(1)} %get-tuple-element.64.w_ref, ...), custom_call_target="tpu_custom_call", output_to_operand_aliasing={{}: (5, {})} | custom-call | bytes 1771200 | tf_op jit(solution)/shard_map/join/pallas_call | solution.py:675
  (2 shorter events, 0.0 us)
Async XLA Ops:
  1.6 7.0 %collective-permute-start = (bf16[48,256]{1,0:T(8,128)(2,1)S(1)}, bf16[48,256]{1,0:T(8,128)(2,1)S(1)}, u32[]{:S(2)}, u32[]{:S(2)}) collective-permute-start(bf16[48,256]{1,0:T(8,128)(2,1)S(1)} %get-tuple-element.36), channel_id=1, source_target_pairs={{0,4},{4,0},{8,12},{12,8},{1,5},{5,1},{9,13},{13,9},{2,6},{6,2},{1... | collective-permute-start | bytes 73736 | tf_op jit(solution)/shard_map/ppermute | solution.py:612
  2.1 6.5 %collective-permute-start.1 = (bf16[48,256]{1,0:T(8,128)(2,1)S(1)}, bf16[48,256]{1,0:T(8,128)(2,1)S(1)}, u32[]{:S(2)}, u32[]{:S(2)}) collective-permute-start(bf16[48,256]{1,0:T(8,128)(2,1)S(1)} %get-tuple-element.37), channel_id=1, source_target_pairs={{0,8},{4,12},{8,0},{12,4},{1,9},{5,13},{9,1},{13,5},{2,10},{6,14},... | collective-permute-start | bytes 73736 | tf_op jit(solution)/shard_map/ppermute | solution.py:612
  4.7 3.9 %collective-permute-start.2 = (bf16[48,256]{1,0:T(8,128)(2,1)S(1)}, bf16[48,256]{1,0:T(8,128)(2,1)S(1)}, u32[]{:S(2)}, u32[]{:S(2)}) collective-permute-start(bf16[48,256]{1,0:T(8,128)(2,1)S(1)} %get-tuple-element.38), channel_id=1, source_target_pairs={{0,12},{4,8},{8,4},{12,0},{1,13},{5,9},{9,5},{13,1},{2,14},{6,10},... | collective-permute-start | bytes 73736 | tf_op jit(solution)/shard_map/ppermute | solution.py:612
  4.8 12.2 %collective-permute-start.5 = (bf16[42,40,128]{2,1,0:T(8,128)(2,1)S(1)}, bf16[42,40,128]{2,1,0:T(8,128)(2,1)S(1)}, u32[]{:S(2)}, u32[]{:S(2)}) collective-permute-start(bf16[42,40,128]{2,1,0:T(8,128)(2,1)S(1)} %get-tuple-element.54), channel_id=1, source_target_pairs={{0,1},{1,0},{2,3},{3,2},{4,5},{5,4},{6,7},{7,6},{8,9},{9,8},{10,11... | collective-permute-start | bytes 1290248 | tf_op jit(solution)/shard_map/ppermute | solution.py:575
  6.6 6.7 %collective-permute-start.3 = (bf16[41,40,128]{2,1,0:T(8,128)(2,1)S(1)}, bf16[41,40,128]{2,1,0:T(8,128)(2,1)S(1)}, u32[]{:S(2)}, u32[]{:S(2)}) collective-permute-start(bf16[41,40,128]{2,1,0:T(8,128)(2,1)S(1)} %get-tuple-element.39.block_ref), channel_id=1, source_target_pairs={{0,12},{1,5},{2,14},{3,7},{4,0},{5,9},{6,2},{7,11},{8,4},{9,13},{1... | collective-permute-start | bytes 1259528 | tf_op jit(solution)/shard_map/ppermute | solution.py:575
  12.0 10.5 %collective-permute-start.7 = (bf16[40,40,128]{2,1,0:T(8,128)(2,1)S(1)}, bf16[40,40,128]{2,1,0:T(8,128)(2,1)S(1)}, u32[]{:S(2)}, u32[]{:S(2)}) collective-permute-start(bf16[40,40,128]{2,1,0:T(8,128)(2,1)S(1)} %get-tuple-element.49.own_ref), channel_id=1, source_target_pairs={{0,4},{1,8},{2,6},{3,10},{4,13},{5,1},{6,15},{7,3},{8,12},{9,0},{1... | collective-permute-start | bytes 1228808 | tf_op jit(solution)/shard_map/ppermute | solution.py:575
  13.3 9.7 %collective-permute-start.4 = (bf16[40,40,128]{2,1,0:T(8,128)(2,1)S(1)}, bf16[40,40,128]{2,1,0:T(8,128)(2,1)S(1)}, u32[]{:S(2)}, u32[]{:S(2)}) collective-permute-start(bf16[40,40,128]{2,1,0:T(8,128)(2,1)S(1)} %other.1.other_ref), channel_id=1, source_target_pairs={{0,4},{1,5},{2,6},{3,7},{4,0},{5,1},{6,2},{7,3},{8,12},{9,13},{10,... | collective-permute-start | bytes 1228808 | tf_op jit(solution)/shard_map/ppermute | solution.py:575
  19.8 3.2 %collective-permute-start.6 = (bf16[40,40,128]{2,1,0:T(8,128)(2,1)S(1)}, bf16[40,40,128]{2,1,0:T(8,128)(2,1)S(1)}, u32[]{:S(2)}, u32[]{:S(2)}) collective-permute-start(bf16[40,40,128]{2,1,0:T(8,128)(2,1)S(1)} %get-tuple-element.56.met_ref), channel_id=1, source_target_pairs={{0,4},{1,5},{2,6},{3,7},{4,0},{5,1},{6,2},{7,3},{8,12},{9,13},{10,... | collective-permute-start | bytes 1228808 | tf_op jit(solution)/shard_map/ppermute | solution.py:575
  22.5 1.7 %collective-permute-start.8 = (bf16[40,40,128]{2,1,0:T(8,128)(2,1)S(1)}, bf16[40,40,128]{2,1,0:T(8,128)(2,1)S(1)}, u32[]{:S(2)}, u32[]{:S(2)}) collective-permute-start(bf16[40,40,128]{2,1,0:T(8,128)(2,1)S(1)} %collective-permute-done.7.far_ref), channel_id=1, source_target_pairs={{0,4},{1,5},{2,6},{3,7},{4,0},{5,1},{6,2},{7,3},{8,12},{9,13},{10,... | collective-permute-start | bytes 1228808 | tf_op jit(solution)/shard_map/ppermute | solution.py:575
  25.3 18.3 %collective-permute-start.12 = (bf16[8,40,128]{2,1,0:T(8,128)(2,1)S(1)}, bf16[8,40,128]{2,1,0:T(8,128)(2,1)S(1)}, u32[]{:S(2)}, u32[]{:S(2)}) collective-permute-start(bf16[8,40,128]{2,1,0:T(8,128)(2,1)S(1)} %sums.10), channel_id=1, source_target_pairs={{0,2},{1,3},{2,0},{3,1},{4,6},{5,7},{6,4},{7,5},{8,10},{9,11},{10,... | collective-permute-start | bytes 245768 | tf_op jit(solution)/shard_map/ppermute | solution.py:575
  29.0 14.6 %collective-permute-start.13 = (bf16[8,40,128]{2,1,0:T(8,128)(2,1)S(1)}, bf16[8,40,128]{2,1,0:T(8,128)(2,1)S(1)}, u32[]{:S(2)}, u32[]{:S(2)}) collective-permute-start(bf16[8,40,128]{2,1,0:T(8,128)(2,1)S(1)} %sums.11), channel_id=1, source_target_pairs={{0,2},{1,3},{2,0},{3,1},{4,6},{5,7},{6,4},{7,5},{8,10},{9,11},{10,... | collective-permute-start | bytes 245768 | tf_op jit(solution)/shard_map/ppermute | solution.py:575
  30.6 14.0 %collective-permute-start.10 = (bf16[8,40,128]{2,1,0:T(8,128)(2,1)S(1)}, bf16[8,40,128]{2,1,0:T(8,128)(2,1)S(1)}, u32[]{:S(2)}, u32[]{:S(2)}) collective-permute-start(bf16[8,40,128]{2,1,0:T(8,128)(2,1)S(1)} %sums.8), channel_id=1, source_target_pairs={{0,2},{1,3},{2,0},{3,1},{4,6},{5,7},{6,4},{7,5},{8,10},{9,11},{10,... | collective-permute-start | bytes 245768 | tf_op jit(solution)/shard_map/ppermute | solution.py:575
  34.3 11.2 %collective-permute-start.11 = (bf16[8,40,128]{2,1,0:T(8,128)(2,1)S(1)}, bf16[8,40,128]{2,1,0:T(8,128)(2,1)S(1)}, u32[]{:S(2)}, u32[]{:S(2)}) collective-permute-start(bf16[8,40,128]{2,1,0:T(8,128)(2,1)S(1)} %sums.9), channel_id=1, source_target_pairs={{0,2},{1,3},{2,0},{3,1},{4,6},{5,7},{6,4},{7,5},{8,10},{9,11},{10,... | collective-permute-start | bytes 245768 | tf_op jit(solution)/shard_map/ppermute | solution.py:575
  35.8 10.8 %collective-permute-start.9 = (bf16[8,40,128]{2,1,0:T(8,128)(2,1)S(1)}, bf16[8,40,128]{2,1,0:T(8,128)(2,1)S(1)}, u32[]{:S(2)}, u32[]{:S(2)}) collective-permute-start(bf16[8,40,128]{2,1,0:T(8,128)(2,1)S(1)} %sums.7), channel_id=1, source_target_pairs={{0,2},{1,3},{2,0},{3,1},{4,6},{5,7},{6,4},{7,5},{8,10},{9,11},{10,... | collective-permute-start | bytes 245768 | tf_op jit(solution)/shard_map/ppermute | solution.py:575

commit v19 on v15

--- a/solution.py
+++ b/solution.py
@@ -322,7 +322,7 @@
     half, terms, both = t_ref.shape
     chans, own_i, total = both // 2, 2 * half, seqs * 4
     for r in range(4):
-        m = msgs[r][pl.ds(0, own_i), :128].astype(f32)
+        m = msgs[r][:, :128].astype(f32)[:own_i]
         for s in range(seqs):
             lane = lane0 + s * width
             moved = pltpu.roll(m, 128 - lane, 1) if lane else m
@@ -384,9 +384,11 @@
 
     def use(rows, psums, flat):
         rights = gated(block_ref, rows, flat, w_right)
+        some = len(rows) // 2
+        for n in (0, some):
+            norm_ref[pl.ds(rows[n] * own_j, some * own_j), :] = flat[n * own_j : (n + some) * own_j]
         for n, at in enumerate(rows):
             psum_ref[at] = psums[n]
-            norm_ref[pl.ds(at * own_j, own_j), :] = flat[n * own_j : (n + 1) * own_j]
             flat_ref[pl.ds(at * own_j, own_j), :] = rights[n]
 
     block_norms(block_ref, t_ref, right_ref[0], r * own_i, z * own_j, idt_ref, bias_ref, use)

time: 46.7 us -> 46.7 us (level)
  no operation moved by 1% of the time
where the time goes in v19:
time: 46.7 us; the launch traced here: 46.5 us
  Pallas kernels  22.4 us (48%)
  starting transfers between devices  20.1 us (43%)
  waiting for transfers between devices  3.66 us (8%)
    ppermute x11, starting transfers between devices, move(): return lax.ppermute(value, ('row', 'col'), pairs)  18.3 us
    pallas_call x11, Pallas kernels, call(): pl.pallas_call(body, out_shape=out_shape, in_specs=[VMEM] * len(args), ou...  16.8 us
    pallas_call x3, Pallas kernels, paired_plan(): pl.pallas_call(functools.partial(join_body, first, len(parts)), out_shape...  3.1 us
    ppermute x11, waiting for transfers between devices, move(): return lax.ppermute(value, ('row', 'col'), pairs)  3.05 us
    ppermute x3, starting transfers between devices, paired_plan(): lax.ppermute(msgs[d], 'row', [(r, r ^ d) for r in range(4)])  1.86 us
    pallas_call x1, Pallas kernels, paired_plan(): pl.pallas_call(open_body, out_shape=[struct((height, lanes), bf16)] * 4 +...  1.6 us
  transfers between devices with their start and end apart: 14, of which 6 were waited for; matrix products, arithmetic and copies ran while one was open for 0% of the time, Pallas kernels for 40%

profile of v19, /device:TPU:0, one launch (start us, length us, event | category | flops | bytes accessed | tf_op | source)
XLA Modules:
  0.0 46.5 jit_solution(14708423107994308304)
XLA Ops:
  0.0 1.6 %open.1 = (bf16[48,256]{1,0:T(8,128)(2,1)S(1)}, bf16[48,256]{1,0:T(8,128)(2,1)S(1)}, bf16[48,256]{1,0:T(8,128)(2,1)S(1)}, bf16[48,256]{1,0:T(8,128)(2,1)S(1)}, b...) custom-call(bf16[2,160,256]{2,1,0:T(8,128)(2,1)} %x_hbm.1, ...), custom_call_target="tpu_custom_call" | custom-call | bytes 5535000 | tf_op jit(solution)/shard_map/open/pallas_call | solution.py:586
  1.6 3.1 %collective-permute-start.5 = (bf16[43,40,128]{2,1,0:T(8,128)(2,1)S(1)}, bf16[43,40,128]{2,1,0:T(8,128)(2,1)S(1)}, u32[]{:S(2)}, u32[]{:S(2)}) collective-permute-start(bf16[43,40,128]{2,1,0:T(8,128)(2,1)S(1)} %get-tuple-element.44), channel_id=1, source_target_pairs={{0,1},{1,0},{2,3},{3,2},{4,5},{5,4},{6,7},{7,6},{8,9},{9,8},{10,11... | collective-permute-start | bytes 1320968 | tf_op jit(solution)/shard_map/ppermute | solution.py:566
  4.7 0.0 collective-permute-start
  4.7 1.5 %collective-permute-start.1 = (bf16[48,256]{1,0:T(8,128)(2,1)S(1)}, bf16[48,256]{1,0:T(8,128)(2,1)S(1)}, u32[]{:S(2)}, u32[]{:S(2)}) collective-permute-start(bf16[48,256]{1,0:T(8,128)(2,1)S(1)} %get-tuple-element.33), channel_id=1, source_target_pairs={{0,8},{4,12},{8,0},{12,4},{1,9},{5,13},{9,1},{13,5},{2,10},{6,14},... | collective-permute-start | bytes 73736 | tf_op jit(solution)/shard_map/ppermute | solution.py:603
  6.2 0.4 collective-permute-start.2
  6.6 1.4 %collective-permute-start.3 = (bf16[41,40,128]{2,1,0:T(8,128)(2,1)S(1)}, bf16[41,40,128]{2,1,0:T(8,128)(2,1)S(1)}, u32[]{:S(2)}, u32[]{:S(2)}) collective-permute-start(bf16[41,40,128]{2,1,0:T(8,128)(2,1)S(1)} %get-tuple-element.30.block_ref), channel_id=1, source_target_pairs={{0,12},{1,5},{2,14},{3,7},{4,0},{5,9},{6,2},{7,11},{8,4},{9,13},{1... | collective-permute-start | bytes 1259528 | tf_op jit(solution)/shard_map/ppermute | solution.py:566
  7.9 0.9 %ready.1 = (bf16[16,32,256]{2,1,0:T(8,128)(2,1)S(1)}, bf16[2,4,128,256]{3,2,1,0:T(8,128)(2,1)S(1)}, s32[160,128]{1,0:T(8,128)S(1)}) custom-call(bf16[1024,128]{1,0:T(8,128)(2,1)S(1)} %get-tuple-element.35.avg_ref, s32[160]{0:T(256)} %ids_hbm.1), custom_call_target="tpu_custom_call" | custom-call | bytes 5535000 | tf_op jit(solution)/shard_map/ready/pallas_call | solution.py:608
  8.8 0.0 collective-permute-done.refs_1_
  8.8 0.0 collective-permute-done.1.refs_2_
  8.8 0.6 %collective-permute-done.2.refs_3_ = bf16[48,256]{1,0:T(8,128)(2,1)S(1)} collective-permute-done((bf16[48,256]{1,0:T(8,128)(2,1)S(1)}, bf16[48,256]{1,0:T(8,128)(2,1)S(1)}, u32[]{:S(2)}, u32[]{:S(2)}) %collective-permute-start.2) | collective-permute-done | bytes 24608 | tf_op jit(solution)/shard_map/ppermute | solution.py:603
  9.4 0.9 %mix.1 = (bf16[20,256,256]{2,1,0:T(8,128)(2,1)S(1)}, bf16[2,40,256]{2,1,0:T(8,128)(2,1)S(1)}) custom-call(bf16[48,256]{1,0:T(8,128)(2,1)S(1)} %get-tuple-element.31.refs_0_, bf16[48,256]{1,0:T(8,128)(2,1)S(1)} %collective-permute-done.refs_1_, bf16[48,256]{1,0:T(8,128)(2,1)S(1)} %collective-permute-done.1.refs_2_, ...), custom_call_target="tpu_custom_call" | custom-call | bytes 3690000 | tf_op jit(solution)/shard_map/mix/pallas_call | solution.py:569
  10.4 2.4 %own.1 = (bf16[40,40,128]{2,1,0:T(8,128)(2,1)S(1)}, bf16[1600,128]{1,0:T(8,128)(2,1)S(1)}, bf16[40,40,128]{2,1,0:T(8,128)(2,1)S(1)}) custom-call(bf16[41,40,128]{2,1,0:T(8,128)(2,1)S(1)} %get-tuple-element.30.block_ref, bf16[20,256,256]{2,1,0:T(8,128)(2,1)S(1)} %get-tuple-element.38.t_ref, bf16[2,40,256]{2,1,0:T(8,128)(2,1)S(1)} %get-tuple-element.39.right_ref.refs_6_, ...), custom_call_target="tpu_custom_call" | custom-call | bytes 8856000 | tf_op jit(solution)/shard_map/own/pallas_call | solution.py:569
  12.8 0.6 %collective-permute-start.7 = (bf16[40,40,128]{2,1,0:T(8,128)(2,1)S(1)}, bf16[40,40,128]{2,1,0:T(8,128)(2,1)S(1)}, u32[]{:S(2)}, u32[]{:S(2)}) collective-permute-start(bf16[40,40,128]{2,1,0:T(8,128)(2,1)S(1)} %get-tuple-element.43.own_ref), channel_id=1, source_target_pairs={{0,4},{1,8},{2,6},{3,10},{4,13},{5,1},{6,15},{7,3},{8,12},{9,0},{1... | collective-permute-start | bytes 1228808 | tf_op jit(solution)/shard_map/ppermute | solution.py:566
  13.3 0.2 collective-permute-done.3.refs_5_
  13.5 4.4 %collective-permute-start.4 = (bf16[40,40,128]{2,1,0:T(8,128)(2,1)S(1)}, bf16[40,40,128]{2,1,0:T(8,128)(2,1)S(1)}, u32[]{:S(2)}, u32[]{:S(2)}) collective-permute-start(bf16[40,40,128]{2,1,0:T(8,128)(2,1)S(1)} %other.1.other_ref), channel_id=1, source_target_pairs={{0,4},{1,5},{2,6},{3,7},{4,0},{5,1},{6,2},{7,3},{8,12},{9,13},{10,... | collective-permute-start | bytes 1228808 | tf_op jit(solution)/shard_map/ppermute | solution.py:566
  17.9 0.0 collective-permute-done.5.block_ref
  17.9 2.5 %met.1 = (bf16[40,40,128]{2,1,0:T(8,128)(2,1)S(1)}, bf16[40,40,128]{2,1,0:T(8,128)(2,1)S(1)}) custom-call(bf16[43,40,128]{2,1,0:T(8,128)(2,1)S(1)} %collective-permute-done.5.block_ref, bf16[20,256,256]{2,1,0:T(8,128)(2,1)S(1)} %get-tuple-element.38.t_ref, bf16[2,40,256]{2,1,0:T(8,128)(2,1)S(1)} %get-tuple-element.39.right_ref.refs_6_, ...), custom_call_target="tpu_custom_call" | custom-call | bytes 11070000 | tf_op jit(solution)/shard_map/met/pallas_call | solution.py:569
  20.4 0.1 collective-permute-start.6
  20.5 1.1 %collective-permute-done.7.far_ref = bf16[40,40,128]{2,1,0:T(8,128)(2,1)S(1)} collective-permute-done((bf16[40,40,128]{2,1,0:T(8,128)(2,1)S(1)}, bf16[40,40,128]{2,1,0:T(8,128)(2,1)S(1)}, u32[]{:S(2)}, u32[]{:S(2)}) %collective-permute-start.7) | collective-permute-done | bytes 409632 | tf_op jit(solution)/shard_map/ppermute | solution.py:566
  21.7 0.0 collective-permute-start.8
  21.7 0.5 %rest.1 = (bf16[40,40,128]{2,1,0:T(8,128)(2,1)S(1)}, f32[40,40,128]{2,1,0:T(8,128)S(1)}) custom-call(bf16[41,40,128]{2,1,0:T(8,128)(2,1)S(1)} %get-tuple-element.30.block_ref, bf16[1600,128]{1,0:T(8,128)(2,1)S(1)} %get-tuple-element.49.norm_ref, bf16[128,512]{1,0:T(8,128)(2,1)S(1)} %get-tuple-element.42.win_ref.refs_9_, ...), custom_call_target="tpu_custom_call" | custom-call | bytes 2214000 | tf_op jit(solution)/shard_map/rest/pallas_call | solution.py:569
  22.2 0.0 collective-permute-done.4.p_other
  22.2 0.1 collective-permute-done.6.p_met
  22.3 1.2 %collective-permute-done.8.p_far = bf16[40,40,128]{2,1,0:T(8,128)(2,1)S(1)} collective-permute-done((bf16[40,40,128]{2,1,0:T(8,128)(2,1)S(1)}, bf16[40,40,128]{2,1,0:T(8,128)(2,1)S(1)}, u32[]{:S(2)}, u32[]{:S(2)}) %collective-permute-start.8) | collective-permute-done | bytes 409632 | tf_op jit(solution)/shard_map/ppermute | solution.py:566
  23.4 1.0 %sums.10 = bf16[8,40,128]{2,1,0:T(8,128)(2,1)S(1)} custom-call(bf16[40,40,128]{2,1,0:T(8,128)(2,1)S(1)} %get-tuple-element.43.own_ref, bf16[40,40,128]{2,1,0:T(8,128)(2,1)S(1)} %other.1.other_ref, bf16[40,40,128]{2,1,0:T(8,128)(2,1)S(1)} %collective-permute-done.4.p_other, bf16[40,40,128]{2,1,0:T(8,128)(2,1)S(1)} %get-tuple-element.46.met_ref, ...), custom_call_target="tpu_custom_call" | custom-call | bytes 3837600 | tf_op jit(solution)/shard_map/sums/pallas_call | solution.py:569
  24.5 2.7 %collective-permute-start.12 = (bf16[8,40,128]{2,1,0:T(8,128)(2,1)S(1)}, bf16[8,40,128]{2,1,0:T(8,128)(2,1)S(1)}, u32[]{:S(2)}, u32[]{:S(2)}) collective-permute-start(bf16[8,40,128]{2,1,0:T(8,128)(2,1)S(1)} %sums.10), channel_id=1, source_target_pairs={{0,2},{1,3},{2,0},{3,1},{4,6},{5,7},{6,4},{7,5},{8,10},{9,11},{10,... | collective-permute-start | bytes 245768 | tf_op jit(solution)/shard_map/ppermute | solution.py:566
  27.1 1.0 %sums.11 = bf16[8,40,128]{2,1,0:T(8,128)(2,1)S(1)} custom-call(bf16[40,40,128]{2,1,0:T(8,128)(2,1)S(1)} %get-tuple-element.43.own_ref, bf16[40,40,128]{2,1,0:T(8,128)(2,1)S(1)} %other.1.other_ref, bf16[40,40,128]{2,1,0:T(8,128)(2,1)S(1)} %collective-permute-done.4.p_other, bf16[40,40,128]{2,1,0:T(8,128)(2,1)S(1)} %get-tuple-element.46.met_ref, ...), custom_call_target="tpu_custom_call" | custom-call | bytes 3837600 | tf_op jit(solution)/shard_map/sums/pallas_call | solution.py:569
  28.2 0.4 collective-permute-start.13
  28.6 1.0 %sums.8 = bf16[8,40,128]{2,1,0:T(8,128)(2,1)S(1)} custom-call(bf16[40,40,128]{2,1,0:T(8,128)(2,1)S(1)} %get-tuple-element.43.own_ref, bf16[40,40,128]{2,1,0:T(8,128)(2,1)S(1)} %other.1.other_ref, bf16[40,40,128]{2,1,0:T(8,128)(2,1)S(1)} %collective-permute-done.4.p_other, bf16[40,40,128]{2,1,0:T(8,128)(2,1)S(1)} %get-tuple-element.46.met_ref, ...), custom_call_target="tpu_custom_call" | custom-call | bytes 3837600 | tf_op jit(solution)/shard_map/sums/pallas_call | solution.py:569
  29.6 2.7 %collective-permute-start.10 = (bf16[8,40,128]{2,1,0:T(8,128)(2,1)S(1)}, bf16[8,40,128]{2,1,0:T(8,128)(2,1)S(1)}, u32[]{:S(2)}, u32[]{:S(2)}) collective-permute-start(bf16[8,40,128]{2,1,0:T(8,128)(2,1)S(1)} %sums.8), channel_id=1, source_target_pairs={{0,2},{1,3},{2,0},{3,1},{4,6},{5,7},{6,4},{7,5},{8,10},{9,11},{10,... | collective-permute-start | bytes 245768 | tf_op jit(solution)/shard_map/ppermute | solution.py:566
  32.3 1.2 %sums.9 = bf16[8,40,128]{2,1,0:T(8,128)(2,1)S(1)} custom-call(bf16[40,40,128]{2,1,0:T(8,128)(2,1)S(1)} %get-tuple-element.43.own_ref, bf16[40,40,128]{2,1,0:T(8,128)(2,1)S(1)} %other.1.other_ref, bf16[40,40,128]{2,1,0:T(8,128)(2,1)S(1)} %collective-permute-done.4.p_other, bf16[40,40,128]{2,1,0:T(8,128)(2,1)S(1)} %get-tuple-element.46.met_ref, ...), custom_call_target="tpu_custom_call" | custom-call | bytes 3837600 | tf_op jit(solution)/shard_map/sums/pallas_call | solution.py:569
  33.5 0.4 collective-permute-start.11
  33.9 1.0 %sums.7 = bf16[8,40,128]{2,1,0:T(8,128)(2,1)S(1)} custom-call(bf16[40,40,128]{2,1,0:T(8,128)(2,1)S(1)} %get-tuple-element.43.own_ref, bf16[40,40,128]{2,1,0:T(8,128)(2,1)S(1)} %other.1.other_ref, bf16[40,40,128]{2,1,0:T(8,128)(2,1)S(1)} %collective-permute-done.4.p_other, bf16[40,40,128]{2,1,0:T(8,128)(2,1)S(1)} %get-tuple-element.46.met_ref, ...), custom_call_target="tpu_custom_call" | custom-call | bytes 3837600 | tf_op jit(solution)/shard_map/sums/pallas_call | solution.py:569
  34.9 2.7 %collective-permute-start.9 = (bf16[8,40,128]{2,1,0:T(8,128)(2,1)S(1)}, bf16[8,40,128]{2,1,0:T(8,128)(2,1)S(1)}, u32[]{:S(2)}, u32[]{:S(2)}) collective-permute-start(bf16[8,40,128]{2,1,0:T(8,128)(2,1)S(1)} %sums.7), channel_id=1, source_target_pairs={{0,2},{1,3},{2,0},{3,1},{4,6},{5,7},{6,4},{7,5},{8,10},{9,11},{10,... | collective-permute-start | bytes 245768 | tf_op jit(solution)/shard_map/ppermute | solution.py:566
  37.6 5.1 %sums.6.own_ref = f32[40,40,128]{2,1,0:T(8,128)S(1)} custom-call(bf16[40,40,128]{2,1,0:T(8,128)(2,1)S(1)} %get-tuple-element.43.own_ref, bf16[40,40,128]{2,1,0:T(8,128)(2,1)S(1)} %other.1.other_ref, bf16[40,40,128]{2,1,0:T(8,128)(2,1)S(1)} %collective-permute-done.4.p_other, bf16[40,40,128]{2,1,0:T(8,128)(2,1)S(1)} %get-tuple-element.46.met_ref, ...), custom_call_target="tpu_custom_call" | custom-call | bytes 19188000 | tf_op jit(solution)/shard_map/sums/pallas_call | solution.py:569
  42.7 0.0 collective-permute-done.12.refs_0_
  42.7 0.0 collective-permute-done.13.refs_1_
  42.8 1.1 %join.3.refs_2_ = bf16[40,40,128]{2,1,0:T(8,128)(2,1)} custom-call(f32[40,40,128]{2,1,0:T(8,128)S(1)} %sums.6.own_ref, bf16[40,40,128]{2,1,0:T(8,128)(2,1)S(1)} %get-tuple-element.52.psum_ref, f32[40,40,128]{2,1,0:T(8,128)S(1)} %get-tuple-element.53.gate_ref, bf16[128,128]{1,0:T(8,128)(2,1)S(1)} %get-tuple-element.54.w_ref, ...), custom_call_target="tpu_custom_call" | custom-call | bytes 3542400 | tf_op jit(solution)/shard_map/join/pallas_call | solution.py:663
  43.8 0.0 collective-permute-done.10.refs_0_
  43.8 0.0 collective-permute-done.11.refs_1_
  43.8 1.1 %join.4.refs_1_ = bf16[40,40,128]{2,1,0:T(8,128)(2,1)} custom-call(f32[40,40,128]{2,1,0:T(8,128)S(1)} %sums.6.own_ref, bf16[40,40,128]{2,1,0:T(8,128)(2,1)S(1)} %get-tuple-element.52.psum_ref, f32[40,40,128]{2,1,0:T(8,128)S(1)} %get-tuple-element.53.gate_ref, bf16[128,128]{1,0:T(8,128)(2,1)S(1)} %get-tuple-element.54.w_ref, ...), custom_call_target="tpu_custom_call", output_to_operand_aliasing={{}: (6, {})} | custom-call | bytes 3542400 | tf_op jit(solution)/shard_map/join/pallas_call | solution.py:663
  44.9 0.5 %collective-permute-done.9.refs_0_ = bf16[8,40,128]{2,1,0:T(8,128)(2,1)S(1)} collective-permute-done((bf16[8,40,128]{2,1,0:T(8,128)(2,1)S(1)}, bf16[8,40,128]{2,1,0:T(8,128)(2,1)S(1)}, u32[]{:S(2)}, u32[]{:S(2)}) %collective-permute-start.9) | collective-permute-done | bytes 81952 | tf_op jit(solution)/shard_map/ppermute | solution.py:566
  45.4 1.0 %join.5 = bf16[40,40,128]{2,1,0:T(8,128)(2,1)} custom-call(f32[40,40,128]{2,1,0:T(8,128)S(1)} %sums.6.own_ref, bf16[40,40,128]{2,1,0:T(8,128)(2,1)S(1)} %get-tuple-element.52.psum_ref, f32[40,40,128]{2,1,0:T(8,128)S(1)} %get-tuple-element.53.gate_ref, bf16[128,128]{1,0:T(8,128)(2,1)S(1)} %get-tuple-element.54.w_ref, ...), custom_call_target="tpu_custom_call", output_to_operand_aliasing={{}: (5, {})} | custom-call | bytes 1771200 | tf_op jit(solution)/shard_map/join/pallas_call | solution.py:663
  (1 shorter events, 0.0 us)
Async XLA Ops:
  1.6 16.3 %collective-permute-start.5 = (bf16[43,40,128]{2,1,0:T(8,128)(2,1)S(1)}, bf16[43,40,128]{2,1,0:T(8,128)(2,1)S(1)}, u32[]{:S(2)}, u32[]{:S(2)}) collective-permute-start(bf16[43,40,128]{2,1,0:T(8,128)(2,1)S(1)} %get-tuple-element.44), channel_id=1, source_target_pairs={{0,1},{1,0},{2,3},{3,2},{4,5},{5,4},{6,7},{7,6},{8,9},{9,8},{10,11... | collective-permute-start | bytes 1320968 | tf_op jit(solution)/shard_map/ppermute | solution.py:566
  4.7 4.1 %collective-permute-start = (bf16[48,256]{1,0:T(8,128)(2,1)S(1)}, bf16[48,256]{1,0:T(8,128)(2,1)S(1)}, u32[]{:S(2)}, u32[]{:S(2)}) collective-permute-start(bf16[48,256]{1,0:T(8,128)(2,1)S(1)} %get-tuple-element.32), channel_id=1, source_target_pairs={{0,4},{4,0},{8,12},{12,8},{1,5},{5,1},{9,13},{13,9},{2,6},{6,2},{1... | collective-permute-start | bytes 73736 | tf_op jit(solution)/shard_map/ppermute | solution.py:603
  4.7 4.1 %collective-permute-start.1 = (bf16[48,256]{1,0:T(8,128)(2,1)S(1)}, bf16[48,256]{1,0:T(8,128)(2,1)S(1)}, u32[]{:S(2)}, u32[]{:S(2)}) collective-permute-start(bf16[48,256]{1,0:T(8,128)(2,1)S(1)} %get-tuple-element.33), channel_id=1, source_target_pairs={{0,8},{4,12},{8,0},{12,4},{1,9},{5,13},{9,1},{13,5},{2,10},{6,14},... | collective-permute-start | bytes 73736 | tf_op jit(solution)/shard_map/ppermute | solution.py:603
  6.2 3.3 %collective-permute-start.2 = (bf16[48,256]{1,0:T(8,128)(2,1)S(1)}, bf16[48,256]{1,0:T(8,128)(2,1)S(1)}, u32[]{:S(2)}, u32[]{:S(2)}) collective-permute-start(bf16[48,256]{1,0:T(8,128)(2,1)S(1)} %get-tuple-element.34), channel_id=1, source_target_pairs={{0,12},{4,8},{8,4},{12,0},{1,13},{5,9},{9,5},{13,1},{2,14},{6,10},... | collective-permute-start | bytes 73736 | tf_op jit(solution)/shard_map/ppermute | solution.py:603
  6.6 7.0 %collective-permute-start.3 = (bf16[41,40,128]{2,1,0:T(8,128)(2,1)S(1)}, bf16[41,40,128]{2,1,0:T(8,128)(2,1)S(1)}, u32[]{:S(2)}, u32[]{:S(2)}) collective-permute-start(bf16[41,40,128]{2,1,0:T(8,128)(2,1)S(1)} %get-tuple-element.30.block_ref), channel_id=1, source_target_pairs={{0,12},{1,5},{2,14},{3,7},{4,0},{5,9},{6,2},{7,11},{8,4},{9,13},{1... | collective-permute-start | bytes 1259528 | tf_op jit(solution)/shard_map/ppermute | solution.py:566
  12.8 8.9 %collective-permute-start.7 = (bf16[40,40,128]{2,1,0:T(8,128)(2,1)S(1)}, bf16[40,40,128]{2,1,0:T(8,128)(2,1)S(1)}, u32[]{:S(2)}, u32[]{:S(2)}) collective-permute-start(bf16[40,40,128]{2,1,0:T(8,128)(2,1)S(1)} %get-tuple-element.43.own_ref), channel_id=1, source_target_pairs={{0,4},{1,8},{2,6},{3,10},{4,13},{5,1},{6,15},{7,3},{8,12},{9,0},{1... | collective-permute-start | bytes 1228808 | tf_op jit(solution)/shard_map/ppermute | solution.py:566
  13.5 8.6 %collective-permute-start.4 = (bf16[40,40,128]{2,1,0:T(8,128)(2,1)S(1)}, bf16[40,40,128]{2,1,0:T(8,128)(2,1)S(1)}, u32[]{:S(2)}, u32[]{:S(2)}) collective-permute-start(bf16[40,40,128]{2,1,0:T(8,128)(2,1)S(1)} %other.1.other_ref), channel_id=1, source_target_pairs={{0,4},{1,5},{2,6},{3,7},{4,0},{5,1},{6,2},{7,3},{8,12},{9,13},{10,... | collective-permute-start | bytes 1228808 | tf_op jit(solution)/shard_map/ppermute | solution.py:566
  20.4 1.8 %collective-permute-start.6 = (bf16[40,40,128]{2,1,0:T(8,128)(2,1)S(1)}, bf16[40,40,128]{2,1,0:T(8,128)(2,1)S(1)}, u32[]{:S(2)}, u32[]{:S(2)}) collective-permute-start(bf16[40,40,128]{2,1,0:T(8,128)(2,1)S(1)} %get-tuple-element.46.met_ref), channel_id=1, source_target_pairs={{0,4},{1,5},{2,6},{3,7},{4,0},{5,1},{6,2},{7,3},{8,12},{9,13},{10,... | collective-permute-start | bytes 1228808 | tf_op jit(solution)/shard_map/ppermute | solution.py:566
  21.7 1.7 %collective-permute-start.8 = (bf16[40,40,128]{2,1,0:T(8,128)(2,1)S(1)}, bf16[40,40,128]{2,1,0:T(8,128)(2,1)S(1)}, u32[]{:S(2)}, u32[]{:S(2)}) collective-permute-start(bf16[40,40,128]{2,1,0:T(8,128)(2,1)S(1)} %collective-permute-done.7.far_ref), channel_id=1, source_target_pairs={{0,4},{1,5},{2,6},{3,7},{4,0},{5,1},{6,2},{7,3},{8,12},{9,13},{10,... | collective-permute-start | bytes 1228808 | tf_op jit(solution)/shard_map/ppermute | solution.py:566
  24.5 18.3 %collective-permute-start.12 = (bf16[8,40,128]{2,1,0:T(8,128)(2,1)S(1)}, bf16[8,40,128]{2,1,0:T(8,128)(2,1)S(1)}, u32[]{:S(2)}, u32[]{:S(2)}) collective-permute-start(bf16[8,40,128]{2,1,0:T(8,128)(2,1)S(1)} %sums.10), channel_id=1, source_target_pairs={{0,2},{1,3},{2,0},{3,1},{4,6},{5,7},{6,4},{7,5},{8,10},{9,11},{10,... | collective-permute-start | bytes 245768 | tf_op jit(solution)/shard_map/ppermute | solution.py:566
  28.2 14.6 %collective-permute-start.13 = (bf16[8,40,128]{2,1,0:T(8,128)(2,1)S(1)}, bf16[8,40,128]{2,1,0:T(8,128)(2,1)S(1)}, u32[]{:S(2)}, u32[]{:S(2)}) collective-permute-start(bf16[8,40,128]{2,1,0:T(8,128)(2,1)S(1)} %sums.11), channel_id=1, source_target_pairs={{0,2},{1,3},{2,0},{3,1},{4,6},{5,7},{6,4},{7,5},{8,10},{9,11},{10,... | collective-permute-start | bytes 245768 | tf_op jit(solution)/shard_map/ppermute | solution.py:566
  29.6 14.2 %collective-permute-start.10 = (bf16[8,40,128]{2,1,0:T(8,128)(2,1)S(1)}, bf16[8,40,128]{2,1,0:T(8,128)(2,1)S(1)}, u32[]{:S(2)}, u32[]{:S(2)}) collective-permute-start(bf16[8,40,128]{2,1,0:T(8,128)(2,1)S(1)} %sums.8), channel_id=1, source_target_pairs={{0,2},{1,3},{2,0},{3,1},{4,6},{5,7},{6,4},{7,5},{8,10},{9,11},{10,... | collective-permute-start | bytes 245768 | tf_op jit(solution)/shard_map/ppermute | solution.py:566
  33.5 10.3 %collective-permute-start.11 = (bf16[8,40,128]{2,1,0:T(8,128)(2,1)S(1)}, bf16[8,40,128]{2,1,0:T(8,128)(2,1)S(1)}, u32[]{:S(2)}, u32[]{:S(2)}) collective-permute-start(bf16[8,40,128]{2,1,0:T(8,128)(2,1)S(1)} %sums.9), channel_id=1, source_target_pairs={{0,2},{1,3},{2,0},{3,1},{4,6},{5,7},{6,4},{7,5},{8,10},{9,11},{10,... | collective-permute-start | bytes 245768 | tf_op jit(solution)/shard_map/ppermute | solution.py:566
  34.9 10.5 %collective-permute-start.9 = (bf16[8,40,128]{2,1,0:T(8,128)(2,1)S(1)}, bf16[8,40,128]{2,1,0:T(8,128)(2,1)S(1)}, u32[]{:S(2)}, u32[]{:S(2)}) collective-permute-start(bf16[8,40,128]{2,1,0:T(8,128)(2,1)S(1)} %sums.7), channel_id=1, source_target_pairs={{0,2},{1,3},{2,0},{3,1},{4,6},{5,7},{6,4},{7,5},{8,10},{9,11},{10,... | collective-permute-start | bytes 245768 | tf_op jit(solution)/shard_map/ppermute | solution.py:566

commit v20 on v19

--- a/solution.py
+++ b/solution.py
@@ -409,9 +409,15 @@
             gate_ref[i + n] = gate[n * own_j : (n + 1) * own_j]
 
 
-def other_body(seqs, width, *refs):
-    msgs, refs = refs[:4], refs[4:]
-    wq_ref, block_ref, right_ref, idt_ref, bias_ref, win_ref, out_ref, t_ref, xl_ref, flat_ref = refs
+def mix_other_body(seqs, width, *refs):
+    msgs, (wq_ref, t_ref, xl_ref) = refs[:4], refs[4:]
+
+    @pl.when((lax.axis_index("row") % 2) != (lax.axis_index("col") % 2))
+    def _():
+        mix_rows(seqs, width, seqs * width, msgs, wq_ref, t_ref, xl_ref)
+
+
+def other_body(block_ref, t_ref, right_ref, idt_ref, bias_ref, win_ref, out_ref, flat_ref):
     own_j, own_i, _ = out_ref.shape
     r, z = lax.axis_index("row"), lax.axis_index("col")
     side = win_ref.shape[1] // 2
@@ -423,7 +429,6 @@
 
     @pl.when((r % 2) != (z % 2))
     def _():
-        mix_rows(seqs, width, seqs * width, msgs, wq_ref, t_ref, xl_ref)
         block_norms(block_ref, t_ref, right_ref[0], (r ^ 3) * own_i, z * own_j, idt_ref, bias_ref, use)
         for k in range(own_j):
             out_ref[k] = flat_ref[pl.ds(k, own_i, stride=own_j), :].astype(bf16)
@@ -635,11 +640,12 @@
     )
     far = move(right, lambda r, z: (r ^ 1, z) if keeper(r, z) else (r ^ 2, z ^ 1))
     left, gate = call(rest_body, 0.6, [square, struct(couple.shape, f32)], [], raw, norm, w_in, w_gate)
-    other = call(
-        functools.partial(other_body, seqs, width), 3, square,
-        [pltpu.VMEM(t.shape, bf16), pltpu.VMEM((own_i * total, 128), f32)] + flat,
-        *msgs, wq, raw_other, mixed, idt, bias, w_in,
+    msgs, right = lax.optimization_barrier((msgs, right))
+    t_other = call(
+        functools.partial(mix_other_body, seqs, width), 1, struct(t.shape, bf16),
+        [pltpu.VMEM((own_i * total, 128), f32)], *msgs, wq,
     )
+    other = call(other_body, 2.4, square, flat, raw_other, t_other, mixed, idt, bias, w_in)
     p_other = move(other, beside)
     met, *_ = lax.optimization_barrier((met, other))
     met_left, met_right = call(met_body, 3, [square, square], flat, met, t, mixed, idt, bias, w_in)

time: 46.7 us -> 46.8 us (level)
  waiting for transfers between devices: 3.66 us -> 4.57 us
  starting transfers between devices: 20.1 us -> 19.3 us
    ppermute x11, waiting for transfers between devices: 3.05 us -> 3.96 us  [move(): return lax.ppermute(value, ('row', 'col'), pairs)]
    ppermute x11, starting transfers between devices: 18.3 us -> 17.5 us  [move(): return lax.ppermute(value, ('row', 'col'), pairs)]
    pallas_call x11 -> x12, Pallas kernels: 16.8 us -> 16.8 us  [call(): pl.pallas_call(body, out_shape=out_shape, in_specs=[VMEM] * len(args), ou...]
  transfers between devices with their start and end apart: 14 -> 14, of which waited for: 6 -> 5; matrix products, arithmetic and copies ran while one was open for 0% -> 0% of each run, Pallas kernels for 40% -> 40%
where the time goes in v20:
time: 46.8 us; the launch traced here: 46.7 us
  Pallas kernels  22.4 us (48%)
  starting transfers between devices  19.3 us (41%)
  waiting for transfers between devices  4.57 us (10%)
    ppermute x11, starting transfers between devices, move(): return lax.ppermute(value, ('row', 'col'), pairs)  17.5 us
    pallas_call x12, Pallas kernels, call(): pl.pallas_call(body, out_shape=out_shape, in_specs=[VMEM] * len(args), ou...  16.8 us
    ppermute x11, waiting for transfers between devices, move(): return lax.ppermute(value, ('row', 'col'), pairs)  3.96 us
    pallas_call x3, Pallas kernels, paired_plan(): pl.pallas_call(functools.partial(join_body, first, len(parts)), out_shape...  3.11 us
    ppermute x3, starting transfers between devices, paired_plan(): lax.ppermute(msgs[d], 'row', [(r, r ^ d) for r in range(4)])  1.86 us
    pallas_call x1, Pallas kernels, paired_plan(): pl.pallas_call(open_body, out_shape=[struct((height, lanes), bf16)] * 4 +...  1.6 us
  transfers between devices with their start and end apart: 14, of which 5 were waited for; matrix products, arithmetic and copies ran while one was open for 0% of the time, Pallas kernels for 40%

profile of v20, /device:TPU:0, one launch (start us, length us, event | category | flops | bytes accessed | tf_op | source)
XLA Modules:
  0.0 46.7 jit_solution(15542546869606232367)
XLA Ops:
  0.0 1.6 %open.1 = (bf16[48,256]{1,0:T(8,128)(2,1)S(1)}, bf16[48,256]{1,0:T(8,128)(2,1)S(1)}, bf16[48,256]{1,0:T(8,128)(2,1)S(1)}, bf16[48,256]{1,0:T(8,128)(2,1)S(1)}, b...) custom-call(bf16[2,160,256]{2,1,0:T(8,128)(2,1)} %x_hbm.1, ...), custom_call_target="tpu_custom_call" | custom-call | bytes 5535000 | tf_op jit(solution)/shard_map/open/pallas_call | solution.py:591
  1.6 3.1 %collective-permute-start.5 = (bf16[43,40,128]{2,1,0:T(8,128)(2,1)S(1)}, bf16[43,40,128]{2,1,0:T(8,128)(2,1)S(1)}, u32[]{:S(2)}, u32[]{:S(2)}) collective-permute-start(bf16[43,40,128]{2,1,0:T(8,128)(2,1)S(1)} %get-tuple-element.54), channel_id=1, source_target_pairs={{0,1},{1,0},{2,3},{3,2},{4,5},{5,4},{6,7},{7,6},{8,9},{9,8},{10,11... | collective-permute-start | bytes 1320968 | tf_op jit(solution)/shard_map/ppermute | solution.py:571
  4.7 0.0 collective-permute-start
  4.7 1.5 %collective-permute-start.1 = (bf16[48,256]{1,0:T(8,128)(2,1)S(1)}, bf16[48,256]{1,0:T(8,128)(2,1)S(1)}, u32[]{:S(2)}, u32[]{:S(2)}) collective-permute-start(bf16[48,256]{1,0:T(8,128)(2,1)S(1)} %get-tuple-element.37), channel_id=1, source_target_pairs={{0,8},{4,12},{8,0},{12,4},{1,9},{5,13},{9,1},{13,5},{2,10},{6,14},... | collective-permute-start | bytes 73736 | tf_op jit(solution)/shard_map/ppermute | solution.py:608
  6.2 0.4 collective-permute-start.2
  6.6 1.4 %collective-permute-start.3 = (bf16[41,40,128]{2,1,0:T(8,128)(2,1)S(1)}, bf16[41,40,128]{2,1,0:T(8,128)(2,1)S(1)}, u32[]{:S(2)}, u32[]{:S(2)}) collective-permute-start(bf16[41,40,128]{2,1,0:T(8,128)(2,1)S(1)} %get-tuple-element.39.block_ref), channel_id=1, source_target_pairs={{0,12},{1,5},{2,14},{3,7},{4,0},{5,9},{6,2},{7,11},{8,4},{9,13},{1... | collective-permute-start | bytes 1259528 | tf_op jit(solution)/shard_map/ppermute | solution.py:571
  7.9 0.9 %ready.1 = (bf16[16,32,256]{2,1,0:T(8,128)(2,1)S(1)}, bf16[2,4,128,256]{3,2,1,0:T(8,128)(2,1)S(1)}, s32[160,128]{1,0:T(8,128)S(1)}) custom-call(bf16[1024,128]{1,0:T(8,128)(2,1)S(1)} %get-tuple-element.40.avg_ref, s32[160]{0:T(256)} %ids_hbm.1), custom_call_target="tpu_custom_call" | custom-call | bytes 5535000 | tf_op jit(solution)/shard_map/ready/pallas_call | solution.py:613
  8.8 0.0 collective-permute-done.refs_1_
  8.8 0.0 collective-permute-done.1.refs_2_
  8.8 0.6 %collective-permute-done.2.refs_3_ = bf16[48,256]{1,0:T(8,128)(2,1)S(1)} collective-permute-done((bf16[48,256]{1,0:T(8,128)(2,1)S(1)}, bf16[48,256]{1,0:T(8,128)(2,1)S(1)}, u32[]{:S(2)}, u32[]{:S(2)}) %collective-permute-start.2) | collective-permute-done | bytes 24608 | tf_op jit(solution)/shard_map/ppermute | solution.py:608
  9.4 0.9 %mix.1 = (bf16[20,256,256]{2,1,0:T(8,128)(2,1)S(1)}, bf16[2,40,256]{2,1,0:T(8,128)(2,1)S(1)}) custom-call(bf16[48,256]{1,0:T(8,128)(2,1)S(1)} %get-tuple-element.50.refs_0_, bf16[48,256]{1,0:T(8,128)(2,1)S(1)} %collective-permute-done.refs_1_, bf16[48,256]{1,0:T(8,128)(2,1)S(1)} %collective-permute-done.1.refs_2_, ...), custom_call_target="tpu_custom_call" | custom-call | bytes 3690000 | tf_op jit(solution)/shard_map/mix/pallas_call | solution.py:574
  10.4 2.4 %own.1 = (bf16[40,40,128]{2,1,0:T(8,128)(2,1)S(1)}, bf16[1600,128]{1,0:T(8,128)(2,1)S(1)}, bf16[40,40,128]{2,1,0:T(8,128)(2,1)S(1)}) custom-call(bf16[41,40,128]{2,1,0:T(8,128)(2,1)S(1)} %get-tuple-element.39.block_ref, bf16[20,256,256]{2,1,0:T(8,128)(2,1)S(1)} %get-tuple-element.43.t_ref, bf16[2,40,256]{2,1,0:T(8,128)(2,1)S(1)} %get-tuple-element.44.right_ref, ...), custom_call_target="tpu_custom_call" | custom-call | bytes 8856000 | tf_op jit(solution)/shard_map/own/pallas_call | solution.py:574
  12.8 0.6 %collective-permute-start.7 = (bf16[40,40,128]{2,1,0:T(8,128)(2,1)S(1)}, bf16[40,40,128]{2,1,0:T(8,128)(2,1)S(1)}, u32[]{:S(2)}, u32[]{:S(2)}) collective-permute-start(bf16[40,40,128]{2,1,0:T(8,128)(2,1)S(1)} %get-tuple-element.49.own_ref), channel_id=1, source_target_pairs={{0,4},{1,8},{2,6},{3,10},{4,13},{5,1},{6,15},{7,3},{8,12},{9,0},{1... | collective-permute-start | bytes 1228808 | tf_op jit(solution)/shard_map/ppermute | solution.py:571
  13.3 0.2 collective-permute-done.3.block_ref
  13.5 3.6 %collective-permute-start.4 = (bf16[40,40,128]{2,1,0:T(8,128)(2,1)S(1)}, bf16[40,40,128]{2,1,0:T(8,128)(2,1)S(1)}, u32[]{:S(2)}, u32[]{:S(2)}) collective-permute-start(bf16[40,40,128]{2,1,0:T(8,128)(2,1)S(1)} %other.1.other_ref), channel_id=1, source_target_pairs={{0,4},{1,5},{2,6},{3,7},{4,0},{5,1},{6,2},{7,3},{8,12},{9,13},{10,... | collective-permute-start | bytes 1228808 | tf_op jit(solution)/shard_map/ppermute | solution.py:571
  17.1 0.0 collective-permute-done.5.block_ref
  17.1 2.5 %met.1 = (bf16[40,40,128]{2,1,0:T(8,128)(2,1)S(1)}, bf16[40,40,128]{2,1,0:T(8,128)(2,1)S(1)}) custom-call(bf16[43,40,128]{2,1,0:T(8,128)(2,1)S(1)} %collective-permute-done.5.block_ref, bf16[20,256,256]{2,1,0:T(8,128)(2,1)S(1)} %get-tuple-element.43.t_ref, bf16[2,40,256]{2,1,0:T(8,128)(2,1)S(1)} %get-tuple-element.44.right_ref, ...), custom_call_target="tpu_custom_call" | custom-call | bytes 11070000 | tf_op jit(solution)/shard_map/met/pallas_call | solution.py:574
  19.6 0.1 collective-permute-start.6
  19.7 1.9 %collective-permute-done.7.far_ref = bf16[40,40,128]{2,1,0:T(8,128)(2,1)S(1)} collective-permute-done((bf16[40,40,128]{2,1,0:T(8,128)(2,1)S(1)}, bf16[40,40,128]{2,1,0:T(8,128)(2,1)S(1)}, u32[]{:S(2)}, u32[]{:S(2)}) %collective-permute-start.7) | collective-permute-done | bytes 409632 | tf_op jit(solution)/shard_map/ppermute | solution.py:571
  21.7 0.0 collective-permute-start.8
  21.7 0.5 %rest.1 = (bf16[40,40,128]{2,1,0:T(8,128)(2,1)S(1)}, f32[40,40,128]{2,1,0:T(8,128)S(1)}) custom-call(bf16[41,40,128]{2,1,0:T(8,128)(2,1)S(1)} %get-tuple-element.39.block_ref, bf16[1600,128]{1,0:T(8,128)(2,1)S(1)} %get-tuple-element.59.norm_ref, bf16[128,512]{1,0:T(8,128)(2,1)S(1)} %get-tuple-element.47.win_ref, bf16[128,128]{1,0:T(8,128)(2,1)S(1)} %get-tuple-element.60.wgate_ref), custom_call_target="tpu_custom_call" | custom-call | bytes 2214000 | tf_op jit(solution)/shard_map/rest/pallas_call | solution.py:574
  22.2 0.0 collective-permute-done.4.p_other
  22.2 0.0 collective-permute-done.6.p_met
  22.2 1.2 %collective-permute-done.8.p_far = bf16[40,40,128]{2,1,0:T(8,128)(2,1)S(1)} collective-permute-done((bf16[40,40,128]{2,1,0:T(8,128)(2,1)S(1)}, bf16[40,40,128]{2,1,0:T(8,128)(2,1)S(1)}, u32[]{:S(2)}, u32[]{:S(2)}) %collective-permute-start.8) | collective-permute-done | bytes 409632 | tf_op jit(solution)/shard_map/ppermute | solution.py:571
  23.4 1.0 %sums.10 = bf16[8,40,128]{2,1,0:T(8,128)(2,1)S(1)} custom-call(bf16[40,40,128]{2,1,0:T(8,128)(2,1)S(1)} %get-tuple-element.49.own_ref, bf16[40,40,128]{2,1,0:T(8,128)(2,1)S(1)} %other.1.other_ref, bf16[40,40,128]{2,1,0:T(8,128)(2,1)S(1)} %collective-permute-done.4.p_other, bf16[40,40,128]{2,1,0:T(8,128)(2,1)S(1)} %get-tuple-element.56.met_ref, ...), custom_call_target="tpu_custom_call" | custom-call | bytes 3837600 | tf_op jit(solution)/shard_map/sums/pallas_call | solution.py:574
  24.5 2.7 %collective-permute-start.12 = (bf16[8,40,128]{2,1,0:T(8,128)(2,1)S(1)}, bf16[8,40,128]{2,1,0:T(8,128)(2,1)S(1)}, u32[]{:S(2)}, u32[]{:S(2)}) collective-permute-start(bf16[8,40,128]{2,1,0:T(8,128)(2,1)S(1)} %sums.10), channel_id=1, source_target_pairs={{0,2},{1,3},{2,0},{3,1},{4,6},{5,7},{6,4},{7,5},{8,10},{9,11},{10,... | collective-permute-start | bytes 245768 | tf_op jit(solution)/shard_map/ppermute | solution.py:571
  27.1 1.0 %sums.11 = bf16[8,40,128]{2,1,0:T(8,128)(2,1)S(1)} custom-call(bf16[40,40,128]{2,1,0:T(8,128)(2,1)S(1)} %get-tuple-element.49.own_ref, bf16[40,40,128]{2,1,0:T(8,128)(2,1)S(1)} %other.1.other_ref, bf16[40,40,128]{2,1,0:T(8,128)(2,1)S(1)} %collective-permute-done.4.p_other, bf16[40,40,128]{2,1,0:T(8,128)(2,1)S(1)} %get-tuple-element.56.met_ref, ...), custom_call_target="tpu_custom_call" | custom-call | bytes 3837600 | tf_op jit(solution)/shard_map/sums/pallas_call | solution.py:574
  28.2 0.4 collective-permute-start.13
  28.6 1.0 %sums.8 = bf16[8,40,128]{2,1,0:T(8,128)(2,1)S(1)} custom-call(bf16[40,40,128]{2,1,0:T(8,128)(2,1)S(1)} %get-tuple-element.49.own_ref, bf16[40,40,128]{2,1,0:T(8,128)(2,1)S(1)} %other.1.other_ref, bf16[40,40,128]{2,1,0:T(8,128)(2,1)S(1)} %collective-permute-done.4.p_other, bf16[40,40,128]{2,1,0:T(8,128)(2,1)S(1)} %get-tuple-element.56.met_ref, ...), custom_call_target="tpu_custom_call" | custom-call | bytes 3837600 | tf_op jit(solution)/shard_map/sums/pallas_call | solution.py:574
  29.6 2.7 %collective-permute-start.10 = (bf16[8,40,128]{2,1,0:T(8,128)(2,1)S(1)}, bf16[8,40,128]{2,1,0:T(8,128)(2,1)S(1)}, u32[]{:S(2)}, u32[]{:S(2)}) collective-permute-start(bf16[8,40,128]{2,1,0:T(8,128)(2,1)S(1)} %sums.8), channel_id=1, source_target_pairs={{0,2},{1,3},{2,0},{3,1},{4,6},{5,7},{6,4},{7,5},{8,10},{9,11},{10,... | collective-permute-start | bytes 245768 | tf_op jit(solution)/shard_map/ppermute | solution.py:571
  32.3 1.2 %sums.9 = bf16[8,40,128]{2,1,0:T(8,128)(2,1)S(1)} custom-call(bf16[40,40,128]{2,1,0:T(8,128)(2,1)S(1)} %get-tuple-element.49.own_ref, bf16[40,40,128]{2,1,0:T(8,128)(2,1)S(1)} %other.1.other_ref, bf16[40,40,128]{2,1,0:T(8,128)(2,1)S(1)} %collective-permute-done.4.p_other, bf16[40,40,128]{2,1,0:T(8,128)(2,1)S(1)} %get-tuple-element.56.met_ref, ...), custom_call_target="tpu_custom_call" | custom-call | bytes 3837600 | tf_op jit(solution)/shard_map/sums/pallas_call | solution.py:574
  33.5 0.4 collective-permute-start.11
  33.9 1.0 %sums.7 = bf16[8,40,128]{2,1,0:T(8,128)(2,1)S(1)} custom-call(bf16[40,40,128]{2,1,0:T(8,128)(2,1)S(1)} %get-tuple-element.49.own_ref, bf16[40,40,128]{2,1,0:T(8,128)(2,1)S(1)} %other.1.other_ref, bf16[40,40,128]{2,1,0:T(8,128)(2,1)S(1)} %collective-permute-done.4.p_other, bf16[40,40,128]{2,1,0:T(8,128)(2,1)S(1)} %get-tuple-element.56.met_ref, ...), custom_call_target="tpu_custom_call" | custom-call | bytes 3837600 | tf_op jit(solution)/shard_map/sums/pallas_call | solution.py:574
  34.9 2.7 %collective-permute-start.9 = (bf16[8,40,128]{2,1,0:T(8,128)(2,1)S(1)}, bf16[8,40,128]{2,1,0:T(8,128)(2,1)S(1)}, u32[]{:S(2)}, u32[]{:S(2)}) collective-permute-start(bf16[8,40,128]{2,1,0:T(8,128)(2,1)S(1)} %sums.7), channel_id=1, source_target_pairs={{0,2},{1,3},{2,0},{3,1},{4,6},{5,7},{6,4},{7,5},{8,10},{9,11},{10,... | collective-permute-start | bytes 245768 | tf_op jit(solution)/shard_map/ppermute | solution.py:571
  37.6 5.1 %sums.6.own_ref = f32[40,40,128]{2,1,0:T(8,128)S(1)} custom-call(bf16[40,40,128]{2,1,0:T(8,128)(2,1)S(1)} %get-tuple-element.49.own_ref, bf16[40,40,128]{2,1,0:T(8,128)(2,1)S(1)} %other.1.other_ref, bf16[40,40,128]{2,1,0:T(8,128)(2,1)S(1)} %collective-permute-done.4.p_other, bf16[40,40,128]{2,1,0:T(8,128)(2,1)S(1)} %get-tuple-element.56.met_ref, ...), custom_call_target="tpu_custom_call" | custom-call | bytes 19188000 | tf_op jit(solution)/shard_map/sums/pallas_call | solution.py:574
  42.7 0.0 collective-permute-done.12.refs_0_
  42.7 0.0 collective-permute-done.13.refs_1_
  42.8 1.1 %join.3.refs_2_ = bf16[40,40,128]{2,1,0:T(8,128)(2,1)} custom-call(f32[40,40,128]{2,1,0:T(8,128)S(1)} %sums.6.own_ref, bf16[40,40,128]{2,1,0:T(8,128)(2,1)S(1)} %get-tuple-element.62.psum_ref, f32[40,40,128]{2,1,0:T(8,128)S(1)} %get-tuple-element.63.gate_ref, bf16[128,128]{1,0:T(8,128)(2,1)S(1)} %get-tuple-element.64.w_ref, ...), custom_call_target="tpu_custom_call" | custom-call | bytes 3542400 | tf_op jit(solution)/shard_map/join/pallas_call | solution.py:669
  43.8 0.0 collective-permute-done.10.refs_0_
  43.8 0.0 collective-permute-done.11.refs_1_
  43.9 1.1 %join.4.refs_1_ = bf16[40,40,128]{2,1,0:T(8,128)(2,1)} custom-call(f32[40,40,128]{2,1,0:T(8,128)S(1)} %sums.6.own_ref, bf16[40,40,128]{2,1,0:T(8,128)(2,1)S(1)} %get-tuple-element.62.psum_ref, f32[40,40,128]{2,1,0:T(8,128)S(1)} %get-tuple-element.63.gate_ref, bf16[128,128]{1,0:T(8,128)(2,1)S(1)} %get-tuple-element.64.w_ref, ...), custom_call_target="tpu_custom_call", output_to_operand_aliasing={{}: (6, {})} | custom-call | bytes 3542400 | tf_op jit(solution)/shard_map/join/pallas_call | solution.py:669
  44.9 0.6 %collective-permute-done.9.refs_0_ = bf16[8,40,128]{2,1,0:T(8,128)(2,1)S(1)} collective-permute-done((bf16[8,40,128]{2,1,0:T(8,128)(2,1)S(1)}, bf16[8,40,128]{2,1,0:T(8,128)(2,1)S(1)}, u32[]{:S(2)}, u32[]{:S(2)}) %collective-permute-start.9) | collective-permute-done | bytes 81952 | tf_op jit(solution)/shard_map/ppermute | solution.py:571
  45.5 1.0 %join.5 = bf16[40,40,128]{2,1,0:T(8,128)(2,1)} custom-call(f32[40,40,128]{2,1,0:T(8,128)S(1)} %sums.6.own_ref, bf16[40,40,128]{2,1,0:T(8,128)(2,1)S(1)} %get-tuple-element.62.psum_ref, f32[40,40,128]{2,1,0:T(8,128)S(1)} %get-tuple-element.63.gate_ref, bf16[128,128]{1,0:T(8,128)(2,1)S(1)} %get-tuple-element.64.w_ref, ...), custom_call_target="tpu_custom_call", output_to_operand_aliasing={{}: (5, {})} | custom-call | bytes 1771200 | tf_op jit(solution)/shard_map/join/pallas_call | solution.py:669
  (2 shorter events, 0.0 us)
Async XLA Ops:
  1.6 15.5 %collective-permute-start.5 = (bf16[43,40,128]{2,1,0:T(8,128)(2,1)S(1)}, bf16[43,40,128]{2,1,0:T(8,128)(2,1)S(1)}, u32[]{:S(2)}, u32[]{:S(2)}) collective-permute-start(bf16[43,40,128]{2,1,0:T(8,128)(2,1)S(1)} %get-tuple-element.54), channel_id=1, source_target_pairs={{0,1},{1,0},{2,3},{3,2},{4,5},{5,4},{6,7},{7,6},{8,9},{9,8},{10,11... | collective-permute-start | bytes 1320968 | tf_op jit(solution)/shard_map/ppermute | solution.py:571
  4.7 4.1 %collective-permute-start = (bf16[48,256]{1,0:T(8,128)(2,1)S(1)}, bf16[48,256]{1,0:T(8,128)(2,1)S(1)}, u32[]{:S(2)}, u32[]{:S(2)}) collective-permute-start(bf16[48,256]{1,0:T(8,128)(2,1)S(1)} %get-tuple-element.36), channel_id=1, source_target_pairs={{0,4},{4,0},{8,12},{12,8},{1,5},{5,1},{9,13},{13,9},{2,6},{6,2},{1... | collective-permute-start | bytes 73736 | tf_op jit(solution)/shard_map/ppermute | solution.py:608
  4.7 4.1 %collective-permute-start.1 = (bf16[48,256]{1,0:T(8,128)(2,1)S(1)}, bf16[48,256]{1,0:T(8,128)(2,1)S(1)}, u32[]{:S(2)}, u32[]{:S(2)}) collective-permute-start(bf16[48,256]{1,0:T(8,128)(2,1)S(1)} %get-tuple-element.37), channel_id=1, source_target_pairs={{0,8},{4,12},{8,0},{12,4},{1,9},{5,13},{9,1},{13,5},{2,10},{6,14},... | collective-permute-start | bytes 73736 | tf_op jit(solution)/shard_map/ppermute | solution.py:608
  6.2 3.3 %collective-permute-start.2 = (bf16[48,256]{1,0:T(8,128)(2,1)S(1)}, bf16[48,256]{1,0:T(8,128)(2,1)S(1)}, u32[]{:S(2)}, u32[]{:S(2)}) collective-permute-start(bf16[48,256]{1,0:T(8,128)(2,1)S(1)} %get-tuple-element.38), channel_id=1, source_target_pairs={{0,12},{4,8},{8,4},{12,0},{1,13},{5,9},{9,5},{13,1},{2,14},{6,10},... | collective-permute-start | bytes 73736 | tf_op jit(solution)/shard_map/ppermute | solution.py:608
  6.6 7.0 %collective-permute-start.3 = (bf16[41,40,128]{2,1,0:T(8,128)(2,1)S(1)}, bf16[41,40,128]{2,1,0:T(8,128)(2,1)S(1)}, u32[]{:S(2)}, u32[]{:S(2)}) collective-permute-start(bf16[41,40,128]{2,1,0:T(8,128)(2,1)S(1)} %get-tuple-element.39.block_ref), channel_id=1, source_target_pairs={{0,12},{1,5},{2,14},{3,7},{4,0},{5,9},{6,2},{7,11},{8,4},{9,13},{1... | collective-permute-start | bytes 1259528 | tf_op jit(solution)/shard_map/ppermute | solution.py:571
  12.8 8.9 %collective-permute-start.7 = (bf16[40,40,128]{2,1,0:T(8,128)(2,1)S(1)}, bf16[40,40,128]{2,1,0:T(8,128)(2,1)S(1)}, u32[]{:S(2)}, u32[]{:S(2)}) collective-permute-start(bf16[40,40,128]{2,1,0:T(8,128)(2,1)S(1)} %get-tuple-element.49.own_ref), channel_id=1, source_target_pairs={{0,4},{1,8},{2,6},{3,10},{4,13},{5,1},{6,15},{7,3},{8,12},{9,0},{1... | collective-permute-start | bytes 1228808 | tf_op jit(solution)/shard_map/ppermute | solution.py:571
  13.5 8.6 %collective-permute-start.4 = (bf16[40,40,128]{2,1,0:T(8,128)(2,1)S(1)}, bf16[40,40,128]{2,1,0:T(8,128)(2,1)S(1)}, u32[]{:S(2)}, u32[]{:S(2)}) collective-permute-start(bf16[40,40,128]{2,1,0:T(8,128)(2,1)S(1)} %other.1.other_ref), channel_id=1, source_target_pairs={{0,4},{1,5},{2,6},{3,7},{4,0},{5,1},{6,2},{7,3},{8,12},{9,13},{10,... | collective-permute-start | bytes 1228808 | tf_op jit(solution)/shard_map/ppermute | solution.py:571
  19.6 2.5 %collective-permute-start.6 = (bf16[40,40,128]{2,1,0:T(8,128)(2,1)S(1)}, bf16[40,40,128]{2,1,0:T(8,128)(2,1)S(1)}, u32[]{:S(2)}, u32[]{:S(2)}) collective-permute-start(bf16[40,40,128]{2,1,0:T(8,128)(2,1)S(1)} %get-tuple-element.56.met_ref), channel_id=1, source_target_pairs={{0,4},{1,5},{2,6},{3,7},{4,0},{5,1},{6,2},{7,3},{8,12},{9,13},{10,... | collective-permute-start | bytes 1228808 | tf_op jit(solution)/shard_map/ppermute | solution.py:571
  21.7 1.7 %collective-permute-start.8 = (bf16[40,40,128]{2,1,0:T(8,128)(2,1)S(1)}, bf16[40,40,128]{2,1,0:T(8,128)(2,1)S(1)}, u32[]{:S(2)}, u32[]{:S(2)}) collective-permute-start(bf16[40,40,128]{2,1,0:T(8,128)(2,1)S(1)} %collective-permute-done.7.far_ref), channel_id=1, source_target_pairs={{0,4},{1,5},{2,6},{3,7},{4,0},{5,1},{6,2},{7,3},{8,12},{9,13},{10,... | collective-permute-start | bytes 1228808 | tf_op jit(solution)/shard_map/ppermute | solution.py:571
  24.5 18.3 %collective-permute-start.12 = (bf16[8,40,128]{2,1,0:T(8,128)(2,1)S(1)}, bf16[8,40,128]{2,1,0:T(8,128)(2,1)S(1)}, u32[]{:S(2)}, u32[]{:S(2)}) collective-permute-start(bf16[8,40,128]{2,1,0:T(8,128)(2,1)S(1)} %sums.10), channel_id=1, source_target_pairs={{0,2},{1,3},{2,0},{3,1},{4,6},{5,7},{6,4},{7,5},{8,10},{9,11},{10,... | collective-permute-start | bytes 245768 | tf_op jit(solution)/shard_map/ppermute | solution.py:571
  28.2 14.6 %collective-permute-start.13 = (bf16[8,40,128]{2,1,0:T(8,128)(2,1)S(1)}, bf16[8,40,128]{2,1,0:T(8,128)(2,1)S(1)}, u32[]{:S(2)}, u32[]{:S(2)}) collective-permute-start(bf16[8,40,128]{2,1,0:T(8,128)(2,1)S(1)} %sums.11), channel_id=1, source_target_pairs={{0,2},{1,3},{2,0},{3,1},{4,6},{5,7},{6,4},{7,5},{8,10},{9,11},{10,... | collective-permute-start | bytes 245768 | tf_op jit(solution)/shard_map/ppermute | solution.py:571
  29.6 14.2 %collective-permute-start.10 = (bf16[8,40,128]{2,1,0:T(8,128)(2,1)S(1)}, bf16[8,40,128]{2,1,0:T(8,128)(2,1)S(1)}, u32[]{:S(2)}, u32[]{:S(2)}) collective-permute-start(bf16[8,40,128]{2,1,0:T(8,128)(2,1)S(1)} %sums.8), channel_id=1, source_target_pairs={{0,2},{1,3},{2,0},{3,1},{4,6},{5,7},{6,4},{7,5},{8,10},{9,11},{10,... | collective-permute-start | bytes 245768 | tf_op jit(solution)/shard_map/ppermute | solution.py:571
  33.5 10.3 %collective-permute-start.11 = (bf16[8,40,128]{2,1,0:T(8,128)(2,1)S(1)}, bf16[8,40,128]{2,1,0:T(8,128)(2,1)S(1)}, u32[]{:S(2)}, u32[]{:S(2)}) collective-permute-start(bf16[8,40,128]{2,1,0:T(8,128)(2,1)S(1)} %sums.9), channel_id=1, source_target_pairs={{0,2},{1,3},{2,0},{3,1},{4,6},{5,7},{6,4},{7,5},{8,10},{9,11},{10,... | collective-permute-start | bytes 245768 | tf_op jit(solution)/shard_map/ppermute | solution.py:571
  34.9 10.6 %collective-permute-start.9 = (bf16[8,40,128]{2,1,0:T(8,128)(2,1)S(1)}, bf16[8,40,128]{2,1,0:T(8,128)(2,1)S(1)}, u32[]{:S(2)}, u32[]{:S(2)}) collective-permute-start(bf16[8,40,128]{2,1,0:T(8,128)(2,1)S(1)} %sums.7), channel_id=1, source_target_pairs={{0,2},{1,3},{2,0},{3,1},{4,6},{5,7},{6,4},{7,5},{8,10},{9,11},{10,... | collective-permute-start | bytes 245768 | tf_op jit(solution)/shard_map/ppermute | solution.py:571
